TPU v7x, 32 devices: a whole 2x2x4 slice. The times are simulated.
32 devices in a mesh: group: 2 (over y), dp: 4 (over z), ctx: 4 (over x, core).
Axes of the slice: x: 2, y: 2, z: 4, core: 2. Of those that a mesh axis runs over, the one named last changes fastest.
Arguments:
- query_rows: bfloat16 [8, 640, 2048], P(('group', 'dp'), 'ctx'), parts along dimension 0, may hold values from -6 to 6
- key_rows: bfloat16 [8, 640, 512], P(('group', 'dp'), 'ctx'), parts along dimension 0, may hold values from -6 to 6
- value_rows: bfloat16 [8, 640, 512], P(('group', 'dp'), 'ctx'), parts along dimension 0, may hold values from -6 to 6
- cotangent: bfloat16 [8, 640, 2048], P(('group', 'dp'), 'ctx'), parts along dimension 0, may hold values from -6 to 6
- router_gate: float32 [8, 640], P(('group', 'dp'), 'ctx'), parts along dimension 0, may hold values from 0.25 to 1
- positions: int32 [8, 640], P(('group', 'dp'), 'ctx'), parts along dimension 0, may hold values from 0 to 4096, as said below
Outputs:
- query_grad: bfloat16 [8, 640, 2048], P(('group', 'dp'), 'ctx'), parts along dimension 0
- key_grad: bfloat16 [8, 640, 512], P(('group', 'dp'), 'ctx'), parts along dimension 0
- value_grad: bfloat16 [8, 640, 512], P(('group', 'dp'), 'ctx'), parts along dimension 0
- gate_grad: float32 [8, 640], P(('group', 'dp'), 'ctx'), parts along dimension 0
There are 2 independent parts, one for each index of `group`. A program takes and returns all parts, laid end to end along the dimension named above; each array names one. Nothing has to cross between parts.
Inputs may be any that keep to these rules, and one draw needn't show every extreme that they name: In each sequence, slot block c (slots c * 160 to c * 160 + 159) holds in rising order the routed positions among positions c * 1024 to c * 1024 + 1023, then 4096 in every unused slot. The first and last position of every block of 1024 positions are routed; a sequence routes 128 tokens for each block on average, and some block fills all 160 slots.
All inputs are finite; a program needn't handle non-finite values.
Results may differ from a plain program's by a relative error of at most 0.02.
Values may be sent and summed in bfloat16 or wider, within the bound.
No kernel may reach another device: no remote copies, remote signals or barrier semaphores. Data moves between devices by JAX's collectives and lax.ppermute only.
A program may use at most 128 MiB of HBM per device.

v0:
```python
import jax
import jax.numpy as jnp
from jax import lax
from jax.sharding import PartitionSpec as P

DH = 128
LOCAL = 1024


THETA = 500000.0


def rotate(values, places, sign):
    half = values.shape[-1] // 2
    freq = jnp.power(
        jnp.float32(THETA), -2.0 * jnp.arange(half, dtype=jnp.float32) / values.shape[-1]
    )
    angle = places[:, None] * freq[None, :]
    cosine = jnp.cos(angle)[:, None, :]
    sine = sign * jnp.sin(angle)[:, None, :]
    first = values[..., :half]
    second = values[..., half:]
    return jnp.concatenate(
        [first * cosine - second * sine, second * cosine + first * sine], axis=-1
    )


def per_device(query_rows, key_rows, value_rows, cotangent, router_gate, positions):
    heads_width = query_rows.shape[2]
    group_width = key_rows.shape[2]
    groups = group_width // DH
    ratio = heads_width // group_width
    local_rows = query_rows.shape[1]
    parts = lax.axis_size("ctx")
    own_index = lax.axis_index("ctx")
    scale = DH ** (-0.5)
    places_int = positions[0]
    valid = places_int < parts * LOCAL
    places = places_int.astype(jnp.float32)
    query_rot = rotate(
        query_rows[0].astype(jnp.float32).reshape(local_rows, heads_width // DH, DH), places, 1.0
    ).astype(jnp.bfloat16)
    query_rot = query_rot.reshape(local_rows, groups, ratio, DH).transpose(1, 2, 0, 3)
    key_rot = rotate(
        key_rows[0].astype(jnp.float32).reshape(local_rows, groups, DH), places, 1.0
    ).astype(jnp.bfloat16)
    key_rot = key_rot.reshape(local_rows, group_width)
    value_own = value_rows[0]
    live_count = jnp.sum(valid.astype(jnp.int32)).reshape(1)
    all_counts = lax.all_gather(live_count, "ctx", axis=0, tiled=True)
    query_slot = jnp.arange(local_rows, dtype=jnp.int32)
    device_ids = jnp.arange(parts, dtype=jnp.int32)
    grad_full = (
        cotangent[0]
        .astype(jnp.float32)
        .reshape(local_rows, groups, ratio, DH)
        .transpose(1, 2, 0, 3)
    )
    gate_used = jnp.where(valid, router_gate[0], 0.0)

    def visible(width):
        slot = jnp.arange(width, dtype=jnp.int32)
        owner = slot // local_rows
        inner = slot % local_rows
        owner_count = jnp.sum(
            jnp.where(owner[:, None] == device_ids[None, :], all_counts[None, :], 0), axis=1
        )
        before = owner[None, :] < own_index
        same_block = (owner[None, :] == own_index) & (inner[None, :] <= query_slot[:, None])
        return (before | same_block) & (inner < owner_count)[None, :]

    def piece_scores(key_piece):
        width = key_piece.shape[0]
        mask = visible(width)[None, None]
        grouped = key_piece.reshape(width, groups, DH)
        raw = (
            jnp.einsum("grcd,ngd->grcn", query_rot, grouped, preferred_element_type=jnp.float32)
            * scale
        )
        return (mask, jnp.where(mask, raw, -1e30))

    running_max = jnp.full((groups, ratio, local_rows), -1e30, jnp.float32)
    key_piece = lax.all_gather(key_rot, "ctx", axis=0, tiled=True)
    value_piece = lax.all_gather(value_own, "ctx", axis=0, tiled=True)
    mask, scores = piece_scores(key_piece)
    new_max = jnp.maximum(running_max, jnp.max(scores, axis=-1))
    exp_scores = jnp.where(mask, jnp.exp(scores - new_max[..., None]), 0.0)
    grouped_values = value_piece.reshape(key_piece.shape[0], groups, DH)
    update = jnp.einsum(
        "grcn,ngd->grcd",
        exp_scores.astype(jnp.bfloat16),
        grouped_values,
        preferred_element_type=jnp.float32,
    )
    running_sum = jnp.sum(exp_scores, axis=-1)
    log_total = new_max + jnp.log(running_sum)
    attn = update / running_sum[..., None]
    gate_grad = jnp.where(valid, jnp.sum(grad_full * attn, axis=(0, 1, 3)), 0.0)
    out_grad = (grad_full * gate_used[None, None, :, None]).astype(jnp.bfloat16)
    delta = jnp.sum(out_grad.astype(jnp.float32) * attn, axis=-1)
    log_total, out_grad, delta, gate_grad = (log_total, out_grad, delta, gate_grad)
    key_piece = lax.all_gather(key_rot, "ctx", axis=0, tiled=True)
    value_piece = lax.all_gather(value_own, "ctx", axis=0, tiled=True)
    width = key_piece.shape[0]
    piece_width = key_piece.shape[0]
    mask, scores = piece_scores(key_piece)
    exact_weights = jnp.where(mask, jnp.exp(scores - log_total[..., None]), 0.0)
    weights_low = exact_weights.astype(jnp.bfloat16)
    grouped_values = value_piece.reshape(piece_width, groups, DH)
    prob_grad = jnp.einsum(
        "grcd,ngd->grcn", out_grad, grouped_values, preferred_element_type=jnp.float32
    )
    score_grad = (exact_weights * (prob_grad - delta[..., None])).astype(jnp.bfloat16)
    weights_low, score_grad = (weights_low, score_grad)
    grouped_keys = key_piece.reshape(width, groups, DH)
    query_acc = jnp.einsum(
        "grcn,ngd->grcd", score_grad, grouped_keys, preferred_element_type=jnp.float32
    )
    key_part = (
        jnp.einsum("grcn,grcd->ngd", score_grad, query_rot, preferred_element_type=jnp.float32)
        * scale
    )
    value_part = jnp.einsum(
        "grcn,grcd->ngd", weights_low, out_grad, preferred_element_type=jnp.float32
    )
    block = jnp.concatenate(
        [key_part.reshape(width, group_width), value_part.reshape(width, group_width)], axis=1
    ).astype(jnp.bfloat16)
    back_result = (query_acc, block)
    query_acc = back_result[0]
    summed = lax.psum_scatter(
        back_result[1].astype(jnp.float32).astype(jnp.bfloat16),
        "ctx",
        scatter_dimension=0,
        tiled=True,
    ).astype(jnp.float32)
    query_grad = rotate(
        (query_acc * scale).transpose(2, 0, 1, 3).reshape(local_rows, heads_width // DH, DH),
        places,
        -1.0,
    )
    query_grad = query_grad.astype(jnp.bfloat16).reshape(local_rows, heads_width)
    key_grad = (
        rotate(summed[:, :group_width].reshape(local_rows, groups, DH), places, -1.0)
        .astype(jnp.bfloat16)
        .reshape(local_rows, group_width)
    )
    value_grad = summed[:, group_width:].astype(jnp.bfloat16)
    return (query_grad[None], key_grad[None], value_grad[None], gate_grad[None])


def solution(mesh):
    in_specs = (
        P(("group", "dp"), "ctx", None),
        P(("group", "dp"), "ctx", None),
        P(("group", "dp"), "ctx", None),
        P(("group", "dp"), "ctx", None),
        P(("group", "dp"), "ctx"),
        P(("group", "dp"), "ctx"),
    )
    out_specs = (
        P(("group", "dp"), "ctx", None),
        P(("group", "dp"), "ctx", None),
        P(("group", "dp"), "ctx", None),
        P(("group", "dp"), "ctx"),
    )
    return jax.shard_map(
        per_device, mesh=mesh, in_specs=in_specs, out_specs=out_specs, check_vma=False
    )
```

profile of v0, /device:TPU:0, one launch (start us, length us, event | category | flops | bytes accessed | tf_op | source)
XLA Modules:
  0.0 104.6 jit_solution(16296135337730201016)
XLA Ops:
  7.2 0.0 reduce-scatter.2.cloned.1.call-start
  7.3 1.4 %convert_reduce_fusion = (s32[]{:T(128)}, f32[1,160]{1,0:T(1,128)S(1)}) fusion(s32[1,160]{1,0:T(1,128)} %param.11), kind=kLoop, calls=%fused_computation.67 | loop fusion | flops 639 | bytes 1284 | tf_op jit(solution)/shard_map/reduce_sum | solution.py:49
  8.7 1.0 reshape.306
  9.7 0.0 copy-start.8
  9.7 0.4 broadcast_multiply_fusion
  10.1 0.3 subtract_convert_fusion.3
  10.4 0.2 pad_maximum_fusion.2
  10.7 9.3 %all_gather.12 = bf16[640,512]{1,0:T(8,128)(2,1)S(1)} all-gather(bf16[160,512]{1,0:T(8,128)(2,1)S(1)} %bitcast.87), channel_id=1, replica_groups=mesh['group'=2,'dp'=4,'ctx'=4] {'ctx'}, dimensions={0}, use_global_device_ids=true | all-gather | bytes 819200 | tf_op jit(solution)/shard_map/all_gather | solution.py:102
  20.0 0.1 convert_bitcast_fusion
  20.1 0.2 copy.74
  20.4 0.0 copy-start.12
  20.4 1.9 %fusion.44 = (f32[160,16,64]{2,1,0:T(8,128)}, f32[160,16,64]{2,1,0:T(8,128)}) fusion(f32[160,16,128]{2,1,0:T(8,128)S(1)} %bitcast.75), kind=kLoop, calls=%fused_computation.80 | loop fusion | bytes 2621440 | tf_op jit(solution)/shard_map/slice | solution.py:21
  22.3 0.6 dynamic-slice
  22.9 1.4 %dynamic-update-slice = s32[4]{0:T(128)S(1)} dynamic-update-slice(s32[4]{0:T(128)S(1)} %broadcast.244, s32[1]{0:T(128)} %bitcast, u32[]{:T(128)} %bitcast.1) | dynamic-update-slice | bytes 12
  24.3 0.3 copy.48
  24.6 4.5 %all-reduce = s32[4]{0:T(128)S(1)} all-reduce(s32[4]{0:T(128)S(1)} %dynamic-update-slice), channel_id=1, replica_groups=mesh['group'=2,'dp'=4,'ctx'=4] {'ctx'}, use_global_device_ids=true, to_apply=%add | all-reduce | flops 4 | bytes 32
  29.2 0.1 select_reduce_fusion
  29.3 2.6 %subtract_convert_fusion.1 = (bf16[160,16,64]{2,0,1:T(8,128)(2,1)S(1)}, bf16[160,16,64]{2,0,1:T(8,128)(2,1)S(1)}) fusion(f32[160,16,64]{2,1,0:T(8,128)} %get-tuple-element.12, f32[160,16,64]{2,1,0:T(8,128)} %get-tuple-element.11, f32[160,64]{1,0:T(8,128)S(1)} %get-tuple-element.20, f32[160,64]{1,0:T(8,128)S(1)} %get-tuple-element.21), kind=kLoop, calls=%fused_computation.28 | loop fusion | flops 1310720 | bytes 2048000 | tf_op jit(solution)/shard_map/convert.20
  31.9 0.1 fusion.25
  32.0 1.9 %fusion.3 = (f32[4,4,160]{2,1,0:T(4,128)S(1)}, f32[4,4,160,640]{3,2,1,0:T(8,128)S(1)}) fusion(pred[160,640]{1,0:T(8,128)(4,1)S(1)} %fusion.25, bf16[640,4,128,1]{0,2,3,1:T(8,128)(2,1)S(1)} %bitcast.76, bf16[160,4,4,64]{3,0,2,1:T(8,128)(2,1)S(1)} %bitcast.80, bf16[160,4,4,64]{3,0,2,1:T(8,128)(2,1)S(1)} %bitcast.78), kind=kOutput, calls=%fused_computation.7 | convolution fusion | flops 425653760 | bytes 7976960 | tf_op jit(solution)/shard_map/grcd,ngd->grcn/dot_general | solution.py:77
  33.9 0.0 copy-start.9
  33.9 2.2 %fusion.1 = f32[4,4,160]{2,1,0:T(4,128)S(1)} fusion(f32[4,4,160,640]{3,2,1,0:T(8,128)S(1)} %get-tuple-element.25, f32[4,4,160]{2,1,0:T(4,128)S(1)} %broadcast_maximum_fusion, pred[160,640]{1,0:T(8,128)(4,1)S(1)} %fusion.25), kind=kLoop, calls=%fused_computation.5 | loop fusion | flops 8189440 | bytes 6676480 | tf_op jit(solution)/shard_map/reduce_sum | solution.py:95
  36.1 0.5 copy-done
  36.7 7.5 %all-gather = bf16[1,640,512]{2,1,0:T(8,128)(2,1)S(1)} all-gather(bf16[1,160,512]{2,1,0:T(8,128)(2,1)S(1)} %copy-done.9), channel_id=2, replica_groups=mesh['group'=2,'dp'=4,'ctx'=4] {'ctx'}, dimensions={1}, use_global_device_ids=true | all-gather | bytes 819200 | tf_op jit(solution)/shard_map/all_gather | solution.py:103
  44.2 1.1 %copy.51 = bf16[1,640,512]{1,2,0:T(8,128)(2,1)} copy(bf16[1,640,512]{2,1,0:T(8,128)(2,1)S(1)} %all-gather) | data formatting | bytes 1310720 | tf_op jit(solution)/shard_map/all_gather | solution.py:103
  45.3 3.0 %reshape.309 = f32[160,4,4,128]{3,2,1,0:T(4,128)} reshape(bf16[1,160,2048]{2,1,0:T(8,128)(2,1)} %param.9) | data formatting | bytes 1966080 | tf_op jit(solution)/shard_map/transpose | solution.py:57
  48.3 6.5 %fusion.19 = (f32[160]{0:T(256)S(1)}, f32[4,4,160]{2,1,0:T(4,128)S(1)}, bf16[4,4,160,128]{3,2,1,0:T(8,128)(2,1)S(1)}) fusion(f32[160,4,4,128]{3,2,1,0:T(4,128)} %reshape.309, f32[160]{0:T(256)S(1)} %bitcast.90, f32[4,4,160]{2,1,0:T(4,128)S(1)} %fusion.1, bf16[640,4,128,1]{0,2,3,1:T(8,128)(2,1)} %bitcast.83, f32[4,4,160,640]{3,2,1,0:T(8,128)} %copy-done, ...), kind=kOutput, calls=%fused_computation.22 | convolution fusion | flops 430241120 | bytes 9309440 | tf_op jit(solution)/shard_map/grcn,ngd->grcd/dot_general | solution.py:89
  54.9 0.0 copy-start.6
  54.9 2.9 %fusion.14 = bf16[4,128,640]{2,1,0:T(8,128)(2,1)} fusion(bf16[4,4,160,128]{3,2,1,0:T(8,128)(2,1)S(1)} %get-tuple-element.6, f32[4,4,160,640]{3,2,1,0:T(8,128)S(1)} %bitcast.73, f32[4,4,160]{2,1,0:T(4,128)S(1)} %log_add_fusion, pred[160,640]{1,0:T(8,128)(4,1)S(1)} %fusion.25), kind=kOutput, calls=%fused_computation.16 | convolution fusion | flops 427950080 | bytes 7976960 | tf_op jit(solution)/shard_map/grcn,grcd->ngd/dot_general | solution.py:123
  57.8 2.7 %multiply_convert_fusion = bf16[4,4,160,640]{3,2,1,0:T(8,128)(2,1)S(1)} fusion(f32[4,4,160,640]{3,2,1,0:T(8,128)S(1)} %bitcast.73, f32[4,4,160]{2,1,0:T(4,128)S(1)} %get-tuple-element.5, f32[4,4,160]{2,1,0:T(4,128)S(1)} %log_add_fusion, pred[160,640]{1,0:T(8,128)(4,1)S(1)} %fusion.25, bf16[4,4,160,128]{3,2,1,0:T(8,128)(2,1)S(1)} %get-tuple-element.6, ...), kind=kOutput, calls=%fused_computation | convolution fusion | flops 430899200 | bytes 11264000 | tf_op jit(solution)/shard_map/grcd,ngd->grcn/dot_general | solution.py:110
  60.5 1.2 %fusion.17 = bf16[4,128,640]{2,1,0:T(8,128)(2,1)S(1)} fusion(bf16[4,4,160,640]{3,2,1,0:T(8,128)(2,1)S(1)} %multiply_convert_fusion, bf16[160,4,4,64]{3,0,2,1:T(8,128)(2,1)S(1)} %bitcast.81, bf16[160,4,4,64]{3,0,2,1:T(8,128)(2,1)S(1)} %bitcast.79), kind=kOutput, calls=%fused_computation.17 | convolution fusion | flops 421396480 | bytes 4587520 | tf_op jit(solution)/shard_map/grcn,grcd->ngd/dot_general | solution.py:120
  61.8 0.5 copy-done.1
  62.2 1.1 %copy.56 = bf16[640,512]{1,0:T(8,128)(2,1)} copy(bf16[640,512]{0,1:T(8,128)(2,1)S(1)} %bitcast.82) | data formatting | bytes 1310720 | tf_op jit(solution)/shard_map/reshape | solution.py:127
  63.3 1.1 %copy.57 = bf16[640,512]{1,0:T(8,128)(2,1)} copy(bf16[640,512]{0,1:T(8,128)(2,1)S(1)} %bitcast.85) | data formatting | bytes 1310720 | tf_op jit(solution)/shard_map/reshape | solution.py:127
  64.4 2.6 %pad_maximum_fusion = bf16[640,1024]{1,0:T(8,128)(2,1)} fusion(bf16[640,512]{1,0:T(8,128)(2,1)} %copy.57, bf16[640,512]{1,0:T(8,128)(2,1)} %copy.56), kind=kLoop, calls=%fused_computation.18 | loop fusion | flops 2621440 | bytes 2621440 | tf_op jit(solution)/shard_map/concatenate | solution.py:126
  67.1 0.0 reduce-scatter.2.cloned.1.call-update
  67.1 2.1 %convolution_multiply_fusion = f32[4,4,160,128]{3,2,1,0:T(8,128)S(1)} fusion(bf16[4,4,160,640]{3,2,1,0:T(8,128)(2,1)S(1)} %copy-done.2, bf16[640,4,128,1]{0,2,3,1:T(8,128)(2,1)} %bitcast.77), kind=kOutput, calls=%fused_computation.15 | convolution fusion | flops 419758080 | bytes 5242880 | tf_op jit(solution)/shard_map/grcn,ngd->grcd/dot_general | solution.py:116
  69.2 0.5 subtract_convert_fusion
  69.7 0.4 pad_maximum_fusion.1
  70.1 0.3 copy.55
  70.3 1.1 %convert_element_type.95 = bf16[1,160,2048]{2,1,0:T(8,128)(2,1)} reshape(bf16[160,16,128]{2,1,0:T(8,128)(2,1)S(1)} %copy.55) | data formatting | bytes 1310720 | tf_op jit(solution)/shard_map/convert_element_type | solution.py:142
  71.5 0.6 broadcast_select_fusion
  72.0 22.6 %reduce-scatter.2.cloned.1.call-done = bf16[160,1024]{1,0:T(8,128)(2,1)} async-done(((bf16[640,1024]{1,0:T(8,128)(2,1)}), bf16[160,1024]{1,0:T(8,128)(2,1)}) %reduce-scatter.2.cloned.1.call-update) | async-done | bytes 327696 | tf_op jit(solution)/shard_map/reduce_scatter | solution.py:131
  94.7 1.7 %slice_bitcast_fusion = (bf16[1,160,512]{2,1,0:T(8,128)(2,1)}, f32[160,512]{1,0:T(8,128)S(1)}) fusion(bf16[160,1024]{1,0:T(8,128)(2,1)} %reduce-scatter.2.cloned.1.call-done), kind=kLoop, calls=%fused_computation.41 | loop fusion | flops 81920 | bytes 819200 | tf_op jit(solution)/shard_map/broadcast_in_dim | solution.py:149
  96.4 0.1 reshape.308
  96.5 0.3 subtract_convert_fusion.2
  96.8 0.2 pad_maximum_fusion.3
  97.1 0.7 convert_element_type.97
  (35 shorter events, 0.2 us)
Async XLA Ops:
  7.2 87.5 %reduce-scatter.2.cloned.1.call-start = ((), (), s32[]{:S(2)}) async-start(), calls=%async_computation.1 | async-start | bytes 1638400 | tf_op jit(solution)/shard_map/reduce_scatter | solution.py:131
  9.7 10.3 %copy-start.8 = (bf16[1,160,2048]{2,1,0:T(8,128)(2,1)S(1)}, bf16[1,160,2048]{2,1,0:T(8,128)(2,1)}, u32[]{:S(2)}) copy-start(bf16[1,160,2048]{2,1,0:T(8,128)(2,1)} %param.6) | copy-start | bytes 1966084
  20.4 2.0 %copy-start.12 = (u32[32]{0:T(128)S(1)}, u32[32]{0:T(128)}, u32[]{:S(2)}) copy-start(u32[32]{0:T(128)} %constant.60) | copy-start | bytes 388
  24.6 7.4 %copy-start.3 = (bf16[640,512]{0,1:T(8,128)(2,1)}, bf16[640,512]{0,1:T(8,128)(2,1)S(1)}, u32[]{:S(2)}) copy-start(bf16[640,512]{0,1:T(8,128)(2,1)S(1)} %copy.48) | copy-start | bytes 1966084
  31.9 2.0 %copy-start.4 = (bf16[160,16,64]{2,0,1:T(8,128)(2,1)}, bf16[160,16,64]{2,0,1:T(8,128)(2,1)S(1)}, u32[]{:S(2)}) copy-start(bf16[160,16,64]{2,0,1:T(8,128)(2,1)S(1)} %get-tuple-element.8) | copy-start | bytes 983044
  33.9 2.7 %copy-start = (f32[4,4,160,640]{3,2,1,0:T(8,128)}, f32[4,4,160,640]{3,2,1,0:T(8,128)S(1)}, u32[]{:S(2)}) copy-start(f32[4,4,160,640]{3,2,1,0:T(8,128)S(1)} %get-tuple-element.25) | copy-start | bytes 19660804
  33.9 2.7 %copy-start.9 = (bf16[1,160,512]{2,1,0:T(8,128)(2,1)S(1)}, bf16[1,160,512]{2,1,0:T(8,128)(2,1)}, u32[]{:S(2)}) copy-start(bf16[1,160,512]{2,1,0:T(8,128)(2,1)} %param.8) | copy-start | bytes 491524
  44.2 4.1 %copy-start.10 = (s32[1,160]{1,0:T(1,128)S(1)}, s32[1,160]{1,0:T(1,128)}, u32[]{:S(2)}) copy-start(s32[1,160]{1,0:T(1,128)} %param.11) | copy-start | bytes 1924
  44.2 4.1 %copy-start.11 = (f32[1,160]{1,0:T(1,128)S(1)}, f32[1,160]{1,0:T(1,128)}, u32[]{:S(2)}) copy-start(f32[1,160]{1,0:T(1,128)} %param.10) | copy-start | bytes 1924
  45.2 9.6 %slice-start = ((s8[6553600]{0:T(1024)(128)(4,1)}), s8[2359296]{0:T(1024)(128)(4,1)S(1)}, s32[]{:S(2)}) async-start(s8[6553600]{0:T(1024)(128)(4,1)} %bitcast.72), calls=%async_computation.2 | async-start | bytes 4718592
  48.3 6.6 %slice-start.1 = ((s8[6553600]{0:T(1024)(128)(4,1)}), s8[4194304]{0:T(1024)(128)(4,1)S(1)}, s32[]{:S(2)}) async-start(s8[6553600]{0:T(1024)(128)(4,1)} %bitcast.72), calls=%async_computation.3 | async-start | bytes 8388608
  54.9 2.9 %copy-start.6 = (bf16[1,640,512]{1,2,0:T(8,128)(2,1)S(1)}, bf16[1,640,512]{1,2,0:T(8,128)(2,1)}, u32[]{:S(2)}) copy-start(bf16[1,640,512]{1,2,0:T(8,128)(2,1)} %copy.51) | copy-start | bytes 1966084
  57.8 2.7 %copy-start.5 = (bf16[160,16,64]{2,0,1:T(8,128)(2,1)S(1)}, bf16[160,16,64]{2,0,1:T(8,128)(2,1)}, u32[]{:S(2)}) copy-start(bf16[160,16,64]{2,0,1:T(8,128)(2,1)} %copy-done.4) | copy-start | bytes 983044
  60.5 1.7 %copy-start.1 = (bf16[4,4,160,640]{3,2,1,0:T(8,128)(2,1)}, bf16[4,4,160,640]{3,2,1,0:T(8,128)(2,1)S(1)}, u32[]{:S(2)}) copy-start(bf16[4,4,160,640]{3,2,1,0:T(8,128)(2,1)S(1)} %multiply_convert_fusion) | copy-start | bytes 9830404
  62.2 1.1 %copy-start.7 = (bf16[4,128,640]{2,1,0:T(8,128)(2,1)S(1)}, bf16[4,128,640]{2,1,0:T(8,128)(2,1)}, u32[]{:S(2)}) copy-start(bf16[4,128,640]{2,1,0:T(8,128)(2,1)} %fusion.14) | copy-start | bytes 1966084
  64.4 2.7 %copy-start.2 = (bf16[4,4,160,640]{3,2,1,0:T(8,128)(2,1)S(1)}, bf16[4,4,160,640]{3,2,1,0:T(8,128)(2,1)}, u32[]{:S(2)}) copy-start(bf16[4,4,160,640]{3,2,1,0:T(8,128)(2,1)} %copy-done.1) | copy-start | bytes 9830404
Sparse Core Ops, SparseCore 0:
  67.2 27.4 reduce-scatter.1
where the time goes:
time: 105 us
  waiting for transfers between devices  22.7 us (22%)
  blocking collectives  21.4 us (20%)
  matrix products  17.4 us (17%)
  local copies, waits for them, and re-layouts  15.1 us (14%)
  between operations  14.3 us (14%)
  other arithmetic  13.8 us (13%)
    reduce_scatter x1, waiting for transfers between devices, per_device(): lax.psum_scatter(back_result[1].astype(jnp.float32).astype(jnp.bfloat16),...  22.6 us
    all_gather x1, blocking collectives, per_device(): key_piece = lax.all_gather(key_rot, 'ctx', axis=0, tiled=True)  9.33 us
    all_gather x1, blocking collectives, per_device(): value_piece = lax.all_gather(value_own, 'ctx', axis=0, tiled=True)  7.5 us
    dot_general x1, matrix products, per_device(): jnp.einsum('grcn,ngd->grcd', exp_scores.astype(jnp.bfloat16), grouped_val...  6.54 us
    unnamed x1, blocking collectives  4.55 us
    another operation x4, other arithmetic  3.74 us
    unnamed x35, local copies, waits for them, and re-layouts  3.3 us
    transpose x1, local copies, waits for them, and re-layouts, per_device(): grad_full = cotangent[0].astype(jnp.float32).reshape(local_rows, groups,...  3.04 us
  transfers between devices with their start and end apart: 1, of which 1 were waited for; matrix products, arithmetic and copies ran while one was open for 5% of the time, Pallas kernels for 0%

commit v1 on v0

v1 whole, which is shorter than its diff:
```python
import functools
import math

import jax
import jax.numpy as jnp
from jax import lax
from jax.experimental import pallas as pl
from jax.experimental.pallas import tpu as pltpu
from jax.sharding import PartitionSpec as P

DH = 128
LOCAL = 1024
THETA = 500000.0
EXTRA = 16
HIDDEN = -1e30
SCALE = DH**-0.5
LOG2E = math.log2(math.e)
LN2 = math.log(2.0)
VMEM_LIMIT = 50 * 1024 * 1024

NT = (((1,), (1,)), ((), ()))
NN = (((1,), (0,)), ((), ()))
TN = (((0,), (0,)), ((), ()))


def dot(a, b, dims):
    return lax.dot_general(a, b, dims, preferred_element_type=jnp.float32)


def rotate(values, cosine, sine):
    return values * cosine + pltpu.roll(values, DH // 2, 1) * sine


def pack_kernel(key_ref, value_ref, cos_ref, sin_ref, pos_ref, out_ref, *, groups, limit):
    rows = key_ref.shape[0]
    cosine, sine = cos_ref[...], sin_ref[...]
    for g in range(groups):
        own = key_ref[:, g * DH : (g + 1) * DH].astype(jnp.float32)
        out_ref[:rows, 2 * g * DH : (2 * g + 1) * DH] = rotate(own, cosine, sine).astype(jnp.bfloat16)
        out_ref[:rows, (2 * g + 1) * DH : (2 * g + 2) * DH] = value_ref[:, g * DH : (g + 1) * DH]
    count = jnp.sum(jnp.where(pos_ref[...] < limit, 1.0, 0.0), axis=1, keepdims=True)
    out_ref[rows:, :] = jnp.broadcast_to(count, (EXTRA, out_ref.shape[1])).astype(jnp.bfloat16)


def attention_kernel(query_ref, cot_ref, cos_ref, sin_ref, gate_ref, *refs, blocks, ratio):
    packets = refs[:blocks]
    query_grad_ref, delta_ref = refs[blocks : blocks + 2]
    parts = refs[blocks + 2 : 2 * blocks + 2]
    keys, values, query, cot, weights, score_grads = refs[2 * blocks + 2 :]
    rows = query_ref.shape[0]
    lanes = ratio * rows
    cosine, sine = cos_ref[...], sin_ref[...]
    for j in range(blocks):
        keys[j * rows : (j + 1) * rows, :] = packets[j][:rows, :DH]
        values[j * rows : (j + 1) * rows, :] = packets[j][:rows, DH:]
    for h in range(ratio):
        own = query_ref[:, h * DH : (h + 1) * DH].astype(jnp.float32)
        turned = rotate(own, cosine, sine) * (SCALE * LOG2E)
        query[h * rows : (h + 1) * rows, :] = turned.astype(jnp.bfloat16)
        cot[h * rows : (h + 1) * rows, :] = cot_ref[:, h * DH : (h + 1) * DH]
    for low in range(0, lanes, 256):
        width = min(256, lanes - low)
        here = slice(low, low + width)
        scores = dot(keys[...], query[here, :], NT)
        slot = lax.broadcasted_iota(jnp.int32, (rows, width), 0)
        lane = lax.broadcasted_iota(jnp.int32, (rows, width), 1) + low
        for h in range(1, ratio):
            lane = jnp.where(lane >= rows, lane - rows, lane)
        shown = [jnp.where(slot <= lane, scores[:rows], HIDDEN)]
        slot_f = slot.astype(jnp.float32)
        for j in range(1, blocks):
            count = packets[j][rows:, :DH].astype(jnp.float32)[:1]
            count = jnp.concatenate([count] * (width // DH), axis=1)
            shown.append(jnp.where(slot_f < count, scores[j * rows : (j + 1) * rows], HIDDEN))
        scores = jnp.concatenate(shown, axis=0)
        top = jnp.max(scores, axis=0, keepdims=True)
        raw = jnp.exp2(scores - top)
        inverse = 1.0 / jnp.sum(raw, axis=0, keepdims=True)
        prob_grad = dot(values[...], cot[here, :], NT)
        delta = jnp.sum(raw * prob_grad, axis=0, keepdims=True) * inverse
        delta_ref[:, here] = delta
        gated = raw * (inverse * gate_ref[:, here])
        weights[:, here] = gated.astype(jnp.bfloat16)
        score_grads[:, here] = (gated * (prob_grad - delta)).astype(jnp.bfloat16)
    for j in range(blocks):
        there = slice(j * rows, (j + 1) * rows)
        key_part = dot(score_grads[there, :], query[...], NN) * LN2
        value_part = dot(weights[there, :], cot[...], NN)
        parts[j][:, :DH] = key_part.astype(parts[j].dtype)
        parts[j][:, DH:] = value_part.astype(parts[j].dtype)
    query_acc = dot(score_grads[...], keys[...], TN) * SCALE
    for h in range(ratio):
        query_grad_ref[:, h * DH : (h + 1) * DH] = rotate(
            query_acc[h * rows : (h + 1) * rows], cosine, -sine
        ).astype(jnp.bfloat16)


def finish_kernel(own_ref, cos_ref, sin_ref, *refs, groups):
    got, (key_grad_ref, value_grad_ref) = refs[:-2], refs[-2:]
    total = own_ref[...]
    for ref in got:
        total = total + ref[...].astype(jnp.float32)
    cosine, sine = cos_ref[...], sin_ref[...]
    for g in range(groups):
        here = slice(g * DH, (g + 1) * DH)
        key_sum = total[:, 2 * g * DH : (2 * g + 1) * DH]
        key_grad_ref[:, here] = rotate(key_sum, cosine, -sine).astype(jnp.bfloat16)
        value_grad_ref[:, here] = total[:, (2 * g + 1) * DH : (2 * g + 2) * DH].astype(jnp.bfloat16)


def per_device(query_rows, key_rows, value_rows, cotangent, router_gate, positions):
    rows, heads_width = query_rows.shape[1:]
    group_width = key_rows.shape[2]
    groups = group_width // DH
    ratio = heads_width // group_width
    parts = lax.axis_size("ctx")
    chips = parts // 2
    limit = parts * LOCAL
    params = pltpu.CompilerParams(vmem_limit_bytes=VMEM_LIMIT)

    half = DH // 2
    index = (jnp.arange(DH, dtype=jnp.int32) % half).astype(jnp.float32)
    freq = jnp.power(jnp.float32(THETA), -2.0 * index / DH)
    angle = positions[0].astype(jnp.float32)[:, None] * freq[None, :]
    cosine = jnp.cos(angle)
    sign = jnp.where(jnp.arange(DH) < half, -1.0, 1.0).astype(jnp.float32)
    sine = jnp.sin(angle) * sign
    valid = positions < limit
    gate = jnp.tile(jnp.where(valid, router_gate, 0.0), (1, ratio))

    packet = pl.pallas_call(
        functools.partial(pack_kernel, groups=groups, limit=limit),
        out_shape=jax.ShapeDtypeStruct((rows + EXTRA, 2 * group_width), jnp.bfloat16),
        compiler_params=params,
    )(key_rows[0], value_rows[0], cosine, sine, positions)

    swap = [[(2 * x + k, 2 * x + 1 - k) for x in range(s, chips) for k in range(2)] for s in range(chips)]
    hop = [[(2 * x + k, 2 * (x + s) + k) for x in range(chips - s) for k in range(2)] for s in range(chips)]
    up = [(2 * x, 2 * x + 1) for x in range(chips)]
    back = lambda pairs: [(b, a) for a, b in pairs]

    far = [lax.ppermute(packet, "ctx", hop[s]) for s in range(1, chips)]
    near = lax.ppermute(packet, "ctx", up)
    crossed = [lax.ppermute(far[s - 1], "ctx", swap[s]) for s in range(1, chips)]
    packets = [packet, near] + far + crossed
    blocks = len(packets)

    whole = lambda shape: pl.BlockSpec(shape, lambda g: (0, 0))
    out = pl.pallas_call(
        functools.partial(attention_kernel, blocks=blocks, ratio=ratio),
        grid=(groups,),
        in_specs=[
            pl.BlockSpec((rows, ratio * DH), lambda g: (0, g)),
            pl.BlockSpec((rows, ratio * DH), lambda g: (0, g)),
            whole((rows, DH)),
            whole((rows, DH)),
            whole((1, ratio * rows)),
        ]
        + [pl.BlockSpec((rows + EXTRA, 2 * DH), lambda g: (0, g))] * blocks,
        out_specs=[
            pl.BlockSpec((rows, ratio * DH), lambda g: (0, g)),
            pl.BlockSpec((None, 1, ratio * rows), lambda g: (g, 0, 0)),
        ]
        + [pl.BlockSpec((rows, 2 * DH), lambda g: (0, g))] * blocks,
        out_shape=[
            jax.ShapeDtypeStruct((rows, heads_width), jnp.bfloat16),
            jax.ShapeDtypeStruct((groups, 1, ratio * rows), jnp.float32),
            jax.ShapeDtypeStruct((rows, 2 * group_width), jnp.float32),
        ]
        + [jax.ShapeDtypeStruct((rows, 2 * group_width), jnp.bfloat16)] * (blocks - 1),
        scratch_shapes=[
            pltpu.VMEM((blocks * rows, DH), jnp.bfloat16),
            pltpu.VMEM((blocks * rows, DH), jnp.bfloat16),
            pltpu.VMEM((ratio * rows, DH), jnp.bfloat16),
            pltpu.VMEM((ratio * rows, DH), jnp.bfloat16),
            pltpu.VMEM((blocks * rows, ratio * rows), jnp.bfloat16),
            pltpu.VMEM((blocks * rows, ratio * rows), jnp.bfloat16),
        ],
        compiler_params=params,
    )(query_rows[0], cotangent[0], cosine, sine, gate, *packets)
    query_grad, delta, own_part, near_part = out[:4]
    far_parts, crossed_parts = out[4 : 3 + chips], out[3 + chips :]

    got = [lax.ppermute(near_part, "ctx", back(up))]
    for s in range(1, chips):
        other = lax.ppermute(crossed_parts[s - 1], "ctx", swap[s])
        both = far_parts[s - 1].astype(jnp.float32) + other.astype(jnp.float32)
        got.append(lax.ppermute(both.astype(jnp.bfloat16), "ctx", back(hop[s])))
    gate_grad = jnp.where(valid[0], jnp.sum(delta.reshape(groups * ratio, rows), axis=0), 0.0)
    key_grad, value_grad = pl.pallas_call(
        functools.partial(finish_kernel, groups=groups),
        out_shape=[jax.ShapeDtypeStruct((rows, group_width), jnp.bfloat16)] * 2,
        compiler_params=params,
    )(own_part, cosine, sine, *got)
    return (query_grad[None], key_grad[None], value_grad[None], gate_grad[None])


def solution(mesh):
    wide = P(("group", "dp"), "ctx", None)
    narrow = P(("group", "dp"), "ctx")
    return jax.shard_map(
        per_device,
        mesh=mesh,
        in_specs=(wide, wide, wide, wide, narrow, narrow),
        out_specs=(wide, wide, wide, narrow),
        check_vma=False,
    )
```

time: 105 us -> 47.3 us (0.45)
  blocking collectives: 21.4 us -> 0 us
  matrix products: 17.4 us -> 0 us
  between operations: 14.3 us -> 0.79 us
  local copies, waits for them, and re-layouts: 15.1 us -> 2.45 us
  other arithmetic: 13.8 us -> 1.86 us
  Pallas kernels: 0 us -> 11.9 us
  starting transfers between devices: 0.04 us -> 10.3 us
  waiting for transfers between devices: 22.7 us -> 19.7 us
    reduce_scatter x1 -> x0, waiting for transfers between devices: 22.6 us -> none  [per_device(): lax.psum_scatter(back_result[1].astype(jnp.float32).astype(jnp.bfloat16),...]
    ppermute x0 -> x6, waiting for transfers between devices: none -> 19.7 us  [the longest x1 13.6 us: per_device(): got.append(lax.ppermute(both.astype(jnp.bfloat16), 'ctx', back(hop[s])))]
    dot_general x6 -> x0, matrix products: 17.4 us -> none  [the longest x1 6.54 us: per_device(): jnp.einsum('grcn,ngd->grcd', exp_scores.astype(jnp.bfloat16), grouped_val...]
    all_gather x2 -> x0, blocking collectives: 16.8 us -> none  [the longest x1 9.33 us: per_device(): key_piece = lax.all_gather(key_rot, 'ctx', axis=0, tiled=True)]
    pallas_call x0 -> x3, Pallas kernels: none -> 11.9 us  [the longest x1 10.9 us: per_device(): pl.pallas_call(functools.partial(attention_kernel, blocks=blocks, ratio=r...]
    ppermute x0 -> x6, starting transfers between devices: none -> 10.3 us  [the longest x1 4.86 us: per_device(): far = [lax.ppermute(packet, 'ctx', hop[s]) for s in range(1, chips)]]
    unnamed x1 -> x0, blocking collectives: 4.55 us -> none
    another operation x5 -> x0, other arithmetic: 3.75 us -> none
  transfers between devices with their start and end apart: 1 -> 6, of which waited for: 1 -> 2; matrix products, arithmetic and copies ran while one was open for 5% -> 2% of each run, Pallas kernels for 0% -> 0%
where the time goes in v1:
time: 47.3 us; the launch traced here: 47 us
  waiting for transfers between devices  19.7 us (42%)
  Pallas kernels  11.9 us (25%)
  starting transfers between devices  10.3 us (22%)
  local copies, waits for them, and re-layouts  2.45 us (5%)
  other arithmetic  1.86 us (4%)
  between operations  0.79 us (2%)
    ppermute x1, waiting for transfers between devices, per_device(): got.append(lax.ppermute(both.astype(jnp.bfloat16), 'ctx', back(hop[s])))  13.6 us
    pallas_call x1, Pallas kernels, per_device(): pl.pallas_call(functools.partial(attention_kernel, blocks=blocks, ratio=r...  10.9 us
    ppermute x1, waiting for transfers between devices, per_device(): far = [lax.ppermute(packet, 'ctx', hop[s]) for s in range(1, chips)]  6.14 us
    ppermute x1, starting transfers between devices, per_device(): far = [lax.ppermute(packet, 'ctx', hop[s]) for s in range(1, chips)]  4.86 us
    unnamed x12, local copies, waits for them, and re-layouts  2.28 us
    ppermute x1, starting transfers between devices, per_device(): near = lax.ppermute(packet, 'ctx', up)  1.48 us
    ppermute x1, starting transfers between devices, per_device(): got = [lax.ppermute(near_part, 'ctx', back(up))]  1.29 us
    ppermute x1, starting transfers between devices, per_device(): got.append(lax.ppermute(both.astype(jnp.bfloat16), 'ctx', back(hop[s])))  1.29 us
  transfers between devices with their start and end apart: 6, of which 2 were waited for; matrix products, arithmetic and copies ran while one was open for 2% of the time, Pallas kernels for 0%

profile of v1, /device:TPU:0, one launch (start us, length us, event | category | flops | bytes accessed | tf_op | source)
XLA Modules:
  0.0 47.0 jit_solution(12323788066378696865)
XLA Ops:
  0.6 0.0 copy-start.1
  0.6 0.0 copy-start
  0.7 0.8 %convert_element_type.26 = f32[1,160]{1,0:T(1,128)S(1)} convert(s32[1,160]{1,0:T(1,128)} %pos_ref.1) | non-fusion elementwise | flops 160 | bytes 1280 | tf_op jit(solution)/shard_map/convert_element_type | solution.py:124
  1.4 0.4 fusion
  1.8 0.0 copy-done.1
  1.8 0.0 copy-start.2
  1.8 0.9 %copy-done.2 = bf16[1,160,512]{2,1,0:T(8,128)(2,1)S(1)} copy-done((bf16[1,160,512]{2,1,0:T(8,128)(2,1)S(1)}, bf16[1,160,512]{2,1,0:T(8,128)(2,1)}, u32[]{:S(2)}) %copy-start.2) | copy-done | bytes 163864
  2.7 0.0 copy-start.3
  2.7 0.7 %copy-done.3 = s32[1,160]{1,0:T(1,128)S(1)} copy-done((s32[1,160]{1,0:T(1,128)S(1)}, s32[1,160]{1,0:T(1,128)}, u32[]{:S(2)}) %copy-start.3) | copy-done | bytes 664
  3.4 0.0 copy-start.5
  3.4 0.1 shard_map.93.refs_0_
  3.6 4.9 %collective-permute-start.1 = (bf16[176,1024]{1,0:T(8,128)(2,1)S(1)}, bf16[176,1024]{1,0:T(8,128)(2,1)S(1)}, u32[]{:S(2)}, u32[]{:S(2)}) collective-permute-start(bf16[176,1024]{1,0:T(8,128)(2,1)S(1)} %shard_map.93.refs_0_), channel_id=1, source_target_pairs={{0,2},{1,3},{4,6},{5,7},{8,10},{9,11},{12,14},{13,15},{16,18},{17,... | collective-permute-start | bytes 1081352 | tf_op jit(solution)/shard_map/ppermute | solution.py:142
  8.4 1.5 %collective-permute-start = (bf16[176,1024]{1,0:T(8,128)(2,1)S(1)}, bf16[176,1024]{1,0:T(8,128)(2,1)S(1)}, u32[]{:S(2)}, u32[]{:S(2)}) collective-permute-start(bf16[176,1024]{1,0:T(8,128)(2,1)S(1)} %shard_map.93.refs_0_), channel_id=1, source_target_pairs={{0,1},{2,3},{4,5},{6,7},{8,9},{10,11},{12,13},{14,15},{16,17},{18,... | collective-permute-start | bytes 1081352 | tf_op jit(solution)/shard_map/ppermute | solution.py:143
  9.9 6.1 %collective-permute-done.1.refs_2_ = bf16[176,1024]{1,0:T(8,128)(2,1)S(1)} collective-permute-done((bf16[176,1024]{1,0:T(8,128)(2,1)S(1)}, bf16[176,1024]{1,0:T(8,128)(2,1)S(1)}, u32[]{:S(2)}, u32[]{:S(2)}) %collective-permute-start.1) | collective-permute-done | bytes 360480 | tf_op jit(solution)/shard_map/ppermute | solution.py:142
  16.1 0.7 %collective-permute-start.2 = (bf16[176,1024]{1,0:T(8,128)(2,1)S(1)}, bf16[176,1024]{1,0:T(8,128)(2,1)S(1)}, u32[]{:S(2)}, u32[]{:S(2)}) collective-permute-start(bf16[176,1024]{1,0:T(8,128)(2,1)S(1)} %collective-permute-done.1.refs_2_), channel_id=1, source_target_pairs={{2,3},{3,2},{6,7},{7,6},{10,11},{11,10},{14,15},{15,14},{18,19},{1... | collective-permute-start | bytes 1081352 | tf_op jit(solution)/shard_map/ppermute | solution.py:144
  16.7 0.0 copy-done.5
  16.8 0.1 tile.13.gate_ref
  16.9 0.0 collective-permute-done.refs_1_
  16.9 0.0 collective-permute-done.2.refs_3_
  16.9 0.0 copy-done
  16.9 10.9 %shard_map.94 = (bf16[160,2048]{1,0:T(8,128)(2,1)}, f32[4,1,640]{2,1,0:T(1,128)S(1)}, f32[160,1024]{1,0:T(8,128)S(1)}, bf16[160,1024]{1,0:T(8,128)(2,1)S(1)}, bf...) custom-call(bf16[160,2048]{1,0:T(8,128)(2,1)S(1)} %bitcast.10, bf16[160,2048]{1,0:T(8,128)(2,1)} %bitcast.13, ...), custom_call_target="tpu_custom_call" | custom-call | tf_op jit(solution)/shard_map/pallas_call | solution.py:149
  27.8 0.7 %collective-permute-start.4 = (bf16[160,1024]{1,0:T(8,128)(2,1)S(1)}, bf16[160,1024]{1,0:T(8,128)(2,1)S(1)}, u32[]{:S(2)}, u32[]{:S(2)}) collective-permute-start(bf16[160,1024]{1,0:T(8,128)(2,1)S(1)} %get-tuple-element.16), channel_id=1, source_target_pairs={{2,3},{3,2},{6,7},{7,6},{10,11},{11,10},{14,15},{15,14},{18,19},{1... | collective-permute-start | bytes 983048 | tf_op jit(solution)/shard_map/ppermute | solution.py:186
  28.5 1.3 %collective-permute-start.3 = (bf16[160,1024]{1,0:T(8,128)(2,1)S(1)}, bf16[160,1024]{1,0:T(8,128)(2,1)S(1)}, u32[]{:S(2)}, u32[]{:S(2)}) collective-permute-start(bf16[160,1024]{1,0:T(8,128)(2,1)S(1)} %get-tuple-element.14), channel_id=1, source_target_pairs={{1,0},{3,2},{5,4},{7,6},{9,8},{11,10},{13,12},{15,14},{17,16},{19,... | collective-permute-start | bytes 983048 | tf_op jit(solution)/shard_map/ppermute | solution.py:184
  29.8 0.0 collective-permute-done.4
  29.8 0.1 add_convert_fusion
  29.9 1.3 %collective-permute-start.5 = (bf16[160,1024]{1,0:T(8,128)(2,1)S(1)}, bf16[160,1024]{1,0:T(8,128)(2,1)S(1)}, u32[]{:S(2)}, u32[]{:S(2)}) collective-permute-start(bf16[160,1024]{1,0:T(8,128)(2,1)S(1)} %add_convert_fusion), channel_id=1, source_target_pairs={{2,0},{3,1},{6,4},{7,5},{10,8},{11,9},{14,12},{15,13},{18,16},{19,... | collective-permute-start | bytes 983048 | tf_op jit(solution)/shard_map/ppermute | solution.py:188
  31.2 0.1 reshape.41
  31.4 0.0 copy-start.4
  31.4 0.7 %copy-done.4 = s32[1,160]{1,0:T(1,128)S(1)} copy-done((s32[1,160]{1,0:T(1,128)S(1)}, s32[1,160]{1,0:T(1,128)}, u32[]{:S(2)}) %copy-start.4) | copy-done | bytes 664
  32.0 0.6 %compare_select_fusion = f32[1,160]{1,0:T(1,128)} fusion(f32[1,160]{1,0:T(1,128)S(1)} %bitcast.14, s32[1,160]{1,0:T(1,128)S(1)} %copy-done.4), kind=kLoop, calls=%fused_computation.4 | loop fusion | flops 320 | bytes 1920 | tf_op jit(solution)/shard_map/jit(_where)/select_n | solution.py:189
  32.6 0.0 collective-permute-done.3.refs_0_
  32.6 13.6 %collective-permute-done.5.refs_1_ = bf16[160,1024]{1,0:T(8,128)(2,1)S(1)} collective-permute-done((bf16[160,1024]{1,0:T(8,128)(2,1)S(1)}, bf16[160,1024]{1,0:T(8,128)(2,1)S(1)}, u32[]{:S(2)}, u32[]{:S(2)}) %collective-permute-start.5) | collective-permute-done | bytes 327712 | tf_op jit(solution)/shard_map/ppermute | solution.py:188
  46.2 0.9 %shard_map.95 = (bf16[160,512]{1,0:T(8,128)(2,1)}, bf16[160,512]{1,0:T(8,128)(2,1)}) custom-call(f32[160,1024]{1,0:T(8,128)S(1)} %get-tuple-element.13.own_ref, f32[160,128]{1,0:T(8,128)S(1)} %get-tuple-element.21.cos_ref, f32[160,128]{1,0:T(8,128)S(1)} %get-tuple-element.20.sin_ref, bf16[160,1024]{1,0:T(8,128)(2,1)S(1)} %collective-permute-done.3.refs_0_, ...), custom_call_target="tpu_custom_call" | custom-call | tf_op jit(solution)/shard_map/pallas_call | solution.py:190
  (5 shorter events, 0.1 us)
Async XLA Ops:
  0.6 1.2 %copy-start.1 = (bf16[1,160,512]{2,1,0:T(8,128)(2,1)S(1)}, bf16[1,160,512]{2,1,0:T(8,128)(2,1)}, u32[]{:S(2)}) copy-start(bf16[1,160,512]{2,1,0:T(8,128)(2,1)} %param.7) | copy-start | bytes 491524
  0.6 16.2 %copy-start = (bf16[1,160,2048]{2,1,0:T(8,128)(2,1)S(1)}, bf16[1,160,2048]{2,1,0:T(8,128)(2,1)}, u32[]{:S(2)}) copy-start(bf16[1,160,2048]{2,1,0:T(8,128)(2,1)} %param.6) | copy-start | bytes 1966084
  1.8 0.9 %copy-start.2 = (bf16[1,160,512]{2,1,0:T(8,128)(2,1)S(1)}, bf16[1,160,512]{2,1,0:T(8,128)(2,1)}, u32[]{:S(2)}) copy-start(bf16[1,160,512]{2,1,0:T(8,128)(2,1)} %param.8) | copy-start | bytes 491524
  2.7 0.7 %copy-start.3 = (s32[1,160]{1,0:T(1,128)S(1)}, s32[1,160]{1,0:T(1,128)}, u32[]{:S(2)}) copy-start(s32[1,160]{1,0:T(1,128)} %pos_ref.1) | copy-start | bytes 1924
  3.4 13.3 %copy-start.5 = (f32[1,160]{1,0:T(1,128)S(1)}, f32[1,160]{1,0:T(1,128)}, u32[]{:S(2)}) copy-start(f32[1,160]{1,0:T(1,128)} %param.10) | copy-start | bytes 1924
  3.6 12.5 %collective-permute-start.1 = (bf16[176,1024]{1,0:T(8,128)(2,1)S(1)}, bf16[176,1024]{1,0:T(8,128)(2,1)S(1)}, u32[]{:S(2)}, u32[]{:S(2)}) collective-permute-start(bf16[176,1024]{1,0:T(8,128)(2,1)S(1)} %shard_map.93.refs_0_), channel_id=1, source_target_pairs={{0,2},{1,3},{4,6},{5,7},{8,10},{9,11},{12,14},{13,15},{16,18},{17,... | collective-permute-start | bytes 1081352 | tf_op jit(solution)/shard_map/ppermute | solution.py:142
  8.4 8.4 %collective-permute-start = (bf16[176,1024]{1,0:T(8,128)(2,1)S(1)}, bf16[176,1024]{1,0:T(8,128)(2,1)S(1)}, u32[]{:S(2)}, u32[]{:S(2)}) collective-permute-start(bf16[176,1024]{1,0:T(8,128)(2,1)S(1)} %shard_map.93.refs_0_), channel_id=1, source_target_pairs={{0,1},{2,3},{4,5},{6,7},{8,9},{10,11},{12,13},{14,15},{16,17},{18,... | collective-permute-start | bytes 1081352 | tf_op jit(solution)/shard_map/ppermute | solution.py:143
  16.1 0.8 %collective-permute-start.2 = (bf16[176,1024]{1,0:T(8,128)(2,1)S(1)}, bf16[176,1024]{1,0:T(8,128)(2,1)S(1)}, u32[]{:S(2)}, u32[]{:S(2)}) collective-permute-start(bf16[176,1024]{1,0:T(8,128)(2,1)S(1)} %collective-permute-done.1.refs_2_), channel_id=1, source_target_pairs={{2,3},{3,2},{6,7},{7,6},{10,11},{11,10},{14,15},{15,14},{18,19},{1... | collective-permute-start | bytes 1081352 | tf_op jit(solution)/shard_map/ppermute | solution.py:144
  27.8 2.0 %collective-permute-start.4 = (bf16[160,1024]{1,0:T(8,128)(2,1)S(1)}, bf16[160,1024]{1,0:T(8,128)(2,1)S(1)}, u32[]{:S(2)}, u32[]{:S(2)}) collective-permute-start(bf16[160,1024]{1,0:T(8,128)(2,1)S(1)} %get-tuple-element.16), channel_id=1, source_target_pairs={{2,3},{3,2},{6,7},{7,6},{10,11},{11,10},{14,15},{15,14},{18,19},{1... | collective-permute-start | bytes 983048 | tf_op jit(solution)/shard_map/ppermute | solution.py:186
  28.5 4.1 %collective-permute-start.3 = (bf16[160,1024]{1,0:T(8,128)(2,1)S(1)}, bf16[160,1024]{1,0:T(8,128)(2,1)S(1)}, u32[]{:S(2)}, u32[]{:S(2)}) collective-permute-start(bf16[160,1024]{1,0:T(8,128)(2,1)S(1)} %get-tuple-element.14), channel_id=1, source_target_pairs={{1,0},{3,2},{5,4},{7,6},{9,8},{11,10},{13,12},{15,14},{17,16},{19,... | collective-permute-start | bytes 983048 | tf_op jit(solution)/shard_map/ppermute | solution.py:184
  29.9 16.3 %collective-permute-start.5 = (bf16[160,1024]{1,0:T(8,128)(2,1)S(1)}, bf16[160,1024]{1,0:T(8,128)(2,1)S(1)}, u32[]{:S(2)}, u32[]{:S(2)}) collective-permute-start(bf16[160,1024]{1,0:T(8,128)(2,1)S(1)} %add_convert_fusion), channel_id=1, source_target_pairs={{2,0},{3,1},{6,4},{7,5},{10,8},{11,9},{14,12},{15,13},{18,16},{19,... | collective-permute-start | bytes 983048 | tf_op jit(solution)/shard_map/ppermute | solution.py:188
  31.4 0.7 %copy-start.4 = (s32[1,160]{1,0:T(1,128)S(1)}, s32[1,160]{1,0:T(1,128)}, u32[]{:S(2)}) copy-start(s32[1,160]{1,0:T(1,128)} %pos_ref.1) | copy-start | bytes 1924

commit v2 on v1

v2 whole, which is shorter than its diff:
```python
import functools
import math

import jax
import jax.numpy as jnp
import numpy as np
from jax import lax
from jax.experimental import pallas as pl
from jax.experimental.pallas import tpu as pltpu
from jax.sharding import PartitionSpec as P

DH = 128
LOCAL = 1024
THETA = 500000.0
EXTRA = 16
HIDDEN = -1e30
SCALE = DH**-0.5
LOG2E = math.log2(math.e)
LN2 = math.log(2.0)

NT = (((1,), (1,)), ((), ()))
NN = (((1,), (0,)), ((), ()))
TN = (((0,), (0,)), ((), ()))
F32 = jnp.float32
BF16 = jnp.bfloat16


def few_bits(value, bits):
    unit = 2.0 ** (math.floor(math.log2(value)) + 1 - bits)
    return math.floor(value / unit) * unit


QUARTER_1 = few_bits(math.pi / 2, 10)
QUARTER_2 = few_bits(math.pi / 2 - QUARTER_1, 10)
QUARTER_3 = math.pi / 2 - QUARTER_1 - QUARTER_2


def dot(a, b, dims):
    return lax.dot_general(a, b, dims, preferred_element_type=F32)


def core_of():
    return lax.rem(lax.axis_index("ctx"), 2)


def rotate(values, cosine, sine):
    return values * cosine + pltpu.roll(values, DH // 2, 1) * sine


def sine_cosine(angle):
    turns = jnp.floor(angle * (2.0 / math.pi) + 0.5)
    rest = ((angle - turns * QUARTER_1) - turns * QUARTER_2) - turns * QUARTER_3
    square = rest * rest
    sine = ((-1.9515295891e-4 * square + 8.3321608736e-3) * square - 1.6666654611e-1) * square * rest + rest
    cosine = (2.443315711809948e-5 * square - 1.388731625493765e-3) * square + 4.166664568298827e-2
    cosine = cosine * square * square - 0.5 * square + 1.0
    quarter = turns.astype(jnp.int32)
    odd = (quarter & 1) == 1
    first, second = jnp.where(odd, cosine, sine), jnp.where(odd, sine, cosine)
    return (
        jnp.where((quarter & 2) == 2, -first, first),
        jnp.where(((quarter + 1) & 2) == 2, -second, second),
    )


def split_rows(row, height):
    high = row.astype(BF16).astype(F32)
    middle = (row - high).astype(BF16).astype(F32)
    low = row - high - middle
    line = lax.broadcasted_iota(jnp.int32, (height, row.shape[1]), 0)
    rows = jnp.where(line == 0, high, jnp.where(line == 1, middle, jnp.where(line == 2, low, 0.0)))
    return rows.astype(BF16)


def joined_row(rows):
    return jnp.sum(rows.astype(F32), axis=0, keepdims=True)


def pack_keys_kernel(
    key_in, value_in, pos_in, freq_in, mine_ref, theirs_ref, cos_ref, sin_ref, key, value, pos, freq, sems, *, limit
):
    copies = [
        pltpu.make_async_copy(source, target, sems.at[i])
        for i, (source, target) in enumerate(((pos_in, pos), (freq_in, freq), (key_in, key), (value_in, value)))
    ]
    for copy in copies:
        copy.start()
    rows = key.shape[0]
    half = key.shape[1] // 2
    core = core_of()
    copies[0].wait()
    copies[1].wait()
    places = pos[...]
    count = jnp.sum(jnp.where(places < limit, 1.0, 0.0), axis=1, keepdims=True)
    count = jnp.broadcast_to(count, (EXTRA, 2 * half)).astype(BF16)
    down = lax.broadcasted_iota(jnp.int32, (rows, rows), 0)
    along = lax.broadcasted_iota(jnp.int32, (rows, rows), 1)
    column = jnp.sum(jnp.where(down == along, places.astype(F32), 0.0), axis=1, keepdims=True)
    sine, cosine = sine_cosine(column * freq[...])
    lane = lax.broadcasted_iota(jnp.int32, (rows, DH), 1)
    sine = jnp.where(lane < DH // 2, -sine, sine)
    cos_ref[...] = cosine
    sin_ref[...] = sine
    copies[2].wait()
    copies[3].wait()
    for out_ref, side in ((mine_ref, core), (theirs_ref, 1 - core)):
        for i in range(half // DH):
            there = pl.ds(pl.multiple_of(side * half + i * DH, DH), DH)
            turned = rotate(key[:, there].astype(F32), cosine, sine)
            out_ref[:rows, 2 * i * DH : (2 * i + 1) * DH] = turned.astype(BF16)
            out_ref[:rows, (2 * i + 1) * DH : (2 * i + 2) * DH] = value[:, there]
        out_ref[rows:, :] = count


def pack_queries_kernel(
    query_in, cot_in, cos_in, sin_in, gate_in, mine_in, theirs_in, out_ref, query, cos_ref, sin_ref, gate_ref, sems
):
    rows = query.shape[0]
    half = query.shape[1] // 2
    core = core_of()
    pairs = [
        (query_in, query),
        (cos_in, cos_ref),
        (sin_in, sin_ref),
        (gate_in, gate_ref),
        (mine_in, out_ref.at[core, :, 2 * half :]),
        (theirs_in, out_ref.at[1 - core, :, 2 * half :]),
        (cot_in.at[:, :half], out_ref.at[0, :rows, half : 2 * half]),
        (cot_in.at[:, half:], out_ref.at[1, :rows, half : 2 * half]),
    ]
    copies = [pltpu.make_async_copy(source, target, sems.at[i]) for i, (source, target) in enumerate(pairs)]
    for copy in copies:
        copy.start()
    for copy in copies[:4]:
        copy.wait()
    cosine, sine = cos_ref[...] * (SCALE * LOG2E), sin_ref[...] * (SCALE * LOG2E)
    gate = split_rows(gate_ref[...], EXTRA)
    for side in range(2):
        for i in range(half // DH):
            there = slice(side * half + i * DH, side * half + (i + 1) * DH)
            turned = rotate(query[:, there].astype(F32), cosine, sine)
            out_ref[side, :rows, i * DH : (i + 1) * DH] = turned.astype(BF16)
        out_ref[side, rows:, : gate.shape[1]] = gate
    for copy in copies[4:]:
        copy.wait()


def chunks(low, high):
    return [slice(at, min(at + 256, high)) for at in range(low, high, 256)]


def local_kernel(packets, keys, values, query, cot, gate, raws, grads, tops, sums, crosses, *, ratio):
    rows = packets.shape[1] - EXTRA
    half_groups = keys.shape[0]
    wide = ratio * rows
    half = half_groups * ratio * DH
    for side in range(2):
        there = slice(side * rows, (side + 1) * rows)
        for i in range(half_groups):
            at = 2 * half + 2 * i * DH
            keys[i, there, :] = packets[side, :rows, at : at + DH]
            values[i, there, :] = packets[side, :rows, at + DH : at + 2 * DH]
            for h in range(ratio):
                to = slice(side * wide + h * rows, side * wide + (h + 1) * rows)
                at = (i * ratio + h) * DH
                query[i, to, :] = packets[side, :rows, at : at + DH]
                cot[i, to, :] = packets[side, :rows, half + at : half + at + DH]
        gate[:, side * wide : (side + 1) * wide] = joined_row(packets[side, rows:, :wide])
    count = packets[0, rows:, 2 * half : 2 * half + 256].astype(F32)[:1]
    for i in range(half_groups):
        for block in range(2):
            reach = (block + 1) * rows
            for here in chunks(block * wide, (block + 1) * wide):
                width = here.stop - here.start
                scores = dot(keys[i, :reach, :], query[i, here, :], NT)
                slot = lax.broadcasted_iota(jnp.int32, (rows, width), 0)
                lane = lax.broadcasted_iota(jnp.int32, (rows, width), 1) + (here.start - block * wide)
                for h in range(1, ratio):
                    lane = jnp.where(lane >= rows, lane - rows, lane)
                shown = jnp.where(slot <= lane, scores[block * rows :], HIDDEN)
                if block:
                    before = jnp.where(slot.astype(F32) < count[:, :width], scores[:rows], HIDDEN)
                    shown = jnp.concatenate([before, shown], axis=0)
                top = jnp.max(shown, axis=0, keepdims=True)
                raw = jnp.exp2(shown - top)
                prob_grad = dot(values[i, :reach, :], cot[i, here, :], NT)
                raws[i, :reach, here] = raw
                grads[i, :reach, here] = prob_grad
                tops[i, :, here] = top
                sums[i, :, here] = jnp.sum(raw, axis=0, keepdims=True)
                crosses[i, :, here] = jnp.sum(raw * prob_grad, axis=0, keepdims=True)


def part_of(weights, score_grads, query, cot, out_ref, i, there, lanes):
    key_part = dot(score_grads[i, there, lanes], query[i, lanes, :], NN) * LN2
    value_part = dot(weights[i, there, lanes], cot[i, lanes, :], NN)
    out_ref[:, 2 * i * DH : (2 * i + 1) * DH] = key_part.astype(out_ref.dtype)
    out_ref[:, (2 * i + 1) * DH : (2 * i + 2) * DH] = value_part.astype(out_ref.dtype)


def far_kernel(query, cot, gate, tops, sums, crosses, *refs, blocks):
    packets = refs[:blocks]
    far_keys, weights, score_grads, factors, deltas = refs[blocks : blocks + 5]
    parts = refs[blocks + 5 : 2 * blocks + 5]
    far_values = refs[-1]
    rows = packets[0].shape[0] - EXTRA
    half_groups, lanes = query.shape[:2]
    for j in range(blocks):
        there = slice(j * rows, (j + 1) * rows)
        for i in range(half_groups):
            far_keys[i, there, :] = packets[j][:rows, 2 * i * DH : (2 * i + 1) * DH]
            far_values[i, there, :] = packets[j][:rows, (2 * i + 1) * DH : (2 * i + 2) * DH]
    counts = [packet[rows:, :256].astype(F32)[:1] for packet in packets]
    for i in range(half_groups):
        for here in chunks(0, lanes):
            width = here.stop - here.start
            scores = dot(far_keys[i], query[i, here, :], NT)
            slot = lax.broadcasted_iota(jnp.int32, (rows, width), 0).astype(F32)
            shown = [
                jnp.where(slot < counts[j][:, :width], scores[j * rows : (j + 1) * rows], HIDDEN)
                for j in range(blocks)
            ]
            shown = jnp.concatenate(shown, axis=0)
            old_top = tops[i, :, here]
            top = jnp.maximum(old_top, jnp.max(shown, axis=0, keepdims=True))
            raw = jnp.exp2(shown - top)
            shrink = jnp.exp2(old_top - top)
            inverse = 1.0 / (sums[i, :, here] * shrink + jnp.sum(raw, axis=0, keepdims=True))
            prob_grad = dot(far_values[i], cot[i, here, :], NT)
            cross = crosses[i, :, here] * shrink + jnp.sum(raw * prob_grad, axis=0, keepdims=True)
            delta = cross * inverse
            factor = inverse * gate[:, here]
            factors[i, :, here] = factor * shrink
            deltas[i, :, here] = delta
            gated = raw * factor
            weights[i, :, here] = gated.astype(BF16)
            score_grads[i, :, here] = (gated * (prob_grad - delta)).astype(BF16)
        for j, out_ref in enumerate(parts):
            part_of(weights, score_grads, query, cot, out_ref, i, slice(j * rows, (j + 1) * rows), slice(0, lanes))


def near_kernel(
    raws, grads, factors, deltas, keys, query, cot, far_keys, far_grads,
    part_mine, out_ref, weights, score_grads, parts,
    *, ratio
):
    rows = part_mine.shape[0]
    half_groups = keys.shape[0]
    wide = ratio * rows
    half = half_groups * ratio * DH
    for i in range(half_groups):
        for block in range(2):
            reach = (block + 1) * rows
            for here in chunks(block * wide, (block + 1) * wide):
                gated = raws[i, :reach, here] * factors[i, :, here]
                weights[i, :reach, here] = gated.astype(BF16)
                score_grads[i, :reach, here] = (gated * (grads[i, :reach, here] - deltas[i, :, here])).astype(BF16)
        for block in range(2):
            there, lanes = slice(block * rows, (block + 1) * rows), slice(block * wide, 2 * wide)
            part_of(weights, score_grads, query, cot, parts.at[block], i, there, lanes)
            reach, lanes = (block + 1) * rows, slice(block * wide, (block + 1) * wide)
            total = dot(score_grads[i, :reach, lanes], keys[i, :reach, :], TN)
            total = (total + dot(far_grads[i, :, lanes], far_keys[i], TN)) * SCALE
            for h in range(ratio):
                at = (i * ratio + h) * DH
                out_ref[block, :rows, at : at + DH] = total[h * rows : (h + 1) * rows].astype(BF16)
    part_mine[...] = parts[core_of()]
    for block in range(2):
        out_ref[block, :rows, half:] = parts[block].astype(BF16)
    summed = deltas[0]
    for i in range(1, half_groups):
        summed = summed + deltas[i]
    down = lax.broadcasted_iota(jnp.int32, (wide, rows), 0)
    along = lax.broadcasted_iota(jnp.int32, (wide, rows), 1)
    for h in range(1, ratio):
        down = jnp.where(down >= rows, down - rows, down)
    chosen = jnp.where(down == along, 1.0, 0.0).astype(BF16)
    for block in range(2):
        own = joined_row(dot(split_rows(summed[:, block * wide : (block + 1) * wide], 16), chosen, NN))
        out_ref[block, rows:, :rows] = split_rows(own, EXTRA)


def finish_queries_kernel(back, pos_ref, cos_ref, sin_ref, query_grad, gate_grad, done, *, limit):
    rows = cos_ref.shape[0]
    half = query_grad.shape[1] // 2
    cosine, sine = cos_ref[...], -sin_ref[...]
    for side in range(2):
        for i in range(half // DH):
            there = slice(side * half + i * DH, side * half + (i + 1) * DH)
            turned = rotate(back[side, :rows, i * DH : (i + 1) * DH].astype(F32), cosine, sine)
            query_grad[:, there] = turned.astype(BF16)
    gate = joined_row(back[0, rows:, :rows]) + joined_row(back[1, rows:, :rows])
    gate_grad[...] = jnp.where(pos_ref[...] < limit, gate, 0.0)
    done[...] = jnp.zeros_like(done)


def finish_keys_kernel(part_mine, back, cos_ref, sin_ref, *refs):
    got, (key_grad, value_grad) = refs[:-2], refs[-2:]
    rows, width = part_mine.shape
    half = width // 2
    core = core_of()
    cosine, sine = cos_ref[...], -sin_ref[...]
    total = part_mine[...]
    other = back[1 - core, :rows, back.shape[2] - width :].astype(F32)
    for s in range(len(got) // 2):
        other = other + got[2 * s][...].astype(F32)
        total = total + got[2 * s + 1][...].astype(F32)
    for values, side in ((total, core), (other, 1 - core)):
        for i in range(half // DH):
            there = pl.ds(pl.multiple_of(side * half + i * DH, DH), DH)
            turned = rotate(values[:, 2 * i * DH : (2 * i + 1) * DH], cosine, sine)
            key_grad[:, there] = turned.astype(BF16)
            value_grad[:, there] = values[:, (2 * i + 1) * DH : (2 * i + 2) * DH].astype(BF16)


def per_device(query_rows, key_rows, value_rows, cotangent, router_gate, positions):
    rows, heads_width = query_rows.shape[1:]
    group_width = key_rows.shape[2]
    groups = group_width // DH
    ratio = heads_width // group_width
    half_groups, half_width = groups // 2, heads_width // 2
    parts = lax.axis_size("ctx")
    chips = parts // 2
    limit = parts * LOCAL
    wide = ratio * rows
    params = pltpu.CompilerParams(vmem_limit_bytes=(16 + 4 * chips) * 1024 * 1024)
    full = pltpu.CompilerParams(vmem_limit_bytes=63 * 1024 * 1024)

    def call(kernel, name, outs, *args, scratch=(), after=(), flops=10**6, in_hbm=False):
        used = len(args)
        specs = [pl.BlockSpec(memory_space=pltpu.HBM if in_hbm else pltpu.VMEM)] * used
        specs += [pl.BlockSpec(memory_space=pl.ANY)] * len(after)

        def body(*refs):
            kernel(*refs[:used], *refs[used + len(after) :])

        return pl.pallas_call(
            body,
            out_shape=[jax.ShapeDtypeStruct(*out) for out in outs],
            in_specs=specs,
            scratch_shapes=list(scratch),
            compiler_params=full if in_hbm else params,
            cost_estimate=pl.CostEstimate(flops=flops, bytes_accessed=1000, transcendentals=0),
            name=name,
        )(*args, *after)

    index = np.arange(DH) % (DH // 2)
    freq = jnp.asarray((THETA ** (-2.0 * index / DH)).astype(np.float32))[None]
    packet = ((rows + EXTRA, group_width), BF16)
    table = ((rows, DH), F32)
    kv_mine, kv_theirs, cosine, sine = call(
        functools.partial(pack_keys_kernel, limit=limit),
        "pack_keys",
        [packet, packet, table, table],
        key_rows[0],
        value_rows[0],
        positions,
        freq,
        in_hbm=True,
        scratch=[
            pltpu.VMEM((rows, group_width), BF16),
            pltpu.VMEM((rows, group_width), BF16),
            pltpu.VMEM((1, rows), jnp.int32),
            pltpu.VMEM((1, DH), F32),
            pltpu.SemaphoreType.DMA((4,)),
        ],
    )

    hop = [[(2 * x + k, 2 * (x + s) + k) for x in range(chips - s) for k in range(2)] for s in range(chips)]
    cross = [[(a, b + 1 - 2 * (b % 2)) for a, b in pairs] for pairs in hop]
    back_hop = [[(b, a) for a, b in pairs] for pairs in hop]
    back_cross = [[(b, a) for a, b in pairs] for pairs in cross]

    far_own = [lax.ppermute(kv_mine, "ctx", hop[s]) for s in range(1, chips)]
    far_sib = [lax.ppermute(kv_theirs, "ctx", cross[s]) for s in range(1, chips)]

    gate = jnp.tile(jnp.where(positions < limit, router_gate, 0.0), (1, ratio))
    pairs = [[2 * x, 2 * x + 1] for x in range(chips)]
    swap = lambda both: lax.all_to_all(both, "ctx", 0, 0, axis_index_groups=pairs)
    (packed,) = call(
        pack_queries_kernel,
        "pack_queries",
        [((2, rows + EXTRA, heads_width + group_width), BF16)],
        query_rows[0],
        cotangent[0],
        cosine,
        sine,
        gate,
        kv_mine,
        kv_theirs,
        in_hbm=True,
        scratch=[
            pltpu.VMEM((rows, heads_width), BF16),
            pltpu.VMEM((rows, DH), F32),
            pltpu.VMEM((rows, DH), F32),
            pltpu.VMEM((1, wide), F32),
            pltpu.SemaphoreType.DMA((8,)),
        ],
    )
    packets = swap(packed)

    row = ((half_groups, 1, 2 * wide), F32)
    table = ((half_groups, 2 * rows, 2 * wide), F32)
    kv_table = ((half_groups, 2 * rows, DH), BF16)
    q_table = ((half_groups, 2 * wide, DH), BF16)
    keys, values, query, cot, gate_row, raws, grads, tops, sums, crosses = call(
        functools.partial(local_kernel, ratio=ratio),
        "local_scores",
        [kv_table, kv_table, q_table, q_table, ((1, 2 * wide), F32), table, table, row, row, row],
        packets,
        flops=3 * 10**6,
    )

    blocks = 2 * (chips - 1)
    far_table = ((half_groups, blocks * rows, 2 * wide), BF16)
    part_shape = ((rows, group_width), BF16)
    far_keys, _, far_grads, factors, deltas, *far_parts = call(
        functools.partial(far_kernel, blocks=blocks),
        "far_scores",
        [((half_groups, blocks * rows, DH), BF16), far_table, far_table, row, row] + [part_shape] * blocks,
        query,
        cot,
        gate_row,
        tops,
        sums,
        crosses,
        *far_sib,
        *far_own,
        flops=4 * 10**6,
        scratch=[pltpu.VMEM((half_groups, blocks * rows, DH), BF16)],
    )
    sib_got = [lax.ppermute(far_parts[s - 1], "ctx", back_cross[s]) for s in range(1, chips)]
    own_got = [lax.ppermute(far_parts[chips + s - 2], "ctx", back_hop[s]) for s in range(1, chips)]

    part_mine, packed = call(
        functools.partial(near_kernel, ratio=ratio),
        "near_grads",
        [
            ((rows, group_width), F32),
            ((2, rows + EXTRA, half_width + group_width), BF16),
        ],
        raws,
        grads,
        factors,
        deltas,
        keys,
        query,
        cot,
        far_keys,
        far_grads,
        flops=4 * 10**6,
        scratch=[
            pltpu.VMEM((half_groups, 2 * rows, 2 * wide), BF16),
            pltpu.VMEM((half_groups, 2 * rows, 2 * wide), BF16),
            pltpu.VMEM((2, rows, group_width), F32),
        ],
    )
    back = swap(packed)
    query_grad, gate_grad, done = call(
        functools.partial(finish_queries_kernel, limit=limit),
        "finish_queries",
        [((rows, heads_width), BF16), ((1, rows), F32), ((8, DH), F32)],
        back,
        positions,
        cosine,
        sine,
    )
    key_grad, value_grad = call(
        finish_keys_kernel,
        "finish_keys",
        [((rows, group_width), BF16)] * 2,
        part_mine,
        back,
        cosine,
        sine,
        *[part for pair in zip(sib_got, own_got) for part in pair],
        after=[done],
    )
    return (query_grad[None], key_grad[None], value_grad[None], gate_grad)


def solution(mesh):
    wide = P(("group", "dp"), "ctx", None)
    narrow = P(("group", "dp"), "ctx")
    return jax.shard_map(
        per_device,
        mesh=mesh,
        in_specs=(wide, wide, wide, wide, narrow, narrow),
        out_specs=(wide, wide, wide, narrow),
        check_vma=False,
    )
```

time: 47.3 us -> 38 us (0.80)
  waiting for transfers between devices: 19.7 us -> 1.08 us
  blocking collectives: 0 us -> 11.1 us
  Pallas kernels: 11.9 us -> 14.6 us
  local copies, waits for them, and re-layouts: 2.45 us -> 0.69 us
  starting transfers between devices: 10.3 us -> 8.72 us
  other arithmetic: 1.86 us -> 0.7 us
    ppermute x6 -> x4, waiting for transfers between devices: 19.7 us -> 1.08 us  [the longest x1 1.07 us: per_device(): lax.ppermute(far_parts[chips + s - 2], 'ctx', back_hop[s])]
    all_to_all x0 -> x2, blocking collectives: none -> 11.1 us  [per_device(): lax.all_to_all(both, 'ctx', 0, 0, axis_index_groups=pairs)]
    pallas_call x3 -> x7, Pallas kernels: 11.9 us -> 14.6 us  [call(): pl.pallas_call(body, out_shape=[jax.ShapeDtypeStruct(*out) for out in out...]
    unnamed x12 -> x6, local copies, waits for them, and re-layouts: 2.28 us -> 0.02 us
    ppermute x6 -> x4, starting transfers between devices: 10.3 us -> 8.72 us  [the longest x1 4.85 us: per_device(): far_own = [lax.ppermute(kv_mine, 'ctx', hop[s]) for s in range(1, chips)]]
    convert_element_type x2 -> x0, other arithmetic: 0.85 us -> none  [the longest x1 0.76 us: per_device(): angle = positions[0].astype(jnp.float32)[:, None] * freq[None, :]]
    another operation x2, local copies, waits for them, and re-layouts: 0.09 us -> 0.67 us  [per_device(): gate = jnp.tile(jnp.where(positions < limit, router_gate, 0.0), (1, ratio))]
  transfers between devices with their start and end apart: 6 -> 4, of which waited for: 2 -> 1; matrix products, arithmetic and copies ran while one was open for 2% -> 4% of each run, Pallas kernels for 0% -> 21%
where the time goes in v2:
time: 38 us; the launch traced here: 37.6 us
  Pallas kernels  14.6 us (38%)
  blocking collectives  11.1 us (29%)
  starting transfers between devices  8.72 us (23%)
  waiting for transfers between devices  1.08 us (3%)
  between operations  0.72 us (2%)
  other arithmetic  0.7 us (2%)
  local copies, waits for them, and re-layouts  0.69 us (2%)
    pallas_call x7, Pallas kernels, call(): pl.pallas_call(body, out_shape=[jax.ShapeDtypeStruct(*out) for out in out...  14.6 us
    all_to_all x2, blocking collectives, per_device(): lax.all_to_all(both, 'ctx', 0, 0, axis_index_groups=pairs)  11.1 us
    ppermute x1, starting transfers between devices, per_device(): far_own = [lax.ppermute(kv_mine, 'ctx', hop[s]) for s in range(1, chips)]  4.85 us
    ppermute x1, starting transfers between devices, per_device(): lax.ppermute(kv_theirs, 'ctx', cross[s])  1.3 us
    ppermute x1, starting transfers between devices, per_device(): lax.ppermute(far_parts[chips + s - 2], 'ctx', back_hop[s])  1.29 us
    ppermute x1, starting transfers between devices, per_device(): lax.ppermute(far_parts[s - 1], 'ctx', back_cross[s])  1.28 us
    ppermute x1, waiting for transfers between devices, per_device(): lax.ppermute(far_parts[chips + s - 2], 'ctx', back_hop[s])  1.07 us
  transfers between devices with their start and end apart: 4, of which 1 were waited for; matrix products, arithmetic and copies ran while one was open for 4% of the time, Pallas kernels for 21%

profile of v2, /device:TPU:0, one launch (start us, length us, event | category | flops | bytes accessed | tf_op | source)
XLA Modules:
  0.0 37.6 jit_solution(18222408041241330360)
XLA Ops:
  0.6 1.9 %pack_keys.1 = (bf16[176,512]{1,0:T(8,128)(2,1)}, bf16[176,512]{1,0:T(8,128)(2,1)}, f32[160,128]{1,0:T(8,128)}, f32[160,128]{1,0:T(8,128)}) custom-call(bf16[160,512]{1,0:T(8,128)(2,1)} %bitcast.10, bf16[160,512]{1,0:T(8,128)(2,1)} %bitcast.11, s32[1,160]{1,0:T(1,128)} %refs_1_.1, f32[1,128]{1,0:T(1,128)} %constant.13.refs_3_), custom_call_target="tpu_custom_call" | custom-call | flops 1000000 | bytes 1000 | tf_op jit(solution)/shard_map/pack_keys/pallas_call | solution.py:337
  2.6 4.9 %collective-permute-start.1 = (bf16[176,512]{1,0:T(8,128)(2,1)}, bf16[176,512]{1,0:T(8,128)(2,1)S(1)}, u32[]{:S(2)}, u32[]{:S(2)}) collective-permute-start(bf16[176,512]{1,0:T(8,128)(2,1)} %get-tuple-element.32.refs_5_), channel_id=1, source_target_pairs={{0,2},{1,3},{4,6},{5,7},{8,10},{9,11},{12,14},{13,15},{16,18},{17,... | collective-permute-start | bytes 540680 | tf_op jit(solution)/shard_map/ppermute | solution.py:374
  7.4 1.3 %collective-permute-start = (bf16[176,512]{1,0:T(8,128)(2,1)}, bf16[176,512]{1,0:T(8,128)(2,1)S(1)}, u32[]{:S(2)}, u32[]{:S(2)}) collective-permute-start(bf16[176,512]{1,0:T(8,128)(2,1)} %get-tuple-element.33.refs_6_), channel_id=1, source_target_pairs={{0,3},{1,2},{4,7},{5,6},{8,11},{9,10},{12,15},{13,14},{16,19},{17,... | collective-permute-start | bytes 540680 | tf_op jit(solution)/shard_map/ppermute | solution.py:375
  8.7 0.7 %compare_select_fusion = f32[1,160]{1,0:T(1,128)S(1)} fusion(f32[1,160]{1,0:T(1,128)} %param.11, s32[1,160]{1,0:T(1,128)} %refs_1_.1), kind=kLoop, calls=%fused_computation | loop fusion | flops 320 | bytes 1920 | tf_op jit(solution)/shard_map/jit(_where)/select_n | solution.py:377
  9.4 0.7 %tile.13.refs_4_ = f32[1,640]{1,0:T(1,128)} reshape(f32[4,160]{1,0:T(4,128)S(1)} %tile.12) | data formatting | bytes 5120 | tf_op jit(solution)/shard_map/tile | solution.py:377
  10.1 2.8 %pack_queries.1 = bf16[2,176,2560]{2,1,0:T(8,128)(2,1)} custom-call(bf16[160,2048]{1,0:T(8,128)(2,1)} %bitcast.8, bf16[160,2048]{1,0:T(8,128)(2,1)} %bitcast.9, f32[160,128]{1,0:T(8,128)} %get-tuple-element.30.refs_2_, f32[160,128]{1,0:T(8,128)} %get-tuple-element.31.refs_3_, f32[1,640]{1,0:T(1,128)} %tile.13.refs_4_, ...), custom_call_target="tpu_custom_call" | custom-call | flops 1000000 | bytes 1000 | tf_op jit(solution)/shard_map/pack_queries/pallas_call | solution.py:337
  12.9 6.4 %all_to_all.10.refs_0_ = bf16[2,176,2560]{2,1,0:T(8,128)(2,1)S(1)} all-to-all(bf16[2,176,2560]{2,1,0:T(8,128)(2,1)} %pack_queries.1), channel_id=1, replica_groups={{0,1},{2,3},{4,5},{6,7},{8,9},{10,11},{12,13},{14,15},{16,17},{18,19},{..., dimensions={0} | all-to-all | bytes 3604480 | tf_op jit(solution)/shard_map/all_to_all | solution.py:379
  19.3 1.7 %local_scores.1 = (bf16[2,320,128]{2,1,0:T(8,128)(2,1)S(1)}, bf16[2,320,128]{2,1,0:T(8,128)(2,1)}, bf16[2,1280,128]{2,1,0:T(8,128)(2,1)S(1)}, bf16[2,1280,128]{2...) custom-call(bf16[2,176,2560]{2,1,0:T(8,128)(2,1)S(1)} %all_to_all.10, ...), custom_call_target="tpu_custom_call" | custom-call | flops 3000000 | bytes 1000 | tf_op jit(solution)/shard_map/local_scores/pallas_call | solution.py:337
  20.9 0.0 collective-permute-done.1.refs_7_
  20.9 0.0 collective-permute-done.refs_6_
  20.9 3.9 %far_scores.1 = (bf16[2,320,128]{2,1,0:T(8,128)(2,1)S(1)}, bf16[2,320,1280]{2,1,0:T(8,128)(2,1)}, bf16[2,320,1280]{2,1,0:T(8,128)(2,1)S(1)}, f32[2,1,1280]{2,1,0...) custom-call(bf16[2,1280,128]{2,1,0:T(8,128)(2,1)S(1)} %get-tuple-element.36.ref, ...), custom_call_target="tpu_custom_call" | custom-call | flops 4000000 | bytes 1000 | tf_op jit(solution)/shard_map/far_scores/pallas_call | solution.py:337
  24.8 1.3 %collective-permute-start.2 = (bf16[160,512]{1,0:T(8,128)(2,1)S(1)}, bf16[160,512]{1,0:T(8,128)(2,1)S(1)}, u32[]{:S(2)}, u32[]{:S(2)}) collective-permute-start(bf16[160,512]{1,0:T(8,128)(2,1)S(1)} %get-tuple-element.50), channel_id=1, source_target_pairs={{3,0},{2,1},{7,4},{6,5},{11,8},{10,9},{15,12},{14,13},{19,16},{18,... | collective-permute-start | bytes 491528 | tf_op jit(solution)/shard_map/ppermute | solution.py:432
  26.1 1.3 %collective-permute-start.3 = (bf16[160,512]{1,0:T(8,128)(2,1)S(1)}, bf16[160,512]{1,0:T(8,128)(2,1)S(1)}, u32[]{:S(2)}, u32[]{:S(2)}) collective-permute-start(bf16[160,512]{1,0:T(8,128)(2,1)S(1)} %get-tuple-element.51), channel_id=1, source_target_pairs={{2,0},{3,1},{6,4},{7,5},{10,8},{11,9},{14,12},{15,13},{18,16},{19,... | collective-permute-start | bytes 491528 | tf_op jit(solution)/shard_map/ppermute | solution.py:433
  27.4 2.3 %near_grads.1 = (f32[160,512]{1,0:T(8,128)S(1)}, bf16[2,176,1536]{2,1,0:T(8,128)(2,1)S(1)}) custom-call(f32[2,320,1280]{2,1,0:T(8,128)S(1)} %get-tuple-element.34.refs_0_, f32[2,320,1280]{2,1,0:T(8,128)S(1)} %get-tuple-element.35.refs_1_, f32[2,1,1280]{2,1,0:T(1,128)S(1)} %get-tuple-element.42.refs_2_, f32[2,1,1280]{2,1,0:T(1,128)S(1)} %get-tuple-element.43.refs_3_, ...), custom_call_target="tpu_custom_call" | custom-call | flops 4000000 | bytes 1000 | tf_op jit(solution)/shard_map/near_grads/pallas_call | solution.py:337
  29.7 0.0 copy-start
  29.7 0.0 copy-start.1
  29.7 0.0 copy-start.2
  29.7 4.7 %all_to_all.11.refs_0_.refs_1_ = bf16[2,176,1536]{2,1,0:T(8,128)(2,1)S(1)} all-to-all(bf16[2,176,1536]{2,1,0:T(8,128)(2,1)S(1)} %get-tuple-element.47), channel_id=1, replica_groups={{0,1},{2,3},{4,5},{6,7},{8,9},{10,11},{12,13},{14,15},{16,17},{18,19},{..., dimensions={0} | all-to-all | bytes 2162688 | tf_op jit(solution)/shard_map/all_to_all | solution.py:379
  34.5 0.0 copy-done
  34.5 0.0 copy-done.1
  34.5 0.0 copy-done.2
  34.5 1.2 %finish_queries.1 = (bf16[160,2048]{1,0:T(8,128)(2,1)}, f32[1,160]{1,0:T(1,128)}, f32[8,128]{1,0:T(8,128)S(1)}) custom-call(bf16[2,176,1536]{2,1,0:T(8,128)(2,1)S(1)} %all_to_all.11.refs_0_.refs_1_, s32[1,160]{1,0:T(1,128)S(1)} %copy-done.2, f32[160,128]{1,0:T(8,128)S(1)} %copy-done, f32[160,128]{1,0:T(8,128)S(1)} %copy-done.1), custom_call_target="tpu_custom_call" | custom-call | flops 1000000 | bytes 1000 | tf_op jit(solution)/shard_map/finish_queries/pallas_call | solution.py:337
  35.7 0.0 collective-permute-done.2.refs_4_
  35.7 1.1 %collective-permute-done.3.refs_5_ = bf16[160,512]{1,0:T(8,128)(2,1)S(1)} collective-permute-done((bf16[160,512]{1,0:T(8,128)(2,1)S(1)}, bf16[160,512]{1,0:T(8,128)(2,1)S(1)}, u32[]{:S(2)}, u32[]{:S(2)}) %collective-permute-start.3) | collective-permute-done | bytes 163872 | tf_op jit(solution)/shard_map/ppermute | solution.py:433
  36.7 0.8 %finish_keys.1 = (bf16[160,512]{1,0:T(8,128)(2,1)}, bf16[160,512]{1,0:T(8,128)(2,1)}) custom-call(f32[160,512]{1,0:T(8,128)S(1)} %get-tuple-element.49.refs_0_, bf16[2,176,1536]{2,1,0:T(8,128)(2,1)S(1)} %all_to_all.11.refs_0_.refs_1_, f32[160,128]{1,0:T(8,128)S(1)} %copy-done, f32[160,128]{1,0:T(8,128)S(1)} %copy-done.1, ...), custom_call_target="tpu_custom_call" | custom-call | flops 1000000 | bytes 1000 | tf_op jit(solution)/shard_map/finish_keys/pallas_call | solution.py:337
  (1 shorter events, 0.0 us)
Async XLA Ops:
  2.6 18.4 %collective-permute-start.1 = (bf16[176,512]{1,0:T(8,128)(2,1)}, bf16[176,512]{1,0:T(8,128)(2,1)S(1)}, u32[]{:S(2)}, u32[]{:S(2)}) collective-permute-start(bf16[176,512]{1,0:T(8,128)(2,1)} %get-tuple-element.32.refs_5_), channel_id=1, source_target_pairs={{0,2},{1,3},{4,6},{5,7},{8,10},{9,11},{12,14},{13,15},{16,18},{17,... | collective-permute-start | bytes 540680 | tf_op jit(solution)/shard_map/ppermute | solution.py:374
  7.4 13.5 %collective-permute-start = (bf16[176,512]{1,0:T(8,128)(2,1)}, bf16[176,512]{1,0:T(8,128)(2,1)S(1)}, u32[]{:S(2)}, u32[]{:S(2)}) collective-permute-start(bf16[176,512]{1,0:T(8,128)(2,1)} %get-tuple-element.33.refs_6_), channel_id=1, source_target_pairs={{0,3},{1,2},{4,7},{5,6},{8,11},{9,10},{12,15},{13,14},{16,19},{17,... | collective-permute-start | bytes 540680 | tf_op jit(solution)/shard_map/ppermute | solution.py:375
  24.8 10.8 %collective-permute-start.2 = (bf16[160,512]{1,0:T(8,128)(2,1)S(1)}, bf16[160,512]{1,0:T(8,128)(2,1)S(1)}, u32[]{:S(2)}, u32[]{:S(2)}) collective-permute-start(bf16[160,512]{1,0:T(8,128)(2,1)S(1)} %get-tuple-element.50), channel_id=1, source_target_pairs={{3,0},{2,1},{7,4},{6,5},{11,8},{10,9},{15,12},{14,13},{19,16},{18,... | collective-permute-start | bytes 491528 | tf_op jit(solution)/shard_map/ppermute | solution.py:432
  26.1 10.6 %collective-permute-start.3 = (bf16[160,512]{1,0:T(8,128)(2,1)S(1)}, bf16[160,512]{1,0:T(8,128)(2,1)S(1)}, u32[]{:S(2)}, u32[]{:S(2)}) collective-permute-start(bf16[160,512]{1,0:T(8,128)(2,1)S(1)} %get-tuple-element.51), channel_id=1, source_target_pairs={{2,0},{3,1},{6,4},{7,5},{10,8},{11,9},{14,12},{15,13},{18,16},{19,... | collective-permute-start | bytes 491528 | tf_op jit(solution)/shard_map/ppermute | solution.py:433
  29.7 4.8 %copy-start = (f32[160,128]{1,0:T(8,128)S(1)}, f32[160,128]{1,0:T(8,128)}, u32[]{:S(2)}) copy-start(f32[160,128]{1,0:T(8,128)} %get-tuple-element.30.refs_2_) | copy-start | bytes 245764
  29.7 4.7 %copy-start.1 = (f32[160,128]{1,0:T(8,128)S(1)}, f32[160,128]{1,0:T(8,128)}, u32[]{:S(2)}) copy-start(f32[160,128]{1,0:T(8,128)} %get-tuple-element.31.refs_3_) | copy-start | bytes 245764
  29.7 4.7 %copy-start.2 = (s32[1,160]{1,0:T(1,128)S(1)}, s32[1,160]{1,0:T(1,128)}, u32[]{:S(2)}) copy-start(s32[1,160]{1,0:T(1,128)} %refs_1_.1) | copy-start | bytes 1924

commit v3 on v2

--- a/solution.py
+++ b/solution.py
@@ -76,23 +76,26 @@
     return jnp.sum(rows.astype(F32), axis=0, keepdims=True)
 
 
-def pack_keys_kernel(
-    key_in, value_in, pos_in, freq_in, mine_ref, theirs_ref, cos_ref, sin_ref, key, value, pos, freq, sems, *, limit
+def pack_kernel(
+    key_in, value_in, query_in, cot_in, gate_in, pos_in, freq_in, mine_out, theirs_out, packed_out, cos_out, sin_out,
+    key, value, query, gate, pos, freq, mine, theirs, packed, cos_ref, sin_ref, sems, out_sems, *, limit
 ):
-    copies = [
-        pltpu.make_async_copy(source, target, sems.at[i])
-        for i, (source, target) in enumerate(((pos_in, pos), (freq_in, freq), (key_in, key), (value_in, value)))
-    ]
-    for copy in copies:
+    rows, width = key.shape
+    side_width = width // 2
+    half = query.shape[1] // 2
+    core = core_of()
+    loads = [(pos_in, pos), (freq_in, freq), (key_in, key), (value_in, value), (gate_in, gate), (query_in, query)]
+    for side in range(2):
+        there = slice(side * half, (side + 1) * half)
+        loads.append((cot_in.at[:, there], packed_out.at[side, :rows, half : 2 * half]))
+    loads = [pltpu.make_async_copy(source, target, sems.at[i]) for i, (source, target) in enumerate(loads)]
+    for copy in loads:
         copy.start()
-    rows = key.shape[0]
-    half = key.shape[1] // 2
-    core = core_of()
-    copies[0].wait()
-    copies[1].wait()
+    loads[0].wait()
+    loads[1].wait()
     places = pos[...]
     count = jnp.sum(jnp.where(places < limit, 1.0, 0.0), axis=1, keepdims=True)
-    count = jnp.broadcast_to(count, (EXTRA, 2 * half)).astype(BF16)
+    count = jnp.broadcast_to(count, (EXTRA, width)).astype(BF16)
     down = lax.broadcasted_iota(jnp.int32, (rows, rows), 0)
     along = lax.broadcasted_iota(jnp.int32, (rows, rows), 1)
     column = jnp.sum(jnp.where(down == along, places.astype(F32), 0.0), axis=1, keepdims=True)
@@ -101,48 +104,50 @@
     sine = jnp.where(lane < DH // 2, -sine, sine)
     cos_ref[...] = cosine
     sin_ref[...] = sine
-    copies[2].wait()
-    copies[3].wait()
-    for out_ref, side in ((mine_ref, core), (theirs_ref, 1 - core)):
-        for i in range(half // DH):
-            there = pl.ds(pl.multiple_of(side * half + i * DH, DH), DH)
+    loads[2].wait()
+    loads[3].wait()
+    for out_ref, side in ((mine, core), (theirs, 1 - core)):
+        for i in range(side_width // DH):
+            there = pl.ds(pl.multiple_of(side * side_width + i * DH, DH), DH)
             turned = rotate(key[:, there].astype(F32), cosine, sine)
             out_ref[:rows, 2 * i * DH : (2 * i + 1) * DH] = turned.astype(BF16)
             out_ref[:rows, (2 * i + 1) * DH : (2 * i + 2) * DH] = value[:, there]
         out_ref[rows:, :] = count
-
-
-def pack_queries_kernel(
-    query_in, cot_in, cos_in, sin_in, gate_in, mine_in, theirs_in, out_ref, query, cos_ref, sin_ref, gate_ref, sems
-):
-    rows = query.shape[0]
-    half = query.shape[1] // 2
-    core = core_of()
-    pairs = [
-        (query_in, query),
-        (cos_in, cos_ref),
-        (sin_in, sin_ref),
-        (gate_in, gate_ref),
-        (mine_in, out_ref.at[core, :, 2 * half :]),
-        (theirs_in, out_ref.at[1 - core, :, 2 * half :]),
-        (cot_in.at[:, :half], out_ref.at[0, :rows, half : 2 * half]),
-        (cot_in.at[:, half:], out_ref.at[1, :rows, half : 2 * half]),
+    stores = [
+        (mine, mine_out),
+        (theirs, theirs_out),
+        (cos_ref, cos_out),
+        (sin_ref, sin_out),
+        (mine, packed_out.at[core, :, 2 * half :]),
+        (theirs, packed_out.at[1 - core, :, 2 * half :]),
     ]
-    copies = [pltpu.make_async_copy(source, target, sems.at[i]) for i, (source, target) in enumerate(pairs)]
-    for copy in copies:
+    stores += [(packed.at[side], packed_out.at[side, :, :half]) for side in range(2)]
+    stores = [pltpu.make_async_copy(source, target, out_sems.at[i]) for i, (source, target) in enumerate(stores)]
+    for copy in stores[:6]:
         copy.start()
-    for copy in copies[:4]:
-        copy.wait()
-    cosine, sine = cos_ref[...] * (SCALE * LOG2E), sin_ref[...] * (SCALE * LOG2E)
-    gate = split_rows(gate_ref[...], EXTRA)
+    loads[4].wait()
+    loads[5].wait()
+    gates = split_rows(jnp.where(places < limit, gate[...], 0.0), EXTRA)
+    cosine, sine = cosine * (SCALE * LOG2E), sine * (SCALE * LOG2E)
     for side in range(2):
         for i in range(half // DH):
             there = slice(side * half + i * DH, side * half + (i + 1) * DH)
             turned = rotate(query[:, there].astype(F32), cosine, sine)
-            out_ref[side, :rows, i * DH : (i + 1) * DH] = turned.astype(BF16)
-        out_ref[side, rows:, : gate.shape[1]] = gate
-    for copy in copies[4:]:
+            packed[side, :rows, i * DH : (i + 1) * DH] = turned.astype(BF16)
+        packed[side, rows:, :rows] = gates
+        stores[6 + side].start()
+    for copy in loads[6:] + stores:
         copy.wait()
+
+
+def chosen(shape, ratio, dim):
+    down = lax.broadcasted_iota(jnp.int32, shape, 0)
+    along = lax.broadcasted_iota(jnp.int32, shape, 1)
+    rows = shape[1 - dim]
+    long, short = (down, along) if dim == 0 else (along, down)
+    for _ in range(1, ratio):
+        long = jnp.where(long >= rows, long - rows, long)
+    return jnp.where(long == short, 1.0, 0.0).astype(BF16)
 
 
 def chunks(low, high):
@@ -165,7 +170,8 @@
                 at = (i * ratio + h) * DH
                 query[i, to, :] = packets[side, :rows, at : at + DH]
                 cot[i, to, :] = packets[side, :rows, half + at : half + at + DH]
-        gate[:, side * wide : (side + 1) * wide] = joined_row(packets[side, rows:, :wide])
+        gates = dot(packets[side, rows:, :rows], chosen((rows, wide), ratio, 1), NN)
+        gate[:, side * wide : (side + 1) * wide] = joined_row(gates)
     count = packets[0, rows:, 2 * half : 2 * half + 256].astype(F32)[:1]
     for i in range(half_groups):
         for block in range(2):
@@ -210,38 +216,49 @@
         for i in range(half_groups):
             far_keys[i, there, :] = packets[j][:rows, 2 * i * DH : (2 * i + 1) * DH]
             far_values[i, there, :] = packets[j][:rows, (2 * i + 1) * DH : (2 * i + 2) * DH]
-    counts = [packet[rows:, :256].astype(F32)[:1] for packet in packets]
-    for i in range(half_groups):
-        for here in chunks(0, lanes):
-            width = here.stop - here.start
-            scores = dot(far_keys[i], query[i, here, :], NT)
-            slot = lax.broadcasted_iota(jnp.int32, (rows, width), 0).astype(F32)
-            shown = [
-                jnp.where(slot < counts[j][:, :width], scores[j * rows : (j + 1) * rows], HIDDEN)
-                for j in range(blocks)
-            ]
-            shown = jnp.concatenate(shown, axis=0)
-            old_top = tops[i, :, here]
-            top = jnp.maximum(old_top, jnp.max(shown, axis=0, keepdims=True))
-            raw = jnp.exp2(shown - top)
-            shrink = jnp.exp2(old_top - top)
-            inverse = 1.0 / (sums[i, :, here] * shrink + jnp.sum(raw, axis=0, keepdims=True))
-            prob_grad = dot(far_values[i], cot[i, here, :], NT)
-            cross = crosses[i, :, here] * shrink + jnp.sum(raw * prob_grad, axis=0, keepdims=True)
-            delta = cross * inverse
-            factor = inverse * gate[:, here]
-            factors[i, :, here] = factor * shrink
-            deltas[i, :, here] = delta
-            gated = raw * factor
-            weights[i, :, here] = gated.astype(BF16)
-            score_grads[i, :, here] = (gated * (prob_grad - delta)).astype(BF16)
-        for j, out_ref in enumerate(parts):
-            part_of(weights, score_grads, query, cot, out_ref, i, slice(j * rows, (j + 1) * rows), slice(0, lanes))
+    alone = lax.axis_index("ctx") < 2
+
+    @pl.when(alone)
+    def _():
+        for i in range(half_groups):
+            inverse = 1.0 / sums[i]
+            factors[i] = inverse * gate[...]
+            deltas[i] = crosses[i] * inverse
+
+    @pl.when(jnp.logical_not(alone))
+    def _():
+        counts = [packet[rows:, :256].astype(F32)[:1] for packet in packets]
+        for i in range(half_groups):
+            for here in chunks(0, lanes):
+                width = here.stop - here.start
+                scores = dot(far_keys[i], query[i, here, :], NT)
+                slot = lax.broadcasted_iota(jnp.int32, (rows, width), 0).astype(F32)
+                shown = [
+                    jnp.where(slot < counts[j][:, :width], scores[j * rows : (j + 1) * rows], HIDDEN)
+                    for j in range(blocks)
+                ]
+                shown = jnp.concatenate(shown, axis=0)
+                old_top = tops[i, :, here]
+                top = jnp.maximum(old_top, jnp.max(shown, axis=0, keepdims=True))
+                raw = jnp.exp2(shown - top)
+                shrink = jnp.exp2(old_top - top)
+                inverse = 1.0 / (sums[i, :, here] * shrink + jnp.sum(raw, axis=0, keepdims=True))
+                prob_grad = dot(far_values[i], cot[i, here, :], NT)
+                cross = crosses[i, :, here] * shrink + jnp.sum(raw * prob_grad, axis=0, keepdims=True)
+                delta = cross * inverse
+                factor = inverse * gate[:, here]
+                factors[i, :, here] = factor * shrink
+                deltas[i, :, here] = delta
+                gated = raw * factor
+                weights[i, :, here] = gated.astype(BF16)
+                score_grads[i, :, here] = (gated * (prob_grad - delta)).astype(BF16)
+            for j, out_ref in enumerate(parts):
+                part_of(weights, score_grads, query, cot, out_ref, i, slice(j * rows, (j + 1) * rows), slice(0, lanes))
 
 
 def near_kernel(
     raws, grads, factors, deltas, keys, query, cot, far_keys, far_grads,
-    part_mine, out_ref, weights, score_grads, parts,
+    part_mine, out_ref, weights, score_grads, parts, acc,
     *, ratio
 ):
     rows = part_mine.shape[0]
@@ -259,30 +276,36 @@
             there, lanes = slice(block * rows, (block + 1) * rows), slice(block * wide, 2 * wide)
             part_of(weights, score_grads, query, cot, parts.at[block], i, there, lanes)
             reach, lanes = (block + 1) * rows, slice(block * wide, (block + 1) * wide)
-            total = dot(score_grads[i, :reach, lanes], keys[i, :reach, :], TN)
-            total = (total + dot(far_grads[i, :, lanes], far_keys[i], TN)) * SCALE
+            acc[i, lanes, :] = dot(score_grads[i, :reach, lanes], keys[i, :reach, :], TN)
+
+    @pl.when(lax.axis_index("ctx") >= 2)
+    def _():
+        for i in range(half_groups):
+            acc[i] += dot(far_grads[i], far_keys[i], TN)
+
+    for i in range(half_groups):
+        for block in range(2):
             for h in range(ratio):
                 at = (i * ratio + h) * DH
-                out_ref[block, :rows, at : at + DH] = total[h * rows : (h + 1) * rows].astype(BF16)
+                low = block * wide + h * rows
+                out_ref[block, :rows, at : at + DH] = (acc[i, low : low + rows] * SCALE).astype(BF16)
     part_mine[...] = parts[core_of()]
     for block in range(2):
         out_ref[block, :rows, half:] = parts[block].astype(BF16)
     summed = deltas[0]
     for i in range(1, half_groups):
         summed = summed + deltas[i]
-    down = lax.broadcasted_iota(jnp.int32, (wide, rows), 0)
-    along = lax.broadcasted_iota(jnp.int32, (wide, rows), 1)
-    for h in range(1, ratio):
-        down = jnp.where(down >= rows, down - rows, down)
-    chosen = jnp.where(down == along, 1.0, 0.0).astype(BF16)
     for block in range(2):
-        own = joined_row(dot(split_rows(summed[:, block * wide : (block + 1) * wide], 16), chosen, NN))
+        own = split_rows(summed[:, block * wide : (block + 1) * wide], 16)
+        own = joined_row(dot(own, chosen((wide, rows), ratio, 0), NN))
         out_ref[block, rows:, :rows] = split_rows(own, EXTRA)
 
 
-def finish_queries_kernel(back, pos_ref, cos_ref, sin_ref, query_grad, gate_grad, done, *, limit):
-    rows = cos_ref.shape[0]
-    half = query_grad.shape[1] // 2
+def finish_kernel(back, part_mine, pos_ref, cos_ref, sin_ref, *refs, limit):
+    got, (query_grad, key_grad, value_grad, gate_grad) = refs[:-4], refs[-4:]
+    rows, width = part_mine.shape
+    half, side_width = query_grad.shape[1] // 2, width // 2
+    core = core_of()
     cosine, sine = cos_ref[...], -sin_ref[...]
     for side in range(2):
         for i in range(half // DH):
@@ -291,23 +314,14 @@
             query_grad[:, there] = turned.astype(BF16)
     gate = joined_row(back[0, rows:, :rows]) + joined_row(back[1, rows:, :rows])
     gate_grad[...] = jnp.where(pos_ref[...] < limit, gate, 0.0)
-    done[...] = jnp.zeros_like(done)
-
-
-def finish_keys_kernel(part_mine, back, cos_ref, sin_ref, *refs):
-    got, (key_grad, value_grad) = refs[:-2], refs[-2:]
-    rows, width = part_mine.shape
-    half = width // 2
-    core = core_of()
-    cosine, sine = cos_ref[...], -sin_ref[...]
     total = part_mine[...]
-    other = back[1 - core, :rows, back.shape[2] - width :].astype(F32)
+    other = back[1 - core, :rows, half:].astype(F32)
     for s in range(len(got) // 2):
         other = other + got[2 * s][...].astype(F32)
         total = total + got[2 * s + 1][...].astype(F32)
     for values, side in ((total, core), (other, 1 - core)):
-        for i in range(half // DH):
-            there = pl.ds(pl.multiple_of(side * half + i * DH, DH), DH)
+        for i in range(side_width // DH):
+            there = pl.ds(pl.multiple_of(side * side_width + i * DH, DH), DH)
             turned = rotate(values[:, 2 * i * DH : (2 * i + 1) * DH], cosine, sine)
             key_grad[:, there] = turned.astype(BF16)
             value_grad[:, there] = values[:, (2 * i + 1) * DH : (2 * i + 2) * DH].astype(BF16)
@@ -326,43 +340,50 @@
     params = pltpu.CompilerParams(vmem_limit_bytes=(16 + 4 * chips) * 1024 * 1024)
     full = pltpu.CompilerParams(vmem_limit_bytes=63 * 1024 * 1024)
 
-    def call(kernel, name, outs, *args, scratch=(), after=(), flops=10**6, in_hbm=False):
-        used = len(args)
-        specs = [pl.BlockSpec(memory_space=pltpu.HBM if in_hbm else pltpu.VMEM)] * used
-        specs += [pl.BlockSpec(memory_space=pl.ANY)] * len(after)
-
-        def body(*refs):
-            kernel(*refs[:used], *refs[used + len(after) :])
-
+    def call(kernel, name, outs, *args, scratch=(), flops=10**6, in_hbm=False):
+        spec = pl.BlockSpec(memory_space=pltpu.HBM if in_hbm else pltpu.VMEM)
         return pl.pallas_call(
-            body,
+            kernel,
             out_shape=[jax.ShapeDtypeStruct(*out) for out in outs],
-            in_specs=specs,
+            in_specs=[spec] * len(args),
+            out_specs=[spec] * len(outs),
             scratch_shapes=list(scratch),
             compiler_params=full if in_hbm else params,
             cost_estimate=pl.CostEstimate(flops=flops, bytes_accessed=1000, transcendentals=0),
             name=name,
-        )(*args, *after)
+        )(*args)
 
     index = np.arange(DH) % (DH // 2)
     freq = jnp.asarray((THETA ** (-2.0 * index / DH)).astype(np.float32))[None]
     packet = ((rows + EXTRA, group_width), BF16)
+    packets_shape = ((2, rows + EXTRA, heads_width + group_width), BF16)
     table = ((rows, DH), F32)
-    kv_mine, kv_theirs, cosine, sine = call(
-        functools.partial(pack_keys_kernel, limit=limit),
-        "pack_keys",
-        [packet, packet, table, table],
+    kv_mine, kv_theirs, packed, cosine, sine = call(
+        functools.partial(pack_kernel, limit=limit),
+        "pack",
+        [packet, packet, packets_shape, table, table],
         key_rows[0],
         value_rows[0],
+        query_rows[0],
+        cotangent[0],
+        router_gate,
         positions,
         freq,
         in_hbm=True,
         scratch=[
             pltpu.VMEM((rows, group_width), BF16),
             pltpu.VMEM((rows, group_width), BF16),
+            pltpu.VMEM((rows, heads_width), BF16),
+            pltpu.VMEM((1, rows), F32),
             pltpu.VMEM((1, rows), jnp.int32),
             pltpu.VMEM((1, DH), F32),
-            pltpu.SemaphoreType.DMA((4,)),
+            pltpu.VMEM(*packet),
+            pltpu.VMEM(*packet),
+            pltpu.VMEM((2, rows + EXTRA, half_width), BF16),
+            pltpu.VMEM(*table),
+            pltpu.VMEM(*table),
+            pltpu.SemaphoreType.DMA((8,)),
+            pltpu.SemaphoreType.DMA((8,)),
         ],
     )
 
@@ -374,29 +395,8 @@
     far_own = [lax.ppermute(kv_mine, "ctx", hop[s]) for s in range(1, chips)]
     far_sib = [lax.ppermute(kv_theirs, "ctx", cross[s]) for s in range(1, chips)]
 
-    gate = jnp.tile(jnp.where(positions < limit, router_gate, 0.0), (1, ratio))
     pairs = [[2 * x, 2 * x + 1] for x in range(chips)]
     swap = lambda both: lax.all_to_all(both, "ctx", 0, 0, axis_index_groups=pairs)
-    (packed,) = call(
-        pack_queries_kernel,
-        "pack_queries",
-        [((2, rows + EXTRA, heads_width + group_width), BF16)],
-        query_rows[0],
-        cotangent[0],
-        cosine,
-        sine,
-        gate,
-        kv_mine,
-        kv_theirs,
-        in_hbm=True,
-        scratch=[
-            pltpu.VMEM((rows, heads_width), BF16),
-            pltpu.VMEM((rows, DH), F32),
-            pltpu.VMEM((rows, DH), F32),
-            pltpu.VMEM((1, wide), F32),
-            pltpu.SemaphoreType.DMA((8,)),
-        ],
-    )
     packets = swap(packed)
 
     row = ((half_groups, 1, 2 * wide), F32)
@@ -453,28 +453,20 @@
             pltpu.VMEM((half_groups, 2 * rows, 2 * wide), BF16),
             pltpu.VMEM((half_groups, 2 * rows, 2 * wide), BF16),
             pltpu.VMEM((2, rows, group_width), F32),
+            pltpu.VMEM((half_groups, 2 * wide, DH), F32),
         ],
     )
     back = swap(packed)
-    query_grad, gate_grad, done = call(
-        functools.partial(finish_queries_kernel, limit=limit),
-        "finish_queries",
-        [((rows, heads_width), BF16), ((1, rows), F32), ((8, DH), F32)],
+    query_grad, key_grad, value_grad, gate_grad = call(
+        functools.partial(finish_kernel, limit=limit),
+        "finish",
+        [((rows, heads_width), BF16)] + [((rows, group_width), BF16)] * 2 + [((1, rows), F32)],
         back,
+        part_mine,
         positions,
         cosine,
         sine,
-    )
-    key_grad, value_grad = call(
-        finish_keys_kernel,
-        "finish_keys",
-        [((rows, group_width), BF16)] * 2,
-        part_mine,
-        back,
-        cosine,
-        sine,
         *[part for pair in zip(sib_got, own_got) for part in pair],
-        after=[done],
     )
     return (query_grad[None], key_grad[None], value_grad[None], gate_grad)
 

time: 38 us -> 53 us (1.39)
  Pallas kernels: 14.6 us -> 27.4 us
  waiting for transfers between devices: 1.08 us -> 4.65 us
  other arithmetic: 0.7 us -> 0 us
  local copies, waits for them, and re-layouts: 0.69 us -> 0.02 us
    pallas_call x7 -> x5, Pallas kernels: 14.6 us -> 27.4 us  [call(): pl.pallas_call(kernel, out_shape=[jax.ShapeDtypeStruct(*out) for out in o...]
    ppermute x1, starting transfers between devices: 4.85 us -> 1.85 us  [per_device(): far_own = [lax.ppermute(kv_mine, 'ctx', hop[s]) for s in range(1, chips)]]
    ppermute x1, starting transfers between devices: 1.3 us -> 4.29 us  [per_device(): lax.ppermute(kv_theirs, 'ctx', cross[s])]
    ppermute x1, waiting for transfers between devices: 1.07 us -> 4.05 us  [per_device(): lax.ppermute(far_parts[chips + s - 2], 'ctx', back_hop[s])]
    select_n x1 -> x0, other arithmetic: 0.7 us -> none  [per_device(): gate = jnp.tile(jnp.where(positions < limit, router_gate, 0.0), (1, ratio))]
    another operation x2 -> x0, local copies, waits for them, and re-layouts: 0.67 us -> none  [per_device(): gate = jnp.tile(jnp.where(positions < limit, router_gate, 0.0), (1, ratio))]
    ppermute x1, waiting for transfers between devices: 0.01 us -> 0.59 us  [per_device(): lax.ppermute(far_parts[s - 1], 'ctx', back_cross[s])]
  transfers between devices with their start and end apart: 4 -> 4, of which waited for: 1 -> 2; matrix products, arithmetic and copies ran while one was open for 4% -> 0% of each run, Pallas kernels for 21% -> 7%
where the time goes in v3:
time: 53 us; the launch traced here: 52.6 us
  Pallas kernels  27.4 us (52%)
  blocking collectives  11.1 us (21%)
  starting transfers between devices  8.72 us (16%)
  waiting for transfers between devices  4.65 us (9%)
  between operations  0.71 us (1%)
    pallas_call x5, Pallas kernels, call(): pl.pallas_call(kernel, out_shape=[jax.ShapeDtypeStruct(*out) for out in o...  27.4 us
    all_to_all x2, blocking collectives, per_device(): lax.all_to_all(both, 'ctx', 0, 0, axis_index_groups=pairs)  11.1 us
    ppermute x1, starting transfers between devices, per_device(): lax.ppermute(kv_theirs, 'ctx', cross[s])  4.29 us
    ppermute x1, waiting for transfers between devices, per_device(): lax.ppermute(far_parts[chips + s - 2], 'ctx', back_hop[s])  4.05 us
    ppermute x1, starting transfers between devices, per_device(): far_own = [lax.ppermute(kv_mine, 'ctx', hop[s]) for s in range(1, chips)]  1.85 us
    ppermute x1, starting transfers between devices, per_device(): lax.ppermute(far_parts[chips + s - 2], 'ctx', back_hop[s])  1.29 us
    ppermute x1, starting transfers between devices, per_device(): lax.ppermute(far_parts[s - 1], 'ctx', back_cross[s])  1.28 us
  transfers between devices with their start and end apart: 4, of which 2 were waited for; matrix products, arithmetic and copies ran while one was open for 0% of the time, Pallas kernels for 7%

profile of v3, /device:TPU:0, one launch (start us, length us, event | category | flops | bytes accessed | tf_op | source)
XLA Modules:
  0.0 52.6 jit_solution(11321866621816025166)
XLA Ops:
  0.6 21.1 %pack.1 = (bf16[176,512]{1,0:T(8,128)(2,1)}, bf16[176,512]{1,0:T(8,128)(2,1)}, bf16[2,176,2560]{2,1,0:T(8,128)(2,1)}, f32[160,128]{1,0:T(8,128)}, f32[160,128]{1,0:T(8,128)}) custom-call(bf16[160,512]{1,0:T(8,128)(2,1)} %bitcast.9, bf16[160,512]{1,0:T(8,128)(2,1)} %bitcast.10, bf16[160,2048]{1,0:T(8,128)(2,1)} %bitcast.7, bf16[160,2048]{1,0:T(8,128)(2,1)} %bitcast.8, ...), custom_call_target="tpu_custom_call" | custom-call | flops 1000000 | bytes 1000 | tf_op jit(solution)/shard_map/pack/pallas_call | solution.py:345
  21.8 4.3 %collective-permute-start = (bf16[176,512]{1,0:T(8,128)(2,1)}, bf16[176,512]{1,0:T(8,128)(2,1)S(1)}, u32[]{:S(2)}, u32[]{:S(2)}) collective-permute-start(bf16[176,512]{1,0:T(8,128)(2,1)} %get-tuple-element.39), channel_id=1, source_target_pairs={{0,3},{1,2},{4,7},{5,6},{8,11},{9,10},{12,15},{13,14},{16,19},{17,... | collective-permute-start | bytes 540680 | tf_op jit(solution)/shard_map/ppermute | solution.py:396
  26.1 1.9 %collective-permute-start.1 = (bf16[176,512]{1,0:T(8,128)(2,1)}, bf16[176,512]{1,0:T(8,128)(2,1)S(1)}, u32[]{:S(2)}, u32[]{:S(2)}) collective-permute-start(bf16[176,512]{1,0:T(8,128)(2,1)} %get-tuple-element.40), channel_id=1, source_target_pairs={{0,2},{1,3},{4,6},{5,7},{8,10},{9,11},{12,14},{13,15},{16,18},{17,... | collective-permute-start | bytes 540680 | tf_op jit(solution)/shard_map/ppermute | solution.py:395
  27.9 6.4 %all_to_all.10.packets = bf16[2,176,2560]{2,1,0:T(8,128)(2,1)S(1)} all-to-all(bf16[2,176,2560]{2,1,0:T(8,128)(2,1)} %get-tuple-element.30), channel_id=1, replica_groups={{0,1},{2,3},{4,5},{6,7},{8,9},{10,11},{12,13},{14,15},{16,17},{18,19},{..., dimensions={0} | all-to-all | bytes 3604480 | tf_op jit(solution)/shard_map/all_to_all | solution.py:399
  34.3 1.8 %local_scores.1 = (bf16[2,320,128]{2,1,0:T(8,128)(2,1)S(1)}, bf16[2,320,128]{2,1,0:T(8,128)(2,1)}, bf16[2,1280,128]{2,1,0:T(8,128)(2,1)S(1)}, bf16[2,1280,128]{2...) custom-call(bf16[2,176,2560]{2,1,0:T(8,128)(2,1)S(1)} %all_to_all.10, ...), custom_call_target="tpu_custom_call" | custom-call | flops 3000000 | bytes 1000 | tf_op jit(solution)/shard_map/local_scores/pallas_call | solution.py:345
  36.1 0.0 collective-permute-done.refs_0_
  36.1 0.0 collective-permute-done.1.refs_1_
  36.1 1.3 %far_scores.1 = (bf16[2,320,128]{2,1,0:T(8,128)(2,1)S(1)}, bf16[2,320,1280]{2,1,0:T(8,128)(2,1)}, bf16[2,320,1280]{2,1,0:T(8,128)(2,1)S(1)}, f32[2,1,1280]{2,1,0...) custom-call(bf16[2,1280,128]{2,1,0:T(8,128)(2,1)S(1)} %get-tuple-element.33.que, ...), custom_call_target="tpu_custom_call" | custom-call | flops 4000000 | bytes 1000 | tf_op jit(solution)/shard_map/far_scores/pallas_call | solution.py:345
  37.4 1.3 %collective-permute-start.2 = (bf16[160,512]{1,0:T(8,128)(2,1)S(1)}, bf16[160,512]{1,0:T(8,128)(2,1)S(1)}, u32[]{:S(2)}, u32[]{:S(2)}) collective-permute-start(bf16[160,512]{1,0:T(8,128)(2,1)S(1)} %get-tuple-element.50), channel_id=1, source_target_pairs={{3,0},{2,1},{7,4},{6,5},{11,8},{10,9},{15,12},{14,13},{19,16},{18,... | collective-permute-start | bytes 491528 | tf_op jit(solution)/shard_map/ppermute | solution.py:432
  38.7 1.3 %collective-permute-start.3 = (bf16[160,512]{1,0:T(8,128)(2,1)S(1)}, bf16[160,512]{1,0:T(8,128)(2,1)S(1)}, u32[]{:S(2)}, u32[]{:S(2)}) collective-permute-start(bf16[160,512]{1,0:T(8,128)(2,1)S(1)} %get-tuple-element.51), channel_id=1, source_target_pairs={{2,0},{3,1},{6,4},{7,5},{10,8},{11,9},{14,12},{15,13},{18,16},{19,... | collective-permute-start | bytes 491528 | tf_op jit(solution)/shard_map/ppermute | solution.py:433
  40.0 1.9 %near_grads.1 = (f32[160,512]{1,0:T(8,128)S(1)}, bf16[2,176,1536]{2,1,0:T(8,128)(2,1)S(1)}) custom-call(f32[2,320,1280]{2,1,0:T(8,128)S(1)} %get-tuple-element.31.raws, f32[2,320,1280]{2,1,0:T(8,128)S(1)} %get-tuple-element.32.grads, f32[2,1,1280]{2,1,0:T(1,128)S(1)} %get-tuple-element.41.factors, f32[2,1,1280]{2,1,0:T(1,128)S(1)} %get-tuple-element.42.deltas, ...), custom_call_target="tpu_custom_call" | custom-call | flops 4000000 | bytes 1000 | tf_op jit(solution)/shard_map/near_grads/pallas_call | solution.py:345
  41.8 0.0 copy-start
  41.8 0.0 copy-start.1
  41.9 0.0 copy-start.2
  41.9 4.7 %all_to_all.11.back = bf16[2,176,1536]{2,1,0:T(8,128)(2,1)S(1)} all-to-all(bf16[2,176,1536]{2,1,0:T(8,128)(2,1)S(1)} %get-tuple-element.46), channel_id=1, replica_groups={{0,1},{2,3},{4,5},{6,7},{8,9},{10,11},{12,13},{14,15},{16,17},{18,19},{..., dimensions={0} | all-to-all | bytes 2162688 | tf_op jit(solution)/shard_map/all_to_all | solution.py:399
  46.6 0.6 %collective-permute-done.2.refs_0_ = bf16[160,512]{1,0:T(8,128)(2,1)S(1)} collective-permute-done((bf16[160,512]{1,0:T(8,128)(2,1)S(1)}, bf16[160,512]{1,0:T(8,128)(2,1)S(1)}, u32[]{:S(2)}, u32[]{:S(2)}) %collective-permute-start.2) | collective-permute-done | bytes 163872 | tf_op jit(solution)/shard_map/ppermute | solution.py:432
  47.2 4.0 %collective-permute-done.3.refs_1_ = bf16[160,512]{1,0:T(8,128)(2,1)S(1)} collective-permute-done((bf16[160,512]{1,0:T(8,128)(2,1)S(1)}, bf16[160,512]{1,0:T(8,128)(2,1)S(1)}, u32[]{:S(2)}, u32[]{:S(2)}) %collective-permute-start.3) | collective-permute-done | bytes 163872 | tf_op jit(solution)/shard_map/ppermute | solution.py:433
  51.2 0.0 copy-done
  51.2 0.0 copy-done.1
  51.2 0.0 copy-done.2
  51.2 1.4 %finish.1 = (bf16[160,2048]{1,0:T(8,128)(2,1)}, bf16[160,512]{1,0:T(8,128)(2,1)}, bf16[160,512]{1,0:T(8,128)(2,1)}, f32[1,160]{1,0:T(1,128)}) custom-call(bf16[2,176,1536]{2,1,0:T(8,128)(2,1)S(1)} %all_to_all.11.back, f32[160,512]{1,0:T(8,128)S(1)} %get-tuple-element.47.part_mine, s32[1,160]{1,0:T(1,128)S(1)} %copy-done.2, f32[160,128]{1,0:T(8,128)S(1)} %copy-done, ...), custom_call_target="tpu_custom_call" | custom-call | flops 1000000 | bytes 1000 | tf_op jit(solution)/shard_map/finish/pallas_call | solution.py:345
Async XLA Ops:
  21.8 14.3 %collective-permute-start = (bf16[176,512]{1,0:T(8,128)(2,1)}, bf16[176,512]{1,0:T(8,128)(2,1)S(1)}, u32[]{:S(2)}, u32[]{:S(2)}) collective-permute-start(bf16[176,512]{1,0:T(8,128)(2,1)} %get-tuple-element.39), channel_id=1, source_target_pairs={{0,3},{1,2},{4,7},{5,6},{8,11},{9,10},{12,15},{13,14},{16,19},{17,... | collective-permute-start | bytes 540680 | tf_op jit(solution)/shard_map/ppermute | solution.py:396
  26.1 10.1 %collective-permute-start.1 = (bf16[176,512]{1,0:T(8,128)(2,1)}, bf16[176,512]{1,0:T(8,128)(2,1)S(1)}, u32[]{:S(2)}, u32[]{:S(2)}) collective-permute-start(bf16[176,512]{1,0:T(8,128)(2,1)} %get-tuple-element.40), channel_id=1, source_target_pairs={{0,2},{1,3},{4,6},{5,7},{8,10},{9,11},{12,14},{13,15},{16,18},{17,... | collective-permute-start | bytes 540680 | tf_op jit(solution)/shard_map/ppermute | solution.py:395
  37.4 9.8 %collective-permute-start.2 = (bf16[160,512]{1,0:T(8,128)(2,1)S(1)}, bf16[160,512]{1,0:T(8,128)(2,1)S(1)}, u32[]{:S(2)}, u32[]{:S(2)}) collective-permute-start(bf16[160,512]{1,0:T(8,128)(2,1)S(1)} %get-tuple-element.50), channel_id=1, source_target_pairs={{3,0},{2,1},{7,4},{6,5},{11,8},{10,9},{15,12},{14,13},{19,16},{18,... | collective-permute-start | bytes 491528 | tf_op jit(solution)/shard_map/ppermute | solution.py:432
  38.7 12.6 %collective-permute-start.3 = (bf16[160,512]{1,0:T(8,128)(2,1)S(1)}, bf16[160,512]{1,0:T(8,128)(2,1)S(1)}, u32[]{:S(2)}, u32[]{:S(2)}) collective-permute-start(bf16[160,512]{1,0:T(8,128)(2,1)S(1)} %get-tuple-element.51), channel_id=1, source_target_pairs={{2,0},{3,1},{6,4},{7,5},{10,8},{11,9},{14,12},{15,13},{18,16},{19,... | collective-permute-start | bytes 491528 | tf_op jit(solution)/shard_map/ppermute | solution.py:433
  41.8 9.4 %copy-start = (f32[160,128]{1,0:T(8,128)S(1)}, f32[160,128]{1,0:T(8,128)}, u32[]{:S(2)}) copy-start(f32[160,128]{1,0:T(8,128)} %get-tuple-element.48.cos_ref) | copy-start | bytes 245764
  41.8 9.4 %copy-start.1 = (f32[160,128]{1,0:T(8,128)S(1)}, f32[160,128]{1,0:T(8,128)}, u32[]{:S(2)}) copy-start(f32[160,128]{1,0:T(8,128)} %get-tuple-element.49.sin_ref) | copy-start | bytes 245764
  41.9 9.4 %copy-start.2 = (s32[1,160]{1,0:T(1,128)S(1)}, s32[1,160]{1,0:T(1,128)}, u32[]{:S(2)}) copy-start(s32[1,160]{1,0:T(1,128)} %pos_ref.1) | copy-start | bytes 1924

commit v4 on v3

--- a/solution.py
+++ b/solution.py
@@ -77,8 +77,8 @@
 
 
 def pack_kernel(
-    key_in, value_in, query_in, cot_in, gate_in, pos_in, freq_in, mine_out, theirs_out, packed_out, cos_out, sin_out,
-    key, value, query, gate, pos, freq, mine, theirs, packed, cos_ref, sin_ref, sems, out_sems, *, limit
+    key_in, value_in, query_in, cot_in, gate_in, pos_in, freq_in, mine, theirs, packed, cos_ref, sin_ref,
+    key, value, query, gate, pos, freq, sems, *, limit
 ):
     rows, width = key.shape
     side_width = width // 2
@@ -87,7 +87,7 @@
     loads = [(pos_in, pos), (freq_in, freq), (key_in, key), (value_in, value), (gate_in, gate), (query_in, query)]
     for side in range(2):
         there = slice(side * half, (side + 1) * half)
-        loads.append((cot_in.at[:, there], packed_out.at[side, :rows, half : 2 * half]))
+        loads.append((cot_in.at[:, there], packed.at[side, :rows, half : 2 * half]))
     loads = [pltpu.make_async_copy(source, target, sems.at[i]) for i, (source, target) in enumerate(loads)]
     for copy in loads:
         copy.start()
@@ -113,18 +113,7 @@
             out_ref[:rows, 2 * i * DH : (2 * i + 1) * DH] = turned.astype(BF16)
             out_ref[:rows, (2 * i + 1) * DH : (2 * i + 2) * DH] = value[:, there]
         out_ref[rows:, :] = count
-    stores = [
-        (mine, mine_out),
-        (theirs, theirs_out),
-        (cos_ref, cos_out),
-        (sin_ref, sin_out),
-        (mine, packed_out.at[core, :, 2 * half :]),
-        (theirs, packed_out.at[1 - core, :, 2 * half :]),
-    ]
-    stores += [(packed.at[side], packed_out.at[side, :, :half]) for side in range(2)]
-    stores = [pltpu.make_async_copy(source, target, out_sems.at[i]) for i, (source, target) in enumerate(stores)]
-    for copy in stores[:6]:
-        copy.start()
+        packed[side, :, 2 * half :] = out_ref[...]
     loads[4].wait()
     loads[5].wait()
     gates = split_rows(jnp.where(places < limit, gate[...], 0.0), EXTRA)
@@ -135,8 +124,7 @@
             turned = rotate(query[:, there].astype(F32), cosine, sine)
             packed[side, :rows, i * DH : (i + 1) * DH] = turned.astype(BF16)
         packed[side, rows:, :rows] = gates
-        stores[6 + side].start()
-    for copy in loads[6:] + stores:
+    for copy in loads[6:]:
         copy.wait()
 
 
@@ -338,17 +326,17 @@
     limit = parts * LOCAL
     wide = ratio * rows
     params = pltpu.CompilerParams(vmem_limit_bytes=(16 + 4 * chips) * 1024 * 1024)
-    full = pltpu.CompilerParams(vmem_limit_bytes=63 * 1024 * 1024)
 
     def call(kernel, name, outs, *args, scratch=(), flops=10**6, in_hbm=False):
+        if in_hbm:
+            args = [pltpu.with_memory_space_constraint(arg, pltpu.HBM) for arg in args]
         spec = pl.BlockSpec(memory_space=pltpu.HBM if in_hbm else pltpu.VMEM)
         return pl.pallas_call(
             kernel,
             out_shape=[jax.ShapeDtypeStruct(*out) for out in outs],
             in_specs=[spec] * len(args),
-            out_specs=[spec] * len(outs),
             scratch_shapes=list(scratch),
-            compiler_params=full if in_hbm else params,
+            compiler_params=params,
             cost_estimate=pl.CostEstimate(flops=flops, bytes_accessed=1000, transcendentals=0),
             name=name,
         )(*args)
@@ -377,12 +365,6 @@
             pltpu.VMEM((1, rows), F32),
             pltpu.VMEM((1, rows), jnp.int32),
             pltpu.VMEM((1, DH), F32),
-            pltpu.VMEM(*packet),
-            pltpu.VMEM(*packet),
-            pltpu.VMEM((2, rows + EXTRA, half_width), BF16),
-            pltpu.VMEM(*table),
-            pltpu.VMEM(*table),
-            pltpu.SemaphoreType.DMA((8,)),
             pltpu.SemaphoreType.DMA((8,)),
         ],
     )

time: 53 us -> 33.3 us (0.63)
  Pallas kernels: 27.4 us -> 8.09 us
  blocking collectives: 11.1 us -> 9.75 us
  waiting for transfers between devices: 4.65 us -> 5.79 us
    pallas_call x5, Pallas kernels: 27.4 us -> 8.09 us  [call(): pl.pallas_call(kernel, out_shape=[jax.ShapeDtypeStruct(*out) for out in o...]
    all_to_all x2, blocking collectives: 11.1 us -> 9.75 us  [per_device(): lax.all_to_all(both, 'ctx', 0, 0, axis_index_groups=pairs)]
    ppermute x1, waiting for transfers between devices: 0.59 us -> 1.74 us  [per_device(): lax.ppermute(far_parts[s - 1], 'ctx', back_cross[s])]
  transfers between devices with their start and end apart: 4 -> 4, of which waited for: 2 -> 2; matrix products, arithmetic and copies ran while one was open for 0% -> 0% of each run, Pallas kernels for 7% -> 11%
where the time goes in v4:
time: 33.3 us; the launch traced here: 33 us
  blocking collectives  9.75 us (29%)
  starting transfers between devices  8.72 us (26%)
  Pallas kernels  8.09 us (24%)
  waiting for transfers between devices  5.79 us (17%)
  between operations  0.69 us (2%)
    all_to_all x2, blocking collectives, per_device(): lax.all_to_all(both, 'ctx', 0, 0, axis_index_groups=pairs)  9.75 us
    pallas_call x5, Pallas kernels, call(): pl.pallas_call(kernel, out_shape=[jax.ShapeDtypeStruct(*out) for out in o...  8.09 us
    ppermute x1, starting transfers between devices, per_device(): lax.ppermute(kv_theirs, 'ctx', cross[s])  4.29 us
    ppermute x1, waiting for transfers between devices, per_device(): lax.ppermute(far_parts[chips + s - 2], 'ctx', back_hop[s])  4.05 us
    ppermute x1, starting transfers between devices, per_device(): far_own = [lax.ppermute(kv_mine, 'ctx', hop[s]) for s in range(1, chips)]  1.85 us
    ppermute x1, waiting for transfers between devices, per_device(): lax.ppermute(far_parts[s - 1], 'ctx', back_cross[s])  1.74 us
    ppermute x1, starting transfers between devices, per_device(): lax.ppermute(far_parts[chips + s - 2], 'ctx', back_hop[s])  1.29 us
    ppermute x1, starting transfers between devices, per_device(): lax.ppermute(far_parts[s - 1], 'ctx', back_cross[s])  1.28 us
  transfers between devices with their start and end apart: 4, of which 2 were waited for; matrix products, arithmetic and copies ran while one was open for 0% of the time, Pallas kernels for 11%

profile of v4, /device:TPU:0, one launch (start us, length us, event | category | flops | bytes accessed | tf_op | source)
XLA Modules:
  0.0 33.0 jit_solution(13561489357698484025)
XLA Ops:
  0.6 1.8 %pack.1 = (bf16[176,512]{1,0:T(8,128)(2,1)S(1)}, bf16[176,512]{1,0:T(8,128)(2,1)S(1)}, bf16[2,176,2560]{2,1,0:T(8,128)(2,1)S(1)}, f32[160,128]{1,0:T(8,128)S(1)}, f32[160,128]{1,0:T(8,128)S(1)}) custom-call(bf16[160,512]{1,0:T(8,128)(2,1)} %bitcast.9, bf16[160,512]{1,0:T(8,128)(2,1)} %bitcast.10, bf16[160,2048]{1,0:T(8,128)(2,1)} %bitcast.7, ...), custom_call_target="tpu_custom_call" | custom-call | flops 1000000 | bytes 1000 | tf_op jit(solution)/shard_map/pack/pallas_call | solution.py:334
  2.4 4.3 %collective-permute-start = (bf16[176,512]{1,0:T(8,128)(2,1)S(1)}, bf16[176,512]{1,0:T(8,128)(2,1)S(1)}, u32[]{:S(2)}, u32[]{:S(2)}) collective-permute-start(bf16[176,512]{1,0:T(8,128)(2,1)S(1)} %get-tuple-element.39), channel_id=1, source_target_pairs={{0,3},{1,2},{4,7},{5,6},{8,11},{9,10},{12,15},{13,14},{16,19},{17,... | collective-permute-start | bytes 540680 | tf_op jit(solution)/shard_map/ppermute | solution.py:378
  6.7 1.9 %collective-permute-start.1 = (bf16[176,512]{1,0:T(8,128)(2,1)S(1)}, bf16[176,512]{1,0:T(8,128)(2,1)S(1)}, u32[]{:S(2)}, u32[]{:S(2)}) collective-permute-start(bf16[176,512]{1,0:T(8,128)(2,1)S(1)} %get-tuple-element.40), channel_id=1, source_target_pairs={{0,2},{1,3},{4,6},{5,7},{8,10},{9,11},{12,14},{13,15},{16,18},{17,... | collective-permute-start | bytes 540680 | tf_op jit(solution)/shard_map/ppermute | solution.py:377
  8.6 5.2 %all_to_all.10.packets = bf16[2,176,2560]{2,1,0:T(8,128)(2,1)S(1)} all-to-all(bf16[2,176,2560]{2,1,0:T(8,128)(2,1)S(1)} %get-tuple-element.30), channel_id=1, replica_groups={{0,1},{2,3},{4,5},{6,7},{8,9},{10,11},{12,13},{14,15},{16,17},{18,19},{..., dimensions={0} | all-to-all | bytes 3604480 | tf_op jit(solution)/shard_map/all_to_all | solution.py:381
  13.8 1.8 %local_scores.1 = (bf16[2,320,128]{2,1,0:T(8,128)(2,1)S(1)}, bf16[2,320,128]{2,1,0:T(8,128)(2,1)}, bf16[2,1280,128]{2,1,0:T(8,128)(2,1)S(1)}, bf16[2,1280,128]{2...) custom-call(bf16[2,176,2560]{2,1,0:T(8,128)(2,1)S(1)} %all_to_all.10, ...), custom_call_target="tpu_custom_call" | custom-call | flops 3000000 | bytes 1000 | tf_op jit(solution)/shard_map/local_scores/pallas_call | solution.py:334
  15.6 0.0 collective-permute-done.refs_0_
  15.6 0.0 collective-permute-done.1.refs_1_
  15.6 1.3 %far_scores.1 = (bf16[2,320,128]{2,1,0:T(8,128)(2,1)S(1)}, bf16[2,320,1280]{2,1,0:T(8,128)(2,1)}, bf16[2,320,1280]{2,1,0:T(8,128)(2,1)S(1)}, f32[2,1,1280]{2,1,0...) custom-call(bf16[2,1280,128]{2,1,0:T(8,128)(2,1)S(1)} %get-tuple-element.33.que, ...), custom_call_target="tpu_custom_call" | custom-call | flops 4000000 | bytes 1000 | tf_op jit(solution)/shard_map/far_scores/pallas_call | solution.py:334
  16.8 1.3 %collective-permute-start.2 = (bf16[160,512]{1,0:T(8,128)(2,1)S(1)}, bf16[160,512]{1,0:T(8,128)(2,1)S(1)}, u32[]{:S(2)}, u32[]{:S(2)}) collective-permute-start(bf16[160,512]{1,0:T(8,128)(2,1)S(1)} %get-tuple-element.50), channel_id=1, source_target_pairs={{3,0},{2,1},{7,4},{6,5},{11,8},{10,9},{15,12},{14,13},{19,16},{18,... | collective-permute-start | bytes 491528 | tf_op jit(solution)/shard_map/ppermute | solution.py:414
  18.1 1.3 %collective-permute-start.3 = (bf16[160,512]{1,0:T(8,128)(2,1)S(1)}, bf16[160,512]{1,0:T(8,128)(2,1)S(1)}, u32[]{:S(2)}, u32[]{:S(2)}) collective-permute-start(bf16[160,512]{1,0:T(8,128)(2,1)S(1)} %get-tuple-element.51), channel_id=1, source_target_pairs={{2,0},{3,1},{6,4},{7,5},{10,8},{11,9},{14,12},{15,13},{18,16},{19,... | collective-permute-start | bytes 491528 | tf_op jit(solution)/shard_map/ppermute | solution.py:415
  19.4 1.9 %near_grads.1 = (f32[160,512]{1,0:T(8,128)S(1)}, bf16[2,176,1536]{2,1,0:T(8,128)(2,1)S(1)}) custom-call(f32[2,320,1280]{2,1,0:T(8,128)S(1)} %get-tuple-element.31.raws, f32[2,320,1280]{2,1,0:T(8,128)S(1)} %get-tuple-element.32.grads, f32[2,1,1280]{2,1,0:T(1,128)S(1)} %get-tuple-element.41.factors, f32[2,1,1280]{2,1,0:T(1,128)S(1)} %get-tuple-element.42.deltas, ...), custom_call_target="tpu_custom_call" | custom-call | flops 4000000 | bytes 1000 | tf_op jit(solution)/shard_map/near_grads/pallas_call | solution.py:334
  21.3 0.0 copy-start
  21.3 4.6 %all_to_all.11.back = bf16[2,176,1536]{2,1,0:T(8,128)(2,1)S(1)} all-to-all(bf16[2,176,1536]{2,1,0:T(8,128)(2,1)S(1)} %get-tuple-element.46), channel_id=1, replica_groups={{0,1},{2,3},{4,5},{6,7},{8,9},{10,11},{12,13},{14,15},{16,17},{18,19},{..., dimensions={0} | all-to-all | bytes 2162688 | tf_op jit(solution)/shard_map/all_to_all | solution.py:381
  25.9 1.7 %collective-permute-done.2.refs_0_ = bf16[160,512]{1,0:T(8,128)(2,1)S(1)} collective-permute-done((bf16[160,512]{1,0:T(8,128)(2,1)S(1)}, bf16[160,512]{1,0:T(8,128)(2,1)S(1)}, u32[]{:S(2)}, u32[]{:S(2)}) %collective-permute-start.2) | collective-permute-done | bytes 163872 | tf_op jit(solution)/shard_map/ppermute | solution.py:414
  27.6 4.0 %collective-permute-done.3.refs_1_ = bf16[160,512]{1,0:T(8,128)(2,1)S(1)} collective-permute-done((bf16[160,512]{1,0:T(8,128)(2,1)S(1)}, bf16[160,512]{1,0:T(8,128)(2,1)S(1)}, u32[]{:S(2)}, u32[]{:S(2)}) %collective-permute-start.3) | collective-permute-done | bytes 163872 | tf_op jit(solution)/shard_map/ppermute | solution.py:415
  31.7 0.0 copy-done
  31.7 1.4 %finish.1 = (bf16[160,2048]{1,0:T(8,128)(2,1)}, bf16[160,512]{1,0:T(8,128)(2,1)}, bf16[160,512]{1,0:T(8,128)(2,1)}, f32[1,160]{1,0:T(1,128)}) custom-call(bf16[2,176,1536]{2,1,0:T(8,128)(2,1)S(1)} %all_to_all.11.back, f32[160,512]{1,0:T(8,128)S(1)} %get-tuple-element.47.part_mine, s32[1,160]{1,0:T(1,128)S(1)} %copy-done, ...), custom_call_target="tpu_custom_call" | custom-call | flops 1000000 | bytes 1000 | tf_op jit(solution)/shard_map/finish/pallas_call | solution.py:334
Async XLA Ops:
  2.4 13.1 %collective-permute-start = (bf16[176,512]{1,0:T(8,128)(2,1)S(1)}, bf16[176,512]{1,0:T(8,128)(2,1)S(1)}, u32[]{:S(2)}, u32[]{:S(2)}) collective-permute-start(bf16[176,512]{1,0:T(8,128)(2,1)S(1)} %get-tuple-element.39), channel_id=1, source_target_pairs={{0,3},{1,2},{4,7},{5,6},{8,11},{9,10},{12,15},{13,14},{16,19},{17,... | collective-permute-start | bytes 540680 | tf_op jit(solution)/shard_map/ppermute | solution.py:378
  6.7 8.9 %collective-permute-start.1 = (bf16[176,512]{1,0:T(8,128)(2,1)S(1)}, bf16[176,512]{1,0:T(8,128)(2,1)S(1)}, u32[]{:S(2)}, u32[]{:S(2)}) collective-permute-start(bf16[176,512]{1,0:T(8,128)(2,1)S(1)} %get-tuple-element.40), channel_id=1, source_target_pairs={{0,2},{1,3},{4,6},{5,7},{8,10},{9,11},{12,14},{13,15},{16,18},{17,... | collective-permute-start | bytes 540680 | tf_op jit(solution)/shard_map/ppermute | solution.py:377
  16.8 10.8 %collective-permute-start.2 = (bf16[160,512]{1,0:T(8,128)(2,1)S(1)}, bf16[160,512]{1,0:T(8,128)(2,1)S(1)}, u32[]{:S(2)}, u32[]{:S(2)}) collective-permute-start(bf16[160,512]{1,0:T(8,128)(2,1)S(1)} %get-tuple-element.50), channel_id=1, source_target_pairs={{3,0},{2,1},{7,4},{6,5},{11,8},{10,9},{15,12},{14,13},{19,16},{18,... | collective-permute-start | bytes 491528 | tf_op jit(solution)/shard_map/ppermute | solution.py:414
  18.1 13.5 %collective-permute-start.3 = (bf16[160,512]{1,0:T(8,128)(2,1)S(1)}, bf16[160,512]{1,0:T(8,128)(2,1)S(1)}, u32[]{:S(2)}, u32[]{:S(2)}) collective-permute-start(bf16[160,512]{1,0:T(8,128)(2,1)S(1)} %get-tuple-element.51), channel_id=1, source_target_pairs={{2,0},{3,1},{6,4},{7,5},{10,8},{11,9},{14,12},{15,13},{18,16},{19,... | collective-permute-start | bytes 491528 | tf_op jit(solution)/shard_map/ppermute | solution.py:415
  21.3 10.4 %copy-start = (s32[1,160]{1,0:T(1,128)S(1)}, s32[1,160]{1,0:T(1,128)}, u32[]{:S(2)}) copy-start(s32[1,160]{1,0:T(1,128)} %pos_ref.1) | copy-start | bytes 1924

commit v5 on v4

--- a/solution.py
+++ b/solution.py
@@ -14,6 +14,7 @@
 THETA = 500000.0
 EXTRA = 16
 HIDDEN = -1e30
+UNUSED = 2.0**14
 SCALE = DH**-0.5
 LOG2E = math.log2(math.e)
 LN2 = math.log(2.0)
@@ -106,14 +107,16 @@
     sin_ref[...] = sine
     loads[2].wait()
     loads[3].wait()
+    used = jnp.broadcast_to(column, (rows, DH)) < limit
     for out_ref, side in ((mine, core), (theirs, 1 - core)):
         for i in range(side_width // DH):
             there = pl.ds(pl.multiple_of(side * side_width + i * DH, DH), DH)
             turned = rotate(key[:, there].astype(F32), cosine, sine)
-            out_ref[:rows, 2 * i * DH : (2 * i + 1) * DH] = turned.astype(BF16)
-            out_ref[:rows, (2 * i + 1) * DH : (2 * i + 2) * DH] = value[:, there]
-        out_ref[rows:, :] = count
-        packed[side, :, 2 * half :] = out_ref[...]
+            out_ref[:, 2 * i * DH : (2 * i + 1) * DH] = jnp.where(used, turned, UNUSED).astype(BF16)
+            out_ref[:, (2 * i + 1) * DH : (2 * i + 2) * DH] = value[:, there]
+            packed[side, :rows, 2 * half + 2 * i * DH : 2 * half + (2 * i + 1) * DH] = turned.astype(BF16)
+            packed[side, :rows, 2 * half + (2 * i + 1) * DH : 2 * half + (2 * i + 2) * DH] = value[:, there]
+        packed[side, rows:, 2 * half :] = count
     loads[4].wait()
     loads[5].wait()
     gates = split_rows(jnp.where(places < limit, gate[...], 0.0), EXTRA)
@@ -192,18 +195,51 @@
     out_ref[:, (2 * i + 1) * DH : (2 * i + 2) * DH] = value_part.astype(out_ref.dtype)
 
 
-def far_kernel(query, cot, gate, tops, sums, crosses, *refs, blocks):
-    packets = refs[:blocks]
-    far_keys, weights, score_grads, factors, deltas = refs[blocks : blocks + 5]
-    parts = refs[blocks + 5 : 2 * blocks + 5]
-    far_values = refs[-1]
-    rows = packets[0].shape[0] - EXTRA
+def used_slots(packet, here):
+    chip = lax.div(lax.axis_index("ctx"), 2)
+    key = packet[:, :DH].astype(F32)[:, :1]
+    return jnp.broadcast_to(key, (packet.shape[0], 256)) < jnp.where(chip >= here, UNUSED / 2, -UNUSED)
+
+
+def early_kernel(query, cot, tops, sums, crosses, packet, raws, grads, new_tops, new_sums, new_crosses):
     half_groups, lanes = query.shape[:2]
-    for j in range(blocks):
-        there = slice(j * rows, (j + 1) * rows)
+    alone = lax.axis_index("ctx") < 2
+
+    @pl.when(alone)
+    def _():
+        new_tops[...] = tops[...]
+        new_sums[...] = sums[...]
+        new_crosses[...] = crosses[...]
+
+    @pl.when(jnp.logical_not(alone))
+    def _():
+        used = used_slots(packet, 1)
         for i in range(half_groups):
-            far_keys[i, there, :] = packets[j][:rows, 2 * i * DH : (2 * i + 1) * DH]
-            far_values[i, there, :] = packets[j][:rows, (2 * i + 1) * DH : (2 * i + 2) * DH]
+            key = packet[:, 2 * i * DH : (2 * i + 1) * DH]
+            value = packet[:, (2 * i + 1) * DH : (2 * i + 2) * DH]
+            for here in chunks(0, lanes):
+                width = here.stop - here.start
+                shown = jnp.where(used[:, :width], dot(key, query[i, here, :], NT), HIDDEN)
+                old_top = tops[i, :, here]
+                top = jnp.maximum(old_top, jnp.max(shown, axis=0, keepdims=True))
+                raw = jnp.exp2(shown - top)
+                shrink = jnp.exp2(old_top - top)
+                prob_grad = dot(value, cot[i, here, :], NT)
+                raws[i, :, here] = raw
+                grads[i, :, here] = prob_grad
+                new_tops[i, :, here] = top
+                new_sums[i, :, here] = sums[i, :, here] * shrink + jnp.sum(raw, axis=0, keepdims=True)
+                cross = jnp.sum(raw * prob_grad, axis=0, keepdims=True)
+                new_crosses[i, :, here] = crosses[i, :, here] * shrink + cross
+
+
+def far_kernel(query, cot, gate, first_tops, raws, grads, tops, sums, crosses, early, *refs, blocks):
+    packets = refs[: blocks - 1]
+    far_keys, weights, score_grads, factors, deltas = refs[blocks - 1 : blocks + 4]
+    parts = refs[blocks + 4 : -2]
+    late_keys, late_values = refs[-2:]
+    rows = early.shape[0]
+    half_groups, lanes = query.shape[:2]
     alone = lax.axis_index("ctx") < 2
 
     @pl.when(alone)
@@ -215,15 +251,22 @@
 
     @pl.when(jnp.logical_not(alone))
     def _():
-        counts = [packet[rows:, :256].astype(F32)[:1] for packet in packets]
+        for i in range(half_groups):
+            far_keys[i, :rows, :] = early[:, 2 * i * DH : (2 * i + 1) * DH]
+            for j, packet in enumerate(packets):
+                there = slice(j * rows, (j + 1) * rows)
+                far_keys[i, (j + 1) * rows : (j + 2) * rows, :] = packet[:, 2 * i * DH : (2 * i + 1) * DH]
+                late_keys[i, there, :] = packet[:, 2 * i * DH : (2 * i + 1) * DH]
+                late_values[i, there, :] = packet[:, (2 * i + 1) * DH : (2 * i + 2) * DH]
+        hops = blocks // 2
+        used = [used_slots(packet, (j + 1) % hops + 1) for j, packet in enumerate(packets)]
         for i in range(half_groups):
             for here in chunks(0, lanes):
                 width = here.stop - here.start
-                scores = dot(far_keys[i], query[i, here, :], NT)
-                slot = lax.broadcasted_iota(jnp.int32, (rows, width), 0).astype(F32)
+                scores = dot(late_keys[i], query[i, here, :], NT)
                 shown = [
-                    jnp.where(slot < counts[j][:, :width], scores[j * rows : (j + 1) * rows], HIDDEN)
-                    for j in range(blocks)
+                    jnp.where(used[j][:, :width], scores[j * rows : (j + 1) * rows], HIDDEN)
+                    for j in range(blocks - 1)
                 ]
                 shown = jnp.concatenate(shown, axis=0)
                 old_top = tops[i, :, here]
@@ -231,17 +274,32 @@
                 raw = jnp.exp2(shown - top)
                 shrink = jnp.exp2(old_top - top)
                 inverse = 1.0 / (sums[i, :, here] * shrink + jnp.sum(raw, axis=0, keepdims=True))
-                prob_grad = dot(far_values[i], cot[i, here, :], NT)
+                prob_grad = dot(late_values[i], cot[i, here, :], NT)
                 cross = crosses[i, :, here] * shrink + jnp.sum(raw * prob_grad, axis=0, keepdims=True)
                 delta = cross * inverse
                 factor = inverse * gate[:, here]
-                factors[i, :, here] = factor * shrink
+                factors[i, :, here] = factor * jnp.exp2(first_tops[i, :, here] - top)
                 deltas[i, :, here] = delta
                 gated = raw * factor
-                weights[i, :, here] = gated.astype(BF16)
-                score_grads[i, :, here] = (gated * (prob_grad - delta)).astype(BF16)
+                weights[i, rows:, here] = gated.astype(BF16)
+                score_grads[i, rows:, here] = (gated * (prob_grad - delta)).astype(BF16)
+                gated = raws[i, :, here] * (factor * shrink)
+                weights[i, :rows, here] = gated.astype(BF16)
+                score_grads[i, :rows, here] = (gated * (grads[i, :, here] - delta)).astype(BF16)
             for j, out_ref in enumerate(parts):
                 part_of(weights, score_grads, query, cot, out_ref, i, slice(j * rows, (j + 1) * rows), slice(0, lanes))
+
+
+def far_rest_kernel(weights, score_grads, query, cot, *parts):
+    rows = parts[0].shape[0]
+    half_groups, lanes = query.shape[:2]
+
+    @pl.when(lax.axis_index("ctx") >= 2)
+    def _():
+        for j, out_ref in enumerate(parts):
+            there = slice((len(parts) + j) * rows, (len(parts) + j + 1) * rows)
+            for i in range(half_groups):
+                part_of(weights, score_grads, query, cot, out_ref, i, there, slice(0, lanes))
 
 
 def near_kernel(
@@ -289,11 +347,17 @@
         out_ref[block, rows:, :rows] = split_rows(own, EXTRA)
 
 
-def finish_kernel(back, part_mine, pos_ref, cos_ref, sin_ref, *refs, limit):
-    got, (query_grad, key_grad, value_grad, gate_grad) = refs[:-4], refs[-4:]
-    rows, width = part_mine.shape
-    half, side_width = query_grad.shape[1] // 2, width // 2
-    core = core_of()
+def turn_back(values, out_key, out_value, cosine, sine, starts):
+    for i, there in enumerate(starts):
+        turned = rotate(values[:, 2 * i * DH : (2 * i + 1) * DH], cosine, sine)
+        out_key[:, there] = turned.astype(BF16)
+        out_value[:, there] = values[:, (2 * i + 1) * DH : (2 * i + 2) * DH].astype(BF16)
+
+
+def finish_queries_kernel(back, pos_ref, cos_ref, sin_ref, *refs, limit):
+    got, (query_grad, gate_grad, key_part, value_part) = refs[:-4], refs[-4:]
+    rows = cos_ref.shape[0]
+    half = query_grad.shape[1] // 2
     cosine, sine = cos_ref[...], -sin_ref[...]
     for side in range(2):
         for i in range(half // DH):
@@ -302,17 +366,25 @@
             query_grad[:, there] = turned.astype(BF16)
     gate = joined_row(back[0, rows:, :rows]) + joined_row(back[1, rows:, :rows])
     gate_grad[...] = jnp.where(pos_ref[...] < limit, gate, 0.0)
+    other = back[1 - core_of(), :rows, half:].astype(F32)
+    for ref in got:
+        other = other + ref[...].astype(F32)
+    starts = [slice(i * DH, (i + 1) * DH) for i in range(key_part.shape[1] // DH)]
+    turn_back(other, key_part, value_part, cosine, sine, starts)
+
+
+def finish_keys_kernel(part_mine, key_part, value_part, cos_ref, sin_ref, *refs):
+    got, (key_grad, value_grad) = refs[:-2], refs[-2:]
+    half = key_part.shape[1]
+    core = core_of()
     total = part_mine[...]
-    other = back[1 - core, :rows, half:].astype(F32)
-    for s in range(len(got) // 2):
-        other = other + got[2 * s][...].astype(F32)
-        total = total + got[2 * s + 1][...].astype(F32)
-    for values, side in ((total, core), (other, 1 - core)):
-        for i in range(side_width // DH):
-            there = pl.ds(pl.multiple_of(side * side_width + i * DH, DH), DH)
-            turned = rotate(values[:, 2 * i * DH : (2 * i + 1) * DH], cosine, sine)
-            key_grad[:, there] = turned.astype(BF16)
-            value_grad[:, there] = values[:, (2 * i + 1) * DH : (2 * i + 2) * DH].astype(BF16)
+    for ref in got:
+        total = total + ref[...].astype(F32)
+    starts = [pl.ds(pl.multiple_of(core * half + i * DH, DH), DH) for i in range(half // DH)]
+    turn_back(total, key_grad, value_grad, cos_ref[...], -sin_ref[...], starts)
+    there = pl.ds(pl.multiple_of((1 - core) * half, DH), half)
+    key_grad[:, there] = key_part[...]
+    value_grad[:, there] = value_part[...]
 
 
 def per_device(query_rows, key_rows, value_rows, cotangent, router_gate, positions):
@@ -343,7 +415,7 @@
 
     index = np.arange(DH) % (DH // 2)
     freq = jnp.asarray((THETA ** (-2.0 * index / DH)).astype(np.float32))[None]
-    packet = ((rows + EXTRA, group_width), BF16)
+    packet = ((rows, group_width), BF16)
     packets_shape = ((2, rows + EXTRA, heads_width + group_width), BF16)
     table = ((rows, DH), F32)
     kv_mine, kv_theirs, packed, cosine, sine = call(
@@ -395,24 +467,31 @@
 
     blocks = 2 * (chips - 1)
     far_table = ((half_groups, blocks * rows, 2 * wide), BF16)
-    part_shape = ((rows, group_width), BF16)
-    far_keys, _, far_grads, factors, deltas, *far_parts = call(
+    table = ((half_groups, rows, 2 * wide), F32)
+    late = ((half_groups, (blocks - 1) * rows, DH), BF16)
+    early_raws, early_grads, early_tops, sums, crosses = call(
+        early_kernel, "early_scores", [table, table, row, row, row], query, cot, tops, sums, crosses, far_sib[0]
+    )
+    far_keys, weights, far_grads, factors, deltas, *sib_parts = call(
         functools.partial(far_kernel, blocks=blocks),
         "far_scores",
-        [((half_groups, blocks * rows, DH), BF16), far_table, far_table, row, row] + [part_shape] * blocks,
+        [((half_groups, blocks * rows, DH), BF16), far_table, far_table, row, row] + [packet] * (chips - 1),
         query,
         cot,
         gate_row,
         tops,
+        early_raws,
+        early_grads,
+        early_tops,
         sums,
         crosses,
         *far_sib,
         *far_own,
-        flops=4 * 10**6,
-        scratch=[pltpu.VMEM((half_groups, blocks * rows, DH), BF16)],
-    )
-    sib_got = [lax.ppermute(far_parts[s - 1], "ctx", back_cross[s]) for s in range(1, chips)]
-    own_got = [lax.ppermute(far_parts[chips + s - 2], "ctx", back_hop[s]) for s in range(1, chips)]
+        scratch=[pltpu.VMEM(*late), pltpu.VMEM(*late)],
+    )
+    sib_got = [lax.ppermute(sib_parts[s - 1], "ctx", back_cross[s]) for s in range(1, chips)]
+    own_parts = call(far_rest_kernel, "far_rest", [packet] * (chips - 1), weights, far_grads, query, cot)
+    own_got = [lax.ppermute(own_parts[s - 1], "ctx", back_hop[s]) for s in range(1, chips)]
 
     part_mine, packed = call(
         functools.partial(near_kernel, ratio=ratio),
@@ -439,16 +518,28 @@
         ],
     )
     back = swap(packed)
-    query_grad, key_grad, value_grad, gate_grad = call(
-        functools.partial(finish_kernel, limit=limit),
-        "finish",
-        [((rows, heads_width), BF16)] + [((rows, group_width), BF16)] * 2 + [((1, rows), F32)],
+    side = ((rows, group_width // 2), BF16)
+    query_grad, gate_grad, key_part, value_part = call(
+        functools.partial(finish_queries_kernel, limit=limit),
+        "finish_queries",
+        [((rows, heads_width), BF16), ((1, rows), F32), side, side],
         back,
-        part_mine,
         positions,
         cosine,
         sine,
-        *[part for pair in zip(sib_got, own_got) for part in pair],
+        *sib_got,
+        flops=3 * 10**8,
+    )
+    key_grad, value_grad = call(
+        finish_keys_kernel,
+        "finish_keys",
+        [((rows, group_width), BF16)] * 2,
+        part_mine,
+        key_part,
+        value_part,
+        cosine,
+        sine,
+        *own_got,
     )
     return (query_grad[None], key_grad[None], value_grad[None], gate_grad)
 

time: 33.3 us -> 29.6 us (0.89)
  waiting for transfers between devices: 5.79 us -> 2.62 us
  Pallas kernels: 8.09 us -> 7.48 us
    ppermute x2, waiting for transfers between devices: 5.79 us -> 2.62 us  [the longest x1 2.61 us: per_device(): lax.ppermute(own_parts[s - 1], 'ctx', back_hop[s])]
    pallas_call x5 -> x8, Pallas kernels: 8.09 us -> 7.48 us  [call(): pl.pallas_call(kernel, out_shape=[jax.ShapeDtypeStruct(*out) for out in o...]
  transfers between devices with their start and end apart: 4 -> 4, of which waited for: 2 -> 1; matrix products, arithmetic and copies ran while one was open for 0% -> 0% of each run, Pallas kernels for 11% -> 17%
where the time goes in v5:
time: 29.6 us; the launch traced here: 29.3 us
  blocking collectives  9.75 us (33%)
  starting transfers between devices  8.73 us (29%)
  Pallas kernels  7.48 us (25%)
  waiting for transfers between devices  2.62 us (9%)
  between operations  0.72 us (2%)
    all_to_all x2, blocking collectives, per_device(): lax.all_to_all(both, 'ctx', 0, 0, axis_index_groups=pairs)  9.75 us
    pallas_call x8, Pallas kernels, call(): pl.pallas_call(kernel, out_shape=[jax.ShapeDtypeStruct(*out) for out in o...  7.48 us
    ppermute x1, starting transfers between devices, per_device(): lax.ppermute(kv_theirs, 'ctx', cross[s])  4.29 us
    ppermute x1, waiting for transfers between devices, per_device(): lax.ppermute(own_parts[s - 1], 'ctx', back_hop[s])  2.61 us
    ppermute x1, starting transfers between devices, per_device(): far_own = [lax.ppermute(kv_mine, 'ctx', hop[s]) for s in range(1, chips)]  1.85 us
    ppermute x1, starting transfers between devices, per_device(): lax.ppermute(own_parts[s - 1], 'ctx', back_hop[s])  1.29 us
    ppermute x1, starting transfers between devices, per_device(): lax.ppermute(sib_parts[s - 1], 'ctx', back_cross[s])  1.29 us
  transfers between devices with their start and end apart: 4, of which 1 were waited for; matrix products, arithmetic and copies ran while one was open for 0% of the time, Pallas kernels for 17%

profile of v5, /device:TPU:0, one launch (start us, length us, event | category | flops | bytes accessed | tf_op | source)
XLA Modules:
  0.0 29.3 jit_solution(3151613324446194024)
XLA Ops:
  0.6 1.8 %pack.1 = (bf16[160,512]{1,0:T(8,128)(2,1)S(1)}, bf16[160,512]{1,0:T(8,128)(2,1)S(1)}, bf16[2,176,2560]{2,1,0:T(8,128)(2,1)S(1)}, f32[160,128]{1,0:T(8,128)S(1)}, f32[160,128]{1,0:T(8,128)S(1)}) custom-call(bf16[160,512]{1,0:T(8,128)(2,1)} %bitcast.9, bf16[160,512]{1,0:T(8,128)(2,1)} %bitcast.10, bf16[160,2048]{1,0:T(8,128)(2,1)} %bitcast.7, ...), custom_call_target="tpu_custom_call" | custom-call | flops 1000000 | bytes 1000 | tf_op jit(solution)/shard_map/pack/pallas_call | solution.py:406
  2.4 4.3 %collective-permute-start = (bf16[160,512]{1,0:T(8,128)(2,1)S(1)}, bf16[160,512]{1,0:T(8,128)(2,1)S(1)}, u32[]{:S(2)}, u32[]{:S(2)}) collective-permute-start(bf16[160,512]{1,0:T(8,128)(2,1)S(1)} %get-tuple-element.46), channel_id=1, source_target_pairs={{0,3},{1,2},{4,7},{5,6},{8,11},{9,10},{12,15},{13,14},{16,19},{17,... | collective-permute-start | bytes 491528 | tf_op jit(solution)/shard_map/ppermute | solution.py:450
  6.7 1.9 %collective-permute-start.1 = (bf16[160,512]{1,0:T(8,128)(2,1)S(1)}, bf16[160,512]{1,0:T(8,128)(2,1)S(1)}, u32[]{:S(2)}, u32[]{:S(2)}) collective-permute-start(bf16[160,512]{1,0:T(8,128)(2,1)S(1)} %get-tuple-element.52), channel_id=1, source_target_pairs={{0,2},{1,3},{4,6},{5,7},{8,10},{9,11},{12,14},{13,15},{16,18},{17,... | collective-permute-start | bytes 491528 | tf_op jit(solution)/shard_map/ppermute | solution.py:449
  8.6 5.2 %all_to_all.10.packets = bf16[2,176,2560]{2,1,0:T(8,128)(2,1)S(1)} all-to-all(bf16[2,176,2560]{2,1,0:T(8,128)(2,1)S(1)} %get-tuple-element.37), channel_id=1, replica_groups={{0,1},{2,3},{4,5},{6,7},{8,9},{10,11},{12,13},{14,15},{16,17},{18,19},{..., dimensions={0} | all-to-all | bytes 3604480 | tf_op jit(solution)/shard_map/all_to_all | solution.py:453
  13.8 1.8 %local_scores.1 = (bf16[2,320,128]{2,1,0:T(8,128)(2,1)S(1)}, bf16[2,320,128]{2,1,0:T(8,128)(2,1)}, bf16[2,1280,128]{2,1,0:T(8,128)(2,1)S(1)}, bf16[2,1280,128]{2...) custom-call(bf16[2,176,2560]{2,1,0:T(8,128)(2,1)S(1)} %all_to_all.10, ...), custom_call_target="tpu_custom_call" | custom-call | flops 3000000 | bytes 1000 | tf_op jit(solution)/shard_map/local_scores/pallas_call | solution.py:406
  15.6 0.0 collective-permute-done.packet.early
  15.6 0.0 collective-permute-done.1.refs_0_
  15.6 1.3 %collective-permute-start.2 = (bf16[160,512]{1,0:T(8,128)(2,1)S(1)}, bf16[160,512]{1,0:T(8,128)(2,1)S(1)}, u32[]{:S(2)}, u32[]{:S(2)}) collective-permute-start(bf16[160,512]{1,0:T(8,128)(2,1)S(1)} %get-tuple-element.61), channel_id=1, source_target_pairs={{3,0},{2,1},{7,4},{6,5},{11,8},{10,9},{15,12},{14,13},{19,16},{18,... | collective-permute-start | bytes 491528 | tf_op jit(solution)/shard_map/ppermute | solution.py:492
  16.9 1.3 %collective-permute-start.3 = (bf16[160,512]{1,0:T(8,128)(2,1)S(1)}, bf16[160,512]{1,0:T(8,128)(2,1)S(1)}, u32[]{:S(2)}, u32[]{:S(2)}) collective-permute-start(bf16[160,512]{1,0:T(8,128)(2,1)S(1)} %far_rest.1), channel_id=1, source_target_pairs={{2,0},{3,1},{6,4},{7,5},{10,8},{11,9},{14,12},{15,13},{18,16},{19,... | collective-permute-start | bytes 491528 | tf_op jit(solution)/shard_map/ppermute | solution.py:494
  18.2 1.8 %near_grads.1 = (f32[160,512]{1,0:T(8,128)S(1)}, bf16[2,176,1536]{2,1,0:T(8,128)(2,1)S(1)}) custom-call(f32[2,320,1280]{2,1,0:T(8,128)S(1)} %get-tuple-element.38.raws, f32[2,320,1280]{2,1,0:T(8,128)S(1)} %get-tuple-element.39.grads, f32[2,1,1280]{2,1,0:T(1,128)S(1)} %get-tuple-element.53.factors, f32[2,1,1280]{2,1,0:T(1,128)S(1)} %get-tuple-element.54.deltas, ...), custom_call_target="tpu_custom_call" | custom-call | flops 4000000 | bytes 1000 | tf_op jit(solution)/shard_map/near_grads/pallas_call | solution.py:406
  20.1 0.0 copy-start
  20.1 4.6 %all_to_all.11.back = bf16[2,176,1536]{2,1,0:T(8,128)(2,1)S(1)} all-to-all(bf16[2,176,1536]{2,1,0:T(8,128)(2,1)S(1)} %get-tuple-element.58), channel_id=1, replica_groups={{0,1},{2,3},{4,5},{6,7},{8,9},{10,11},{12,13},{14,15},{16,17},{18,19},{..., dimensions={0} | all-to-all | bytes 2162688 | tf_op jit(solution)/shard_map/all_to_all | solution.py:453
  24.7 0.0 collective-permute-done.2.refs_0_
  24.7 0.0 copy-done
  24.7 1.2 %finish_queries.1 = (bf16[160,2048]{1,0:T(8,128)(2,1)}, f32[1,160]{1,0:T(1,128)}, bf16[160,256]{1,0:T(8,128)(2,1)S(1)}, bf16[160,256]{1,0:T(8,128)(2,1)S(1)}) custom-call(bf16[2,176,1536]{2,1,0:T(8,128)(2,1)S(1)} %all_to_all.11.back, s32[1,160]{1,0:T(1,128)S(1)} %copy-done, f32[160,128]{1,0:T(8,128)S(1)} %get-tuple-element.59.cos_ref, ...), custom_call_target="tpu_custom_call" | custom-call | flops 300000000 | bytes 1000 | tf_op jit(solution)/shard_map/finish_queries/pallas_call | solution.py:406
  25.9 2.6 %collective-permute-done.3.refs_0_ = bf16[160,512]{1,0:T(8,128)(2,1)S(1)} collective-permute-done((bf16[160,512]{1,0:T(8,128)(2,1)S(1)}, bf16[160,512]{1,0:T(8,128)(2,1)S(1)}, u32[]{:S(2)}, u32[]{:S(2)}) %collective-permute-start.3) | collective-permute-done | bytes 163872 | tf_op jit(solution)/shard_map/ppermute | solution.py:494
  28.5 0.8 %finish_keys.1 = (bf16[160,512]{1,0:T(8,128)(2,1)}, bf16[160,512]{1,0:T(8,128)(2,1)}) custom-call(f32[160,512]{1,0:T(8,128)S(1)} %get-tuple-element.63.part_mine, bf16[160,256]{1,0:T(8,128)(2,1)S(1)} %get-tuple-element.64.key_part, bf16[160,256]{1,0:T(8,128)(2,1)S(1)} %get-tuple-element.65.value_part, f32[160,128]{1,0:T(8,128)S(1)} %get-tuple-element.59.cos_ref, ...), custom_call_target="tpu_custom_call" | custom-call | flops 1000000 | bytes 1000 | tf_op jit(solution)/shard_map/finish_keys/pallas_call | solution.py:406
  (3 shorter events, 0.0 us)
Async XLA Ops:
  2.4 13.1 %collective-permute-start = (bf16[160,512]{1,0:T(8,128)(2,1)S(1)}, bf16[160,512]{1,0:T(8,128)(2,1)S(1)}, u32[]{:S(2)}, u32[]{:S(2)}) collective-permute-start(bf16[160,512]{1,0:T(8,128)(2,1)S(1)} %get-tuple-element.46), channel_id=1, source_target_pairs={{0,3},{1,2},{4,7},{5,6},{8,11},{9,10},{12,15},{13,14},{16,19},{17,... | collective-permute-start | bytes 491528 | tf_op jit(solution)/shard_map/ppermute | solution.py:450
  6.7 8.8 %collective-permute-start.1 = (bf16[160,512]{1,0:T(8,128)(2,1)S(1)}, bf16[160,512]{1,0:T(8,128)(2,1)S(1)}, u32[]{:S(2)}, u32[]{:S(2)}) collective-permute-start(bf16[160,512]{1,0:T(8,128)(2,1)S(1)} %get-tuple-element.52), channel_id=1, source_target_pairs={{0,2},{1,3},{4,6},{5,7},{8,10},{9,11},{12,14},{13,15},{16,18},{17,... | collective-permute-start | bytes 491528 | tf_op jit(solution)/shard_map/ppermute | solution.py:449
  15.6 9.1 %collective-permute-start.2 = (bf16[160,512]{1,0:T(8,128)(2,1)S(1)}, bf16[160,512]{1,0:T(8,128)(2,1)S(1)}, u32[]{:S(2)}, u32[]{:S(2)}) collective-permute-start(bf16[160,512]{1,0:T(8,128)(2,1)S(1)} %get-tuple-element.61), channel_id=1, source_target_pairs={{3,0},{2,1},{7,4},{6,5},{11,8},{10,9},{15,12},{14,13},{19,16},{18,... | collective-permute-start | bytes 491528 | tf_op jit(solution)/shard_map/ppermute | solution.py:492
  16.9 11.6 %collective-permute-start.3 = (bf16[160,512]{1,0:T(8,128)(2,1)S(1)}, bf16[160,512]{1,0:T(8,128)(2,1)S(1)}, u32[]{:S(2)}, u32[]{:S(2)}) collective-permute-start(bf16[160,512]{1,0:T(8,128)(2,1)S(1)} %far_rest.1), channel_id=1, source_target_pairs={{2,0},{3,1},{6,4},{7,5},{10,8},{11,9},{14,12},{15,13},{18,16},{19,... | collective-permute-start | bytes 491528 | tf_op jit(solution)/shard_map/ppermute | solution.py:494
  20.1 4.6 %copy-start = (s32[1,160]{1,0:T(1,128)S(1)}, s32[1,160]{1,0:T(1,128)}, u32[]{:S(2)}) copy-start(s32[1,160]{1,0:T(1,128)} %pos_ref.1) | copy-start | bytes 1924

commit v6 on v5

--- a/solution.py
+++ b/solution.py
@@ -304,7 +304,7 @@
 
 def near_kernel(
     raws, grads, factors, deltas, keys, query, cot, far_keys, far_grads,
-    part_mine, out_ref, weights, score_grads, parts, acc,
+    part_mine, query_mine, gate_mine, theirs, weights, score_grads, parts, acc,
     *, ratio
 ):
     rows = part_mine.shape[0]
@@ -329,22 +329,24 @@
         for i in range(half_groups):
             acc[i] += dot(far_grads[i], far_keys[i], TN)
 
-    for i in range(half_groups):
-        for block in range(2):
+    core = core_of()
+    for out_ref, block in ((theirs, 1 - core), (query_mine, core)):
+        for i in range(half_groups):
             for h in range(ratio):
                 at = (i * ratio + h) * DH
-                low = block * wide + h * rows
-                out_ref[block, :rows, at : at + DH] = (acc[i, low : low + rows] * SCALE).astype(BF16)
-    part_mine[...] = parts[core_of()]
-    for block in range(2):
-        out_ref[block, :rows, half:] = parts[block].astype(BF16)
+                low = pl.ds(pl.multiple_of(block * wide + h * rows, 16), rows)
+                out_ref[:rows, at : at + DH] = (acc[i, low, :] * SCALE).astype(BF16)
+    part_mine[...] = parts[core]
+    theirs[:rows, half:] = parts[1 - core].astype(BF16)
     summed = deltas[0]
     for i in range(1, half_groups):
         summed = summed + deltas[i]
+    gates = []
     for block in range(2):
         own = split_rows(summed[:, block * wide : (block + 1) * wide], 16)
-        own = joined_row(dot(own, chosen((wide, rows), ratio, 0), NN))
-        out_ref[block, rows:, :rows] = split_rows(own, EXTRA)
+        gates.append(joined_row(dot(own, chosen((wide, rows), ratio, 0), NN)))
+    gate_mine[...] = jnp.where(core == 0, gates[0], gates[1])
+    theirs[rows:, :rows] = split_rows(jnp.where(core == 0, gates[1], gates[0]), EXTRA)
 
 
 def turn_back(values, out_key, out_value, cosine, sine, starts):
@@ -354,19 +356,19 @@
         out_value[:, there] = values[:, (2 * i + 1) * DH : (2 * i + 2) * DH].astype(BF16)
 
 
-def finish_queries_kernel(back, pos_ref, cos_ref, sin_ref, *refs, limit):
+def finish_queries_kernel(back, query_mine, gate_mine, pos_ref, cos_ref, sin_ref, *refs, limit):
     got, (query_grad, gate_grad, key_part, value_part) = refs[:-4], refs[-4:]
-    rows = cos_ref.shape[0]
-    half = query_grad.shape[1] // 2
+    rows, half = query_mine.shape
+    core = core_of()
     cosine, sine = cos_ref[...], -sin_ref[...]
-    for side in range(2):
+    for side, ref in ((core, query_mine), (1 - core, back.at[1 - core])):
         for i in range(half // DH):
-            there = slice(side * half + i * DH, side * half + (i + 1) * DH)
-            turned = rotate(back[side, :rows, i * DH : (i + 1) * DH].astype(F32), cosine, sine)
+            there = pl.ds(pl.multiple_of(side * half + i * DH, DH), DH)
+            turned = rotate(ref[:rows, i * DH : (i + 1) * DH].astype(F32), cosine, sine)
             query_grad[:, there] = turned.astype(BF16)
-    gate = joined_row(back[0, rows:, :rows]) + joined_row(back[1, rows:, :rows])
+    gate = gate_mine[...] + joined_row(back[1 - core, rows:, :rows])
     gate_grad[...] = jnp.where(pos_ref[...] < limit, gate, 0.0)
-    other = back[1 - core_of(), :rows, half:].astype(F32)
+    other = back[1 - core, :rows, half:].astype(F32)
     for ref in got:
         other = other + ref[...].astype(F32)
     starts = [slice(i * DH, (i + 1) * DH) for i in range(key_part.shape[1] // DH)]
@@ -493,12 +495,14 @@
     own_parts = call(far_rest_kernel, "far_rest", [packet] * (chips - 1), weights, far_grads, query, cot)
     own_got = [lax.ppermute(own_parts[s - 1], "ctx", back_hop[s]) for s in range(1, chips)]
 
-    part_mine, packed = call(
+    part_mine, query_mine, gate_mine, theirs = call(
         functools.partial(near_kernel, ratio=ratio),
         "near_grads",
         [
             ((rows, group_width), F32),
-            ((2, rows + EXTRA, half_width + group_width), BF16),
+            ((rows, half_width), BF16),
+            ((1, rows), F32),
+            ((rows + EXTRA, half_width + group_width), BF16),
         ],
         raws,
         grads,
@@ -517,13 +521,15 @@
             pltpu.VMEM((half_groups, 2 * wide, DH), F32),
         ],
     )
-    back = swap(packed)
+    back = lax.all_gather(theirs, "ctx", axis_index_groups=pairs)
     side = ((rows, group_width // 2), BF16)
     query_grad, gate_grad, key_part, value_part = call(
         functools.partial(finish_queries_kernel, limit=limit),
         "finish_queries",
         [((rows, heads_width), BF16), ((1, rows), F32), side, side],
         back,
+        query_mine,
+        gate_mine,
         positions,
         cosine,
         sine,

time: 29.6 us -> 52.3 us (1.77)
  between operations: 0.72 us -> 14.1 us
  local copies, waits for them, and re-layouts: 0.01 us -> 7.17 us
  waiting for transfers between devices: 2.62 us -> 8.01 us
  blocking collectives: 9.75 us -> 5.16 us
  Pallas kernels: 7.48 us -> 8.7 us
    unnamed x2 -> x18, local copies, waits for them, and re-layouts: 0.01 us -> 7.17 us
    ppermute x1, waiting for transfers between devices: 0.01 us -> 5.06 us  [per_device(): lax.ppermute(sib_parts[s - 1], 'ctx', back_cross[s])]
    all_to_all x2 -> x1, blocking collectives: 9.75 us -> 5.16 us  [per_device(): lax.all_to_all(both, 'ctx', 0, 0, axis_index_groups=pairs)]
    all_gather x0 -> x1, waiting for transfers between devices: none -> 2.93 us  [per_device(): back = lax.all_gather(theirs, 'ctx', axis_index_groups=pairs)]
    ppermute x1, waiting for transfers between devices: 2.61 us -> 0.01 us  [per_device(): lax.ppermute(own_parts[s - 1], 'ctx', back_hop[s])]
    pallas_call x8, Pallas kernels: 7.48 us -> 8.7 us  [call(): pl.pallas_call(kernel, out_shape=[jax.ShapeDtypeStruct(*out) for out in o...]
  transfers between devices with their start and end apart: 4 -> 5, of which waited for: 1 -> 2; matrix products, arithmetic and copies ran while one was open for 0% -> 0% of each run, Pallas kernels for 17% -> 7%
where the time goes in v6:
time: 52.3 us; the launch traced here: 51.9 us
  between operations  14.1 us (27%)
  starting transfers between devices  8.75 us (17%)
  Pallas kernels  8.7 us (17%)
  waiting for transfers between devices  8.01 us (15%)
  local copies, waits for them, and re-layouts  7.17 us (14%)
  blocking collectives  5.16 us (10%)
    pallas_call x8, Pallas kernels, call(): pl.pallas_call(kernel, out_shape=[jax.ShapeDtypeStruct(*out) for out in o...  8.7 us
    unnamed x18, local copies, waits for them, and re-layouts  7.17 us
    all_to_all x1, blocking collectives, per_device(): lax.all_to_all(both, 'ctx', 0, 0, axis_index_groups=pairs)  5.16 us
    ppermute x1, waiting for transfers between devices, per_device(): lax.ppermute(sib_parts[s - 1], 'ctx', back_cross[s])  5.06 us
    ppermute x1, starting transfers between devices, per_device(): lax.ppermute(kv_theirs, 'ctx', cross[s])  4.29 us
    all_gather x1, waiting for transfers between devices, per_device(): back = lax.all_gather(theirs, 'ctx', axis_index_groups=pairs)  2.93 us
    ppermute x1, starting transfers between devices, per_device(): far_own = [lax.ppermute(kv_mine, 'ctx', hop[s]) for s in range(1, chips)]  1.85 us
    ppermute x1, starting transfers between devices, per_device(): lax.ppermute(sib_parts[s - 1], 'ctx', back_cross[s])  1.29 us
  transfers between devices with their start and end apart: 5, of which 2 were waited for; matrix products, arithmetic and copies ran while one was open for 0% of the time, Pallas kernels for 7%

profile of v6, /device:TPU:0, one launch (start us, length us, event | category | flops | bytes accessed | tf_op | source)
XLA Modules:
  0.0 51.9 jit_solution(3195341528956913273)
XLA Ops:
  7.2 0.0 all-gather.3.cloned.1.call-start
  7.2 1.8 %pack.1 = (bf16[160,512]{1,0:T(8,128)(2,1)S(1)}, bf16[160,512]{1,0:T(8,128)(2,1)S(1)}, bf16[2,176,2560]{2,1,0:T(8,128)(2,1)S(1)}, f32[160,128]{1,0:T(8,128)S(1)}, f32[160,128]{1,0:T(8,128)S(1)}) custom-call(bf16[160,512]{1,0:T(8,128)(2,1)} %bitcast.11, bf16[160,512]{1,0:T(8,128)(2,1)} %bitcast.12, bf16[160,2048]{1,0:T(8,128)(2,1)} %bitcast.9, ...), custom_call_target="tpu_custom_call" | custom-call | flops 1000000 | bytes 1000 | tf_op jit(solution)/shard_map/pack/pallas_call | solution.py:408
  9.0 4.3 %collective-permute-start = (bf16[160,512]{1,0:T(8,128)(2,1)S(1)}, bf16[160,512]{1,0:T(8,128)(2,1)S(1)}, u32[]{:S(2)}, u32[]{:S(2)}) collective-permute-start(bf16[160,512]{1,0:T(8,128)(2,1)S(1)} %get-tuple-element.48), channel_id=1, source_target_pairs={{0,3},{1,2},{4,7},{5,6},{8,11},{9,10},{12,15},{13,14},{16,19},{17,... | collective-permute-start | bytes 491528 | tf_op jit(solution)/shard_map/ppermute | solution.py:452
  13.3 1.9 %collective-permute-start.1 = (bf16[160,512]{1,0:T(8,128)(2,1)S(1)}, bf16[160,512]{1,0:T(8,128)(2,1)S(1)}, u32[]{:S(2)}, u32[]{:S(2)}) collective-permute-start(bf16[160,512]{1,0:T(8,128)(2,1)S(1)} %get-tuple-element.54), channel_id=1, source_target_pairs={{0,2},{1,3},{4,6},{5,7},{8,10},{9,11},{12,14},{13,15},{16,18},{17,... | collective-permute-start | bytes 491528 | tf_op jit(solution)/shard_map/ppermute | solution.py:451
  15.2 5.2 %all_to_all.5.packets = bf16[2,176,2560]{2,1,0:T(8,128)(2,1)S(1)} all-to-all(bf16[2,176,2560]{2,1,0:T(8,128)(2,1)S(1)} %get-tuple-element.39), channel_id=1, replica_groups={{0,1},{2,3},{4,5},{6,7},{8,9},{10,11},{12,13},{14,15},{16,17},{18,19},{..., dimensions={0} | all-to-all | bytes 3604480 | tf_op jit(solution)/shard_map/all_to_all | solution.py:455
  20.3 1.8 %local_scores.1 = (bf16[2,320,128]{2,1,0:T(8,128)(2,1)S(1)}, bf16[2,320,128]{2,1,0:T(8,128)(2,1)}, bf16[2,1280,128]{2,1,0:T(8,128)(2,1)S(1)}, bf16[2,1280,128]{2...) custom-call(bf16[2,176,2560]{2,1,0:T(8,128)(2,1)S(1)} %all_to_all.5., ...), custom_call_target="tpu_custom_call" | custom-call | flops 3000000 | bytes 1000 | tf_op jit(solution)/shard_map/local_scores/pallas_call | solution.py:408
  22.1 0.0 collective-permute-done.packet.early
  22.1 0.0 collective-permute-done.1.refs_0_
  22.2 0.0 copy-start
  22.2 1.2 %copy-done = bf16[2,320,1280]{2,1,0:T(8,128)(2,1)} copy-done((bf16[2,320,1280]{2,1,0:T(8,128)(2,1)}, bf16[2,320,1280]{2,1,0:T(8,128)(2,1)S(1)}, u32[]{:S(2)}) %copy-start) | copy-done | bytes 1638424
  23.4 0.0 copy-start.8
  23.4 2.4 %near_grads.1 = (f32[160,512]{1,0:T(8,128)S(1)}, bf16[160,1024]{1,0:T(8,128)(2,1)S(1)}, f32[1,160]{1,0:T(1,128)S(1)}, bf16[176,1536]{1,0:T(8,128)(2,1)}) custom-call(f32[2,320,1280]{2,1,0:T(8,128)S(1)} %get-tuple-element.40.raws, f32[2,320,1280]{2,1,0:T(8,128)S(1)} %get-tuple-element.41.grads, f32[2,1,1280]{2,1,0:T(1,128)S(1)} %get-tuple-element.55.factors, ...), custom_call_target="tpu_custom_call" | custom-call | flops 4000000 | bytes 1000 | tf_op jit(solution)/shard_map/near_grads/pallas_call | solution.py:408
  25.8 0.0 copy-done.8
  25.8 0.0 copy-start.3
  25.8 0.8 %copy-done.3 = bf16[160,1024]{1,0:T(8,128)(2,1)} copy-done((bf16[160,1024]{1,0:T(8,128)(2,1)}, bf16[160,1024]{1,0:T(8,128)(2,1)S(1)}, u32[]{:S(2)}) %copy-start.3) | copy-done | bytes 327704
  26.5 0.0 all-gather.3.cloned.1.call-update
  26.6 1.3 %collective-permute-start.2 = (bf16[160,512]{1,0:T(8,128)(2,1)}, bf16[160,512]{1,0:T(8,128)(2,1)S(1)}, u32[]{:S(2)}, u32[]{:S(2)}) collective-permute-start(bf16[160,512]{1,0:T(8,128)(2,1)} %copy-done.8), channel_id=1, source_target_pairs={{3,0},{2,1},{7,4},{6,5},{11,8},{10,9},{15,12},{14,13},{19,16},{18,... | collective-permute-start | bytes 491528 | tf_op jit(solution)/shard_map/ppermute | solution.py:494
  27.9 0.0 copy-start.1
  27.9 1.4 %copy-done.1 = bf16[2,320,1280]{2,1,0:T(8,128)(2,1)S(1)} copy-done((bf16[2,320,1280]{2,1,0:T(8,128)(2,1)S(1)}, bf16[2,320,1280]{2,1,0:T(8,128)(2,1)}, u32[]{:S(2)}) %copy-start.1) | copy-done | bytes 1638424
  29.3 0.0 copy-start.7
  29.3 0.7 %far_rest.1 = bf16[160,512]{1,0:T(8,128)(2,1)} custom-call(bf16[2,320,1280]{2,1,0:T(8,128)(2,1)S(1)} %copy-done.1, bf16[2,320,1280]{2,1,0:T(8,128)(2,1)S(1)} %get-tuple-element.59.far_grads.score_grads, bf16[2,1280,128]{2,1,0:T(8,128)(2,1)S(1)} %get-tuple-element.42.query, bf16[2,1280,128]{2,1,0:T(8,128)(2,1)S(1)} %get-tuple-element.43.cot), custom_call_target="tpu_custom_call" | custom-call | flops 1000000 | bytes 1000 | tf_op jit(solution)/shard_map/far_rest/pallas_call | solution.py:408
  30.0 1.3 %collective-permute-start.3 = (bf16[160,512]{1,0:T(8,128)(2,1)}, bf16[160,512]{1,0:T(8,128)(2,1)S(1)}, u32[]{:S(2)}, u32[]{:S(2)}) collective-permute-start(bf16[160,512]{1,0:T(8,128)(2,1)} %far_rest.1), channel_id=1, source_target_pairs={{2,0},{3,1},{6,4},{7,5},{10,8},{11,9},{14,12},{15,13},{18,16},{19,... | collective-permute-start | bytes 491528 | tf_op jit(solution)/shard_map/ppermute | solution.py:496
  31.3 5.1 %collective-permute-done.2.refs_0_ = bf16[160,512]{1,0:T(8,128)(2,1)S(1)} collective-permute-done((bf16[160,512]{1,0:T(8,128)(2,1)}, bf16[160,512]{1,0:T(8,128)(2,1)S(1)}, u32[]{:S(2)}, u32[]{:S(2)}) %collective-permute-start.2) | collective-permute-done | bytes 163872 | tf_op jit(solution)/shard_map/ppermute | solution.py:494
  36.3 0.0 copy-start.5
  36.3 0.7 %copy-done.5 = bf16[160,512]{1,0:T(8,128)(2,1)} copy-done((bf16[160,512]{1,0:T(8,128)(2,1)}, bf16[160,512]{1,0:T(8,128)(2,1)S(1)}, u32[]{:S(2)}) %copy-start.5) | copy-done | bytes 163864
  37.0 2.9 %all-gather.3.cloned.1.call-done = bf16[352,1536]{1,0:T(8,128)(2,1)} async-done(((bf16[176,1536]{1,0:T(8,128)(2,1)}), bf16[352,1536]{1,0:T(8,128)(2,1)}) %all-gather.3.cloned.1.call-update) | async-done | bytes 1081360 | tf_op jit(solution)/shard_map/all_gather | solution.py:524
  39.9 0.0 copy-done.7
  39.9 0.0 copy-start.2
  39.9 1.2 %copy-done.2 = bf16[352,1536]{1,0:T(8,128)(2,1)S(1)} copy-done((bf16[352,1536]{1,0:T(8,128)(2,1)S(1)}, bf16[352,1536]{1,0:T(8,128)(2,1)}, u32[]{:S(2)}) %copy-start.2) | copy-done | bytes 1081368
  41.1 0.0 copy-start.4
  41.2 1.0 %copy-done.4 = bf16[160,1024]{1,0:T(8,128)(2,1)S(1)} copy-done((bf16[160,1024]{1,0:T(8,128)(2,1)S(1)}, bf16[160,1024]{1,0:T(8,128)(2,1)}, u32[]{:S(2)}) %copy-start.4) | copy-done | bytes 327704
  42.1 0.0 copy-start.6
  42.1 0.9 %copy-done.6 = bf16[160,512]{1,0:T(8,128)(2,1)S(1)} copy-done((bf16[160,512]{1,0:T(8,128)(2,1)S(1)}, bf16[160,512]{1,0:T(8,128)(2,1)}, u32[]{:S(2)}) %copy-start.6) | copy-done | bytes 163864
  43.0 1.2 %finish_queries.1 = (bf16[160,2048]{1,0:T(8,128)(2,1)}, f32[1,160]{1,0:T(1,128)}, bf16[160,256]{1,0:T(8,128)(2,1)S(1)}, bf16[160,256]{1,0:T(8,128)(2,1)S(1)}) custom-call(bf16[2,176,1536]{2,1,0:T(8,128)(2,1)S(1)} %bitcast.8, bf16[160,1024]{1,0:T(8,128)(2,1)S(1)} %copy-done.4, f32[1,160]{1,0:T(1,128)S(1)} %get-tuple-element.62.gate_mine, ...), custom_call_target="tpu_custom_call" | custom-call | flops 300000000 | bytes 1000 | tf_op jit(solution)/shard_map/finish_queries/pallas_call | solution.py:408
  44.3 0.0 collective-permute-done.3.refs_0_
  44.3 0.8 %finish_keys.1 = (bf16[160,512]{1,0:T(8,128)(2,1)}, bf16[160,512]{1,0:T(8,128)(2,1)}) custom-call(f32[160,512]{1,0:T(8,128)S(1)} %get-tuple-element.67.part_mine, bf16[160,256]{1,0:T(8,128)(2,1)S(1)} %get-tuple-element.68.key_part, bf16[160,256]{1,0:T(8,128)(2,1)S(1)} %get-tuple-element.69.value_part, f32[160,128]{1,0:T(8,128)S(1)} %get-tuple-element.63.cos_ref, ...), custom_call_target="tpu_custom_call" | custom-call | flops 1000000 | bytes 1000 | tf_op jit(solution)/shard_map/finish_keys/pallas_call | solution.py:408
  (2 shorter events, 0.0 us)
Async XLA Ops:
  7.2 32.7 %all-gather.3.cloned.1.call-start = ((), (), s32[]{:S(2)}) async-start(), calls=%async_computation.1 | async-start | bytes 1622016 | tf_op jit(solution)/shard_map/all_gather | solution.py:524
  9.0 13.1 %collective-permute-start = (bf16[160,512]{1,0:T(8,128)(2,1)S(1)}, bf16[160,512]{1,0:T(8,128)(2,1)S(1)}, u32[]{:S(2)}, u32[]{:S(2)}) collective-permute-start(bf16[160,512]{1,0:T(8,128)(2,1)S(1)} %get-tuple-element.48), channel_id=1, source_target_pairs={{0,3},{1,2},{4,7},{5,6},{8,11},{9,10},{12,15},{13,14},{16,19},{17,... | collective-permute-start | bytes 491528 | tf_op jit(solution)/shard_map/ppermute | solution.py:452
  13.3 8.8 %collective-permute-start.1 = (bf16[160,512]{1,0:T(8,128)(2,1)S(1)}, bf16[160,512]{1,0:T(8,128)(2,1)S(1)}, u32[]{:S(2)}, u32[]{:S(2)}) collective-permute-start(bf16[160,512]{1,0:T(8,128)(2,1)S(1)} %get-tuple-element.54), channel_id=1, source_target_pairs={{0,2},{1,3},{4,6},{5,7},{8,10},{9,11},{12,14},{13,15},{16,18},{17,... | collective-permute-start | bytes 491528 | tf_op jit(solution)/shard_map/ppermute | solution.py:451
  22.2 1.2 %copy-start = (bf16[2,320,1280]{2,1,0:T(8,128)(2,1)}, bf16[2,320,1280]{2,1,0:T(8,128)(2,1)S(1)}, u32[]{:S(2)}) copy-start(bf16[2,320,1280]{2,1,0:T(8,128)(2,1)S(1)} %get-tuple-element.70.weights) | copy-start | bytes 4915204
  23.4 2.4 %copy-start.8 = (bf16[160,512]{1,0:T(8,128)(2,1)}, bf16[160,512]{1,0:T(8,128)(2,1)S(1)}, u32[]{:S(2)}) copy-start(bf16[160,512]{1,0:T(8,128)(2,1)S(1)} %get-tuple-element.65) | copy-start | bytes 491524
  25.8 0.8 %copy-start.3 = (bf16[160,1024]{1,0:T(8,128)(2,1)}, bf16[160,1024]{1,0:T(8,128)(2,1)S(1)}, u32[]{:S(2)}) copy-start(bf16[160,1024]{1,0:T(8,128)(2,1)S(1)} %get-tuple-element.61.query_mine) | copy-start | bytes 983044
  26.6 9.8 %collective-permute-start.2 = (bf16[160,512]{1,0:T(8,128)(2,1)}, bf16[160,512]{1,0:T(8,128)(2,1)S(1)}, u32[]{:S(2)}, u32[]{:S(2)}) collective-permute-start(bf16[160,512]{1,0:T(8,128)(2,1)} %copy-done.8), channel_id=1, source_target_pairs={{3,0},{2,1},{7,4},{6,5},{11,8},{10,9},{15,12},{14,13},{19,16},{18,... | collective-permute-start | bytes 491528 | tf_op jit(solution)/shard_map/ppermute | solution.py:494
  27.9 1.4 %copy-start.1 = (bf16[2,320,1280]{2,1,0:T(8,128)(2,1)S(1)}, bf16[2,320,1280]{2,1,0:T(8,128)(2,1)}, u32[]{:S(2)}) copy-start(bf16[2,320,1280]{2,1,0:T(8,128)(2,1)} %copy-done) | copy-start | bytes 4915204
  29.3 10.6 %copy-start.7 = (s32[1,160]{1,0:T(1,128)S(1)}, s32[1,160]{1,0:T(1,128)}, u32[]{:S(2)}) copy-start(s32[1,160]{1,0:T(1,128)} %pos_ref.1) | copy-start | bytes 1924
  30.0 14.3 %collective-permute-start.3 = (bf16[160,512]{1,0:T(8,128)(2,1)}, bf16[160,512]{1,0:T(8,128)(2,1)S(1)}, u32[]{:S(2)}, u32[]{:S(2)}) collective-permute-start(bf16[160,512]{1,0:T(8,128)(2,1)} %far_rest.1), channel_id=1, source_target_pairs={{2,0},{3,1},{6,4},{7,5},{10,8},{11,9},{14,12},{15,13},{18,16},{19,... | collective-permute-start | bytes 491528 | tf_op jit(solution)/shard_map/ppermute | solution.py:496
  36.3 0.7 %copy-start.5 = (bf16[160,512]{1,0:T(8,128)(2,1)}, bf16[160,512]{1,0:T(8,128)(2,1)S(1)}, u32[]{:S(2)}) copy-start(bf16[160,512]{1,0:T(8,128)(2,1)S(1)} %collective-permute-done.2.refs_0_) | copy-start | bytes 491524
  39.9 1.2 %copy-start.2 = (bf16[352,1536]{1,0:T(8,128)(2,1)S(1)}, bf16[352,1536]{1,0:T(8,128)(2,1)}, u32[]{:S(2)}) copy-start(bf16[352,1536]{1,0:T(8,128)(2,1)} %all-gather.3.cloned.1.call-done) | copy-start | bytes 3244036
  41.1 1.0 %copy-start.4 = (bf16[160,1024]{1,0:T(8,128)(2,1)S(1)}, bf16[160,1024]{1,0:T(8,128)(2,1)}, u32[]{:S(2)}) copy-start(bf16[160,1024]{1,0:T(8,128)(2,1)} %copy-done.3) | copy-start | bytes 983044
  42.1 0.9 %copy-start.6 = (bf16[160,512]{1,0:T(8,128)(2,1)S(1)}, bf16[160,512]{1,0:T(8,128)(2,1)}, u32[]{:S(2)}) copy-start(bf16[160,512]{1,0:T(8,128)(2,1)} %copy-done.5) | copy-start | bytes 491524
Sparse Core Ops, SparseCore 0:
  26.7 13.1 all-gather.2

commit v7 on v5

--- a/solution.py
+++ b/solution.py
@@ -77,58 +77,57 @@
     return jnp.sum(rows.astype(F32), axis=0, keepdims=True)
 
 
-def pack_kernel(
-    key_in, value_in, query_in, cot_in, gate_in, pos_in, freq_in, mine, theirs, packed, cos_ref, sin_ref,
-    key, value, query, gate, pos, freq, sems, *, limit
+def pack_keys_kernel(
+    key_in, value_in, pos_in, freq_in, mine, theirs, packed, cos_ref, sin_ref, count_ref, key, value, pos, freq, sems,
+    *, limit
 ):
-    rows, width = key.shape
-    side_width = width // 2
-    half = query.shape[1] // 2
-    core = core_of()
-    loads = [(pos_in, pos), (freq_in, freq), (key_in, key), (value_in, value), (gate_in, gate), (query_in, query)]
-    for side in range(2):
-        there = slice(side * half, (side + 1) * half)
-        loads.append((cot_in.at[:, there], packed.at[side, :rows, half : 2 * half]))
+    loads = [(pos_in, pos), (freq_in, freq), (key_in, key), (value_in, value)]
     loads = [pltpu.make_async_copy(source, target, sems.at[i]) for i, (source, target) in enumerate(loads)]
     for copy in loads:
         copy.start()
+    rows, width = key.shape
+    side_width = width // 2
+    core = core_of()
+    down = lax.broadcasted_iota(jnp.int32, (rows, rows), 0)
+    along = lax.broadcasted_iota(jnp.int32, (rows, rows), 1)
+    lane = lax.broadcasted_iota(jnp.int32, (rows, DH), 1)
     loads[0].wait()
     loads[1].wait()
     places = pos[...]
     count = jnp.sum(jnp.where(places < limit, 1.0, 0.0), axis=1, keepdims=True)
-    count = jnp.broadcast_to(count, (EXTRA, width)).astype(BF16)
-    down = lax.broadcasted_iota(jnp.int32, (rows, rows), 0)
-    along = lax.broadcasted_iota(jnp.int32, (rows, rows), 1)
+    count_ref[...] = jnp.broadcast_to(count, count_ref.shape).astype(BF16)
     column = jnp.sum(jnp.where(down == along, places.astype(F32), 0.0), axis=1, keepdims=True)
     sine, cosine = sine_cosine(column * freq[...])
-    lane = lax.broadcasted_iota(jnp.int32, (rows, DH), 1)
     sine = jnp.where(lane < DH // 2, -sine, sine)
     cos_ref[...] = cosine
     sin_ref[...] = sine
+    used = jnp.broadcast_to(column, (rows, DH)) < limit
     loads[2].wait()
     loads[3].wait()
-    used = jnp.broadcast_to(column, (rows, DH)) < limit
     for out_ref, side in ((mine, core), (theirs, 1 - core)):
         for i in range(side_width // DH):
             there = pl.ds(pl.multiple_of(side * side_width + i * DH, DH), DH)
             turned = rotate(key[:, there].astype(F32), cosine, sine)
             out_ref[:, 2 * i * DH : (2 * i + 1) * DH] = jnp.where(used, turned, UNUSED).astype(BF16)
             out_ref[:, (2 * i + 1) * DH : (2 * i + 2) * DH] = value[:, there]
-            packed[side, :rows, 2 * half + 2 * i * DH : 2 * half + (2 * i + 1) * DH] = turned.astype(BF16)
-            packed[side, :rows, 2 * half + (2 * i + 1) * DH : 2 * half + (2 * i + 2) * DH] = value[:, there]
-        packed[side, rows:, 2 * half :] = count
-    loads[4].wait()
-    loads[5].wait()
-    gates = split_rows(jnp.where(places < limit, gate[...], 0.0), EXTRA)
-    cosine, sine = cosine * (SCALE * LOG2E), sine * (SCALE * LOG2E)
+            packed[side, :, 2 * i * DH : (2 * i + 1) * DH] = turned.astype(BF16)
+            packed[side, :, (2 * i + 1) * DH : (2 * i + 2) * DH] = value[:, there]
+
+
+def pack_queries_kernel(query, cot, gate, pos, cos_ref, sin_ref, count, kv, packed, *, limit):
+    rows = query.shape[0]
+    half = query.shape[1] // 2
+    gates = split_rows(jnp.where(pos[...] < limit, gate[...], 0.0), EXTRA)
+    cosine, sine = cos_ref[...] * (SCALE * LOG2E), sin_ref[...] * (SCALE * LOG2E)
     for side in range(2):
         for i in range(half // DH):
             there = slice(side * half + i * DH, side * half + (i + 1) * DH)
             turned = rotate(query[:, there].astype(F32), cosine, sine)
             packed[side, :rows, i * DH : (i + 1) * DH] = turned.astype(BF16)
+        packed[side, :rows, half : 2 * half] = cot[:, side * half : (side + 1) * half]
+        packed[side, :rows, 2 * half :] = kv[side]
         packed[side, rows:, :rows] = gates
-    for copy in loads[6:]:
-        copy.wait()
+        packed[side, rows:, 2 * half : 2 * half + 256] = count[...]
 
 
 def chosen(shape, ratio, dim):
@@ -235,9 +234,8 @@
 
 def far_kernel(query, cot, gate, first_tops, raws, grads, tops, sums, crosses, early, *refs, blocks):
     packets = refs[: blocks - 1]
-    far_keys, weights, score_grads, factors, deltas = refs[blocks - 1 : blocks + 4]
-    parts = refs[blocks + 4 : -2]
-    late_keys, late_values = refs[-2:]
+    far_keys, weights, score_grads, late_raws, late_grads = refs[blocks - 1 : blocks + 4]
+    factors, late_factors, deltas, part, late_keys, late_values = refs[blocks + 4 :]
     rows = early.shape[0]
     half_groups, lanes = query.shape[:2]
     alone = lax.axis_index("ctx") < 2
@@ -275,30 +273,36 @@
                 shrink = jnp.exp2(old_top - top)
                 inverse = 1.0 / (sums[i, :, here] * shrink + jnp.sum(raw, axis=0, keepdims=True))
                 prob_grad = dot(late_values[i], cot[i, here, :], NT)
+                late_raws[i, :, here] = raw.astype(late_raws.dtype)
+                late_grads[i, :, here] = prob_grad.astype(late_grads.dtype)
                 cross = crosses[i, :, here] * shrink + jnp.sum(raw * prob_grad, axis=0, keepdims=True)
                 delta = cross * inverse
                 factor = inverse * gate[:, here]
                 factors[i, :, here] = factor * jnp.exp2(first_tops[i, :, here] - top)
+                late_factors[i, :, here] = factor
                 deltas[i, :, here] = delta
-                gated = raw * factor
-                weights[i, rows:, here] = gated.astype(BF16)
-                score_grads[i, rows:, here] = (gated * (prob_grad - delta)).astype(BF16)
                 gated = raws[i, :, here] * (factor * shrink)
-                weights[i, :rows, here] = gated.astype(BF16)
-                score_grads[i, :rows, here] = (gated * (grads[i, :, here] - delta)).astype(BF16)
-            for j, out_ref in enumerate(parts):
-                part_of(weights, score_grads, query, cot, out_ref, i, slice(j * rows, (j + 1) * rows), slice(0, lanes))
-
-
-def far_rest_kernel(weights, score_grads, query, cot, *parts):
-    rows = parts[0].shape[0]
+                weights[i, :, here] = gated.astype(BF16)
+                score_grads[i, :, here] = (gated * (grads[i, :, here] - delta)).astype(BF16)
+            part_of(weights, score_grads, query, cot, part, i, slice(0, rows), slice(0, lanes))
+
+
+def far_rest_kernel(raws, grads, factors, deltas, early_grads, query, cot, score_grads, *refs):
+    parts, weights = refs[:-1], refs[-1]
+    rows = early_grads.shape[1]
     half_groups, lanes = query.shape[:2]
 
     @pl.when(lax.axis_index("ctx") >= 2)
     def _():
-        for j, out_ref in enumerate(parts):
-            there = slice((len(parts) + j) * rows, (len(parts) + j + 1) * rows)
-            for i in range(half_groups):
+        for i in range(half_groups):
+            score_grads[i, :rows, :] = early_grads[i]
+            for here in chunks(0, lanes):
+                gated = raws[i, :, here].astype(F32) * factors[i, :, here]
+                weights[i, rows:, here] = gated.astype(BF16)
+                rest = grads[i, :, here].astype(F32) - deltas[i, :, here]
+                score_grads[i, rows:, here] = (gated * rest).astype(BF16)
+            for j, out_ref in enumerate(parts):
+                there = slice((j + 1) * rows, (j + 2) * rows)
                 part_of(weights, score_grads, query, cot, out_ref, i, there, slice(0, lanes))
 
 
@@ -416,41 +420,49 @@
     index = np.arange(DH) % (DH // 2)
     freq = jnp.asarray((THETA ** (-2.0 * index / DH)).astype(np.float32))[None]
     packet = ((rows, group_width), BF16)
-    packets_shape = ((2, rows + EXTRA, heads_width + group_width), BF16)
     table = ((rows, DH), F32)
-    kv_mine, kv_theirs, packed, cosine, sine = call(
-        functools.partial(pack_kernel, limit=limit),
-        "pack",
-        [packet, packet, packets_shape, table, table],
+    kv_mine, kv_theirs, kv_both, cosine, sine, count = call(
+        functools.partial(pack_keys_kernel, limit=limit),
+        "pack_keys",
+        [packet, packet, ((2, rows, group_width), BF16), table, table, ((EXTRA, 256), BF16)],
         key_rows[0],
         value_rows[0],
+        positions,
+        freq,
+        in_hbm=True,
+        flops=5 * 10**9,
+        scratch=[
+            pltpu.VMEM((rows, group_width), BF16),
+            pltpu.VMEM((rows, group_width), BF16),
+            pltpu.VMEM((1, rows), jnp.int32),
+            pltpu.VMEM((1, DH), F32),
+            pltpu.SemaphoreType.DMA((4,)),
+        ],
+    )
+
+    hop = [[(2 * x + k, 2 * (x + s) + k) for x in range(chips - s) for k in range(2)] for s in range(chips)]
+    cross = [[(a, b + 1 - 2 * (b % 2)) for a, b in pairs] for pairs in hop]
+    back_hop = [[(b, a) for a, b in pairs] for pairs in hop]
+    back_cross = [[(b, a) for a, b in pairs] for pairs in cross]
+
+    far_own = [lax.ppermute(kv_mine, "ctx", hop[s]) for s in range(1, chips)]
+    far_sib = [lax.ppermute(kv_theirs, "ctx", cross[s]) for s in range(1, chips)]
+
+    pairs = [[2 * x, 2 * x + 1] for x in range(chips)]
+    swap = lambda both: lax.all_to_all(both, "ctx", 0, 0, axis_index_groups=pairs)
+    (packed,) = call(
+        functools.partial(pack_queries_kernel, limit=limit),
+        "pack_queries",
+        [((2, rows + EXTRA, heads_width + group_width), BF16)],
         query_rows[0],
         cotangent[0],
         router_gate,
         positions,
-        freq,
-        in_hbm=True,
-        scratch=[
-            pltpu.VMEM((rows, group_width), BF16),
-            pltpu.VMEM((rows, group_width), BF16),
-            pltpu.VMEM((rows, heads_width), BF16),
-            pltpu.VMEM((1, rows), F32),
-            pltpu.VMEM((1, rows), jnp.int32),
-            pltpu.VMEM((1, DH), F32),
-            pltpu.SemaphoreType.DMA((8,)),
-        ],
-    )
-
-    hop = [[(2 * x + k, 2 * (x + s) + k) for x in range(chips - s) for k in range(2)] for s in range(chips)]
-    cross = [[(a, b + 1 - 2 * (b % 2)) for a, b in pairs] for pairs in hop]
-    back_hop = [[(b, a) for a, b in pairs] for pairs in hop]
-    back_cross = [[(b, a) for a, b in pairs] for pairs in cross]
-
-    far_own = [lax.ppermute(kv_mine, "ctx", hop[s]) for s in range(1, chips)]
-    far_sib = [lax.ppermute(kv_theirs, "ctx", cross[s]) for s in range(1, chips)]
-
-    pairs = [[2 * x, 2 * x + 1] for x in range(chips)]
-    swap = lambda both: lax.all_to_all(both, "ctx", 0, 0, axis_index_groups=pairs)
+        cosine,
+        sine,
+        count,
+        kv_both,
+    )
     packets = swap(packed)
 
     row = ((half_groups, 1, 2 * wide), F32)
@@ -466,16 +478,19 @@
     )
 
     blocks = 2 * (chips - 1)
+    table = ((half_groups, rows, 2 * wide), F32)
+    low_table = ((half_groups, rows, 2 * wide), BF16)
+    late = (half_groups, (blocks - 1) * rows, 2 * wide)
+    late_table = (late, F32 if chips == 2 else BF16)
+    late_rows = pltpu.VMEM((half_groups, (blocks - 1) * rows, DH), BF16)
     far_table = ((half_groups, blocks * rows, 2 * wide), BF16)
-    table = ((half_groups, rows, 2 * wide), F32)
-    late = ((half_groups, (blocks - 1) * rows, DH), BF16)
     early_raws, early_grads, early_tops, sums, crosses = call(
         early_kernel, "early_scores", [table, table, row, row, row], query, cot, tops, sums, crosses, far_sib[0]
     )
-    far_keys, weights, far_grads, factors, deltas, *sib_parts = call(
+    far_keys, _, early_low, late_raws, late_grads, factors, late_factors, deltas, early_part = call(
         functools.partial(far_kernel, blocks=blocks),
         "far_scores",
-        [((half_groups, blocks * rows, DH), BF16), far_table, far_table, row, row] + [packet] * (chips - 1),
+        [((half_groups, blocks * rows, DH), BF16), low_table, low_table, late_table, late_table, row, row, row, packet],
         query,
         cot,
         gate_row,
@@ -487,11 +502,24 @@
         crosses,
         *far_sib,
         *far_own,
-        scratch=[pltpu.VMEM(*late), pltpu.VMEM(*late)],
-    )
-    sib_got = [lax.ppermute(sib_parts[s - 1], "ctx", back_cross[s]) for s in range(1, chips)]
-    own_parts = call(far_rest_kernel, "far_rest", [packet] * (chips - 1), weights, far_grads, query, cot)
-    own_got = [lax.ppermute(own_parts[s - 1], "ctx", back_hop[s]) for s in range(1, chips)]
+        scratch=[late_rows, late_rows],
+    )
+    sib_got = [lax.ppermute(early_part, "ctx", back_cross[1])]
+    far_grads, *parts = call(
+        far_rest_kernel,
+        "far_rest",
+        [far_table] + [packet] * (blocks - 1),
+        late_raws,
+        late_grads,
+        late_factors,
+        deltas,
+        early_low,
+        query,
+        cot,
+        scratch=[pltpu.VMEM(*far_table)],
+    )
+    sib_got += [lax.ppermute(parts[s - 2], "ctx", back_cross[s]) for s in range(2, chips)]
+    own_got = [lax.ppermute(parts[chips + s - 3], "ctx", back_hop[s]) for s in range(1, chips)]
 
     part_mine, packed = call(
         functools.partial(near_kernel, ratio=ratio),

time: 29.6 us -> 29.7 us (level)
  Pallas kernels: 7.48 us -> 8.44 us
  waiting for transfers between devices: 2.62 us -> 1.73 us
    pallas_call x8 -> x9, Pallas kernels: 7.48 us -> 8.44 us  [call(): pl.pallas_call(kernel, out_shape=[jax.ShapeDtypeStruct(*out) for out in o...]
    ppermute x2, waiting for transfers between devices: 2.62 us -> 1.72 us  [the longest x1 1.72 us: per_device(): lax.ppermute(parts[chips + s - 3], 'ctx', back_hop[s])]
  transfers between devices with their start and end apart: 4 -> 4, of which waited for: 1 -> 1; matrix products, arithmetic and copies ran while one was open for 0% -> 0% of each run, Pallas kernels for 17% -> 18%
where the time goes in v7:
time: 29.7 us; the launch traced here: 29.4 us
  blocking collectives  9.74 us (33%)
  starting transfers between devices  8.72 us (29%)
  Pallas kernels  8.44 us (28%)
  waiting for transfers between devices  1.73 us (6%)
  between operations  0.77 us (3%)
    all_to_all x2, blocking collectives, per_device(): lax.all_to_all(both, 'ctx', 0, 0, axis_index_groups=pairs)  9.74 us
    pallas_call x9, Pallas kernels, call(): pl.pallas_call(kernel, out_shape=[jax.ShapeDtypeStruct(*out) for out in o...  8.44 us
    ppermute x1, starting transfers between devices, per_device(): lax.ppermute(kv_theirs, 'ctx', cross[s])  4.29 us
    ppermute x1, starting transfers between devices, per_device(): far_own = [lax.ppermute(kv_mine, 'ctx', hop[s]) for s in range(1, chips)]  1.85 us
    ppermute x1, waiting for transfers between devices, per_device(): lax.ppermute(parts[chips + s - 3], 'ctx', back_hop[s])  1.72 us
    ppermute x1, starting transfers between devices, per_device(): lax.ppermute(parts[chips + s - 3], 'ctx', back_hop[s])  1.29 us
    ppermute x1, starting transfers between devices, per_device(): sib_got = [lax.ppermute(early_part, 'ctx', back_cross[1])]  1.28 us
  transfers between devices with their start and end apart: 4, of which 1 were waited for; matrix products, arithmetic and copies ran while one was open for 0% of the time, Pallas kernels for 18%

profile of v7, /device:TPU:0, one launch (start us, length us, event | category | flops | bytes accessed | tf_op | source)
XLA Modules:
  0.0 29.4 jit_solution(1823207761181952103)
XLA Ops:
  0.6 0.0 copy-start
  0.6 0.0 copy-start.1
  0.7 0.0 copy-start.2
  0.7 0.0 copy-start.3
  0.7 1.3 %pack_keys.1 = (bf16[160,512]{1,0:T(8,128)(2,1)S(1)}, bf16[160,512]{1,0:T(8,128)(2,1)S(1)}, bf16[2,160,512]{2,1,0:T(8,128)(2,1)S(1)}, f32[160,128]{1,0:T(8,128)S...) custom-call(bf16[160,512]{1,0:T(8,128)(2,1)} %bitcast.10, bf16[160,512]{1,0:T(8,128)(2,1)} %bitcast.11, ...), custom_call_target="tpu_custom_call" | custom-call | flops 5000000000 | bytes 1000 | tf_op jit(solution)/shard_map/pack_keys/pallas_call | solution.py:410
  2.0 4.3 %collective-permute-start = (bf16[160,512]{1,0:T(8,128)(2,1)S(1)}, bf16[160,512]{1,0:T(8,128)(2,1)S(1)}, u32[]{:S(2)}, u32[]{:S(2)}) collective-permute-start(bf16[160,512]{1,0:T(8,128)(2,1)S(1)} %get-tuple-element.54), channel_id=1, source_target_pairs={{0,3},{1,2},{4,7},{5,6},{8,11},{9,10},{12,15},{13,14},{16,19},{17,... | collective-permute-start | bytes 491528 | tf_op jit(solution)/shard_map/ppermute | solution.py:449
  6.3 1.9 %collective-permute-start.1 = (bf16[160,512]{1,0:T(8,128)(2,1)S(1)}, bf16[160,512]{1,0:T(8,128)(2,1)S(1)}, u32[]{:S(2)}, u32[]{:S(2)}) collective-permute-start(bf16[160,512]{1,0:T(8,128)(2,1)S(1)} %get-tuple-element.60), channel_id=1, source_target_pairs={{0,2},{1,3},{4,6},{5,7},{8,10},{9,11},{12,14},{13,15},{16,18},{17,... | collective-permute-start | bytes 491528 | tf_op jit(solution)/shard_map/ppermute | solution.py:448
  8.2 0.0 copy-done
  8.2 0.0 copy-done.1
  8.2 0.0 copy-done.2
  8.2 0.0 copy-done.3
  8.2 0.5 %pack_queries.1 = bf16[2,176,2560]{2,1,0:T(8,128)(2,1)S(1)} custom-call(bf16[160,2048]{1,0:T(8,128)(2,1)S(1)} %bitcast.7, bf16[160,2048]{1,0:T(8,128)(2,1)S(1)} %bitcast.8, f32[1,160]{1,0:T(1,128)S(1)} %copy-done.3, s32[1,160]{1,0:T(1,128)S(1)} %copy-done.2, f32[160,128]{1,0:T(8,128)S(1)} %get-tuple-element.42.cos_ref, ...), custom_call_target="tpu_custom_call" | custom-call | flops 1000000 | bytes 1000 | tf_op jit(solution)/shard_map/pack_queries/pallas_call | solution.py:410
  8.7 5.2 %all_to_all.10.packets = bf16[2,176,2560]{2,1,0:T(8,128)(2,1)S(1)} all-to-all(bf16[2,176,2560]{2,1,0:T(8,128)(2,1)S(1)} %pack_queries.1), channel_id=1, replica_groups={{0,1},{2,3},{4,5},{6,7},{8,9},{10,11},{12,13},{14,15},{16,17},{18,19},{..., dimensions={0} | all-to-all | bytes 3604480 | tf_op jit(solution)/shard_map/all_to_all | solution.py:452
  13.8 1.8 %local_scores.1 = (bf16[2,320,128]{2,1,0:T(8,128)(2,1)S(1)}, bf16[2,320,128]{2,1,0:T(8,128)(2,1)}, bf16[2,1280,128]{2,1,0:T(8,128)(2,1)S(1)}, bf16[2,1280,128]{2...) custom-call(bf16[2,176,2560]{2,1,0:T(8,128)(2,1)S(1)} %all_to_all.10, ...), custom_call_target="tpu_custom_call" | custom-call | flops 3000000 | bytes 1000 | tf_op jit(solution)/shard_map/local_scores/pallas_call | solution.py:410
  15.7 0.0 collective-permute-done.packet.early
  15.7 0.0 collective-permute-done.1.refs_0_
  15.7 0.9 %far_scores.1 = (bf16[2,320,128]{2,1,0:T(8,128)(2,1)S(1)}, bf16[2,160,1280]{2,1,0:T(8,128)(2,1)}, bf16[2,160,1280]{2,1,0:T(8,128)(2,1)S(1)}, f32[2,160,1280]{2,1...) custom-call(bf16[2,1280,128]{2,1,0:T(8,128)(2,1)S(1)} %get-tuple-ele, ...), custom_call_target="tpu_custom_call" | custom-call | flops 1000000 | bytes 1000 | tf_op jit(solution)/shard_map/far_scores/pallas_call | solution.py:410
  16.6 1.3 %collective-permute-start.2 = (bf16[160,512]{1,0:T(8,128)(2,1)S(1)}, bf16[160,512]{1,0:T(8,128)(2,1)S(1)}, u32[]{:S(2)}, u32[]{:S(2)}) collective-permute-start(bf16[160,512]{1,0:T(8,128)(2,1)S(1)} %get-tuple-element.71), channel_id=1, source_target_pairs={{3,0},{2,1},{7,4},{6,5},{11,8},{10,9},{15,12},{14,13},{19,16},{18,... | collective-permute-start | bytes 491528 | tf_op jit(solution)/shard_map/ppermute | solution.py:507
  17.9 1.3 %collective-permute-start.3 = (bf16[160,512]{1,0:T(8,128)(2,1)S(1)}, bf16[160,512]{1,0:T(8,128)(2,1)S(1)}, u32[]{:S(2)}, u32[]{:S(2)}) collective-permute-start(bf16[160,512]{1,0:T(8,128)(2,1)S(1)} %get-tuple-element.76), channel_id=1, source_target_pairs={{2,0},{3,1},{6,4},{7,5},{10,8},{11,9},{14,12},{15,13},{18,16},{19,... | collective-permute-start | bytes 491528 | tf_op jit(solution)/shard_map/ppermute | solution.py:522
  19.2 1.8 %near_grads.1 = (f32[160,512]{1,0:T(8,128)S(1)}, bf16[2,176,1536]{2,1,0:T(8,128)(2,1)S(1)}) custom-call(f32[2,320,1280]{2,1,0:T(8,128)S(1)} %get-tuple-element.46.raws, f32[2,320,1280]{2,1,0:T(8,128)S(1)} %get-tuple-element.47.grads, f32[2,1,1280]{2,1,0:T(1,128)S(1)} %get-tuple-element.61.factors, f32[2,1,1280]{2,1,0:T(1,128)S(1)} %get-tuple-element.62.deltas, ...), custom_call_target="tpu_custom_call" | custom-call | flops 4000000 | bytes 1000 | tf_op jit(solution)/shard_map/near_grads/pallas_call | solution.py:410
  21.1 4.6 %all_to_all.11.back = bf16[2,176,1536]{2,1,0:T(8,128)(2,1)S(1)} all-to-all(bf16[2,176,1536]{2,1,0:T(8,128)(2,1)S(1)} %get-tuple-element.70), channel_id=1, replica_groups={{0,1},{2,3},{4,5},{6,7},{8,9},{10,11},{12,13},{14,15},{16,17},{18,19},{..., dimensions={0} | all-to-all | bytes 2162688 | tf_op jit(solution)/shard_map/all_to_all | solution.py:452
  25.7 0.0 collective-permute-done.2.refs_0_
  25.7 1.2 %finish_queries.1 = (bf16[160,2048]{1,0:T(8,128)(2,1)}, f32[1,160]{1,0:T(1,128)}, bf16[160,256]{1,0:T(8,128)(2,1)S(1)}, bf16[160,256]{1,0:T(8,128)(2,1)S(1)}) custom-call(bf16[2,176,1536]{2,1,0:T(8,128)(2,1)S(1)} %all_to_all.11.back, s32[1,160]{1,0:T(1,128)S(1)} %copy-done.2, f32[160,128]{1,0:T(8,128)S(1)} %get-tuple-element.42.cos_ref, ...), custom_call_target="tpu_custom_call" | custom-call | flops 300000000 | bytes 1000 | tf_op jit(solution)/shard_map/finish_queries/pallas_call | solution.py:410
  26.9 1.7 %collective-permute-done.3.refs_0_ = bf16[160,512]{1,0:T(8,128)(2,1)S(1)} collective-permute-done((bf16[160,512]{1,0:T(8,128)(2,1)S(1)}, bf16[160,512]{1,0:T(8,128)(2,1)S(1)}, u32[]{:S(2)}, u32[]{:S(2)}) %collective-permute-start.3) | collective-permute-done | bytes 163872 | tf_op jit(solution)/shard_map/ppermute | solution.py:522
  28.6 0.8 %finish_keys.1 = (bf16[160,512]{1,0:T(8,128)(2,1)}, bf16[160,512]{1,0:T(8,128)(2,1)}) custom-call(f32[160,512]{1,0:T(8,128)S(1)} %get-tuple-element.73.part_mine, bf16[160,256]{1,0:T(8,128)(2,1)S(1)} %get-tuple-element.74.key_part, bf16[160,256]{1,0:T(8,128)(2,1)S(1)} %get-tuple-element.75.value_part, f32[160,128]{1,0:T(8,128)S(1)} %get-tuple-element.42.cos_ref, ...), custom_call_target="tpu_custom_call" | custom-call | flops 1000000 | bytes 1000 | tf_op jit(solution)/shard_map/finish_keys/pallas_call | solution.py:410
  (2 shorter events, 0.0 us)
Async XLA Ops:
  0.6 7.5 %copy-start = (bf16[1,160,2048]{2,1,0:T(8,128)(2,1)S(1)}, bf16[1,160,2048]{2,1,0:T(8,128)(2,1)}, u32[]{:S(2)}) copy-start(bf16[1,160,2048]{2,1,0:T(8,128)(2,1)} %param.7) | copy-start | bytes 1966084
  0.6 7.5 %copy-start.1 = (bf16[1,160,2048]{2,1,0:T(8,128)(2,1)S(1)}, bf16[1,160,2048]{2,1,0:T(8,128)(2,1)}, u32[]{:S(2)}) copy-start(bf16[1,160,2048]{2,1,0:T(8,128)(2,1)} %param.10) | copy-start | bytes 1966084
  0.7 7.5 %copy-start.2 = (s32[1,160]{1,0:T(1,128)S(1)}, s32[1,160]{1,0:T(1,128)}, u32[]{:S(2)}) copy-start(s32[1,160]{1,0:T(1,128)} %pos_ref.1) | copy-start | bytes 1924
  0.7 7.5 %copy-start.3 = (f32[1,160]{1,0:T(1,128)S(1)}, f32[1,160]{1,0:T(1,128)}, u32[]{:S(2)}) copy-start(f32[1,160]{1,0:T(1,128)} %gate.1) | copy-start | bytes 1924
  2.0 13.7 %collective-permute-start = (bf16[160,512]{1,0:T(8,128)(2,1)S(1)}, bf16[160,512]{1,0:T(8,128)(2,1)S(1)}, u32[]{:S(2)}, u32[]{:S(2)}) collective-permute-start(bf16[160,512]{1,0:T(8,128)(2,1)S(1)} %get-tuple-element.54), channel_id=1, source_target_pairs={{0,3},{1,2},{4,7},{5,6},{8,11},{9,10},{12,15},{13,14},{16,19},{17,... | collective-permute-start | bytes 491528 | tf_op jit(solution)/shard_map/ppermute | solution.py:449
  6.3 9.4 %collective-permute-start.1 = (bf16[160,512]{1,0:T(8,128)(2,1)S(1)}, bf16[160,512]{1,0:T(8,128)(2,1)S(1)}, u32[]{:S(2)}, u32[]{:S(2)}) collective-permute-start(bf16[160,512]{1,0:T(8,128)(2,1)S(1)} %get-tuple-element.60), channel_id=1, source_target_pairs={{0,2},{1,3},{4,6},{5,7},{8,10},{9,11},{12,14},{13,15},{16,18},{17,... | collective-permute-start | bytes 491528 | tf_op jit(solution)/shard_map/ppermute | solution.py:448
  16.6 9.1 %collective-permute-start.2 = (bf16[160,512]{1,0:T(8,128)(2,1)S(1)}, bf16[160,512]{1,0:T(8,128)(2,1)S(1)}, u32[]{:S(2)}, u32[]{:S(2)}) collective-permute-start(bf16[160,512]{1,0:T(8,128)(2,1)S(1)} %get-tuple-element.71), channel_id=1, source_target_pairs={{3,0},{2,1},{7,4},{6,5},{11,8},{10,9},{15,12},{14,13},{19,16},{18,... | collective-permute-start | bytes 491528 | tf_op jit(solution)/shard_map/ppermute | solution.py:507
  17.9 10.7 %collective-permute-start.3 = (bf16[160,512]{1,0:T(8,128)(2,1)S(1)}, bf16[160,512]{1,0:T(8,128)(2,1)S(1)}, u32[]{:S(2)}, u32[]{:S(2)}) collective-permute-start(bf16[160,512]{1,0:T(8,128)(2,1)S(1)} %get-tuple-element.76), channel_id=1, source_target_pairs={{2,0},{3,1},{6,4},{7,5},{10,8},{11,9},{14,12},{15,13},{18,16},{19,... | collective-permute-start | bytes 491528 | tf_op jit(solution)/shard_map/ppermute | solution.py:522

commit v8 on v7

--- a/solution.py
+++ b/solution.py
@@ -144,7 +144,7 @@
     return [slice(at, min(at + 256, high)) for at in range(low, high, 256)]
 
 
-def local_kernel(packets, keys, values, query, cot, gate, raws, grads, tops, sums, crosses, *, ratio):
+def local_kernel(packets, keys, query, cot, gate, raws, grads, tops, sums, crosses, values, *, ratio):
     rows = packets.shape[1] - EXTRA
     half_groups = keys.shape[0]
     wide = ratio * rows
@@ -234,8 +234,8 @@
 
 def far_kernel(query, cot, gate, first_tops, raws, grads, tops, sums, crosses, early, *refs, blocks):
     packets = refs[: blocks - 1]
-    far_keys, weights, score_grads, late_raws, late_grads = refs[blocks - 1 : blocks + 4]
-    factors, late_factors, deltas, part, late_keys, late_values = refs[blocks + 4 :]
+    far_keys, score_grads, late_raws, late_grads, factors, late_factors, deltas, part = refs[blocks - 1 : -3]
+    late_keys, late_values, weights = refs[-3:]
     rows = early.shape[0]
     half_groups, lanes = query.shape[:2]
     alone = lax.axis_index("ctx") < 2
@@ -469,11 +469,12 @@
     table = ((half_groups, 2 * rows, 2 * wide), F32)
     kv_table = ((half_groups, 2 * rows, DH), BF16)
     q_table = ((half_groups, 2 * wide, DH), BF16)
-    keys, values, query, cot, gate_row, raws, grads, tops, sums, crosses = call(
+    keys, query, cot, gate_row, raws, grads, tops, sums, crosses = call(
         functools.partial(local_kernel, ratio=ratio),
         "local_scores",
-        [kv_table, kv_table, q_table, q_table, ((1, 2 * wide), F32), table, table, row, row, row],
+        [kv_table, q_table, q_table, ((1, 2 * wide), F32), table, table, row, row, row],
         packets,
+        scratch=[pltpu.VMEM(*kv_table)],
         flops=3 * 10**6,
     )
 
@@ -487,10 +488,10 @@
     early_raws, early_grads, early_tops, sums, crosses = call(
         early_kernel, "early_scores", [table, table, row, row, row], query, cot, tops, sums, crosses, far_sib[0]
     )
-    far_keys, _, early_low, late_raws, late_grads, factors, late_factors, deltas, early_part = call(
+    far_keys, early_low, late_raws, late_grads, factors, late_factors, deltas, early_part = call(
         functools.partial(far_kernel, blocks=blocks),
         "far_scores",
-        [((half_groups, blocks * rows, DH), BF16), low_table, low_table, late_table, late_table, row, row, row, packet],
+        [((half_groups, blocks * rows, DH), BF16), low_table, late_table, late_table, row, row, row, packet],
         query,
         cot,
         gate_row,
@@ -502,7 +503,7 @@
         crosses,
         *far_sib,
         *far_own,
-        scratch=[late_rows, late_rows],
+        scratch=[late_rows, late_rows, pltpu.VMEM(*low_table)],
     )
     sib_got = [lax.ppermute(early_part, "ctx", back_cross[1])]
     far_grads, *parts = call(

time: 29.7 us -> 28.8 us (0.970)
  Pallas kernels: 8.44 us -> 7.09 us
  waiting for transfers between devices: 1.73 us -> 2.11 us
    pallas_call x9, Pallas kernels: 8.44 us -> 7.09 us  [call(): pl.pallas_call(kernel, out_shape=[jax.ShapeDtypeStruct(*out) for out in o...]
    ppermute x1, waiting for transfers between devices: 1.72 us -> 2.1 us  [per_device(): lax.ppermute(parts[chips + s - 3], 'ctx', back_hop[s])]
  transfers between devices with their start and end apart: 4 -> 4, of which waited for: 1 -> 1; matrix products, arithmetic and copies ran while one was open for 0% -> 0% of each run, Pallas kernels for 18% -> 17%
where the time goes in v8:
time: 28.8 us; the launch traced here: 28.5 us
  blocking collectives  9.74 us (34%)
  starting transfers between devices  8.73 us (30%)
  Pallas kernels  7.09 us (25%)
  waiting for transfers between devices  2.11 us (7%)
  between operations  0.78 us (3%)
    all_to_all x2, blocking collectives, per_device(): lax.all_to_all(both, 'ctx', 0, 0, axis_index_groups=pairs)  9.74 us
    pallas_call x9, Pallas kernels, call(): pl.pallas_call(kernel, out_shape=[jax.ShapeDtypeStruct(*out) for out in o...  7.09 us
    ppermute x1, starting transfers between devices, per_device(): lax.ppermute(kv_theirs, 'ctx', cross[s])  4.29 us
    ppermute x1, waiting for transfers between devices, per_device(): lax.ppermute(parts[chips + s - 3], 'ctx', back_hop[s])  2.1 us
    ppermute x1, starting transfers between devices, per_device(): far_own = [lax.ppermute(kv_mine, 'ctx', hop[s]) for s in range(1, chips)]  1.85 us
    ppermute x1, starting transfers between devices, per_device(): sib_got = [lax.ppermute(early_part, 'ctx', back_cross[1])]  1.29 us
    ppermute x1, starting transfers between devices, per_device(): lax.ppermute(parts[chips + s - 3], 'ctx', back_hop[s])  1.29 us
  transfers between devices with their start and end apart: 4, of which 1 were waited for; matrix products, arithmetic and copies ran while one was open for 0% of the time, Pallas kernels for 17%

profile of v8, /device:TPU:0, one launch (start us, length us, event | category | flops | bytes accessed | tf_op | source)
XLA Modules:
  0.0 28.5 jit_solution(9087842020758405308)
XLA Ops:
  0.6 0.0 copy-start
  0.6 0.0 copy-start.1
  0.7 0.0 copy-start.2
  0.7 0.0 copy-start.3
  0.7 1.3 %pack_keys.1 = (bf16[160,512]{1,0:T(8,128)(2,1)S(1)}, bf16[160,512]{1,0:T(8,128)(2,1)S(1)}, bf16[2,160,512]{2,1,0:T(8,128)(2,1)S(1)}, f32[160,128]{1,0:T(8,128)S...) custom-call(bf16[160,512]{1,0:T(8,128)(2,1)} %bitcast.10, bf16[160,512]{1,0:T(8,128)(2,1)} %bitcast.11, ...), custom_call_target="tpu_custom_call" | custom-call | flops 5000000000 | bytes 1000 | tf_op jit(solution)/shard_map/pack_keys/pallas_call | solution.py:410
  2.0 4.3 %collective-permute-start = (bf16[160,512]{1,0:T(8,128)(2,1)S(1)}, bf16[160,512]{1,0:T(8,128)(2,1)S(1)}, u32[]{:S(2)}, u32[]{:S(2)}) collective-permute-start(bf16[160,512]{1,0:T(8,128)(2,1)S(1)} %get-tuple-element.54), channel_id=1, source_target_pairs={{0,3},{1,2},{4,7},{5,6},{8,11},{9,10},{12,15},{13,14},{16,19},{17,... | collective-permute-start | bytes 491528 | tf_op jit(solution)/shard_map/ppermute | solution.py:449
  6.3 1.9 %collective-permute-start.1 = (bf16[160,512]{1,0:T(8,128)(2,1)S(1)}, bf16[160,512]{1,0:T(8,128)(2,1)S(1)}, u32[]{:S(2)}, u32[]{:S(2)}) collective-permute-start(bf16[160,512]{1,0:T(8,128)(2,1)S(1)} %get-tuple-element.60), channel_id=1, source_target_pairs={{0,2},{1,3},{4,6},{5,7},{8,10},{9,11},{12,14},{13,15},{16,18},{17,... | collective-permute-start | bytes 491528 | tf_op jit(solution)/shard_map/ppermute | solution.py:448
  8.2 0.0 copy-done
  8.2 0.0 copy-done.1
  8.2 0.0 copy-done.2
  8.2 0.0 copy-done.3
  8.2 0.5 %pack_queries.1 = bf16[2,176,2560]{2,1,0:T(8,128)(2,1)S(1)} custom-call(bf16[160,2048]{1,0:T(8,128)(2,1)S(1)} %bitcast.7, bf16[160,2048]{1,0:T(8,128)(2,1)S(1)} %bitcast.8, f32[1,160]{1,0:T(1,128)S(1)} %copy-done.3, s32[1,160]{1,0:T(1,128)S(1)} %copy-done.2, f32[160,128]{1,0:T(8,128)S(1)} %get-tuple-element.42.cos_ref, ...), custom_call_target="tpu_custom_call" | custom-call | flops 1000000 | bytes 1000 | tf_op jit(solution)/shard_map/pack_queries/pallas_call | solution.py:410
  8.7 5.2 %all_to_all.10.packets = bf16[2,176,2560]{2,1,0:T(8,128)(2,1)S(1)} all-to-all(bf16[2,176,2560]{2,1,0:T(8,128)(2,1)S(1)} %pack_queries.1), channel_id=1, replica_groups={{0,1},{2,3},{4,5},{6,7},{8,9},{10,11},{12,13},{14,15},{16,17},{18,19},{..., dimensions={0} | all-to-all | bytes 3604480 | tf_op jit(solution)/shard_map/all_to_all | solution.py:452
  13.8 1.4 %local_scores.1 = (bf16[2,320,128]{2,1,0:T(8,128)(2,1)S(1)}, bf16[2,1280,128]{2,1,0:T(8,128)(2,1)S(1)}, bf16[2,1280,128]{2,1,0:T(8,128)(2,1)S(1)}, f32[1,1280]{1...) custom-call(bf16[2,176,2560]{2,1,0:T(8,128)(2,1)S(1)} %all_to_all.10, ...), custom_call_target="tpu_custom_call" | custom-call | flops 3000000 | bytes 1000 | tf_op jit(solution)/shard_map/local_scores/pallas_call | solution.py:410
  15.2 0.0 collective-permute-done.packet.early
  15.2 0.0 collective-permute-done.1.refs_0_
  15.3 1.3 %collective-permute-start.2 = (bf16[160,512]{1,0:T(8,128)(2,1)S(1)}, bf16[160,512]{1,0:T(8,128)(2,1)S(1)}, u32[]{:S(2)}, u32[]{:S(2)}) collective-permute-start(bf16[160,512]{1,0:T(8,128)(2,1)S(1)} %get-tuple-element.71), channel_id=1, source_target_pairs={{3,0},{2,1},{7,4},{6,5},{11,8},{10,9},{15,12},{14,13},{19,16},{18,... | collective-permute-start | bytes 491528 | tf_op jit(solution)/shard_map/ppermute | solution.py:508
  16.6 1.3 %collective-permute-start.3 = (bf16[160,512]{1,0:T(8,128)(2,1)S(1)}, bf16[160,512]{1,0:T(8,128)(2,1)S(1)}, u32[]{:S(2)}, u32[]{:S(2)}) collective-permute-start(bf16[160,512]{1,0:T(8,128)(2,1)S(1)} %get-tuple-element.76), channel_id=1, source_target_pairs={{2,0},{3,1},{6,4},{7,5},{10,8},{11,9},{14,12},{15,13},{18,16},{19,... | collective-permute-start | bytes 491528 | tf_op jit(solution)/shard_map/ppermute | solution.py:523
  17.9 1.8 %near_grads.1 = (f32[160,512]{1,0:T(8,128)S(1)}, bf16[2,176,1536]{2,1,0:T(8,128)(2,1)S(1)}) custom-call(f32[2,320,1280]{2,1,0:T(8,128)S(1)} %get-tuple-element.46.raws, f32[2,320,1280]{2,1,0:T(8,128)S(1)} %get-tuple-element.47.grads, f32[2,1,1280]{2,1,0:T(1,128)S(1)} %get-tuple-element.61.factors, f32[2,1,1280]{2,1,0:T(1,128)S(1)} %get-tuple-element.62.deltas, ...), custom_call_target="tpu_custom_call" | custom-call | flops 4000000 | bytes 1000 | tf_op jit(solution)/shard_map/near_grads/pallas_call | solution.py:410
  19.8 4.6 %all_to_all.11.back = bf16[2,176,1536]{2,1,0:T(8,128)(2,1)S(1)} all-to-all(bf16[2,176,1536]{2,1,0:T(8,128)(2,1)S(1)} %get-tuple-element.70), channel_id=1, replica_groups={{0,1},{2,3},{4,5},{6,7},{8,9},{10,11},{12,13},{14,15},{16,17},{18,19},{..., dimensions={0} | all-to-all | bytes 2162688 | tf_op jit(solution)/shard_map/all_to_all | solution.py:452
  24.4 0.0 collective-permute-done.2.refs_0_
  24.4 1.2 %finish_queries.1 = (bf16[160,2048]{1,0:T(8,128)(2,1)}, f32[1,160]{1,0:T(1,128)}, bf16[160,256]{1,0:T(8,128)(2,1)S(1)}, bf16[160,256]{1,0:T(8,128)(2,1)S(1)}) custom-call(bf16[2,176,1536]{2,1,0:T(8,128)(2,1)S(1)} %all_to_all.11.back, s32[1,160]{1,0:T(1,128)S(1)} %copy-done.2, f32[160,128]{1,0:T(8,128)S(1)} %get-tuple-element.42.cos_ref, ...), custom_call_target="tpu_custom_call" | custom-call | flops 300000000 | bytes 1000 | tf_op jit(solution)/shard_map/finish_queries/pallas_call | solution.py:410
  25.6 2.1 %collective-permute-done.3.refs_0_ = bf16[160,512]{1,0:T(8,128)(2,1)S(1)} collective-permute-done((bf16[160,512]{1,0:T(8,128)(2,1)S(1)}, bf16[160,512]{1,0:T(8,128)(2,1)S(1)}, u32[]{:S(2)}, u32[]{:S(2)}) %collective-permute-start.3) | collective-permute-done | bytes 163872 | tf_op jit(solution)/shard_map/ppermute | solution.py:523
  27.7 0.8 %finish_keys.1 = (bf16[160,512]{1,0:T(8,128)(2,1)}, bf16[160,512]{1,0:T(8,128)(2,1)}) custom-call(f32[160,512]{1,0:T(8,128)S(1)} %get-tuple-element.73.part_mine, bf16[160,256]{1,0:T(8,128)(2,1)S(1)} %get-tuple-element.74.key_part, bf16[160,256]{1,0:T(8,128)(2,1)S(1)} %get-tuple-element.75.value_part, f32[160,128]{1,0:T(8,128)S(1)} %get-tuple-element.42.cos_ref, ...), custom_call_target="tpu_custom_call" | custom-call | flops 1000000 | bytes 1000 | tf_op jit(solution)/shard_map/finish_keys/pallas_call | solution.py:410
  (3 shorter events, 0.1 us)
Async XLA Ops:
  0.6 7.5 %copy-start = (bf16[1,160,2048]{2,1,0:T(8,128)(2,1)S(1)}, bf16[1,160,2048]{2,1,0:T(8,128)(2,1)}, u32[]{:S(2)}) copy-start(bf16[1,160,2048]{2,1,0:T(8,128)(2,1)} %param.7) | copy-start | bytes 1966084
  0.6 7.5 %copy-start.1 = (bf16[1,160,2048]{2,1,0:T(8,128)(2,1)S(1)}, bf16[1,160,2048]{2,1,0:T(8,128)(2,1)}, u32[]{:S(2)}) copy-start(bf16[1,160,2048]{2,1,0:T(8,128)(2,1)} %param.10) | copy-start | bytes 1966084
  0.7 7.5 %copy-start.2 = (s32[1,160]{1,0:T(1,128)S(1)}, s32[1,160]{1,0:T(1,128)}, u32[]{:S(2)}) copy-start(s32[1,160]{1,0:T(1,128)} %pos_ref.1) | copy-start | bytes 1924
  0.7 7.5 %copy-start.3 = (f32[1,160]{1,0:T(1,128)S(1)}, f32[1,160]{1,0:T(1,128)}, u32[]{:S(2)}) copy-start(f32[1,160]{1,0:T(1,128)} %gate.1) | copy-start | bytes 1924
  2.0 13.2 %collective-permute-start = (bf16[160,512]{1,0:T(8,128)(2,1)S(1)}, bf16[160,512]{1,0:T(8,128)(2,1)S(1)}, u32[]{:S(2)}, u32[]{:S(2)}) collective-permute-start(bf16[160,512]{1,0:T(8,128)(2,1)S(1)} %get-tuple-element.54), channel_id=1, source_target_pairs={{0,3},{1,2},{4,7},{5,6},{8,11},{9,10},{12,15},{13,14},{16,19},{17,... | collective-permute-start | bytes 491528 | tf_op jit(solution)/shard_map/ppermute | solution.py:449
  6.3 8.9 %collective-permute-start.1 = (bf16[160,512]{1,0:T(8,128)(2,1)S(1)}, bf16[160,512]{1,0:T(8,128)(2,1)S(1)}, u32[]{:S(2)}, u32[]{:S(2)}) collective-permute-start(bf16[160,512]{1,0:T(8,128)(2,1)S(1)} %get-tuple-element.60), channel_id=1, source_target_pairs={{0,2},{1,3},{4,6},{5,7},{8,10},{9,11},{12,14},{13,15},{16,18},{17,... | collective-permute-start | bytes 491528 | tf_op jit(solution)/shard_map/ppermute | solution.py:448
  15.3 9.1 %collective-permute-start.2 = (bf16[160,512]{1,0:T(8,128)(2,1)S(1)}, bf16[160,512]{1,0:T(8,128)(2,1)S(1)}, u32[]{:S(2)}, u32[]{:S(2)}) collective-permute-start(bf16[160,512]{1,0:T(8,128)(2,1)S(1)} %get-tuple-element.71), channel_id=1, source_target_pairs={{3,0},{2,1},{7,4},{6,5},{11,8},{10,9},{15,12},{14,13},{19,16},{18,... | collective-permute-start | bytes 491528 | tf_op jit(solution)/shard_map/ppermute | solution.py:508
  16.6 11.1 %collective-permute-start.3 = (bf16[160,512]{1,0:T(8,128)(2,1)S(1)}, bf16[160,512]{1,0:T(8,128)(2,1)S(1)}, u32[]{:S(2)}, u32[]{:S(2)}) collective-permute-start(bf16[160,512]{1,0:T(8,128)(2,1)S(1)} %get-tuple-element.76), channel_id=1, source_target_pairs={{2,0},{3,1},{6,4},{7,5},{10,8},{11,9},{14,12},{15,13},{18,16},{19,... | collective-permute-start | bytes 491528 | tf_op jit(solution)/shard_map/ppermute | solution.py:523

commit v9 on v4

v9 whole, which is shorter than its diff:
```python
import functools
import math

import jax
import jax.numpy as jnp
import numpy as np
from jax import lax
from jax.experimental import pallas as pl
from jax.experimental.pallas import tpu as pltpu
from jax.sharding import PartitionSpec as P

DH = 128
LOCAL = 1024
THETA = 500000.0
EXTRA = 16
HIDDEN = -1e30
UNUSED = 2.0**14
SCALE = DH**-0.5
LOG2E = math.log2(math.e)
LN2 = math.log(2.0)

NT = (((1,), (1,)), ((), ()))
NN = (((1,), (0,)), ((), ()))
TN = (((0,), (0,)), ((), ()))
F32 = jnp.float32
BF16 = jnp.bfloat16


def few_bits(value, bits):
    unit = 2.0 ** (math.floor(math.log2(value)) + 1 - bits)
    return math.floor(value / unit) * unit


QUARTER_1 = few_bits(math.pi / 2, 10)
QUARTER_2 = few_bits(math.pi / 2 - QUARTER_1, 10)
QUARTER_3 = math.pi / 2 - QUARTER_1 - QUARTER_2


def dot(a, b, dims):
    return lax.dot_general(a, b, dims, preferred_element_type=F32)


def core_of():
    return lax.rem(lax.axis_index("ctx"), 2)


def rotate(values, cosine, sine):
    return values * cosine + pltpu.roll(values, DH // 2, 1) * sine


def sine_cosine(angle):
    turns = jnp.floor(angle * (2.0 / math.pi) + 0.5)
    rest = ((angle - turns * QUARTER_1) - turns * QUARTER_2) - turns * QUARTER_3
    square = rest * rest
    sine = ((-1.9515295891e-4 * square + 8.3321608736e-3) * square - 1.6666654611e-1) * square * rest + rest
    cosine = (2.443315711809948e-5 * square - 1.388731625493765e-3) * square + 4.166664568298827e-2
    cosine = cosine * square * square - 0.5 * square + 1.0
    quarter = turns.astype(jnp.int32)
    odd = (quarter & 1) == 1
    first, second = jnp.where(odd, cosine, sine), jnp.where(odd, sine, cosine)
    return (
        jnp.where((quarter & 2) == 2, -first, first),
        jnp.where(((quarter + 1) & 2) == 2, -second, second),
    )


def split_rows(row, height):
    high = row.astype(BF16).astype(F32)
    middle = (row - high).astype(BF16).astype(F32)
    low = row - high - middle
    line = lax.broadcasted_iota(jnp.int32, (height, row.shape[1]), 0)
    rows = jnp.where(line == 0, high, jnp.where(line == 1, middle, jnp.where(line == 2, low, 0.0)))
    return rows.astype(BF16)


def joined_row(rows):
    return jnp.sum(rows.astype(F32), axis=0, keepdims=True)


def pack_keys_kernel(
    key_in, value_in, pos_in, freq_in, key_mine, key_theirs, value_mine, value_theirs, cos_ref, sin_ref,
    key, value, pos, freq, sems, *, limit
):
    loads = [(pos_in, pos), (freq_in, freq), (key_in, key), (value_in, value)]
    loads = [pltpu.make_async_copy(source, target, sems.at[i]) for i, (source, target) in enumerate(loads)]
    for copy in loads:
        copy.start()
    rows, width = key.shape
    half = width // 2
    core = core_of()
    down = lax.broadcasted_iota(jnp.int32, (rows, rows), 0)
    along = lax.broadcasted_iota(jnp.int32, (rows, rows), 1)
    lane = lax.broadcasted_iota(jnp.int32, (rows, DH), 1)
    loads[0].wait()
    loads[1].wait()
    column = jnp.sum(jnp.where(down == along, pos[...].astype(F32), 0.0), axis=1, keepdims=True)
    sine, cosine = sine_cosine(column * freq[...])
    sine = jnp.where(lane < DH // 2, -sine, sine)
    cos_ref[...] = cosine
    sin_ref[...] = sine
    used = jnp.broadcast_to(column, (rows, DH)) < limit
    loads[2].wait()
    loads[3].wait()
    for key_out, value_out, side in ((key_mine, value_mine, core), (key_theirs, value_theirs, 1 - core)):
        for i in range(half // DH):
            there = pl.ds(pl.multiple_of(side * half + i * DH, DH), DH)
            turned = rotate(key[:, there].astype(F32), cosine, sine)
            key_out[:, i * DH : (i + 1) * DH] = jnp.where(used, turned, UNUSED).astype(BF16)
            value_out[:, i * DH : (i + 1) * DH] = value[:, there]


def pack_queries_kernel(query, cot, gate, pos, cos_ref, sin_ref, key, value, mine, theirs, gate_mine, *, limit):
    rows = query.shape[0]
    half, width = query.shape[1] // 2, key.shape[1]
    core = core_of()
    used_gate = jnp.where(pos[...] < limit, gate[...], 0.0)
    gate_mine[...] = used_gate
    theirs[rows:, :rows] = split_rows(used_gate, EXTRA)
    theirs[:rows, 2 * half : 2 * half + width] = key[...]
    theirs[:rows, 2 * half + width :] = value[...]
    cosine, sine = cos_ref[...] * (SCALE * LOG2E), sin_ref[...] * (SCALE * LOG2E)
    for out_ref, side in ((mine, core), (theirs, 1 - core)):
        for i in range(half // DH):
            there = pl.ds(pl.multiple_of(side * half + i * DH, DH), DH)
            turned = rotate(query[:, there].astype(F32), cosine, sine)
            out_ref[:rows, i * DH : (i + 1) * DH] = turned.astype(BF16)
        out_ref[:rows, half : 2 * half] = cot[:, pl.ds(pl.multiple_of(side * half, DH), half)]


def chosen(shape, ratio, dim):
    down = lax.broadcasted_iota(jnp.int32, shape, 0)
    along = lax.broadcasted_iota(jnp.int32, shape, 1)
    rows = shape[1 - dim]
    long, short = (down, along) if dim == 0 else (along, down)
    for _ in range(1, ratio):
        long = jnp.where(long >= rows, long - rows, long)
    return jnp.where(long == short, 1.0, 0.0).astype(BF16)


def chunks(low, high):
    return [slice(at, min(at + 256, high)) for at in range(low, high, 256)]


def used_slots(key, here):
    chip = lax.div(lax.axis_index("ctx"), 2)
    first = key[:, :DH].astype(F32)[:, :1]
    return jnp.broadcast_to(first, (key.shape[0], 256)) < jnp.where(chip >= here, UNUSED / 2, -UNUSED)


def local_kernel(
    key_mine, value_mine, mine, gate_mine, sib, keys, query, cot, gate, raws, grads, tops, sums, crosses, values,
    *, ratio
):
    rows = key_mine.shape[0]
    half_groups = keys.shape[0]
    wide = ratio * rows
    half = half_groups * ratio * DH
    core = core_of()
    spread = chosen((rows, wide), ratio, 1)
    key_sib = sib.at[:rows, 2 * half : 2 * half + half_groups * DH]
    value_sib = sib.at[:rows, 2 * half + half_groups * DH :]
    for key, value, packet, side in ((key_mine, value_mine, mine, core), (key_sib, value_sib, sib, 1 - core)):
        there = pl.ds(pl.multiple_of(side * rows, 16), rows)
        for i in range(half_groups):
            keys[i, there, :] = key[:, i * DH : (i + 1) * DH]
            values[i, there, :] = value[:, i * DH : (i + 1) * DH]
            for h in range(ratio):
                to = pl.ds(pl.multiple_of(side * wide + h * rows, 16), rows)
                at = (i * ratio + h) * DH
                query[i, to, :] = packet[:rows, at : at + DH]
                cot[i, to, :] = packet[:rows, half + at : half + at + DH]
    own = joined_row(dot(split_rows(gate_mine[...], EXTRA), spread, NN))
    other = joined_row(dot(sib[rows:, :rows], spread, NN))
    gate[:, :wide] = jnp.where(core == 0, own, other)
    gate[:, wide:] = jnp.where(core == 0, other, own)
    used = used_slots(keys[0, :rows, :], 0)
    for i in range(half_groups):
        for block in range(2):
            reach = (block + 1) * rows
            for here in chunks(block * wide, (block + 1) * wide):
                width = here.stop - here.start
                scores = dot(keys[i, :reach, :], query[i, here, :], NT)
                slot = lax.broadcasted_iota(jnp.int32, (rows, width), 0)
                lane = lax.broadcasted_iota(jnp.int32, (rows, width), 1) + (here.start - block * wide)
                for h in range(1, ratio):
                    lane = jnp.where(lane >= rows, lane - rows, lane)
                shown = jnp.where(slot <= lane, scores[block * rows :], HIDDEN)
                if block:
                    before = jnp.where(used[:, :width], scores[:rows], HIDDEN)
                    shown = jnp.concatenate([before, shown], axis=0)
                top = jnp.max(shown, axis=0, keepdims=True)
                raw = jnp.exp2(shown - top)
                prob_grad = dot(values[i, :reach, :], cot[i, here, :], NT)
                raws[i, :reach, here] = raw
                grads[i, :reach, here] = prob_grad
                tops[i, :, here] = top
                sums[i, :, here] = jnp.sum(raw, axis=0, keepdims=True)
                crosses[i, :, here] = jnp.sum(raw * prob_grad, axis=0, keepdims=True)


def part_of(weights, score_grads, query, cot, out_ref, i, there, lanes):
    key_part = dot(score_grads[i, there, lanes], query[i, lanes, :], NN) * LN2
    value_part = dot(weights[i, there, lanes], cot[i, lanes, :], NN)
    out_ref[:, 2 * i * DH : (2 * i + 1) * DH] = key_part.astype(out_ref.dtype)
    out_ref[:, (2 * i + 1) * DH : (2 * i + 2) * DH] = value_part.astype(out_ref.dtype)


def far_keys_kernel(query, cot, gate, tops, sums, *refs, blocks):
    packets = refs[:blocks]
    far_keys, raws, factors, far_factors, shrinks, inverses = refs[blocks : blocks + 6]
    parts, weights = refs[blocks + 6 : -1], refs[-1]
    rows = packets[0].shape[0]
    half_groups, lanes = query.shape[:2]
    alone = lax.axis_index("ctx") < 2

    @pl.when(alone)
    def _():
        for i in range(half_groups):
            inverse = 1.0 / sums[i]
            factors[i] = inverse * gate[...]
            inverses[i] = inverse

    @pl.when(jnp.logical_not(alone))
    def _():
        for i in range(half_groups):
            for j, packet in enumerate(packets):
                far_keys[i, j * rows : (j + 1) * rows, :] = packet[:, i * DH : (i + 1) * DH]
        used = [used_slots(packet, j % (blocks // 2) + 1) for j, packet in enumerate(packets)]
        for i in range(half_groups):
            for here in chunks(0, lanes):
                width = here.stop - here.start
                scores = dot(far_keys[i], query[i, here, :], NT)
                shown = [
                    jnp.where(used[j][:, :width], scores[j * rows : (j + 1) * rows], HIDDEN) for j in range(blocks)
                ]
                shown = jnp.concatenate(shown, axis=0)
                old_top = tops[i, :, here]
                top = jnp.maximum(old_top, jnp.max(shown, axis=0, keepdims=True))
                raw = jnp.exp2(shown - top)
                shrink = jnp.exp2(old_top - top)
                inverse = 1.0 / (sums[i, :, here] * shrink + jnp.sum(raw, axis=0, keepdims=True))
                factor = inverse * gate[:, here]
                factors[i, :, here] = factor * shrink
                far_factors[i, :, here] = factor
                shrinks[i, :, here] = shrink
                inverses[i, :, here] = inverse
                raws[i, :, here] = raw.astype(raws.dtype)
                weights[i, :, here] = (raw * factor).astype(BF16)
            for j, out_ref in enumerate(parts):
                there = slice(j * rows, (j + 1) * rows)
                out_ref[:, i * DH : (i + 1) * DH] = dot(weights[i, there, :], cot[i], NN).astype(BF16)


def far_values_kernel(query, cot, raws, far_factors, shrinks, inverses, crosses, *refs, blocks):
    packets = refs[:blocks]
    score_grads, deltas = refs[blocks : blocks + 2]
    parts, far_values = refs[blocks + 2 : -1], refs[-1]
    rows = packets[0].shape[0]
    half_groups, lanes = query.shape[:2]
    alone = lax.axis_index("ctx") < 2

    @pl.when(alone)
    def _():
        for i in range(half_groups):
            deltas[i] = crosses[i] * inverses[i]

    @pl.when(jnp.logical_not(alone))
    def _():
        for i in range(half_groups):
            for j, packet in enumerate(packets):
                far_values[i, j * rows : (j + 1) * rows, :] = packet[:, i * DH : (i + 1) * DH]
        for i in range(half_groups):
            for here in chunks(0, lanes):
                raw = raws[i, :, here].astype(F32)
                prob_grad = dot(far_values[i], cot[i, here, :], NT)
                cross = jnp.sum(raw * prob_grad, axis=0, keepdims=True)
                delta = (crosses[i, :, here] * shrinks[i, :, here] + cross) * inverses[i, :, here]
                deltas[i, :, here] = delta
                score_grad = raw * far_factors[i, :, here] * (prob_grad - delta)
                score_grads[i, :, here] = score_grad.astype(BF16)
            for j, out_ref in enumerate(parts):
                there = slice(j * rows, (j + 1) * rows)
                part = dot(score_grads[i, there, :], query[i], NN) * LN2
                out_ref[:, i * DH : (i + 1) * DH] = part.astype(BF16)


def near_kernel(
    raws, grads, factors, deltas, keys, query, cot, far_keys, far_grads,
    part_mine, out_ref, weights, score_grads, parts, acc,
    *, ratio
):
    rows = part_mine.shape[0]
    half_groups = keys.shape[0]
    wide = ratio * rows
    half = half_groups * ratio * DH
    for i in range(half_groups):
        for block in range(2):
            reach = (block + 1) * rows
            for here in chunks(block * wide, (block + 1) * wide):
                gated = raws[i, :reach, here] * factors[i, :, here]
                weights[i, :reach, here] = gated.astype(BF16)
                score_grads[i, :reach, here] = (gated * (grads[i, :reach, here] - deltas[i, :, here])).astype(BF16)
        for block in range(2):
            there, lanes = slice(block * rows, (block + 1) * rows), slice(block * wide, 2 * wide)
            part_of(weights, score_grads, query, cot, parts.at[block], i, there, lanes)
            reach, lanes = (block + 1) * rows, slice(block * wide, (block + 1) * wide)
            acc[i, :, lanes] = dot(keys[i, :reach, :], score_grads[i, :reach, lanes], TN)

    @pl.when(lax.axis_index("ctx") >= 2)
    def _():
        for i in range(half_groups):
            acc[i] += dot(far_keys[i], far_grads[i], TN)

    for i in range(half_groups):
        total = jnp.transpose(acc[i] * SCALE).astype(BF16)
        for block in range(2):
            for h in range(ratio):
                at = (i * ratio + h) * DH
                low = block * wide + h * rows
                out_ref[block, :rows, at : at + DH] = total[low : low + rows]
    part_mine[...] = parts[core_of()]
    for block in range(2):
        out_ref[block, :rows, half:] = parts[block].astype(BF16)
    summed = deltas[0]
    for i in range(1, half_groups):
        summed = summed + deltas[i]
    for block in range(2):
        own = split_rows(summed[:, block * wide : (block + 1) * wide], 16)
        own = joined_row(dot(own, chosen((wide, rows), ratio, 0), NN))
        out_ref[block, rows:, :rows] = split_rows(own, EXTRA)


def sum_values_kernel(back, part_mine, *refs):
    got, (own, other) = refs[:-2], refs[-2:]
    rows, half = own.shape
    start = back.shape[2] - 2 * half
    core = core_of()
    for i in range(half // DH):
        here = slice(i * DH, (i + 1) * DH)
        there = (2 * i + 1) * DH
        mine = part_mine[:, there : there + DH]
        theirs = back[1 - core, :rows, start + there : start + there + DH].astype(F32)
        for s in range(len(got) // 2):
            theirs = theirs + got[2 * s][:, here].astype(F32)
            mine = mine + got[2 * s + 1][:, here].astype(F32)
        own[:, here] = mine.astype(BF16)
        other[:, here] = theirs.astype(BF16)


def finish_kernel(back, part_mine, pos_ref, cos_ref, sin_ref, value_own, value_other, *refs, limit):
    got, (query_grad, key_grad, value_grad, gate_grad) = refs[:-4], refs[-4:]
    rows, half = value_own.shape
    wide = query_grad.shape[1] // 2
    core = core_of()
    cosine, sine = cos_ref[...], -sin_ref[...]
    value_grad[:, pl.ds(pl.multiple_of(core * half, DH), half)] = value_own[...]
    value_grad[:, pl.ds(pl.multiple_of((1 - core) * half, DH), half)] = value_other[...]
    gate = joined_row(back[0, rows:, :rows]) + joined_row(back[1, rows:, :rows])
    gate_grad[...] = jnp.where(pos_ref[...] < limit, gate, 0.0)
    for i in range(half // DH):
        here = slice(i * DH, (i + 1) * DH)
        mine = part_mine[:, 2 * i * DH : (2 * i + 1) * DH]
        theirs = back[1 - core, :rows, wide + 2 * i * DH : wide + (2 * i + 1) * DH].astype(F32)
        for s in range(len(got) // 2):
            theirs = theirs + got[2 * s][:, here].astype(F32)
            mine = mine + got[2 * s + 1][:, here].astype(F32)
        for total, side in ((mine, core), (theirs, 1 - core)):
            there = pl.ds(pl.multiple_of(side * half + i * DH, DH), DH)
            key_grad[:, there] = rotate(total, cosine, sine).astype(BF16)
    for side in range(2):
        for i in range(wide // DH):
            turned = rotate(back[side, :rows, i * DH : (i + 1) * DH].astype(F32), cosine, sine)
            query_grad[:, side * wide + i * DH : side * wide + (i + 1) * DH] = turned.astype(BF16)


def per_device(query_rows, key_rows, value_rows, cotangent, router_gate, positions):
    rows, heads_width = query_rows.shape[1:]
    group_width = key_rows.shape[2]
    groups = group_width // DH
    ratio = heads_width // group_width
    half_groups, half_width = groups // 2, heads_width // 2
    parts = lax.axis_size("ctx")
    chips = parts // 2
    limit = parts * LOCAL
    wide = ratio * rows
    params = pltpu.CompilerParams(vmem_limit_bytes=(16 + 4 * chips) * 1024 * 1024)

    def call(kernel, name, outs, *args, scratch=(), flops=10**6, in_hbm=False):
        if in_hbm:
            args = [pltpu.with_memory_space_constraint(arg, pltpu.HBM) for arg in args]
        spec = pl.BlockSpec(memory_space=pltpu.HBM if in_hbm else pltpu.VMEM)
        return pl.pallas_call(
            kernel,
            out_shape=[jax.ShapeDtypeStruct(*out) for out in outs],
            in_specs=[spec] * len(args),
            scratch_shapes=list(scratch),
            compiler_params=params,
            cost_estimate=pl.CostEstimate(flops=flops, bytes_accessed=1000, transcendentals=0),
            name=name,
        )(*args)

    index = np.arange(DH) % (DH // 2)
    freq = jnp.asarray((THETA ** (-2.0 * index / DH)).astype(np.float32))[None]
    packet = ((rows, group_width // 2), BF16)
    table = ((rows, DH), F32)
    key_mine, key_theirs, value_mine, value_theirs, cosine, sine = call(
        functools.partial(pack_keys_kernel, limit=limit),
        "pack_keys",
        [packet, packet, packet, packet, table, table],
        key_rows[0],
        value_rows[0],
        positions,
        freq,
        in_hbm=True,
        flops=5 * 10**9,
        scratch=[
            pltpu.VMEM((rows, group_width), BF16),
            pltpu.VMEM((rows, group_width), BF16),
            pltpu.VMEM((1, rows), jnp.int32),
            pltpu.VMEM((1, DH), F32),
            pltpu.SemaphoreType.DMA((4,)),
        ],
    )

    hop = [[(2 * x + k, 2 * (x + s) + k) for x in range(chips - s) for k in range(2)] for s in range(chips)]
    cross = [[(a, b + 1 - 2 * (b % 2)) for a, b in pairs] for pairs in hop]
    back_hop = [[(b, a) for a, b in pairs] for pairs in hop]
    back_cross = [[(b, a) for a, b in pairs] for pairs in cross]

    steps = range(1, chips)

    def send(sib, own, sib_pairs, own_pairs):
        sib = [lax.ppermute(sib[s - 1], "ctx", sib_pairs[s]) for s in steps]
        return sib, [lax.ppermute(own[s - 1], "ctx", own_pairs[s]) for s in steps]

    sib_keys, own_keys = send([key_theirs] * chips, [key_mine] * chips, cross, hop)
    sib_values, own_values = send([value_theirs] * chips, [value_mine] * chips, cross, hop)

    pairs = [[2 * x, 2 * x + 1] for x in range(chips)]
    mine, theirs, gate_mine = call(
        functools.partial(pack_queries_kernel, limit=limit),
        "pack_queries",
        [((rows, heads_width), BF16), ((rows + EXTRA, heads_width + group_width), BF16), ((1, rows), F32)],
        query_rows[0],
        cotangent[0],
        router_gate,
        positions,
        cosine,
        sine,
        key_theirs,
        value_theirs,
    )
    sib = lax.ppermute(theirs, "ctx", [pair for a, b in pairs for pair in ((a, b), (b, a))])

    row = ((half_groups, 1, 2 * wide), F32)
    table = ((half_groups, 2 * rows, 2 * wide), F32)
    kv_table = ((half_groups, 2 * rows, DH), BF16)
    q_table = ((half_groups, 2 * wide, DH), BF16)
    keys, query, cot, gate_row, raws, grads, tops, sums, crosses = call(
        functools.partial(local_kernel, ratio=ratio),
        "local_scores",
        [kv_table, q_table, q_table, ((1, 2 * wide), F32), table, table, row, row, row],
        key_mine,
        value_mine,
        mine,
        gate_mine,
        sib,
        scratch=[pltpu.VMEM(*kv_table)],
        flops=3 * 10**6,
    )

    blocks = 2 * (chips - 1)
    far_rows = ((half_groups, blocks * rows, DH), BF16)
    far_low = ((half_groups, blocks * rows, 2 * wide), BF16)
    far_table = (far_low[0], F32 if chips == 2 else BF16)
    far_keys, far_raws, factors, far_factors, shrinks, inverses, *parts = call(
        functools.partial(far_keys_kernel, blocks=blocks),
        "far_keys",
        [far_rows, far_table, row, row, row, row] + [packet] * blocks,
        query,
        cot,
        gate_row,
        tops,
        sums,
        *sib_keys,
        *own_keys,
        scratch=[pltpu.VMEM(*far_low)],
    )
    sib_value_got, own_value_got = send(parts[: chips - 1], parts[chips - 1 :], back_cross, back_hop)
    far_grads, deltas, *parts = call(
        functools.partial(far_values_kernel, blocks=blocks),
        "far_values",
        [far_low, row] + [packet] * blocks,
        query,
        cot,
        far_raws,
        far_factors,
        shrinks,
        inverses,
        crosses,
        *sib_values,
        *own_values,
        scratch=[pltpu.VMEM(*far_rows)],
    )
    sib_key_got, own_key_got = send(parts[: chips - 1], parts[chips - 1 :], back_cross, back_hop)

    part_mine, packed = call(
        functools.partial(near_kernel, ratio=ratio),
        "near_grads",
        [
            ((rows, group_width), F32),
            ((2, rows + EXTRA, half_width + group_width), BF16),
        ],
        raws,
        grads,
        factors,
        deltas,
        keys,
        query,
        cot,
        far_keys,
        far_grads,
        flops=4 * 10**6,
        scratch=[
            pltpu.VMEM((half_groups, 2 * rows, 2 * wide), BF16),
            pltpu.VMEM((half_groups, 2 * rows, 2 * wide), BF16),
            pltpu.VMEM((2, rows, group_width), F32),
            pltpu.VMEM((half_groups, DH, 2 * wide), F32),
        ],
    )
    back = lax.all_to_all(packed, "ctx", 0, 0, axis_index_groups=pairs)
    value_own, value_other = call(
        sum_values_kernel,
        "sum_values",
        [packet, packet],
        back,
        part_mine,
        *[part for pair in zip(sib_value_got, own_value_got) for part in pair],
        flops=3 * 10**8,
    )
    query_grad, key_grad, value_grad, gate_grad = call(
        functools.partial(finish_kernel, limit=limit),
        "finish",
        [((rows, heads_width), BF16)] + [((rows, group_width), BF16)] * 2 + [((1, rows), F32)],
        back,
        part_mine,
        positions,
        cosine,
        sine,
        value_own,
        value_other,
        *[part for pair in zip(sib_key_got, own_key_got) for part in pair],
    )
    return (query_grad[None], key_grad[None], value_grad[None], gate_grad)


def solution(mesh):
    wide = P(("group", "dp"), "ctx", None)
    narrow = P(("group", "dp"), "ctx")
    return jax.shard_map(
        per_device,
        mesh=mesh,
        in_specs=(wide, wide, wide, wide, narrow, narrow),
        out_specs=(wide, wide, wide, narrow),
        check_vma=False,
    )
```

time: 33.3 us -> 28.7 us (0.86)
  the two profiles are of different devices: /device:TPU:0 before, /device:TPU:3 now
where the time goes in v9:
time: 28.7 us; the launch traced here: 28.3 us
  starting transfers between devices  11.1 us (39%)
  Pallas kernels  10.4 us (36%)
  blocking collectives  4.32 us (15%)
  waiting for transfers between devices  1.63 us (6%)
  between operations  0.82 us (3%)
    pallas_call x8, Pallas kernels, call(): pl.pallas_call(kernel, out_shape=[jax.ShapeDtypeStruct(*out) for out in o...  10.4 us
    ppermute x4, starting transfers between devices, send(): sib = [lax.ppermute(sib[s - 1], 'ctx', sib_pairs[s]) for s in steps]  5.17 us
    ppermute x4, starting transfers between devices, send(): return (sib, [lax.ppermute(own[s - 1], 'ctx', own_pairs[s]) for s in steps])  5.16 us
    all_to_all x1, blocking collectives, per_device(): back = lax.all_to_all(packed, 'ctx', 0, 0, axis_index_groups=pairs)  4.32 us
    ppermute x4, waiting for transfers between devices, send(): sib = [lax.ppermute(sib[s - 1], 'ctx', sib_pairs[s]) for s in steps]  1.62 us
    ppermute x1, starting transfers between devices, per_device(): lax.ppermute(theirs, 'ctx', [pair for a, b in pairs for pair in ((a, b),...  0.74 us
  transfers between devices with their start and end apart: 9, of which 1 were waited for; matrix products, arithmetic and copies ran while one was open for 0% of the time, Pallas kernels for 25%

profile of v9, /device:TPU:3, one launch (start us, length us, event | category | flops | bytes accessed | tf_op | source)
XLA Modules:
  0.0 28.3 jit_solution(8732944199236085012)
XLA Ops:
  0.6 0.0 copy-start
  0.6 0.0 copy-start.1
  0.7 0.0 copy-start.2
  0.7 0.0 copy-start.3
  0.7 1.3 %pack_keys.1 = (bf16[160,256]{1,0:T(8,128)(2,1)S(1)}, bf16[160,256]{1,0:T(8,128)(2,1)S(1)}, bf16[160,256]{1,0:T(8,128)(2,1)S(1)}, bf16[160,256]{1,0:T(8,128)(2,1...) custom-call(bf16[160,512]{1,0:T(8,128)(2,1)} %bitcast.10, bf16[160,512]{1,0:T(8,128)(2,1)} %bitcast.11, ...), custom_call_target="tpu_custom_call" | custom-call | flops 5000000000 | bytes 1000 | tf_op jit(solution)/shard_map/pack_keys/pallas_call | solution.py:392
  2.0 0.0 copy-done
  2.0 0.1 copy-done.1
  2.1 0.0 copy-done.2
  2.1 0.0 copy-done.3
  2.1 0.5 %pack_queries.1 = (bf16[160,2048]{1,0:T(8,128)(2,1)S(1)}, bf16[176,2560]{1,0:T(8,128)(2,1)S(1)}, f32[1,160]{1,0:T(1,128)S(1)}) custom-call(bf16[160,2048]{1,0:T(8,128)(2,1)S(1)} %bitcast.7, bf16[160,2048]{1,0:T(8,128)(2,1)S(1)} %bitcast.8, f32[1,160]{1,0:T(1,128)S(1)} %copy-done.3, s32[1,160]{1,0:T(1,128)S(1)} %copy-done.2, ...), custom_call_target="tpu_custom_call" | custom-call | flops 1000000 | bytes 1000 | tf_op jit(solution)/shard_map/pack_queries/pallas_call | solution.py:392
  2.6 0.7 %collective-permute-start = (bf16[176,2560]{1,0:T(8,128)(2,1)S(1)}, bf16[176,2560]{1,0:T(8,128)(2,1)S(1)}, u32[]{:S(2)}, u32[]{:S(2)}) collective-permute-start(bf16[176,2560]{1,0:T(8,128)(2,1)S(1)} %get-tuple-element.50), channel_id=1, source_target_pairs={{0,1},{1,0},{2,3},{3,2},{4,5},{5,4},{6,7},{7,6},{8,9},{9,8},{10,11... | collective-permute-start | bytes 2703368 | tf_op jit(solution)/shard_map/ppermute | solution.py:453
  3.4 1.3 %collective-permute-start.2 = (bf16[160,256]{1,0:T(8,128)(2,1)S(1)}, bf16[160,256]{1,0:T(8,128)(2,1)S(1)}, u32[]{:S(2)}, u32[]{:S(2)}) collective-permute-start(bf16[160,256]{1,0:T(8,128)(2,1)S(1)} %get-tuple-element.42.key_mine), channel_id=1, source_target_pairs={{0,2},{1,3},{4,6},{5,7},{8,10},{9,11},{12,14},{13,15},{16,18},{17,... | collective-permute-start | bytes 245768 | tf_op jit(solution)/shard_map/ppermute | solution.py:434
  4.7 1.3 %collective-permute-start.1 = (bf16[160,256]{1,0:T(8,128)(2,1)S(1)}, bf16[160,256]{1,0:T(8,128)(2,1)S(1)}, u32[]{:S(2)}, u32[]{:S(2)}) collective-permute-start(bf16[160,256]{1,0:T(8,128)(2,1)S(1)} %get-tuple-element.46.key), channel_id=1, source_target_pairs={{0,3},{1,2},{4,7},{5,6},{8,11},{9,10},{12,15},{13,14},{16,19},{17,... | collective-permute-start | bytes 245768 | tf_op jit(solution)/shard_map/ppermute | solution.py:433
  6.0 1.3 %collective-permute-start.4 = (bf16[160,256]{1,0:T(8,128)(2,1)S(1)}, bf16[160,256]{1,0:T(8,128)(2,1)S(1)}, u32[]{:S(2)}, u32[]{:S(2)}) collective-permute-start(bf16[160,256]{1,0:T(8,128)(2,1)S(1)} %get-tuple-element.43.value_mine), channel_id=1, source_target_pairs={{0,2},{1,3},{4,6},{5,7},{8,10},{9,11},{12,14},{13,15},{16,18},{17,... | collective-permute-start | bytes 245768 | tf_op jit(solution)/shard_map/ppermute | solution.py:434
  7.3 1.3 %collective-permute-start.3 = (bf16[160,256]{1,0:T(8,128)(2,1)S(1)}, bf16[160,256]{1,0:T(8,128)(2,1)S(1)}, u32[]{:S(2)}, u32[]{:S(2)}) collective-permute-start(bf16[160,256]{1,0:T(8,128)(2,1)S(1)} %get-tuple-element.47.value), channel_id=1, source_target_pairs={{0,3},{1,2},{4,7},{5,6},{8,11},{9,10},{12,15},{13,14},{16,19},{17,... | collective-permute-start | bytes 245768 | tf_op jit(solution)/shard_map/ppermute | solution.py:433
  8.6 0.0 collective-permute-done.sib
  8.6 1.4 %local_scores.1 = (bf16[2,320,128]{2,1,0:T(8,128)(2,1)S(1)}, bf16[2,1280,128]{2,1,0:T(8,128)(2,1)S(1)}, bf16[2,1280,128]{2,1,0:T(8,128)(2,1)S(1)}, f32[1,1280]{1...) custom-call(bf16[160,256]{1,0:T(8,128)(2,1)S(1)} %get-tuple-element., ...), custom_call_target="tpu_custom_call" | custom-call | flops 3000000 | bytes 1000 | tf_op jit(solution)/shard_map/local_scores/pallas_call | solution.py:392
  10.0 0.0 collective-permute-done.2.refs_1_
  10.0 1.6 %collective-permute-done.1.refs_0_ = bf16[160,256]{1,0:T(8,128)(2,1)S(1)} collective-permute-done((bf16[160,256]{1,0:T(8,128)(2,1)S(1)}, bf16[160,256]{1,0:T(8,128)(2,1)S(1)}, u32[]{:S(2)}, u32[]{:S(2)}) %collective-permute-start.1) | collective-permute-done | bytes 81952 | tf_op jit(solution)/shard_map/ppermute | solution.py:433
  11.6 1.7 %far_keys.1 = (bf16[2,320,128]{2,1,0:T(8,128)(2,1)S(1)}, f32[2,320,1280]{2,1,0:T(8,128)S(1)}, f32[2,1,1280]{2,1,0:T(1,128)S(1)}, f32[2,1,1280]{2,1,0:T(1,128)S(1...) custom-call(bf16[2,1280,128]{2,1,0:T(8,128)(2,1)S(1)} %get-tuple-ele, ...), custom_call_target="tpu_custom_call" | custom-call | flops 1000000 | bytes 1000 | tf_op jit(solution)/shard_map/far_keys/pallas_call | solution.py:392
  13.3 1.3 %collective-permute-start.5 = (bf16[160,256]{1,0:T(8,128)(2,1)S(1)}, bf16[160,256]{1,0:T(8,128)(2,1)S(1)}, u32[]{:S(2)}, u32[]{:S(2)}) collective-permute-start(bf16[160,256]{1,0:T(8,128)(2,1)S(1)} %get-tuple-element.70), channel_id=1, source_target_pairs={{3,0},{2,1},{7,4},{6,5},{11,8},{10,9},{15,12},{14,13},{19,16},{18,... | collective-permute-start | bytes 245768 | tf_op jit(solution)/shard_map/ppermute | solution.py:433
  14.6 1.3 %collective-permute-start.6 = (bf16[160,256]{1,0:T(8,128)(2,1)S(1)}, bf16[160,256]{1,0:T(8,128)(2,1)S(1)}, u32[]{:S(2)}, u32[]{:S(2)}) collective-permute-start(bf16[160,256]{1,0:T(8,128)(2,1)S(1)} %get-tuple-element.71), channel_id=1, source_target_pairs={{2,0},{3,1},{6,4},{7,5},{10,8},{11,9},{14,12},{15,13},{18,16},{19,... | collective-permute-start | bytes 245768 | tf_op jit(solution)/shard_map/ppermute | solution.py:434
  15.9 0.0 collective-permute-done.4.refs_1_
  15.9 0.0 collective-permute-done.3.refs_0_
  15.9 1.9 %far_values.1 = (bf16[2,320,1280]{2,1,0:T(8,128)(2,1)S(1)}, f32[2,1,1280]{2,1,0:T(1,128)S(1)}, bf16[160,256]{1,0:T(8,128)(2,1)S(1)}, bf16[160,256]{1,0:T(8,128)(2,1)S(1)}) custom-call(bf16[2,1280,128]{2,1,0:T(8,128)(2,1)S(1)} %get-tuple-element.53.query, bf16[2,1280,128]{2,1,0:T(8,128)(2,1)S(1)} %get-tuple-element.54.cot, ...), custom_call_target="tpu_custom_call" | custom-call | flops 1000000 | bytes 1000 | tf_op jit(solution)/shard_map/far_values/pallas_call | solution.py:392
  17.8 1.3 %collective-permute-start.7 = (bf16[160,256]{1,0:T(8,128)(2,1)S(1)}, bf16[160,256]{1,0:T(8,128)(2,1)S(1)}, u32[]{:S(2)}, u32[]{:S(2)}) collective-permute-start(bf16[160,256]{1,0:T(8,128)(2,1)S(1)} %get-tuple-element.74), channel_id=1, source_target_pairs={{3,0},{2,1},{7,4},{6,5},{11,8},{10,9},{15,12},{14,13},{19,16},{18,... | collective-permute-start | bytes 245768 | tf_op jit(solution)/shard_map/ppermute | solution.py:433
  19.1 1.3 %collective-permute-start.8 = (bf16[160,256]{1,0:T(8,128)(2,1)S(1)}, bf16[160,256]{1,0:T(8,128)(2,1)S(1)}, u32[]{:S(2)}, u32[]{:S(2)}) collective-permute-start(bf16[160,256]{1,0:T(8,128)(2,1)S(1)} %get-tuple-element.75), channel_id=1, source_target_pairs={{2,0},{3,1},{6,4},{7,5},{10,8},{11,9},{14,12},{15,13},{18,16},{19,... | collective-permute-start | bytes 245768 | tf_op jit(solution)/shard_map/ppermute | solution.py:434
  20.4 2.2 %near_grads.1 = (f32[160,512]{1,0:T(8,128)S(1)}, bf16[2,176,1536]{2,1,0:T(8,128)(2,1)S(1)}) custom-call(f32[2,320,1280]{2,1,0:T(8,128)S(1)} %get-tuple-element.51.raws, f32[2,320,1280]{2,1,0:T(8,128)S(1)} %get-tuple-element.52.grads, f32[2,1,1280]{2,1,0:T(1,128)S(1)} %get-tuple-element.58.factors, f32[2,1,1280]{2,1,0:T(1,128)S(1)} %get-tuple-element.64.deltas, ...), custom_call_target="tpu_custom_call" | custom-call | flops 4000000 | bytes 1000 | tf_op jit(solution)/shard_map/near_grads/pallas_call | solution.py:392
  22.5 4.3 %all_to_all.5.back = bf16[2,176,1536]{2,1,0:T(8,128)(2,1)S(1)} all-to-all(bf16[2,176,1536]{2,1,0:T(8,128)(2,1)S(1)} %get-tuple-element.68), channel_id=1, replica_groups={{0,1},{2,3},{4,5},{6,7},{8,9},{10,11},{12,13},{14,15},{16,17},{18,19},{..., dimensions={0} | all-to-all | bytes 2162688 | tf_op jit(solution)/shard_map/all_to_all | solution.py:531
  26.9 0.0 collective-permute-done.5.refs_0_
  26.9 0.0 collective-permute-done.6.refs_1_
  26.9 0.0 collective-permute-done.7.refs_0_
  26.9 0.0 collective-permute-done.8.refs_1_
  26.9 1.4 %finish.1 = (bf16[160,2048]{1,0:T(8,128)(2,1)}, bf16[160,512]{1,0:T(8,128)(2,1)}, bf16[160,512]{1,0:T(8,128)(2,1)}, f32[1,160]{1,0:T(1,128)}) custom-call(bf16[2,176,1536]{2,1,0:T(8,128)(2,1)S(1)} %all_to_all.5.back, f32[160,512]{1,0:T(8,128)S(1)} %get-tuple-element.69.part_mine, s32[1,160]{1,0:T(1,128)S(1)} %copy-done.2, ...), custom_call_target="tpu_custom_call" | custom-call | flops 1000000 | bytes 1000 | tf_op jit(solution)/shard_map/finish/pallas_call | solution.py:392
  (1 shorter events, 0.0 us)
Async XLA Ops:
  0.6 1.4 %copy-start = (bf16[1,160,2048]{2,1,0:T(8,128)(2,1)S(1)}, bf16[1,160,2048]{2,1,0:T(8,128)(2,1)}, u32[]{:S(2)}) copy-start(bf16[1,160,2048]{2,1,0:T(8,128)(2,1)} %param.7) | copy-start | bytes 1966084
  0.6 1.5 %copy-start.1 = (bf16[1,160,2048]{2,1,0:T(8,128)(2,1)S(1)}, bf16[1,160,2048]{2,1,0:T(8,128)(2,1)}, u32[]{:S(2)}) copy-start(bf16[1,160,2048]{2,1,0:T(8,128)(2,1)} %param.10) | copy-start | bytes 1966084
  0.7 1.5 %copy-start.2 = (s32[1,160]{1,0:T(1,128)S(1)}, s32[1,160]{1,0:T(1,128)}, u32[]{:S(2)}) copy-start(s32[1,160]{1,0:T(1,128)} %pos_ref.1) | copy-start | bytes 1924
  0.7 1.4 %copy-start.3 = (f32[1,160]{1,0:T(1,128)S(1)}, f32[1,160]{1,0:T(1,128)}, u32[]{:S(2)}) copy-start(f32[1,160]{1,0:T(1,128)} %gate.1) | copy-start | bytes 1924
  2.6 5.9 %collective-permute-start = (bf16[176,2560]{1,0:T(8,128)(2,1)S(1)}, bf16[176,2560]{1,0:T(8,128)(2,1)S(1)}, u32[]{:S(2)}, u32[]{:S(2)}) collective-permute-start(bf16[176,2560]{1,0:T(8,128)(2,1)S(1)} %get-tuple-element.50), channel_id=1, source_target_pairs={{0,1},{1,0},{2,3},{3,2},{4,5},{5,4},{6,7},{7,6},{8,9},{9,8},{10,11... | collective-permute-start | bytes 2703368 | tf_op jit(solution)/shard_map/ppermute | solution.py:453
  3.4 6.6 %collective-permute-start.2 = (bf16[160,256]{1,0:T(8,128)(2,1)S(1)}, bf16[160,256]{1,0:T(8,128)(2,1)S(1)}, u32[]{:S(2)}, u32[]{:S(2)}) collective-permute-start(bf16[160,256]{1,0:T(8,128)(2,1)S(1)} %get-tuple-element.42.key_mine), channel_id=1, source_target_pairs={{0,2},{1,3},{4,6},{5,7},{8,10},{9,11},{12,14},{13,15},{16,18},{17,... | collective-permute-start | bytes 245768 | tf_op jit(solution)/shard_map/ppermute | solution.py:434
  4.7 6.9 %collective-permute-start.1 = (bf16[160,256]{1,0:T(8,128)(2,1)S(1)}, bf16[160,256]{1,0:T(8,128)(2,1)S(1)}, u32[]{:S(2)}, u32[]{:S(2)}) collective-permute-start(bf16[160,256]{1,0:T(8,128)(2,1)S(1)} %get-tuple-element.46.key), channel_id=1, source_target_pairs={{0,3},{1,2},{4,7},{5,6},{8,11},{9,10},{12,15},{13,14},{16,19},{17,... | collective-permute-start | bytes 245768 | tf_op jit(solution)/shard_map/ppermute | solution.py:433
  6.0 9.9 %collective-permute-start.4 = (bf16[160,256]{1,0:T(8,128)(2,1)S(1)}, bf16[160,256]{1,0:T(8,128)(2,1)S(1)}, u32[]{:S(2)}, u32[]{:S(2)}) collective-permute-start(bf16[160,256]{1,0:T(8,128)(2,1)S(1)} %get-tuple-element.43.value_mine), channel_id=1, source_target_pairs={{0,2},{1,3},{4,6},{5,7},{8,10},{9,11},{12,14},{13,15},{16,18},{17,... | collective-permute-start | bytes 245768 | tf_op jit(solution)/shard_map/ppermute | solution.py:434
  7.3 8.6 %collective-permute-start.3 = (bf16[160,256]{1,0:T(8,128)(2,1)S(1)}, bf16[160,256]{1,0:T(8,128)(2,1)S(1)}, u32[]{:S(2)}, u32[]{:S(2)}) collective-permute-start(bf16[160,256]{1,0:T(8,128)(2,1)S(1)} %get-tuple-element.47.value), channel_id=1, source_target_pairs={{0,3},{1,2},{4,7},{5,6},{8,11},{9,10},{12,15},{13,14},{16,19},{17,... | collective-permute-start | bytes 245768 | tf_op jit(solution)/shard_map/ppermute | solution.py:433
  13.3 13.6 %collective-permute-start.5 = (bf16[160,256]{1,0:T(8,128)(2,1)S(1)}, bf16[160,256]{1,0:T(8,128)(2,1)S(1)}, u32[]{:S(2)}, u32[]{:S(2)}) collective-permute-start(bf16[160,256]{1,0:T(8,128)(2,1)S(1)} %get-tuple-element.70), channel_id=1, source_target_pairs={{3,0},{2,1},{7,4},{6,5},{11,8},{10,9},{15,12},{14,13},{19,16},{18,... | collective-permute-start | bytes 245768 | tf_op jit(solution)/shard_map/ppermute | solution.py:433
  14.6 12.3 %collective-permute-start.6 = (bf16[160,256]{1,0:T(8,128)(2,1)S(1)}, bf16[160,256]{1,0:T(8,128)(2,1)S(1)}, u32[]{:S(2)}, u32[]{:S(2)}) collective-permute-start(bf16[160,256]{1,0:T(8,128)(2,1)S(1)} %get-tuple-element.71), channel_id=1, source_target_pairs={{2,0},{3,1},{6,4},{7,5},{10,8},{11,9},{14,12},{15,13},{18,16},{19,... | collective-permute-start | bytes 245768 | tf_op jit(solution)/shard_map/ppermute | solution.py:434
  17.8 9.2 %collective-permute-start.7 = (bf16[160,256]{1,0:T(8,128)(2,1)S(1)}, bf16[160,256]{1,0:T(8,128)(2,1)S(1)}, u32[]{:S(2)}, u32[]{:S(2)}) collective-permute-start(bf16[160,256]{1,0:T(8,128)(2,1)S(1)} %get-tuple-element.74), channel_id=1, source_target_pairs={{3,0},{2,1},{7,4},{6,5},{11,8},{10,9},{15,12},{14,13},{19,16},{18,... | collective-permute-start | bytes 245768 | tf_op jit(solution)/shard_map/ppermute | solution.py:433
  19.1 7.9 %collective-permute-start.8 = (bf16[160,256]{1,0:T(8,128)(2,1)S(1)}, bf16[160,256]{1,0:T(8,128)(2,1)S(1)}, u32[]{:S(2)}, u32[]{:S(2)}) collective-permute-start(bf16[160,256]{1,0:T(8,128)(2,1)S(1)} %get-tuple-element.75), channel_id=1, source_target_pairs={{2,0},{3,1},{6,4},{7,5},{10,8},{11,9},{14,12},{15,13},{18,16},{19,... | collective-permute-start | bytes 245768 | tf_op jit(solution)/shard_map/ppermute | solution.py:434

commit v10 on v9

--- a/solution.py
+++ b/solution.py
@@ -207,8 +207,8 @@
 
 def far_keys_kernel(query, cot, gate, tops, sums, *refs, blocks):
     packets = refs[:blocks]
-    far_keys, raws, factors, far_factors, shrinks, inverses = refs[blocks : blocks + 6]
-    parts, weights = refs[blocks + 6 : -1], refs[-1]
+    far_keys, raws, weights, factors, far_factors, shrinks, inverses = refs[blocks : blocks + 7]
+    parts = refs[blocks + 7 :]
     rows = packets[0].shape[0]
     half_groups, lanes = query.shape[:2]
     alone = lax.axis_index("ctx") < 2
@@ -251,7 +251,7 @@
                 out_ref[:, i * DH : (i + 1) * DH] = dot(weights[i, there, :], cot[i], NN).astype(BF16)
 
 
-def far_values_kernel(query, cot, raws, far_factors, shrinks, inverses, crosses, *refs, blocks):
+def far_values_kernel(query, cot, raws, weights, far_factors, shrinks, inverses, crosses, *refs, blocks):
     packets = refs[:blocks]
     score_grads, deltas = refs[blocks : blocks + 2]
     parts, far_values = refs[blocks + 2 : -1], refs[-1]
@@ -282,11 +282,14 @@
                 there = slice(j * rows, (j + 1) * rows)
                 part = dot(score_grads[i, there, :], query[i], NN) * LN2
                 out_ref[:, i * DH : (i + 1) * DH] = part.astype(BF16)
+                if j >= blocks // 2:
+                    part = dot(weights[i, there, :], cot[i], NN)
+                    out_ref[:, (half_groups + i) * DH : (half_groups + i + 1) * DH] = part.astype(BF16)
 
 
 def near_kernel(
-    raws, grads, factors, deltas, keys, query, cot, far_keys, far_grads,
-    part_mine, out_ref, weights, score_grads, parts, acc,
+    raws, grads, factors, deltas, keys, query, cot, far_keys, far_grads, cos_ref, sin_ref,
+    part_mine, query_mine, gate_mine, theirs, weights, score_grads, parts, acc, turned,
     *, ratio
 ):
     rows = part_mine.shape[0]
@@ -311,66 +314,95 @@
         for i in range(half_groups):
             acc[i] += dot(far_keys[i], far_grads[i], TN)
 
+    core = core_of()
+    cosine, sine = cos_ref[...], -sin_ref[...]
     for i in range(half_groups):
-        total = jnp.transpose(acc[i] * SCALE).astype(BF16)
-        for block in range(2):
-            for h in range(ratio):
-                at = (i * ratio + h) * DH
-                low = block * wide + h * rows
-                out_ref[block, :rows, at : at + DH] = total[low : low + rows]
-    part_mine[...] = parts[core_of()]
-    for block in range(2):
-        out_ref[block, :rows, half:] = parts[block].astype(BF16)
+        turned[...] = jnp.transpose(acc[i] * SCALE)
+        for h in range(ratio):
+            here = slice((i * ratio + h) * DH, (i * ratio + h + 1) * DH)
+            own = turned[pl.ds(pl.multiple_of(core * wide + h * rows, 16), rows), :]
+            query_mine[:, here] = rotate(own, cosine, sine).astype(BF16)
+            other = turned[pl.ds(pl.multiple_of((1 - core) * wide + h * rows, 16), rows), :]
+            theirs[:rows, here] = other.astype(BF16)
+    part_mine[...] = parts[core]
+    theirs[:rows, half:] = parts[1 - core].astype(BF16)
     summed = deltas[0]
     for i in range(1, half_groups):
         summed = summed + deltas[i]
+    gates = []
     for block in range(2):
         own = split_rows(summed[:, block * wide : (block + 1) * wide], 16)
-        own = joined_row(dot(own, chosen((wide, rows), ratio, 0), NN))
-        out_ref[block, rows:, :rows] = split_rows(own, EXTRA)
-
-
-def sum_values_kernel(back, part_mine, *refs):
-    got, (own, other) = refs[:-2], refs[-2:]
-    rows, half = own.shape
-    start = back.shape[2] - 2 * half
+        gates.append(joined_row(dot(own, chosen((wide, rows), ratio, 0), NN)))
+    gate_mine[...] = jnp.where(core == 0, gates[0], gates[1])
+    theirs[rows:, :rows] = split_rows(jnp.where(core == 0, gates[1], gates[0]), EXTRA)
+
+
+def sum_first_kernel(*refs):
+    got, other = refs[:-1], refs[-1]
+    total = got[0][...].astype(F32)
+    for ref in got[1:]:
+        total = total + ref[...].astype(F32)
+    other[...] = total
+
+
+def sum_rest_kernel(value_in, part_mine, *refs):
+    got, (key_own, value_own, key_other, value_other) = refs[:-4], refs[-4:]
+    half = value_in.shape[1]
+    value_other[...] = value_in[...]
+    total = got[0][...].astype(F32)
+    for ref in got[2::2]:
+        total = total + ref[...].astype(F32)
+    key_other[...] = total
+    for i in range(half // DH):
+        here, there = slice(i * DH, (i + 1) * DH), slice(half + i * DH, half + (i + 1) * DH)
+        key = part_mine[:, 2 * i * DH : (2 * i + 1) * DH]
+        value = part_mine[:, (2 * i + 1) * DH : (2 * i + 2) * DH]
+        for ref in got[1::2]:
+            key = key + ref[:, here].astype(F32)
+            value = value + ref[:, there].astype(F32)
+        key_own[:, here] = key
+        value_own[:, here] = value
+
+
+def finish_kernel(
+    back, query_mine, gate_mine, key_own, value_own, key_other, value_other, pos_ref, cos_ref, sin_ref,
+    query_out, key_out, value_out, gate_grad, query, key, value, sems, *, limit
+):
+    rows, half = value_own.shape
+    wide = query_mine.shape[1]
     core = core_of()
+    side = lambda which, width, at=0, size=None: pl.ds(pl.multiple_of(which * width + at, DH), size or width)
+    copies = [pltpu.make_async_copy(query_mine, query_out.at[:, side(core, wide)], sems.at[0])]
+    copies[0].start()
+    cosine, sine = cos_ref[...], -sin_ref[...]
     for i in range(half // DH):
         here = slice(i * DH, (i + 1) * DH)
-        there = (2 * i + 1) * DH
-        mine = part_mine[:, there : there + DH]
-        theirs = back[1 - core, :rows, start + there : start + there + DH].astype(F32)
-        for s in range(len(got) // 2):
-            theirs = theirs + got[2 * s][:, here].astype(F32)
-            mine = mine + got[2 * s + 1][:, here].astype(F32)
-        own[:, here] = mine.astype(BF16)
-        other[:, here] = theirs.astype(BF16)
-
-
-def finish_kernel(back, part_mine, pos_ref, cos_ref, sin_ref, value_own, value_other, *refs, limit):
-    got, (query_grad, key_grad, value_grad, gate_grad) = refs[:-4], refs[-4:]
-    rows, half = value_own.shape
-    wide = query_grad.shape[1] // 2
-    core = core_of()
-    cosine, sine = cos_ref[...], -sin_ref[...]
-    value_grad[:, pl.ds(pl.multiple_of(core * half, DH), half)] = value_own[...]
-    value_grad[:, pl.ds(pl.multiple_of((1 - core) * half, DH), half)] = value_other[...]
-    gate = joined_row(back[0, rows:, :rows]) + joined_row(back[1, rows:, :rows])
+        there = wide + 2 * i * DH
+        other_key = key_other[:, here] + back[:rows, there : there + DH].astype(F32)
+        other_value = value_other[:, here] + back[:rows, there + DH : there + 2 * DH].astype(F32)
+        for key_sum, value_sum, which in (
+            (key_own[:, here], value_own[:, here], core),
+            (other_key, other_value, 1 - core),
+        ):
+            to = side(which, half, i * DH, DH)
+            key[:, to] = rotate(key_sum, cosine, sine).astype(BF16)
+            value[:, to] = value_sum.astype(BF16)
+    copies.append(pltpu.make_async_copy(key, key_out, sems.at[1]))
+    copies.append(pltpu.make_async_copy(value, value_out, sems.at[2]))
+    copies[1].start()
+    copies[2].start()
+    for part in range(2):
+        low = part * (wide // 2)
+        for i in range(wide // 2 // DH):
+            here = slice(low + i * DH, low + (i + 1) * DH)
+            query[:, here] = rotate(back[:rows, here].astype(F32), cosine, sine).astype(BF16)
+        to = query_out.at[:, side(1 - core, wide, low, wide // 2)]
+        copies.append(pltpu.make_async_copy(query.at[:, low : low + wide // 2], to, sems.at[3 + part]))
+        copies[-1].start()
+    gate = gate_mine[...] + joined_row(back[rows:, :rows])
     gate_grad[...] = jnp.where(pos_ref[...] < limit, gate, 0.0)
-    for i in range(half // DH):
-        here = slice(i * DH, (i + 1) * DH)
-        mine = part_mine[:, 2 * i * DH : (2 * i + 1) * DH]
-        theirs = back[1 - core, :rows, wide + 2 * i * DH : wide + (2 * i + 1) * DH].astype(F32)
-        for s in range(len(got) // 2):
-            theirs = theirs + got[2 * s][:, here].astype(F32)
-            mine = mine + got[2 * s + 1][:, here].astype(F32)
-        for total, side in ((mine, core), (theirs, 1 - core)):
-            there = pl.ds(pl.multiple_of(side * half + i * DH, DH), DH)
-            key_grad[:, there] = rotate(total, cosine, sine).astype(BF16)
-    for side in range(2):
-        for i in range(wide // DH):
-            turned = rotate(back[side, :rows, i * DH : (i + 1) * DH].astype(F32), cosine, sine)
-            query_grad[:, side * wide + i * DH : side * wide + (i + 1) * DH] = turned.astype(BF16)
+    for copy in copies:
+        copy.wait()
 
 
 def per_device(query_rows, key_rows, value_rows, cotangent, router_gate, positions):
@@ -385,7 +417,7 @@
     wide = ratio * rows
     params = pltpu.CompilerParams(vmem_limit_bytes=(16 + 4 * chips) * 1024 * 1024)
 
-    def call(kernel, name, outs, *args, scratch=(), flops=10**6, in_hbm=False):
+    def call(kernel, name, outs, *args, scratch=(), flops=10**6, in_hbm=False, out_hbm=0):
         if in_hbm:
             args = [pltpu.with_memory_space_constraint(arg, pltpu.HBM) for arg in args]
         spec = pl.BlockSpec(memory_space=pltpu.HBM if in_hbm else pltpu.VMEM)
@@ -393,6 +425,9 @@
             kernel,
             out_shape=[jax.ShapeDtypeStruct(*out) for out in outs],
             in_specs=[spec] * len(args),
+            out_specs=[
+                pl.BlockSpec(memory_space=pltpu.HBM if i < out_hbm else pltpu.VMEM) for i in range(len(outs))
+            ],
             scratch_shapes=list(scratch),
             compiler_params=params,
             cost_estimate=pl.CostEstimate(flops=flops, bytes_accessed=1000, transcendentals=0),
@@ -450,7 +485,8 @@
         key_theirs,
         value_theirs,
     )
-    sib = lax.ppermute(theirs, "ctx", [pair for a, b in pairs for pair in ((a, b), (b, a))])
+    swap = [pair for a, b in pairs for pair in ((a, b), (b, a))]
+    sib = lax.ppermute(theirs, "ctx", swap)
 
     row = ((half_groups, 1, 2 * wide), F32)
     table = ((half_groups, 2 * rows, 2 * wide), F32)
@@ -473,10 +509,10 @@
     far_rows = ((half_groups, blocks * rows, DH), BF16)
     far_low = ((half_groups, blocks * rows, 2 * wide), BF16)
     far_table = (far_low[0], F32 if chips == 2 else BF16)
-    far_keys, far_raws, factors, far_factors, shrinks, inverses, *parts = call(
+    far_keys, far_raws, weights, factors, far_factors, shrinks, inverses, *parts = call(
         functools.partial(far_keys_kernel, blocks=blocks),
         "far_keys",
-        [far_rows, far_table, row, row, row, row] + [packet] * blocks,
+        [far_rows, far_table, far_low, row, row, row, row] + [packet] * (chips - 1),
         query,
         cot,
         gate_row,
@@ -484,16 +520,16 @@
         sums,
         *sib_keys,
         *own_keys,
-        scratch=[pltpu.VMEM(*far_low)],
-    )
-    sib_value_got, own_value_got = send(parts[: chips - 1], parts[chips - 1 :], back_cross, back_hop)
+    )
+    sib_value_got = [lax.ppermute(parts[s - 1], "ctx", back_cross[s]) for s in steps]
     far_grads, deltas, *parts = call(
         functools.partial(far_values_kernel, blocks=blocks),
         "far_values",
-        [far_low, row] + [packet] * blocks,
+        [far_low, row] + [packet] * (chips - 1) + [((rows, group_width), BF16)] * (chips - 1),
         query,
         cot,
         far_raws,
+        weights,
         far_factors,
         shrinks,
         inverses,
@@ -502,14 +538,16 @@
         *own_values,
         scratch=[pltpu.VMEM(*far_rows)],
     )
-    sib_key_got, own_key_got = send(parts[: chips - 1], parts[chips - 1 :], back_cross, back_hop)
-
-    part_mine, packed = call(
+    sib_key_got, own_got = send(parts[: chips - 1], parts[chips - 1 :], back_cross, back_hop)
+
+    part_mine, query_mine, gate_mine, theirs = call(
         functools.partial(near_kernel, ratio=ratio),
         "near_grads",
         [
             ((rows, group_width), F32),
-            ((2, rows + EXTRA, half_width + group_width), BF16),
+            ((rows, half_width), BF16),
+            ((1, rows), F32),
+            ((rows + EXTRA, half_width + group_width), BF16),
         ],
         raws,
         grads,
@@ -520,36 +558,47 @@
         cot,
         far_keys,
         far_grads,
+        cosine,
+        sine,
         flops=4 * 10**6,
         scratch=[
             pltpu.VMEM((half_groups, 2 * rows, 2 * wide), BF16),
             pltpu.VMEM((half_groups, 2 * rows, 2 * wide), BF16),
             pltpu.VMEM((2, rows, group_width), F32),
             pltpu.VMEM((half_groups, DH, 2 * wide), F32),
+            pltpu.VMEM((2 * wide, DH), F32),
         ],
     )
-    back = lax.all_to_all(packed, "ctx", 0, 0, axis_index_groups=pairs)
-    value_own, value_other = call(
-        sum_values_kernel,
-        "sum_values",
-        [packet, packet],
-        back,
+    back = lax.ppermute(theirs, "ctx", swap)
+    total = ((rows, group_width // 2), F32)
+    (value_other,) = call(sum_first_kernel, "sum_first", [total], *sib_value_got, flops=5 * 10**9)
+    sums = call(
+        sum_rest_kernel,
+        "sum_rest",
+        [total] * 4,
+        value_other,
         part_mine,
-        *[part for pair in zip(sib_value_got, own_value_got) for part in pair],
-        flops=3 * 10**8,
+        *[part for pair in zip(sib_key_got, own_got) for part in pair],
+        flops=5 * 10**9,
     )
     query_grad, key_grad, value_grad, gate_grad = call(
         functools.partial(finish_kernel, limit=limit),
         "finish",
         [((rows, heads_width), BF16)] + [((rows, group_width), BF16)] * 2 + [((1, rows), F32)],
         back,
-        part_mine,
+        query_mine,
+        gate_mine,
+        *sums,
         positions,
         cosine,
         sine,
-        value_own,
-        value_other,
-        *[part for pair in zip(sib_key_got, own_key_got) for part in pair],
+        out_hbm=3,
+        scratch=[
+            pltpu.VMEM((rows, half_width), BF16),
+            pltpu.VMEM((rows, group_width), BF16),
+            pltpu.VMEM((rows, group_width), BF16),
+            pltpu.SemaphoreType.DMA((5,)),
+        ],
     )
     return (query_grad[None], key_grad[None], value_grad[None], gate_grad)
 

time: 28.7 us -> 28.1 us (0.979)
  the two profiles are of different devices: /device:TPU:3 before, /device:TPU:0 now
where the time goes in v10:
time: 28.1 us; the launch traced here: 27.6 us
  starting transfers between devices  12.8 us (46%)
  Pallas kernels  7.14 us (25%)
  waiting for transfers between devices  6.7 us (24%)
  between operations  0.82 us (3%)
    pallas_call x9, Pallas kernels, call(): pl.pallas_call(kernel, out_shape=[jax.ShapeDtypeStruct(*out) for out in o...  7.14 us
    ppermute x3, starting transfers between devices, send(): sib = [lax.ppermute(sib[s - 1], 'ctx', sib_pairs[s]) for s in steps]  7.08 us
    ppermute x3, waiting for transfers between devices, send(): sib = [lax.ppermute(sib[s - 1], 'ctx', sib_pairs[s]) for s in steps]  5.82 us
    ppermute x3, starting transfers between devices, send(): return (sib, [lax.ppermute(own[s - 1], 'ctx', own_pairs[s]) for s in steps])  3.87 us
    ppermute x1, starting transfers between devices, per_device(): lax.ppermute(parts[s - 1], 'ctx', back_cross[s])  1.29 us
    ppermute x3, waiting for transfers between devices, send(): return (sib, [lax.ppermute(own[s - 1], 'ctx', own_pairs[s]) for s in steps])  0.87 us
  transfers between devices with their start and end apart: 9, of which 3 were waited for; matrix products, arithmetic and copies ran while one was open for 0% of the time, Pallas kernels for 13%

profile of v10, /device:TPU:0, one launch (start us, length us, event | category | flops | bytes accessed | tf_op | source)
XLA Modules:
  0.0 27.6 jit_solution(8129071351428440803)
XLA Ops:
  0.6 0.0 copy-start
  0.6 0.0 copy-start.1
  0.7 0.0 copy-start.2
  0.7 0.0 copy-start.3
  0.7 1.3 %pack_keys.1 = (bf16[160,256]{1,0:T(8,128)(2,1)S(1)}, bf16[160,256]{1,0:T(8,128)(2,1)S(1)}, bf16[160,256]{1,0:T(8,128)(2,1)S(1)}, bf16[160,256]{1,0:T(8,128)(2,1...) custom-call(bf16[160,512]{1,0:T(8,128)(2,1)} %bitcast.10, bf16[160,512]{1,0:T(8,128)(2,1)} %bitcast.11, ...), custom_call_target="tpu_custom_call" | custom-call | flops 5000000000 | bytes 1000 | tf_op jit(solution)/shard_map/pack_keys/pallas_call | solution.py:424
  2.0 0.0 copy-done
  2.0 0.1 copy-done.1
  2.1 0.0 copy-done.2
  2.1 0.0 copy-done.3
  2.1 0.5 %pack_queries.1 = (bf16[160,2048]{1,0:T(8,128)(2,1)S(1)}, bf16[176,2560]{1,0:T(8,128)(2,1)S(1)}, f32[1,160]{1,0:T(1,128)S(1)}) custom-call(bf16[160,2048]{1,0:T(8,128)(2,1)S(1)} %bitcast.7, bf16[160,2048]{1,0:T(8,128)(2,1)S(1)} %bitcast.8, f32[1,160]{1,0:T(1,128)S(1)} %copy-done.3, s32[1,160]{1,0:T(1,128)S(1)} %copy-done.2, ...), custom_call_target="tpu_custom_call" | custom-call | flops 1000000 | bytes 1000 | tf_op jit(solution)/shard_map/pack_queries/pallas_call | solution.py:424
  2.6 0.5 %collective-permute-start = (bf16[176,2560]{1,0:T(8,128)(2,1)S(1)}, bf16[176,2560]{1,0:T(8,128)(2,1)S(1)}, u32[]{:S(2)}, u32[]{:S(2)}) collective-permute-start(bf16[176,2560]{1,0:T(8,128)(2,1)S(1)} %get-tuple-element.54), channel_id=1, source_target_pairs={{0,1},{1,0},{2,3},{3,2},{4,5},{5,4},{6,7},{7,6},{8,9},{9,8},{10,11... | collective-permute-start | bytes 2703368 | tf_op jit(solution)/shard_map/ppermute | solution.py:489
  3.2 4.5 %collective-permute-start.1 = (bf16[160,256]{1,0:T(8,128)(2,1)S(1)}, bf16[160,256]{1,0:T(8,128)(2,1)S(1)}, u32[]{:S(2)}, u32[]{:S(2)}) collective-permute-start(bf16[160,256]{1,0:T(8,128)(2,1)S(1)} %get-tuple-element.50.key), channel_id=1, source_target_pairs={{0,3},{1,2},{4,7},{5,6},{8,11},{9,10},{12,15},{13,14},{16,19},{17,... | collective-permute-start | bytes 245768 | tf_op jit(solution)/shard_map/ppermute | solution.py:468
  7.7 1.3 %collective-permute-start.2 = (bf16[160,256]{1,0:T(8,128)(2,1)S(1)}, bf16[160,256]{1,0:T(8,128)(2,1)S(1)}, u32[]{:S(2)}, u32[]{:S(2)}) collective-permute-start(bf16[160,256]{1,0:T(8,128)(2,1)S(1)} %get-tuple-element.46.key_mine), channel_id=1, source_target_pairs={{0,2},{1,3},{4,6},{5,7},{8,10},{9,11},{12,14},{13,15},{16,18},{17,... | collective-permute-start | bytes 245768 | tf_op jit(solution)/shard_map/ppermute | solution.py:469
  9.0 1.3 %collective-permute-start.3 = (bf16[160,256]{1,0:T(8,128)(2,1)S(1)}, bf16[160,256]{1,0:T(8,128)(2,1)S(1)}, u32[]{:S(2)}, u32[]{:S(2)}) collective-permute-start(bf16[160,256]{1,0:T(8,128)(2,1)S(1)} %get-tuple-element.51.value), channel_id=1, source_target_pairs={{0,3},{1,2},{4,7},{5,6},{8,11},{9,10},{12,15},{13,14},{16,19},{17,... | collective-permute-start | bytes 245768 | tf_op jit(solution)/shard_map/ppermute | solution.py:468
  10.3 1.3 %collective-permute-start.4 = (bf16[160,256]{1,0:T(8,128)(2,1)S(1)}, bf16[160,256]{1,0:T(8,128)(2,1)S(1)}, u32[]{:S(2)}, u32[]{:S(2)}) collective-permute-start(bf16[160,256]{1,0:T(8,128)(2,1)S(1)} %get-tuple-element.47.value_mine), channel_id=1, source_target_pairs={{0,2},{1,3},{4,6},{5,7},{8,10},{9,11},{12,14},{13,15},{16,18},{17,... | collective-permute-start | bytes 245768 | tf_op jit(solution)/shard_map/ppermute | solution.py:469
  11.6 0.0 collective-permute-done.sib
  11.6 1.4 %local_scores.1 = (bf16[2,320,128]{2,1,0:T(8,128)(2,1)S(1)}, bf16[2,1280,128]{2,1,0:T(8,128)(2,1)S(1)}, bf16[2,1280,128]{2,1,0:T(8,128)(2,1)S(1)}, f32[1,1280]{1...) custom-call(bf16[160,256]{1,0:T(8,128)(2,1)S(1)} %get-tuple-element., ...), custom_call_target="tpu_custom_call" | custom-call | flops 3000000 | bytes 1000 | tf_op jit(solution)/shard_map/local_scores/pallas_call | solution.py:424
  13.0 0.0 collective-permute-done.1.refs_0_
  13.0 0.0 collective-permute-done.2.refs_1_
  13.0 1.3 %collective-permute-start.6 = (bf16[160,256]{1,0:T(8,128)(2,1)S(1)}, bf16[160,256]{1,0:T(8,128)(2,1)S(1)}, u32[]{:S(2)}, u32[]{:S(2)}) collective-permute-start(bf16[160,256]{1,0:T(8,128)(2,1)S(1)} %get-tuple-element.76), channel_id=1, source_target_pairs={{3,0},{2,1},{7,4},{6,5},{11,8},{10,9},{15,12},{14,13},{19,16},{18,... | collective-permute-start | bytes 245768 | tf_op jit(solution)/shard_map/ppermute | solution.py:524
  14.3 0.0 collective-permute-done.3.refs_0_
  14.3 0.8 %collective-permute-done.4.refs_1_ = bf16[160,256]{1,0:T(8,128)(2,1)S(1)} collective-permute-done((bf16[160,256]{1,0:T(8,128)(2,1)S(1)}, bf16[160,256]{1,0:T(8,128)(2,1)S(1)}, u32[]{:S(2)}, u32[]{:S(2)}) %collective-permute-start.4) | collective-permute-done | bytes 81952 | tf_op jit(solution)/shard_map/ppermute | solution.py:469
  15.1 1.3 %collective-permute-start.8 = (bf16[160,512]{1,0:T(8,128)(2,1)S(1)}, bf16[160,512]{1,0:T(8,128)(2,1)S(1)}, u32[]{:S(2)}, u32[]{:S(2)}) collective-permute-start(bf16[160,512]{1,0:T(8,128)(2,1)S(1)} %get-tuple-element.79), channel_id=1, source_target_pairs={{2,0},{3,1},{6,4},{7,5},{10,8},{11,9},{14,12},{15,13},{18,16},{19,... | collective-permute-start | bytes 491528 | tf_op jit(solution)/shard_map/ppermute | solution.py:469
  16.4 1.3 %collective-permute-start.7 = (bf16[160,256]{1,0:T(8,128)(2,1)S(1)}, bf16[160,256]{1,0:T(8,128)(2,1)S(1)}, u32[]{:S(2)}, u32[]{:S(2)}) collective-permute-start(bf16[160,256]{1,0:T(8,128)(2,1)S(1)} %get-tuple-element.78), channel_id=1, source_target_pairs={{3,0},{2,1},{7,4},{6,5},{11,8},{10,9},{15,12},{14,13},{19,16},{18,... | collective-permute-start | bytes 245768 | tf_op jit(solution)/shard_map/ppermute | solution.py:468
  17.7 2.1 %near_grads.1 = (f32[160,512]{1,0:T(8,128)S(1)}, bf16[160,1024]{1,0:T(8,128)(2,1)S(1)}, f32[1,160]{1,0:T(1,128)S(1)}, bf16[176,1536]{1,0:T(8,128)(2,1)S(1)}) custom-call(f32[2,320,1280]{2,1,0:T(8,128)S(1)} %get-tuple-element.55.raws, f32[2,320,1280]{2,1,0:T(8,128)S(1)} %get-tuple-element.56.grads, f32[2,1,1280]{2,1,0:T(1,128)S(1)} %get-tuple-element.62.factors, ...), custom_call_target="tpu_custom_call" | custom-call | flops 4000000 | bytes 1000 | tf_op jit(solution)/shard_map/near_grads/pallas_call | solution.py:424
  19.8 0.1 collective-permute-start.5
  19.9 0.0 collective-permute-done.6.refs_0_
  19.9 5.8 %collective-permute-done.7.refs_0_ = bf16[160,256]{1,0:T(8,128)(2,1)S(1)} collective-permute-done((bf16[160,256]{1,0:T(8,128)(2,1)S(1)}, bf16[160,256]{1,0:T(8,128)(2,1)S(1)}, u32[]{:S(2)}, u32[]{:S(2)}) %collective-permute-start.7) | collective-permute-done | bytes 81952 | tf_op jit(solution)/shard_map/ppermute | solution.py:468
  25.7 0.1 collective-permute-done.8.refs_1_
  25.8 0.1 sum_rest.1
  25.9 0.0 collective-permute-done.5.back
  25.9 1.7 %finish.1 = (bf16[160,2048]{1,0:T(8,128)(2,1)}, bf16[160,512]{1,0:T(8,128)(2,1)}, bf16[160,512]{1,0:T(8,128)(2,1)}, f32[1,160]{1,0:T(1,128)}) custom-call(bf16[176,1536]{1,0:T(8,128)(2,1)S(1)} %collective-permute-done.5.back, bf16[160,1024]{1,0:T(8,128)(2,1)S(1)} %get-tuple-element.74.query_mine, f32[1,160]{1,0:T(1,128)S(1)} %get-tuple-element.75.gate_mine, ...), custom_call_target="tpu_custom_call" | custom-call | flops 1000000 | bytes 1000 | tf_op jit(solution)/shard_map/finish/pallas_call | solution.py:424
  (3 shorter events, 0.0 us)
Async XLA Ops:
  0.6 1.4 %copy-start = (bf16[1,160,2048]{2,1,0:T(8,128)(2,1)S(1)}, bf16[1,160,2048]{2,1,0:T(8,128)(2,1)}, u32[]{:S(2)}) copy-start(bf16[1,160,2048]{2,1,0:T(8,128)(2,1)} %param.7) | copy-start | bytes 1966084
  0.6 1.5 %copy-start.1 = (bf16[1,160,2048]{2,1,0:T(8,128)(2,1)S(1)}, bf16[1,160,2048]{2,1,0:T(8,128)(2,1)}, u32[]{:S(2)}) copy-start(bf16[1,160,2048]{2,1,0:T(8,128)(2,1)} %param.10) | copy-start | bytes 1966084
  0.7 1.5 %copy-start.2 = (s32[1,160]{1,0:T(1,128)S(1)}, s32[1,160]{1,0:T(1,128)}, u32[]{:S(2)}) copy-start(s32[1,160]{1,0:T(1,128)} %pos_ref.1) | copy-start | bytes 1924
  0.7 1.4 %copy-start.3 = (f32[1,160]{1,0:T(1,128)S(1)}, f32[1,160]{1,0:T(1,128)}, u32[]{:S(2)}) copy-start(f32[1,160]{1,0:T(1,128)} %gate.1) | copy-start | bytes 1924
  2.6 8.9 %collective-permute-start = (bf16[176,2560]{1,0:T(8,128)(2,1)S(1)}, bf16[176,2560]{1,0:T(8,128)(2,1)S(1)}, u32[]{:S(2)}, u32[]{:S(2)}) collective-permute-start(bf16[176,2560]{1,0:T(8,128)(2,1)S(1)} %get-tuple-element.54), channel_id=1, source_target_pairs={{0,1},{1,0},{2,3},{3,2},{4,5},{5,4},{6,7},{7,6},{8,9},{9,8},{10,11... | collective-permute-start | bytes 2703368 | tf_op jit(solution)/shard_map/ppermute | solution.py:489
  3.2 9.8 %collective-permute-start.1 = (bf16[160,256]{1,0:T(8,128)(2,1)S(1)}, bf16[160,256]{1,0:T(8,128)(2,1)S(1)}, u32[]{:S(2)}, u32[]{:S(2)}) collective-permute-start(bf16[160,256]{1,0:T(8,128)(2,1)S(1)} %get-tuple-element.50.key), channel_id=1, source_target_pairs={{0,3},{1,2},{4,7},{5,6},{8,11},{9,10},{12,15},{13,14},{16,19},{17,... | collective-permute-start | bytes 245768 | tf_op jit(solution)/shard_map/ppermute | solution.py:468
  7.7 5.3 %collective-permute-start.2 = (bf16[160,256]{1,0:T(8,128)(2,1)S(1)}, bf16[160,256]{1,0:T(8,128)(2,1)S(1)}, u32[]{:S(2)}, u32[]{:S(2)}) collective-permute-start(bf16[160,256]{1,0:T(8,128)(2,1)S(1)} %get-tuple-element.46.key_mine), channel_id=1, source_target_pairs={{0,2},{1,3},{4,6},{5,7},{8,10},{9,11},{12,14},{13,15},{16,18},{17,... | collective-permute-start | bytes 245768 | tf_op jit(solution)/shard_map/ppermute | solution.py:469
  9.0 5.3 %collective-permute-start.3 = (bf16[160,256]{1,0:T(8,128)(2,1)S(1)}, bf16[160,256]{1,0:T(8,128)(2,1)S(1)}, u32[]{:S(2)}, u32[]{:S(2)}) collective-permute-start(bf16[160,256]{1,0:T(8,128)(2,1)S(1)} %get-tuple-element.51.value), channel_id=1, source_target_pairs={{0,3},{1,2},{4,7},{5,6},{8,11},{9,10},{12,15},{13,14},{16,19},{17,... | collective-permute-start | bytes 245768 | tf_op jit(solution)/shard_map/ppermute | solution.py:468
  10.3 4.8 %collective-permute-start.4 = (bf16[160,256]{1,0:T(8,128)(2,1)S(1)}, bf16[160,256]{1,0:T(8,128)(2,1)S(1)}, u32[]{:S(2)}, u32[]{:S(2)}) collective-permute-start(bf16[160,256]{1,0:T(8,128)(2,1)S(1)} %get-tuple-element.47.value_mine), channel_id=1, source_target_pairs={{0,2},{1,3},{4,6},{5,7},{8,10},{9,11},{12,14},{13,15},{16,18},{17,... | collective-permute-start | bytes 245768 | tf_op jit(solution)/shard_map/ppermute | solution.py:469
  13.0 6.9 %collective-permute-start.6 = (bf16[160,256]{1,0:T(8,128)(2,1)S(1)}, bf16[160,256]{1,0:T(8,128)(2,1)S(1)}, u32[]{:S(2)}, u32[]{:S(2)}) collective-permute-start(bf16[160,256]{1,0:T(8,128)(2,1)S(1)} %get-tuple-element.76), channel_id=1, source_target_pairs={{3,0},{2,1},{7,4},{6,5},{11,8},{10,9},{15,12},{14,13},{19,16},{18,... | collective-permute-start | bytes 245768 | tf_op jit(solution)/shard_map/ppermute | solution.py:524
  15.1 10.8 %collective-permute-start.8 = (bf16[160,512]{1,0:T(8,128)(2,1)S(1)}, bf16[160,512]{1,0:T(8,128)(2,1)S(1)}, u32[]{:S(2)}, u32[]{:S(2)}) collective-permute-start(bf16[160,512]{1,0:T(8,128)(2,1)S(1)} %get-tuple-element.79), channel_id=1, source_target_pairs={{2,0},{3,1},{6,4},{7,5},{10,8},{11,9},{14,12},{15,13},{18,16},{19,... | collective-permute-start | bytes 491528 | tf_op jit(solution)/shard_map/ppermute | solution.py:469
  16.4 9.4 %collective-permute-start.7 = (bf16[160,256]{1,0:T(8,128)(2,1)S(1)}, bf16[160,256]{1,0:T(8,128)(2,1)S(1)}, u32[]{:S(2)}, u32[]{:S(2)}) collective-permute-start(bf16[160,256]{1,0:T(8,128)(2,1)S(1)} %get-tuple-element.78), channel_id=1, source_target_pairs={{3,0},{2,1},{7,4},{6,5},{11,8},{10,9},{15,12},{14,13},{19,16},{18,... | collective-permute-start | bytes 245768 | tf_op jit(solution)/shard_map/ppermute | solution.py:468
  19.8 6.1 %collective-permute-start.5 = (bf16[176,1536]{1,0:T(8,128)(2,1)S(1)}, bf16[176,1536]{1,0:T(8,128)(2,1)S(1)}, u32[]{:S(2)}, u32[]{:S(2)}) collective-permute-start(bf16[176,1536]{1,0:T(8,128)(2,1)S(1)} %get-tuple-element.73), channel_id=1, source_target_pairs={{0,1},{1,0},{2,3},{3,2},{4,5},{5,4},{6,7},{7,6},{8,9},{9,8},{10,11... | collective-permute-start | bytes 1622024 | tf_op jit(solution)/shard_map/ppermute | solution.py:572

commit v11 on v10

--- a/solution.py
+++ b/solution.py
@@ -77,23 +77,28 @@
     return jnp.sum(rows.astype(F32), axis=0, keepdims=True)
 
 
-def pack_keys_kernel(
-    key_in, value_in, pos_in, freq_in, key_mine, key_theirs, value_mine, value_theirs, cos_ref, sin_ref,
-    key, value, pos, freq, sems, *, limit
+def pack_kernel(
+    key_in, value_in, query_in, cot_in, gate_in, pos_in, freq_in,
+    key_mine, key_theirs, value_mine, value_theirs, theirs, gate_mine, cos_ref, sin_ref,
+    key, value, query, gate, pos, freq, sems, *, limit
 ):
-    loads = [(pos_in, pos), (freq_in, freq), (key_in, key), (value_in, value)]
+    rows, width = key.shape
+    side_width = width // 2
+    half = query.shape[1]
+    core = core_of()
+    there = pl.ds(pl.multiple_of((1 - core) * half, DH), half)
+    loads = [(pos_in, pos), (freq_in, freq), (key_in, key), (value_in, value), (query_in.at[:, there], query)]
+    loads += [(gate_in, gate), (cot_in.at[:, there], theirs.at[:rows, half : 2 * half])]
     loads = [pltpu.make_async_copy(source, target, sems.at[i]) for i, (source, target) in enumerate(loads)]
     for copy in loads:
         copy.start()
-    rows, width = key.shape
-    half = width // 2
-    core = core_of()
     down = lax.broadcasted_iota(jnp.int32, (rows, rows), 0)
     along = lax.broadcasted_iota(jnp.int32, (rows, rows), 1)
     lane = lax.broadcasted_iota(jnp.int32, (rows, DH), 1)
     loads[0].wait()
     loads[1].wait()
-    column = jnp.sum(jnp.where(down == along, pos[...].astype(F32), 0.0), axis=1, keepdims=True)
+    places = pos[...]
+    column = jnp.sum(jnp.where(down == along, places.astype(F32), 0.0), axis=1, keepdims=True)
     sine, cosine = sine_cosine(column * freq[...])
     sine = jnp.where(lane < DH // 2, -sine, sine)
     cos_ref[...] = cosine
@@ -102,29 +107,23 @@
     loads[2].wait()
     loads[3].wait()
     for key_out, value_out, side in ((key_mine, value_mine, core), (key_theirs, value_theirs, 1 - core)):
-        for i in range(half // DH):
-            there = pl.ds(pl.multiple_of(side * half + i * DH, DH), DH)
-            turned = rotate(key[:, there].astype(F32), cosine, sine)
-            key_out[:, i * DH : (i + 1) * DH] = jnp.where(used, turned, UNUSED).astype(BF16)
-            value_out[:, i * DH : (i + 1) * DH] = value[:, there]
-
-
-def pack_queries_kernel(query, cot, gate, pos, cos_ref, sin_ref, key, value, mine, theirs, gate_mine, *, limit):
-    rows = query.shape[0]
-    half, width = query.shape[1] // 2, key.shape[1]
-    core = core_of()
-    used_gate = jnp.where(pos[...] < limit, gate[...], 0.0)
+        for i in range(side_width // DH):
+            from_ = pl.ds(pl.multiple_of(side * side_width + i * DH, DH), DH)
+            turned = jnp.where(used, rotate(key[:, from_].astype(F32), cosine, sine), UNUSED).astype(BF16)
+            key_out[:, i * DH : (i + 1) * DH] = turned
+            value_out[:, i * DH : (i + 1) * DH] = value[:, from_]
+    theirs[:rows, 2 * half : 2 * half + side_width] = key_theirs[...]
+    theirs[:rows, 2 * half + side_width :] = value_theirs[...]
+    loads[4].wait()
+    cosine, sine = cosine * (SCALE * LOG2E), sine * (SCALE * LOG2E)
+    for i in range(half // DH):
+        here = slice(i * DH, (i + 1) * DH)
+        theirs[:rows, here] = rotate(query[:, here].astype(F32), cosine, sine).astype(BF16)
+    loads[5].wait()
+    used_gate = jnp.where(places < limit, gate[...], 0.0)
     gate_mine[...] = used_gate
     theirs[rows:, :rows] = split_rows(used_gate, EXTRA)
-    theirs[:rows, 2 * half : 2 * half + width] = key[...]
-    theirs[:rows, 2 * half + width :] = value[...]
-    cosine, sine = cos_ref[...] * (SCALE * LOG2E), sin_ref[...] * (SCALE * LOG2E)
-    for out_ref, side in ((mine, core), (theirs, 1 - core)):
-        for i in range(half // DH):
-            there = pl.ds(pl.multiple_of(side * half + i * DH, DH), DH)
-            turned = rotate(query[:, there].astype(F32), cosine, sine)
-            out_ref[:rows, i * DH : (i + 1) * DH] = turned.astype(BF16)
-        out_ref[:rows, half : 2 * half] = cot[:, pl.ds(pl.multiple_of(side * half, DH), half)]
+    loads[6].wait()
 
 
 def chosen(shape, ratio, dim):
@@ -148,8 +147,8 @@
 
 
 def local_kernel(
-    key_mine, value_mine, mine, gate_mine, sib, keys, query, cot, gate, raws, grads, tops, sums, crosses, values,
-    *, ratio
+    key_mine, value_mine, query_in, cot_in, cos_ref, sin_ref, gate_mine, sib,
+    keys, query, cot, gate, raws, grads, tops, sums, crosses, values, *, ratio
 ):
     rows = key_mine.shape[0]
     half_groups = keys.shape[0]
@@ -159,7 +158,8 @@
     spread = chosen((rows, wide), ratio, 1)
     key_sib = sib.at[:rows, 2 * half : 2 * half + half_groups * DH]
     value_sib = sib.at[:rows, 2 * half + half_groups * DH :]
-    for key, value, packet, side in ((key_mine, value_mine, mine, core), (key_sib, value_sib, sib, 1 - core)):
+    cosine, sine = cos_ref[...] * (SCALE * LOG2E), sin_ref[...] * (SCALE * LOG2E)
+    for key, value, side in ((key_mine, value_mine, core), (key_sib, value_sib, 1 - core)):
         there = pl.ds(pl.multiple_of(side * rows, 16), rows)
         for i in range(half_groups):
             keys[i, there, :] = key[:, i * DH : (i + 1) * DH]
@@ -167,8 +167,13 @@
             for h in range(ratio):
                 to = pl.ds(pl.multiple_of(side * wide + h * rows, 16), rows)
                 at = (i * ratio + h) * DH
-                query[i, to, :] = packet[:rows, at : at + DH]
-                cot[i, to, :] = packet[:rows, half + at : half + at + DH]
+                if key is key_mine:
+                    here = pl.ds(pl.multiple_of(core * half + at, DH), DH)
+                    query[i, to, :] = rotate(query_in[:, here].astype(F32), cosine, sine).astype(BF16)
+                    cot[i, to, :] = cot_in[:, here]
+                else:
+                    query[i, to, :] = sib[:rows, at : at + DH]
+                    cot[i, to, :] = sib[:rows, half + at : half + at + DH]
     own = joined_row(dot(split_rows(gate_mine[...], EXTRA), spread, NN))
     other = joined_row(dot(sib[rows:, :rows], spread, NN))
     gate[:, :wide] = jnp.where(core == 0, own, other)
@@ -207,8 +212,8 @@
 
 def far_keys_kernel(query, cot, gate, tops, sums, *refs, blocks):
     packets = refs[:blocks]
-    far_keys, raws, weights, factors, far_factors, shrinks, inverses = refs[blocks : blocks + 7]
-    parts = refs[blocks + 7 :]
+    far_keys, raws, factors, far_factors, shrinks, inverses = refs[blocks : blocks + 6]
+    parts, weights = refs[blocks + 6 : -1], refs[-1]
     rows = packets[0].shape[0]
     half_groups, lanes = query.shape[:2]
     alone = lax.axis_index("ctx") < 2
@@ -251,7 +256,7 @@
                 out_ref[:, i * DH : (i + 1) * DH] = dot(weights[i, there, :], cot[i], NN).astype(BF16)
 
 
-def far_values_kernel(query, cot, raws, weights, far_factors, shrinks, inverses, crosses, *refs, blocks):
+def far_values_kernel(query, cot, raws, far_factors, shrinks, inverses, crosses, *refs, blocks):
     packets = refs[:blocks]
     score_grads, deltas = refs[blocks : blocks + 2]
     parts, far_values = refs[blocks + 2 : -1], refs[-1]
@@ -282,9 +287,6 @@
                 there = slice(j * rows, (j + 1) * rows)
                 part = dot(score_grads[i, there, :], query[i], NN) * LN2
                 out_ref[:, i * DH : (i + 1) * DH] = part.astype(BF16)
-                if j >= blocks // 2:
-                    part = dot(weights[i, there, :], cot[i], NN)
-                    out_ref[:, (half_groups + i) * DH : (half_groups + i + 1) * DH] = part.astype(BF16)
 
 
 def near_kernel(
@@ -337,43 +339,42 @@
     theirs[rows:, :rows] = split_rows(jnp.where(core == 0, gates[1], gates[0]), EXTRA)
 
 
-def sum_first_kernel(*refs):
-    got, other = refs[:-1], refs[-1]
-    total = got[0][...].astype(F32)
-    for ref in got[1:]:
-        total = total + ref[...].astype(F32)
-    other[...] = total
-
-
-def sum_rest_kernel(value_in, part_mine, *refs):
-    got, (key_own, value_own, key_other, value_other) = refs[:-4], refs[-4:]
-    half = value_in.shape[1]
-    value_other[...] = value_in[...]
+def sum_first_kernel(part_mine, *refs):
+    got, (own, other) = refs[:-2], refs[-2:]
     total = got[0][...].astype(F32)
     for ref in got[2::2]:
         total = total + ref[...].astype(F32)
-    key_other[...] = total
-    for i in range(half // DH):
-        here, there = slice(i * DH, (i + 1) * DH), slice(half + i * DH, half + (i + 1) * DH)
-        key = part_mine[:, 2 * i * DH : (2 * i + 1) * DH]
+    other[...] = total
+    for i in range(own.shape[1] // DH):
+        here = slice(i * DH, (i + 1) * DH)
         value = part_mine[:, (2 * i + 1) * DH : (2 * i + 2) * DH]
         for ref in got[1::2]:
+            value = value + ref[:, here].astype(F32)
+        own[:, here] = value
+
+
+def sum_rest_kernel(value_own, part_mine, *refs):
+    got, (own, other) = refs[:-2], refs[-2:]
+    total = got[0][...].astype(F32)
+    for ref in got[2::2]:
+        total = total + ref[...].astype(F32)
+    other[...] = total
+    for i in range(own.shape[1] // DH):
+        here = slice(i * DH, (i + 1) * DH)
+        key = part_mine[:, 2 * i * DH : (2 * i + 1) * DH]
+        for ref in got[1::2]:
             key = key + ref[:, here].astype(F32)
-            value = value + ref[:, there].astype(F32)
-        key_own[:, here] = key
-        value_own[:, here] = value
+        own[:, here] = key
 
 
 def finish_kernel(
     back, query_mine, gate_mine, key_own, value_own, key_other, value_other, pos_ref, cos_ref, sin_ref,
-    query_out, key_out, value_out, gate_grad, query, key, value, sems, *, limit
+    query_grad, key_grad, value_grad, gate_grad, *, limit
 ):
     rows, half = value_own.shape
     wide = query_mine.shape[1]
     core = core_of()
     side = lambda which, width, at=0, size=None: pl.ds(pl.multiple_of(which * width + at, DH), size or width)
-    copies = [pltpu.make_async_copy(query_mine, query_out.at[:, side(core, wide)], sems.at[0])]
-    copies[0].start()
     cosine, sine = cos_ref[...], -sin_ref[...]
     for i in range(half // DH):
         here = slice(i * DH, (i + 1) * DH)
@@ -385,24 +386,14 @@
             (other_key, other_value, 1 - core),
         ):
             to = side(which, half, i * DH, DH)
-            key[:, to] = rotate(key_sum, cosine, sine).astype(BF16)
-            value[:, to] = value_sum.astype(BF16)
-    copies.append(pltpu.make_async_copy(key, key_out, sems.at[1]))
-    copies.append(pltpu.make_async_copy(value, value_out, sems.at[2]))
-    copies[1].start()
-    copies[2].start()
-    for part in range(2):
-        low = part * (wide // 2)
-        for i in range(wide // 2 // DH):
-            here = slice(low + i * DH, low + (i + 1) * DH)
-            query[:, here] = rotate(back[:rows, here].astype(F32), cosine, sine).astype(BF16)
-        to = query_out.at[:, side(1 - core, wide, low, wide // 2)]
-        copies.append(pltpu.make_async_copy(query.at[:, low : low + wide // 2], to, sems.at[3 + part]))
-        copies[-1].start()
+            key_grad[:, to] = rotate(key_sum, cosine, sine).astype(BF16)
+            value_grad[:, to] = value_sum.astype(BF16)
+    query_grad[:, side(core, wide)] = query_mine[...]
+    for i in range(wide // DH):
+        turned = rotate(back[:rows, i * DH : (i + 1) * DH].astype(F32), cosine, sine)
+        query_grad[:, side(1 - core, wide, i * DH, DH)] = turned.astype(BF16)
     gate = gate_mine[...] + joined_row(back[rows:, :rows])
     gate_grad[...] = jnp.where(pos_ref[...] < limit, gate, 0.0)
-    for copy in copies:
-        copy.wait()
 
 
 def per_device(query_rows, key_rows, value_rows, cotangent, router_gate, positions):
@@ -417,7 +408,7 @@
     wide = ratio * rows
     params = pltpu.CompilerParams(vmem_limit_bytes=(16 + 4 * chips) * 1024 * 1024)
 
-    def call(kernel, name, outs, *args, scratch=(), flops=10**6, in_hbm=False, out_hbm=0):
+    def call(kernel, name, outs, *args, scratch=(), flops=10**6, in_hbm=False):
         if in_hbm:
             args = [pltpu.with_memory_space_constraint(arg, pltpu.HBM) for arg in args]
         spec = pl.BlockSpec(memory_space=pltpu.HBM if in_hbm else pltpu.VMEM)
@@ -425,9 +416,6 @@
             kernel,
             out_shape=[jax.ShapeDtypeStruct(*out) for out in outs],
             in_specs=[spec] * len(args),
-            out_specs=[
-                pl.BlockSpec(memory_space=pltpu.HBM if i < out_hbm else pltpu.VMEM) for i in range(len(outs))
-            ],
             scratch_shapes=list(scratch),
             compiler_params=params,
             cost_estimate=pl.CostEstimate(flops=flops, bytes_accessed=1000, transcendentals=0),
@@ -438,12 +426,17 @@
     freq = jnp.asarray((THETA ** (-2.0 * index / DH)).astype(np.float32))[None]
     packet = ((rows, group_width // 2), BF16)
     table = ((rows, DH), F32)
-    key_mine, key_theirs, value_mine, value_theirs, cosine, sine = call(
-        functools.partial(pack_keys_kernel, limit=limit),
-        "pack_keys",
-        [packet, packet, packet, packet, table, table],
+    line = ((1, rows), F32)
+    theirs_shape = ((rows + EXTRA, heads_width + group_width), BF16)
+    key_mine, key_theirs, value_mine, value_theirs, theirs, gate_mine, cosine, sine = call(
+        functools.partial(pack_kernel, limit=limit),
+        "pack",
+        [packet, packet, packet, packet, theirs_shape, line, table, table],
         key_rows[0],
         value_rows[0],
+        query_rows[0],
+        cotangent[0],
+        router_gate,
         positions,
         freq,
         in_hbm=True,
@@ -451,9 +444,11 @@
         scratch=[
             pltpu.VMEM((rows, group_width), BF16),
             pltpu.VMEM((rows, group_width), BF16),
+            pltpu.VMEM((rows, half_width), BF16),
+            pltpu.VMEM(*line),
             pltpu.VMEM((1, rows), jnp.int32),
             pltpu.VMEM((1, DH), F32),
-            pltpu.SemaphoreType.DMA((4,)),
+            pltpu.SemaphoreType.DMA((7,)),
         ],
     )
 
@@ -472,19 +467,6 @@
     sib_values, own_values = send([value_theirs] * chips, [value_mine] * chips, cross, hop)
 
     pairs = [[2 * x, 2 * x + 1] for x in range(chips)]
-    mine, theirs, gate_mine = call(
-        functools.partial(pack_queries_kernel, limit=limit),
-        "pack_queries",
-        [((rows, heads_width), BF16), ((rows + EXTRA, heads_width + group_width), BF16), ((1, rows), F32)],
-        query_rows[0],
-        cotangent[0],
-        router_gate,
-        positions,
-        cosine,
-        sine,
-        key_theirs,
-        value_theirs,
-    )
     swap = [pair for a, b in pairs for pair in ((a, b), (b, a))]
     sib = lax.ppermute(theirs, "ctx", swap)
 
@@ -498,7 +480,10 @@
         [kv_table, q_table, q_table, ((1, 2 * wide), F32), table, table, row, row, row],
         key_mine,
         value_mine,
-        mine,
+        query_rows[0],
+        cotangent[0],
+        cosine,
+        sine,
         gate_mine,
         sib,
         scratch=[pltpu.VMEM(*kv_table)],
@@ -509,10 +494,10 @@
     far_rows = ((half_groups, blocks * rows, DH), BF16)
     far_low = ((half_groups, blocks * rows, 2 * wide), BF16)
     far_table = (far_low[0], F32 if chips == 2 else BF16)
-    far_keys, far_raws, weights, factors, far_factors, shrinks, inverses, *parts = call(
+    far_keys, far_raws, factors, far_factors, shrinks, inverses, *parts = call(
         functools.partial(far_keys_kernel, blocks=blocks),
         "far_keys",
-        [far_rows, far_table, far_low, row, row, row, row] + [packet] * (chips - 1),
+        [far_rows, far_table, row, row, row, row] + [packet] * blocks,
         query,
         cot,
         gate_row,
@@ -520,16 +505,16 @@
         sums,
         *sib_keys,
         *own_keys,
-    )
-    sib_value_got = [lax.ppermute(parts[s - 1], "ctx", back_cross[s]) for s in steps]
+        scratch=[pltpu.VMEM(*far_low)],
+    )
+    sib_value_got, own_value_got = send(parts[: chips - 1], parts[chips - 1 :], back_cross, back_hop)
     far_grads, deltas, *parts = call(
         functools.partial(far_values_kernel, blocks=blocks),
         "far_values",
-        [far_low, row] + [packet] * (chips - 1) + [((rows, group_width), BF16)] * (chips - 1),
+        [far_low, row] + [packet] * blocks,
         query,
         cot,
         far_raws,
-        weights,
         far_factors,
         shrinks,
         inverses,
@@ -538,9 +523,9 @@
         *own_values,
         scratch=[pltpu.VMEM(*far_rows)],
     )
-    sib_key_got, own_got = send(parts[: chips - 1], parts[chips - 1 :], back_cross, back_hop)
-
-    part_mine, query_mine, gate_mine, theirs = call(
+    sib_key_got, own_key_got = send(parts[: chips - 1], parts[chips - 1 :], back_cross, back_hop)
+
+    part_mine, query_mine, gate_part, theirs = call(
         functools.partial(near_kernel, ratio=ratio),
         "near_grads",
         [
@@ -571,34 +556,37 @@
     )
     back = lax.ppermute(theirs, "ctx", swap)
     total = ((rows, group_width // 2), F32)
-    (value_other,) = call(sum_first_kernel, "sum_first", [total], *sib_value_got, flops=5 * 10**9)
-    sums = call(
+    value_own, value_other = call(
+        sum_first_kernel,
+        "sum_first",
+        [total, total],
+        part_mine,
+        *[part for pair in zip(sib_value_got, own_value_got) for part in pair],
+        flops=5 * 10**9,
+    )
+    key_own, key_other = call(
         sum_rest_kernel,
         "sum_rest",
-        [total] * 4,
-        value_other,
+        [total, total],
+        value_own,
         part_mine,
-        *[part for pair in zip(sib_key_got, own_got) for part in pair],
+        *[part for pair in zip(sib_key_got, own_key_got) for part in pair],
         flops=5 * 10**9,
     )
     query_grad, key_grad, value_grad, gate_grad = call(
         functools.partial(finish_kernel, limit=limit),
         "finish",
-        [((rows, heads_width), BF16)] + [((rows, group_width), BF16)] * 2 + [((1, rows), F32)],
+        [((rows, heads_width), BF16)] + [((rows, group_width), BF16)] * 2 + [line],
         back,
         query_mine,
-        gate_mine,
-        *sums,
+        gate_part,
+        key_own,
+        value_own,
+        key_other,
+        value_other,
         positions,
         cosine,
         sine,
-        out_hbm=3,
-        scratch=[
-            pltpu.VMEM((rows, half_width), BF16),
-            pltpu.VMEM((rows, group_width), BF16),
-            pltpu.VMEM((rows, group_width), BF16),
-            pltpu.SemaphoreType.DMA((5,)),
-        ],
     )
     return (query_grad[None], key_grad[None], value_grad[None], gate_grad)
 

time: 28.1 us -> 27.9 us (level)
  waiting for transfers between devices: 6.7 us -> 5.29 us
  starting transfers between devices: 12.8 us -> 14.2 us
  local copies, waits for them, and re-layouts: 0.13 us -> 0.65 us
  Pallas kernels: 7.14 us -> 6.62 us
    ppermute x3 -> x4, waiting for transfers between devices: 5.82 us -> 1.87 us  [send(): sib = [lax.ppermute(sib[s - 1], 'ctx', sib_pairs[s]) for s in steps]]
    ppermute x3 -> x4, waiting for transfers between devices: 0.87 us -> 3.41 us  [send(): return (sib, [lax.ppermute(own[s - 1], 'ctx', own_pairs[s]) for s in steps])]
    ppermute x3 -> x4, starting transfers between devices: 3.87 us -> 5.17 us  [send(): return (sib, [lax.ppermute(own[s - 1], 'ctx', own_pairs[s]) for s in steps])]
    ppermute x3 -> x4, starting transfers between devices: 7.08 us -> 8.38 us  [send(): sib = [lax.ppermute(sib[s - 1], 'ctx', sib_pairs[s]) for s in steps]]
    ppermute x1 -> x0, starting transfers between devices: 1.29 us -> none  [per_device(): lax.ppermute(parts[s - 1], 'ctx', back_cross[s])]
    unnamed x8 -> x6, local copies, waits for them, and re-layouts: 0.13 us -> 0.65 us
    pallas_call x9 -> x8, Pallas kernels: 7.14 us -> 6.62 us  [call(): pl.pallas_call(kernel, out_shape=[jax.ShapeDtypeStruct(*out) for out in o...]
  transfers between devices with their start and end apart: 9 -> 10, of which waited for: 3 -> 3; matrix products, arithmetic and copies ran while one was open for 0% -> 0% of each run, Pallas kernels for 13% -> 14%
where the time goes in v11:
time: 27.9 us; the launch traced here: 27.6 us
  starting transfers between devices  14.2 us (51%)
  Pallas kernels  6.62 us (24%)
  waiting for transfers between devices  5.29 us (19%)
  between operations  0.82 us (3%)
  local copies, waits for them, and re-layouts  0.65 us (2%)
    ppermute x4, starting transfers between devices, send(): sib = [lax.ppermute(sib[s - 1], 'ctx', sib_pairs[s]) for s in steps]  8.38 us
    pallas_call x8, Pallas kernels, call(): pl.pallas_call(kernel, out_shape=[jax.ShapeDtypeStruct(*out) for out in o...  6.62 us
    ppermute x4, starting transfers between devices, send(): return (sib, [lax.ppermute(own[s - 1], 'ctx', own_pairs[s]) for s in steps])  5.17 us
    ppermute x4, waiting for transfers between devices, send(): return (sib, [lax.ppermute(own[s - 1], 'ctx', own_pairs[s]) for s in steps])  3.41 us
    ppermute x4, waiting for transfers between devices, send(): sib = [lax.ppermute(sib[s - 1], 'ctx', sib_pairs[s]) for s in steps]  1.87 us
    unnamed x6, local copies, waits for them, and re-layouts  0.65 us
  transfers between devices with their start and end apart: 10, of which 3 were waited for; matrix products, arithmetic and copies ran while one was open for 0% of the time, Pallas kernels for 14%

profile of v11, /device:TPU:0, one launch (start us, length us, event | category | flops | bytes accessed | tf_op | source)
XLA Modules:
  0.0 27.6 jit_solution(10420653062438542419)
XLA Ops:
  0.6 0.0 copy-start
  0.6 0.0 copy-start.1
  0.7 1.6 %pack.1 = (bf16[160,256]{1,0:T(8,128)(2,1)S(1)}, bf16[160,256]{1,0:T(8,128)(2,1)S(1)}, bf16[160,256]{1,0:T(8,128)(2,1)S(1)}, bf16[160,256]{1,0:T(8,128)(2,1)S(1)...) custom-call(bf16[160,512]{1,0:T(8,128)(2,1)} %bitcast.12, ...), custom_call_target="tpu_custom_call" | custom-call | flops 5000000000 | bytes 1000 | tf_op jit(solution)/shard_map/pack/pallas_call | solution.py:415
  2.2 0.5 %collective-permute-start = (bf16[176,2560]{1,0:T(8,128)(2,1)S(1)}, bf16[176,2560]{1,0:T(8,128)(2,1)S(1)}, u32[]{:S(2)}, u32[]{:S(2)}) collective-permute-start(bf16[176,2560]{1,0:T(8,128)(2,1)S(1)} %get-tuple-element.50), channel_id=1, source_target_pairs={{0,1},{1,0},{2,3},{3,2},{4,5},{5,4},{6,7},{7,6},{8,9},{9,8},{10,11... | collective-permute-start | bytes 2703368 | tf_op jit(solution)/shard_map/ppermute | solution.py:471
  2.8 4.5 %collective-permute-start.1 = (bf16[160,256]{1,0:T(8,128)(2,1)S(1)}, bf16[160,256]{1,0:T(8,128)(2,1)S(1)}, u32[]{:S(2)}, u32[]{:S(2)}) collective-permute-start(bf16[160,256]{1,0:T(8,128)(2,1)S(1)} %get-tuple-element.58), channel_id=1, source_target_pairs={{0,3},{1,2},{4,7},{5,6},{8,11},{9,10},{12,15},{13,14},{16,19},{17,... | collective-permute-start | bytes 245768 | tf_op jit(solution)/shard_map/ppermute | solution.py:463
  7.3 1.3 %collective-permute-start.2 = (bf16[160,256]{1,0:T(8,128)(2,1)S(1)}, bf16[160,256]{1,0:T(8,128)(2,1)S(1)}, u32[]{:S(2)}, u32[]{:S(2)}) collective-permute-start(bf16[160,256]{1,0:T(8,128)(2,1)S(1)} %get-tuple-element.45.key_mine), channel_id=1, source_target_pairs={{0,2},{1,3},{4,6},{5,7},{8,10},{9,11},{12,14},{13,15},{16,18},{17,... | collective-permute-start | bytes 245768 | tf_op jit(solution)/shard_map/ppermute | solution.py:464
  8.6 1.3 %collective-permute-start.3 = (bf16[160,256]{1,0:T(8,128)(2,1)S(1)}, bf16[160,256]{1,0:T(8,128)(2,1)S(1)}, u32[]{:S(2)}, u32[]{:S(2)}) collective-permute-start(bf16[160,256]{1,0:T(8,128)(2,1)S(1)} %get-tuple-element.65), channel_id=1, source_target_pairs={{0,3},{1,2},{4,7},{5,6},{8,11},{9,10},{12,15},{13,14},{16,19},{17,... | collective-permute-start | bytes 245768 | tf_op jit(solution)/shard_map/ppermute | solution.py:463
  9.9 1.3 %collective-permute-start.4 = (bf16[160,256]{1,0:T(8,128)(2,1)S(1)}, bf16[160,256]{1,0:T(8,128)(2,1)S(1)}, u32[]{:S(2)}, u32[]{:S(2)}) collective-permute-start(bf16[160,256]{1,0:T(8,128)(2,1)S(1)} %get-tuple-element.46.value_mine), channel_id=1, source_target_pairs={{0,2},{1,3},{4,6},{5,7},{8,10},{9,11},{12,14},{13,15},{16,18},{17,... | collective-permute-start | bytes 245768 | tf_op jit(solution)/shard_map/ppermute | solution.py:464
  11.2 0.0 collective-permute-done.sib
  11.2 0.0 copy-done
  11.2 0.0 copy-done.1
  11.2 1.5 %local_scores.1 = (bf16[2,320,128]{2,1,0:T(8,128)(2,1)S(1)}, bf16[2,1280,128]{2,1,0:T(8,128)(2,1)S(1)}, bf16[2,1280,128]{2,1,0:T(8,128)(2,1)S(1)}, f32[1,1280]{1...) custom-call(bf16[160,256]{1,0:T(8,128)(2,1)S(1)} %get-tuple-element., ...), custom_call_target="tpu_custom_call" | custom-call | flops 3000000 | bytes 1000 | tf_op jit(solution)/shard_map/local_scores/pallas_call | solution.py:415
  12.7 0.0 collective-permute-done.1.refs_0_
  12.8 0.0 collective-permute-done.2.refs_1_
  12.8 1.3 %collective-permute-start.6 = (bf16[160,256]{1,0:T(8,128)(2,1)S(1)}, bf16[160,256]{1,0:T(8,128)(2,1)S(1)}, u32[]{:S(2)}, u32[]{:S(2)}) collective-permute-start(bf16[160,256]{1,0:T(8,128)(2,1)S(1)} %get-tuple-element.74), channel_id=1, source_target_pairs={{3,0},{2,1},{7,4},{6,5},{11,8},{10,9},{15,12},{14,13},{19,16},{18,... | collective-permute-start | bytes 245768 | tf_op jit(solution)/shard_map/ppermute | solution.py:463
  14.1 1.3 %collective-permute-start.7 = (bf16[160,256]{1,0:T(8,128)(2,1)S(1)}, bf16[160,256]{1,0:T(8,128)(2,1)S(1)}, u32[]{:S(2)}, u32[]{:S(2)}) collective-permute-start(bf16[160,256]{1,0:T(8,128)(2,1)S(1)} %get-tuple-element.75), channel_id=1, source_target_pairs={{2,0},{3,1},{6,4},{7,5},{10,8},{11,9},{14,12},{15,13},{18,16},{19,... | collective-permute-start | bytes 245768 | tf_op jit(solution)/shard_map/ppermute | solution.py:464
  15.4 0.0 collective-permute-done.3.refs_0_
  15.4 0.0 collective-permute-done.4.refs_1_
  15.4 1.3 %collective-permute-start.8 = (bf16[160,256]{1,0:T(8,128)(2,1)S(1)}, bf16[160,256]{1,0:T(8,128)(2,1)S(1)}, u32[]{:S(2)}, u32[]{:S(2)}) collective-permute-start(bf16[160,256]{1,0:T(8,128)(2,1)S(1)} %get-tuple-element.77), channel_id=1, source_target_pairs={{3,0},{2,1},{7,4},{6,5},{11,8},{10,9},{15,12},{14,13},{19,16},{18,... | collective-permute-start | bytes 245768 | tf_op jit(solution)/shard_map/ppermute | solution.py:463
  16.7 1.3 %collective-permute-start.9 = (bf16[160,256]{1,0:T(8,128)(2,1)S(1)}, bf16[160,256]{1,0:T(8,128)(2,1)S(1)}, u32[]{:S(2)}, u32[]{:S(2)}) collective-permute-start(bf16[160,256]{1,0:T(8,128)(2,1)S(1)} %get-tuple-element.78), channel_id=1, source_target_pairs={{2,0},{3,1},{6,4},{7,5},{10,8},{11,9},{14,12},{15,13},{18,16},{19,... | collective-permute-start | bytes 245768 | tf_op jit(solution)/shard_map/ppermute | solution.py:464
  18.0 2.1 %near_grads.1 = (f32[160,512]{1,0:T(8,128)S(1)}, bf16[160,1024]{1,0:T(8,128)(2,1)S(1)}, f32[1,160]{1,0:T(1,128)S(1)}, bf16[176,1536]{1,0:T(8,128)(2,1)S(1)}) custom-call(f32[2,320,1280]{2,1,0:T(8,128)S(1)} %get-tuple-element.51.raws, f32[2,320,1280]{2,1,0:T(8,128)S(1)} %get-tuple-element.52.grads, f32[2,1,1280]{2,1,0:T(1,128)S(1)} %get-tuple-element.59.factors, ...), custom_call_target="tpu_custom_call" | custom-call | flops 4000000 | bytes 1000 | tf_op jit(solution)/shard_map/near_grads/pallas_call | solution.py:415
  20.2 0.2 collective-permute-start.5
  20.4 0.0 collective-permute-done.6.refs_0_
  20.4 0.8 %collective-permute-done.7.refs_1_ = bf16[160,256]{1,0:T(8,128)(2,1)S(1)} collective-permute-done((bf16[160,256]{1,0:T(8,128)(2,1)S(1)}, bf16[160,256]{1,0:T(8,128)(2,1)S(1)}, u32[]{:S(2)}, u32[]{:S(2)}) %collective-permute-start.7) | collective-permute-done | bytes 81952 | tf_op jit(solution)/shard_map/ppermute | solution.py:464
  21.2 1.9 %collective-permute-done.8.refs_0_ = bf16[160,256]{1,0:T(8,128)(2,1)S(1)} collective-permute-done((bf16[160,256]{1,0:T(8,128)(2,1)S(1)}, bf16[160,256]{1,0:T(8,128)(2,1)S(1)}, u32[]{:S(2)}, u32[]{:S(2)}) %collective-permute-start.8) | collective-permute-done | bytes 81952 | tf_op jit(solution)/shard_map/ppermute | solution.py:463
  23.1 2.6 %collective-permute-done.9.refs_1_ = bf16[160,256]{1,0:T(8,128)(2,1)S(1)} collective-permute-done((bf16[160,256]{1,0:T(8,128)(2,1)S(1)}, bf16[160,256]{1,0:T(8,128)(2,1)S(1)}, u32[]{:S(2)}, u32[]{:S(2)}) %collective-permute-start.9) | collective-permute-done | bytes 81952 | tf_op jit(solution)/shard_map/ppermute | solution.py:464
  25.7 0.0 copy-start.2
  25.7 0.0 collective-permute-done.5.back
  25.7 0.6 %copy-done.2 = s32[1,160]{1,0:T(1,128)S(1)} copy-done((s32[1,160]{1,0:T(1,128)S(1)}, s32[1,160]{1,0:T(1,128)}, u32[]{:S(2)}) %copy-start.2) | copy-done | bytes 664
  26.4 1.3 %finish.1 = (bf16[160,2048]{1,0:T(8,128)(2,1)}, bf16[160,512]{1,0:T(8,128)(2,1)}, bf16[160,512]{1,0:T(8,128)(2,1)}, f32[1,160]{1,0:T(1,128)}) custom-call(bf16[176,1536]{1,0:T(8,128)(2,1)S(1)} %collective-permute-done.5.back, bf16[160,1024]{1,0:T(8,128)(2,1)S(1)} %get-tuple-element.71.query_mine, f32[1,160]{1,0:T(1,128)S(1)} %get-tuple-element.72.gate_mine, ...), custom_call_target="tpu_custom_call" | custom-call | flops 1000000 | bytes 1000 | tf_op jit(solution)/shard_map/finish/pallas_call | solution.py:415
  (4 shorter events, 0.1 us)
Async XLA Ops:
  0.6 10.5 %copy-start = (bf16[1,160,2048]{2,1,0:T(8,128)(2,1)S(1)}, bf16[1,160,2048]{2,1,0:T(8,128)(2,1)}, u32[]{:S(2)}) copy-start(bf16[1,160,2048]{2,1,0:T(8,128)(2,1)} %param.7) | copy-start | bytes 1966084
  0.6 10.5 %copy-start.1 = (bf16[1,160,2048]{2,1,0:T(8,128)(2,1)S(1)}, bf16[1,160,2048]{2,1,0:T(8,128)(2,1)}, u32[]{:S(2)}) copy-start(bf16[1,160,2048]{2,1,0:T(8,128)(2,1)} %param.10) | copy-start | bytes 1966084
  2.2 8.9 %collective-permute-start = (bf16[176,2560]{1,0:T(8,128)(2,1)S(1)}, bf16[176,2560]{1,0:T(8,128)(2,1)S(1)}, u32[]{:S(2)}, u32[]{:S(2)}) collective-permute-start(bf16[176,2560]{1,0:T(8,128)(2,1)S(1)} %get-tuple-element.50), channel_id=1, source_target_pairs={{0,1},{1,0},{2,3},{3,2},{4,5},{5,4},{6,7},{7,6},{8,9},{9,8},{10,11... | collective-permute-start | bytes 2703368 | tf_op jit(solution)/shard_map/ppermute | solution.py:471
  2.8 10.0 %collective-permute-start.1 = (bf16[160,256]{1,0:T(8,128)(2,1)S(1)}, bf16[160,256]{1,0:T(8,128)(2,1)S(1)}, u32[]{:S(2)}, u32[]{:S(2)}) collective-permute-start(bf16[160,256]{1,0:T(8,128)(2,1)S(1)} %get-tuple-element.58), channel_id=1, source_target_pairs={{0,3},{1,2},{4,7},{5,6},{8,11},{9,10},{12,15},{13,14},{16,19},{17,... | collective-permute-start | bytes 245768 | tf_op jit(solution)/shard_map/ppermute | solution.py:463
  7.3 5.5 %collective-permute-start.2 = (bf16[160,256]{1,0:T(8,128)(2,1)S(1)}, bf16[160,256]{1,0:T(8,128)(2,1)S(1)}, u32[]{:S(2)}, u32[]{:S(2)}) collective-permute-start(bf16[160,256]{1,0:T(8,128)(2,1)S(1)} %get-tuple-element.45.key_mine), channel_id=1, source_target_pairs={{0,2},{1,3},{4,6},{5,7},{8,10},{9,11},{12,14},{13,15},{16,18},{17,... | collective-permute-start | bytes 245768 | tf_op jit(solution)/shard_map/ppermute | solution.py:464
  8.6 6.8 %collective-permute-start.3 = (bf16[160,256]{1,0:T(8,128)(2,1)S(1)}, bf16[160,256]{1,0:T(8,128)(2,1)S(1)}, u32[]{:S(2)}, u32[]{:S(2)}) collective-permute-start(bf16[160,256]{1,0:T(8,128)(2,1)S(1)} %get-tuple-element.65), channel_id=1, source_target_pairs={{0,3},{1,2},{4,7},{5,6},{8,11},{9,10},{12,15},{13,14},{16,19},{17,... | collective-permute-start | bytes 245768 | tf_op jit(solution)/shard_map/ppermute | solution.py:463
  9.9 5.5 %collective-permute-start.4 = (bf16[160,256]{1,0:T(8,128)(2,1)S(1)}, bf16[160,256]{1,0:T(8,128)(2,1)S(1)}, u32[]{:S(2)}, u32[]{:S(2)}) collective-permute-start(bf16[160,256]{1,0:T(8,128)(2,1)S(1)} %get-tuple-element.46.value_mine), channel_id=1, source_target_pairs={{0,2},{1,3},{4,6},{5,7},{8,10},{9,11},{12,14},{13,15},{16,18},{17,... | collective-permute-start | bytes 245768 | tf_op jit(solution)/shard_map/ppermute | solution.py:464
  12.8 7.6 %collective-permute-start.6 = (bf16[160,256]{1,0:T(8,128)(2,1)S(1)}, bf16[160,256]{1,0:T(8,128)(2,1)S(1)}, u32[]{:S(2)}, u32[]{:S(2)}) collective-permute-start(bf16[160,256]{1,0:T(8,128)(2,1)S(1)} %get-tuple-element.74), channel_id=1, source_target_pairs={{3,0},{2,1},{7,4},{6,5},{11,8},{10,9},{15,12},{14,13},{19,16},{18,... | collective-permute-start | bytes 245768 | tf_op jit(solution)/shard_map/ppermute | solution.py:463
  14.1 7.1 %collective-permute-start.7 = (bf16[160,256]{1,0:T(8,128)(2,1)S(1)}, bf16[160,256]{1,0:T(8,128)(2,1)S(1)}, u32[]{:S(2)}, u32[]{:S(2)}) collective-permute-start(bf16[160,256]{1,0:T(8,128)(2,1)S(1)} %get-tuple-element.75), channel_id=1, source_target_pairs={{2,0},{3,1},{6,4},{7,5},{10,8},{11,9},{14,12},{15,13},{18,16},{19,... | collective-permute-start | bytes 245768 | tf_op jit(solution)/shard_map/ppermute | solution.py:464
  15.4 7.6 %collective-permute-start.8 = (bf16[160,256]{1,0:T(8,128)(2,1)S(1)}, bf16[160,256]{1,0:T(8,128)(2,1)S(1)}, u32[]{:S(2)}, u32[]{:S(2)}) collective-permute-start(bf16[160,256]{1,0:T(8,128)(2,1)S(1)} %get-tuple-element.77), channel_id=1, source_target_pairs={{3,0},{2,1},{7,4},{6,5},{11,8},{10,9},{15,12},{14,13},{19,16},{18,... | collective-permute-start | bytes 245768 | tf_op jit(solution)/shard_map/ppermute | solution.py:463
  16.7 8.9 %collective-permute-start.9 = (bf16[160,256]{1,0:T(8,128)(2,1)S(1)}, bf16[160,256]{1,0:T(8,128)(2,1)S(1)}, u32[]{:S(2)}, u32[]{:S(2)}) collective-permute-start(bf16[160,256]{1,0:T(8,128)(2,1)S(1)} %get-tuple-element.78), channel_id=1, source_target_pairs={{2,0},{3,1},{6,4},{7,5},{10,8},{11,9},{14,12},{15,13},{18,16},{19,... | collective-permute-start | bytes 245768 | tf_op jit(solution)/shard_map/ppermute | solution.py:464
  20.2 5.5 %collective-permute-start.5 = (bf16[176,1536]{1,0:T(8,128)(2,1)S(1)}, bf16[176,1536]{1,0:T(8,128)(2,1)S(1)}, u32[]{:S(2)}, u32[]{:S(2)}) collective-permute-start(bf16[176,1536]{1,0:T(8,128)(2,1)S(1)} %get-tuple-element.70), channel_id=1, source_target_pairs={{0,1},{1,0},{2,3},{3,2},{4,5},{5,4},{6,7},{7,6},{8,9},{9,8},{10,11... | collective-permute-start | bytes 1622024 | tf_op jit(solution)/shard_map/ppermute | solution.py:557
  25.7 0.7 %copy-start.2 = (s32[1,160]{1,0:T(1,128)S(1)}, s32[1,160]{1,0:T(1,128)}, u32[]{:S(2)}) copy-start(s32[1,160]{1,0:T(1,128)} %pos_ref.1) | copy-start | bytes 1924

commit v12 on v11

--- a/solution.py
+++ b/solution.py
@@ -79,7 +79,7 @@
 
 def pack_kernel(
     key_in, value_in, query_in, cot_in, gate_in, pos_in, freq_in,
-    key_mine, key_theirs, value_mine, value_theirs, theirs, gate_mine, cos_ref, sin_ref,
+    key_mine, key_theirs, value_mine, value_theirs, theirs, gate_mine, valid, cos_ref, sin_ref,
     key, value, query, gate, pos, freq, sems, *, limit
 ):
     rows, width = key.shape
@@ -120,6 +120,7 @@
         here = slice(i * DH, (i + 1) * DH)
         theirs[:rows, here] = rotate(query[:, here].astype(F32), cosine, sine).astype(BF16)
     loads[5].wait()
+    valid[...] = jnp.where(places < limit, 1.0, 0.0)
     used_gate = jnp.where(places < limit, gate[...], 0.0)
     gate_mine[...] = used_gate
     theirs[rows:, :rows] = split_rows(used_gate, EXTRA)
@@ -210,7 +211,32 @@
     out_ref[:, (2 * i + 1) * DH : (2 * i + 2) * DH] = value_part.astype(out_ref.dtype)
 
 
-def far_keys_kernel(query, cot, gate, tops, sums, *refs, blocks):
+def early_kernel(query, tops, sums, packet, raws, new_tops, new_sums):
+    half_groups, lanes = query.shape[:2]
+    alone = lax.axis_index("ctx") < 2
+
+    @pl.when(alone)
+    def _():
+        new_tops[...] = tops[...]
+        new_sums[...] = sums[...]
+
+    @pl.when(jnp.logical_not(alone))
+    def _():
+        used = used_slots(packet, 1)
+        for i in range(half_groups):
+            key = packet[:, i * DH : (i + 1) * DH]
+            for here in chunks(0, lanes):
+                width = here.stop - here.start
+                shown = jnp.where(used[:, :width], dot(key, query[i, here, :], NT), HIDDEN)
+                old_top = tops[i, :, here]
+                top = jnp.maximum(old_top, jnp.max(shown, axis=0, keepdims=True))
+                raw = jnp.exp2(shown - top)
+                raws[i, :, here] = raw
+                new_tops[i, :, here] = top
+                new_sums[i, :, here] = sums[i, :, here] * jnp.exp2(old_top - top) + jnp.sum(raw, axis=0, keepdims=True)
+
+
+def far_keys_kernel(query, cot, gate, first_tops, early_raws, tops, sums, *refs, blocks):
     packets = refs[:blocks]
     far_keys, raws, factors, far_factors, shrinks, inverses = refs[blocks : blocks + 6]
     parts, weights = refs[blocks + 6 : -1], refs[-1]
@@ -230,27 +256,32 @@
         for i in range(half_groups):
             for j, packet in enumerate(packets):
                 far_keys[i, j * rows : (j + 1) * rows, :] = packet[:, i * DH : (i + 1) * DH]
-        used = [used_slots(packet, j % (blocks // 2) + 1) for j, packet in enumerate(packets)]
+        used = [used_slots(packets[j], j % (blocks // 2) + 1) for j in range(1, blocks)]
         for i in range(half_groups):
             for here in chunks(0, lanes):
                 width = here.stop - here.start
-                scores = dot(far_keys[i], query[i, here, :], NT)
+                scores = dot(far_keys[i, rows:, :], query[i, here, :], NT)
                 shown = [
-                    jnp.where(used[j][:, :width], scores[j * rows : (j + 1) * rows], HIDDEN) for j in range(blocks)
+                    jnp.where(used[j][:, :width], scores[j * rows : (j + 1) * rows], HIDDEN)
+                    for j in range(blocks - 1)
                 ]
                 shown = jnp.concatenate(shown, axis=0)
                 old_top = tops[i, :, here]
                 top = jnp.maximum(old_top, jnp.max(shown, axis=0, keepdims=True))
                 raw = jnp.exp2(shown - top)
                 shrink = jnp.exp2(old_top - top)
+                first_shrink = jnp.exp2(first_tops[i, :, here] - top)
                 inverse = 1.0 / (sums[i, :, here] * shrink + jnp.sum(raw, axis=0, keepdims=True))
                 factor = inverse * gate[:, here]
-                factors[i, :, here] = factor * shrink
+                factors[i, :, here] = factor * first_shrink
                 far_factors[i, :, here] = factor
-                shrinks[i, :, here] = shrink
+                shrinks[i, :, here] = first_shrink
                 inverses[i, :, here] = inverse
-                raws[i, :, here] = raw.astype(raws.dtype)
-                weights[i, :, here] = (raw * factor).astype(BF16)
+                raws[i, rows:, here] = raw.astype(raws.dtype)
+                weights[i, rows:, here] = (raw * factor).astype(BF16)
+                raw = early_raws[i, :, here] * shrink
+                raws[i, :rows, here] = raw.astype(raws.dtype)
+                weights[i, :rows, here] = (raw * factor).astype(BF16)
             for j, out_ref in enumerate(parts):
                 there = slice(j * rows, (j + 1) * rows)
                 out_ref[:, i * DH : (i + 1) * DH] = dot(weights[i, there, :], cot[i], NN).astype(BF16)
@@ -368,8 +399,8 @@
 
 
 def finish_kernel(
-    back, query_mine, gate_mine, key_own, value_own, key_other, value_other, pos_ref, cos_ref, sin_ref,
-    query_grad, key_grad, value_grad, gate_grad, *, limit
+    back, query_mine, gate_mine, key_own, value_own, key_other, value_other, valid, cos_ref, sin_ref,
+    query_grad, key_grad, value_grad, gate_grad
 ):
     rows, half = value_own.shape
     wide = query_mine.shape[1]
@@ -393,7 +424,7 @@
         turned = rotate(back[:rows, i * DH : (i + 1) * DH].astype(F32), cosine, sine)
         query_grad[:, side(1 - core, wide, i * DH, DH)] = turned.astype(BF16)
     gate = gate_mine[...] + joined_row(back[rows:, :rows])
-    gate_grad[...] = jnp.where(pos_ref[...] < limit, gate, 0.0)
+    gate_grad[...] = jnp.where(valid[...] > 0.0, gate, 0.0)
 
 
 def per_device(query_rows, key_rows, value_rows, cotangent, router_gate, positions):
@@ -428,10 +459,10 @@
     table = ((rows, DH), F32)
     line = ((1, rows), F32)
     theirs_shape = ((rows + EXTRA, heads_width + group_width), BF16)
-    key_mine, key_theirs, value_mine, value_theirs, theirs, gate_mine, cosine, sine = call(
+    key_mine, key_theirs, value_mine, value_theirs, theirs, gate_mine, valid, cosine, sine = call(
         functools.partial(pack_kernel, limit=limit),
         "pack",
-        [packet, packet, packet, packet, theirs_shape, line, table, table],
+        [packet, packet, packet, packet, theirs_shape, line, line, table, table],
         key_rows[0],
         value_rows[0],
         query_rows[0],
@@ -494,6 +525,10 @@
     far_rows = ((half_groups, blocks * rows, DH), BF16)
     far_low = ((half_groups, blocks * rows, 2 * wide), BF16)
     far_table = (far_low[0], F32 if chips == 2 else BF16)
+    early_table = ((half_groups, rows, 2 * wide), F32)
+    early_raws, early_tops, early_sums = call(
+        early_kernel, "early_keys", [early_table, row, row], query, tops, sums, sib_keys[0]
+    )
     far_keys, far_raws, factors, far_factors, shrinks, inverses, *parts = call(
         functools.partial(far_keys_kernel, blocks=blocks),
         "far_keys",
@@ -502,7 +537,9 @@
         cot,
         gate_row,
         tops,
-        sums,
+        early_raws,
+        early_tops,
+        early_sums,
         *sib_keys,
         *own_keys,
         scratch=[pltpu.VMEM(*far_low)],
@@ -574,7 +611,7 @@
         flops=5 * 10**9,
     )
     query_grad, key_grad, value_grad, gate_grad = call(
-        functools.partial(finish_kernel, limit=limit),
+        finish_kernel,
         "finish",
         [((rows, heads_width), BF16)] + [((rows, group_width), BF16)] * 2 + [line],
         back,
@@ -584,7 +621,7 @@
         value_own,
         key_other,
         value_other,
-        positions,
+        valid,
         cosine,
         sine,
     )

time: 27.9 us -> 27.3 us (0.978)
  local copies, waits for them, and re-layouts: 0.65 us -> 0.01 us
    unnamed x6 -> x4, local copies, waits for them, and re-layouts: 0.65 us -> 0.01 us
    ppermute x4, waiting for transfers between devices: 1.87 us -> 2.18 us  [send(): sib = [lax.ppermute(sib[s - 1], 'ctx', sib_pairs[s]) for s in steps]]
    ppermute x4, waiting for transfers between devices: 3.41 us -> 3.11 us  [send(): return (sib, [lax.ppermute(own[s - 1], 'ctx', own_pairs[s]) for s in steps])]
    pallas_call x8 -> x9, Pallas kernels: 6.62 us -> 6.62 us  [call(): pl.pallas_call(kernel, out_shape=[jax.ShapeDtypeStruct(*out) for out in o...]
where the time goes in v12:
time: 27.3 us; the launch traced here: 27 us
  starting transfers between devices  14.2 us (52%)
  Pallas kernels  6.62 us (24%)
  waiting for transfers between devices  5.29 us (19%)
  between operations  0.82 us (3%)
    ppermute x4, starting transfers between devices, send(): sib = [lax.ppermute(sib[s - 1], 'ctx', sib_pairs[s]) for s in steps]  8.38 us
    pallas_call x9, Pallas kernels, call(): pl.pallas_call(kernel, out_shape=[jax.ShapeDtypeStruct(*out) for out in o...  6.62 us
    ppermute x4, starting transfers between devices, send(): return (sib, [lax.ppermute(own[s - 1], 'ctx', own_pairs[s]) for s in steps])  5.17 us
    ppermute x4, waiting for transfers between devices, send(): return (sib, [lax.ppermute(own[s - 1], 'ctx', own_pairs[s]) for s in steps])  3.11 us
    ppermute x4, waiting for transfers between devices, send(): sib = [lax.ppermute(sib[s - 1], 'ctx', sib_pairs[s]) for s in steps]  2.18 us
  transfers between devices with their start and end apart: 10, of which 3 were waited for; matrix products, arithmetic and copies ran while one was open for 0% of the time, Pallas kernels for 14%

profile of v12, /device:TPU:0, one launch (start us, length us, event | category | flops | bytes accessed | tf_op | source)
XLA Modules:
  0.0 27.0 jit_solution(1543336784461700513)
XLA Ops:
  0.6 0.0 copy-start
  0.6 0.0 copy-start.1
  0.7 1.6 %pack.1 = (bf16[160,256]{1,0:T(8,128)(2,1)S(1)}, bf16[160,256]{1,0:T(8,128)(2,1)S(1)}, bf16[160,256]{1,0:T(8,128)(2,1)S(1)}, bf16[160,256]{1,0:T(8,128)(2,1)S(1)...) custom-call(bf16[160,512]{1,0:T(8,128)(2,1)} %bitcast.12, ...), custom_call_target="tpu_custom_call" | custom-call | flops 5000000000 | bytes 1000 | tf_op jit(solution)/shard_map/pack/pallas_call | solution.py:446
  2.2 0.5 %collective-permute-start = (bf16[176,2560]{1,0:T(8,128)(2,1)S(1)}, bf16[176,2560]{1,0:T(8,128)(2,1)S(1)}, u32[]{:S(2)}, u32[]{:S(2)}) collective-permute-start(bf16[176,2560]{1,0:T(8,128)(2,1)S(1)} %get-tuple-element.54), channel_id=1, source_target_pairs={{0,1},{1,0},{2,3},{3,2},{4,5},{5,4},{6,7},{7,6},{8,9},{9,8},{10,11... | collective-permute-start | bytes 2703368 | tf_op jit(solution)/shard_map/ppermute | solution.py:502
  2.8 4.5 %collective-permute-start.1 = (bf16[160,256]{1,0:T(8,128)(2,1)S(1)}, bf16[160,256]{1,0:T(8,128)(2,1)S(1)}, u32[]{:S(2)}, u32[]{:S(2)}) collective-permute-start(bf16[160,256]{1,0:T(8,128)(2,1)S(1)} %get-tuple-element.62), channel_id=1, source_target_pairs={{0,3},{1,2},{4,7},{5,6},{8,11},{9,10},{12,15},{13,14},{16,19},{17,... | collective-permute-start | bytes 245768 | tf_op jit(solution)/shard_map/ppermute | solution.py:494
  7.3 1.3 %collective-permute-start.2 = (bf16[160,256]{1,0:T(8,128)(2,1)S(1)}, bf16[160,256]{1,0:T(8,128)(2,1)S(1)}, u32[]{:S(2)}, u32[]{:S(2)}) collective-permute-start(bf16[160,256]{1,0:T(8,128)(2,1)S(1)} %get-tuple-element.49.key_mine), channel_id=1, source_target_pairs={{0,2},{1,3},{4,6},{5,7},{8,10},{9,11},{12,14},{13,15},{16,18},{17,... | collective-permute-start | bytes 245768 | tf_op jit(solution)/shard_map/ppermute | solution.py:495
  8.6 1.3 %collective-permute-start.3 = (bf16[160,256]{1,0:T(8,128)(2,1)S(1)}, bf16[160,256]{1,0:T(8,128)(2,1)S(1)}, u32[]{:S(2)}, u32[]{:S(2)}) collective-permute-start(bf16[160,256]{1,0:T(8,128)(2,1)S(1)} %get-tuple-element.72), channel_id=1, source_target_pairs={{0,3},{1,2},{4,7},{5,6},{8,11},{9,10},{12,15},{13,14},{16,19},{17,... | collective-permute-start | bytes 245768 | tf_op jit(solution)/shard_map/ppermute | solution.py:494
  9.9 1.3 %collective-permute-start.4 = (bf16[160,256]{1,0:T(8,128)(2,1)S(1)}, bf16[160,256]{1,0:T(8,128)(2,1)S(1)}, u32[]{:S(2)}, u32[]{:S(2)}) collective-permute-start(bf16[160,256]{1,0:T(8,128)(2,1)S(1)} %get-tuple-element.50.value_mine), channel_id=1, source_target_pairs={{0,2},{1,3},{4,6},{5,7},{8,10},{9,11},{12,14},{13,15},{16,18},{17,... | collective-permute-start | bytes 245768 | tf_op jit(solution)/shard_map/ppermute | solution.py:495
  11.2 0.0 collective-permute-done.sib
  11.2 0.0 copy-done
  11.2 0.0 copy-done.1
  11.2 1.5 %local_scores.1 = (bf16[2,320,128]{2,1,0:T(8,128)(2,1)S(1)}, bf16[2,1280,128]{2,1,0:T(8,128)(2,1)S(1)}, bf16[2,1280,128]{2,1,0:T(8,128)(2,1)S(1)}, f32[1,1280]{1...) custom-call(bf16[160,256]{1,0:T(8,128)(2,1)S(1)} %get-tuple-element., ...), custom_call_target="tpu_custom_call" | custom-call | flops 3000000 | bytes 1000 | tf_op jit(solution)/shard_map/local_scores/pallas_call | solution.py:446
  12.7 0.0 collective-permute-done.1.packet.refs_0_
  12.8 0.0 collective-permute-done.2.refs_1_
  12.8 1.3 %collective-permute-start.6 = (bf16[160,256]{1,0:T(8,128)(2,1)S(1)}, bf16[160,256]{1,0:T(8,128)(2,1)S(1)}, u32[]{:S(2)}, u32[]{:S(2)}) collective-permute-start(bf16[160,256]{1,0:T(8,128)(2,1)S(1)} %get-tuple-element.81), channel_id=1, source_target_pairs={{3,0},{2,1},{7,4},{6,5},{11,8},{10,9},{15,12},{14,13},{19,16},{18,... | collective-permute-start | bytes 245768 | tf_op jit(solution)/shard_map/ppermute | solution.py:494
  14.1 1.3 %collective-permute-start.7 = (bf16[160,256]{1,0:T(8,128)(2,1)S(1)}, bf16[160,256]{1,0:T(8,128)(2,1)S(1)}, u32[]{:S(2)}, u32[]{:S(2)}) collective-permute-start(bf16[160,256]{1,0:T(8,128)(2,1)S(1)} %get-tuple-element.82), channel_id=1, source_target_pairs={{2,0},{3,1},{6,4},{7,5},{10,8},{11,9},{14,12},{15,13},{18,16},{19,... | collective-permute-start | bytes 245768 | tf_op jit(solution)/shard_map/ppermute | solution.py:495
  15.4 0.0 collective-permute-done.3.refs_0_
  15.4 0.0 collective-permute-done.4.refs_1_
  15.5 1.3 %collective-permute-start.8 = (bf16[160,256]{1,0:T(8,128)(2,1)S(1)}, bf16[160,256]{1,0:T(8,128)(2,1)S(1)}, u32[]{:S(2)}, u32[]{:S(2)}) collective-permute-start(bf16[160,256]{1,0:T(8,128)(2,1)S(1)} %get-tuple-element.84), channel_id=1, source_target_pairs={{3,0},{2,1},{7,4},{6,5},{11,8},{10,9},{15,12},{14,13},{19,16},{18,... | collective-permute-start | bytes 245768 | tf_op jit(solution)/shard_map/ppermute | solution.py:494
  16.8 1.3 %collective-permute-start.9 = (bf16[160,256]{1,0:T(8,128)(2,1)S(1)}, bf16[160,256]{1,0:T(8,128)(2,1)S(1)}, u32[]{:S(2)}, u32[]{:S(2)}) collective-permute-start(bf16[160,256]{1,0:T(8,128)(2,1)S(1)} %get-tuple-element.85), channel_id=1, source_target_pairs={{2,0},{3,1},{6,4},{7,5},{10,8},{11,9},{14,12},{15,13},{18,16},{19,... | collective-permute-start | bytes 245768 | tf_op jit(solution)/shard_map/ppermute | solution.py:495
  18.1 2.1 %near_grads.1 = (f32[160,512]{1,0:T(8,128)S(1)}, bf16[160,1024]{1,0:T(8,128)(2,1)S(1)}, f32[1,160]{1,0:T(1,128)S(1)}, bf16[176,1536]{1,0:T(8,128)(2,1)S(1)}) custom-call(f32[2,320,1280]{2,1,0:T(8,128)S(1)} %get-tuple-element.55.raws, f32[2,320,1280]{2,1,0:T(8,128)S(1)} %get-tuple-element.56.grads, f32[2,1,1280]{2,1,0:T(1,128)S(1)} %get-tuple-element.66.factors, ...), custom_call_target="tpu_custom_call" | custom-call | flops 4000000 | bytes 1000 | tf_op jit(solution)/shard_map/near_grads/pallas_call | solution.py:446
  20.2 0.2 collective-permute-start.5
  20.4 0.0 collective-permute-done.6.refs_0_
  20.4 0.8 %collective-permute-done.7.refs_1_ = bf16[160,256]{1,0:T(8,128)(2,1)S(1)} collective-permute-done((bf16[160,256]{1,0:T(8,128)(2,1)S(1)}, bf16[160,256]{1,0:T(8,128)(2,1)S(1)}, u32[]{:S(2)}, u32[]{:S(2)}) %collective-permute-start.7) | collective-permute-done | bytes 81952 | tf_op jit(solution)/shard_map/ppermute | solution.py:495
  21.2 2.2 %collective-permute-done.8.refs_0_ = bf16[160,256]{1,0:T(8,128)(2,1)S(1)} collective-permute-done((bf16[160,256]{1,0:T(8,128)(2,1)S(1)}, bf16[160,256]{1,0:T(8,128)(2,1)S(1)}, u32[]{:S(2)}, u32[]{:S(2)}) %collective-permute-start.8) | collective-permute-done | bytes 81952 | tf_op jit(solution)/shard_map/ppermute | solution.py:494
  23.4 2.3 %collective-permute-done.9.refs_1_ = bf16[160,256]{1,0:T(8,128)(2,1)S(1)} collective-permute-done((bf16[160,256]{1,0:T(8,128)(2,1)S(1)}, bf16[160,256]{1,0:T(8,128)(2,1)S(1)}, u32[]{:S(2)}, u32[]{:S(2)}) %collective-permute-start.9) | collective-permute-done | bytes 81952 | tf_op jit(solution)/shard_map/ppermute | solution.py:495
  25.7 0.0 collective-permute-done.5.back
  25.7 1.2 %finish.1 = (bf16[160,2048]{1,0:T(8,128)(2,1)}, bf16[160,512]{1,0:T(8,128)(2,1)}, bf16[160,512]{1,0:T(8,128)(2,1)}, f32[1,160]{1,0:T(1,128)}) custom-call(bf16[176,1536]{1,0:T(8,128)(2,1)S(1)} %collective-permute-done.5.back, bf16[160,1024]{1,0:T(8,128)(2,1)S(1)} %get-tuple-element.78.query_mine, f32[1,160]{1,0:T(1,128)S(1)} %get-tuple-element.79.gate_mine, ...), custom_call_target="tpu_custom_call" | custom-call | flops 1000000 | bytes 1000 | tf_op jit(solution)/shard_map/finish/pallas_call | solution.py:446
  (5 shorter events, 0.1 us)
Async XLA Ops:
  0.6 10.5 %copy-start = (bf16[1,160,2048]{2,1,0:T(8,128)(2,1)S(1)}, bf16[1,160,2048]{2,1,0:T(8,128)(2,1)}, u32[]{:S(2)}) copy-start(bf16[1,160,2048]{2,1,0:T(8,128)(2,1)} %param.7) | copy-start | bytes 1966084
  0.6 10.5 %copy-start.1 = (bf16[1,160,2048]{2,1,0:T(8,128)(2,1)S(1)}, bf16[1,160,2048]{2,1,0:T(8,128)(2,1)}, u32[]{:S(2)}) copy-start(bf16[1,160,2048]{2,1,0:T(8,128)(2,1)} %param.10) | copy-start | bytes 1966084
  2.2 8.9 %collective-permute-start = (bf16[176,2560]{1,0:T(8,128)(2,1)S(1)}, bf16[176,2560]{1,0:T(8,128)(2,1)S(1)}, u32[]{:S(2)}, u32[]{:S(2)}) collective-permute-start(bf16[176,2560]{1,0:T(8,128)(2,1)S(1)} %get-tuple-element.54), channel_id=1, source_target_pairs={{0,1},{1,0},{2,3},{3,2},{4,5},{5,4},{6,7},{7,6},{8,9},{9,8},{10,11... | collective-permute-start | bytes 2703368 | tf_op jit(solution)/shard_map/ppermute | solution.py:502
  2.8 10.0 %collective-permute-start.1 = (bf16[160,256]{1,0:T(8,128)(2,1)S(1)}, bf16[160,256]{1,0:T(8,128)(2,1)S(1)}, u32[]{:S(2)}, u32[]{:S(2)}) collective-permute-start(bf16[160,256]{1,0:T(8,128)(2,1)S(1)} %get-tuple-element.62), channel_id=1, source_target_pairs={{0,3},{1,2},{4,7},{5,6},{8,11},{9,10},{12,15},{13,14},{16,19},{17,... | collective-permute-start | bytes 245768 | tf_op jit(solution)/shard_map/ppermute | solution.py:494
  7.3 5.5 %collective-permute-start.2 = (bf16[160,256]{1,0:T(8,128)(2,1)S(1)}, bf16[160,256]{1,0:T(8,128)(2,1)S(1)}, u32[]{:S(2)}, u32[]{:S(2)}) collective-permute-start(bf16[160,256]{1,0:T(8,128)(2,1)S(1)} %get-tuple-element.49.key_mine), channel_id=1, source_target_pairs={{0,2},{1,3},{4,6},{5,7},{8,10},{9,11},{12,14},{13,15},{16,18},{17,... | collective-permute-start | bytes 245768 | tf_op jit(solution)/shard_map/ppermute | solution.py:495
  8.6 6.9 %collective-permute-start.3 = (bf16[160,256]{1,0:T(8,128)(2,1)S(1)}, bf16[160,256]{1,0:T(8,128)(2,1)S(1)}, u32[]{:S(2)}, u32[]{:S(2)}) collective-permute-start(bf16[160,256]{1,0:T(8,128)(2,1)S(1)} %get-tuple-element.72), channel_id=1, source_target_pairs={{0,3},{1,2},{4,7},{5,6},{8,11},{9,10},{12,15},{13,14},{16,19},{17,... | collective-permute-start | bytes 245768 | tf_op jit(solution)/shard_map/ppermute | solution.py:494
  9.9 5.6 %collective-permute-start.4 = (bf16[160,256]{1,0:T(8,128)(2,1)S(1)}, bf16[160,256]{1,0:T(8,128)(2,1)S(1)}, u32[]{:S(2)}, u32[]{:S(2)}) collective-permute-start(bf16[160,256]{1,0:T(8,128)(2,1)S(1)} %get-tuple-element.50.value_mine), channel_id=1, source_target_pairs={{0,2},{1,3},{4,6},{5,7},{8,10},{9,11},{12,14},{13,15},{16,18},{17,... | collective-permute-start | bytes 245768 | tf_op jit(solution)/shard_map/ppermute | solution.py:495
  12.8 7.6 %collective-permute-start.6 = (bf16[160,256]{1,0:T(8,128)(2,1)S(1)}, bf16[160,256]{1,0:T(8,128)(2,1)S(1)}, u32[]{:S(2)}, u32[]{:S(2)}) collective-permute-start(bf16[160,256]{1,0:T(8,128)(2,1)S(1)} %get-tuple-element.81), channel_id=1, source_target_pairs={{3,0},{2,1},{7,4},{6,5},{11,8},{10,9},{15,12},{14,13},{19,16},{18,... | collective-permute-start | bytes 245768 | tf_op jit(solution)/shard_map/ppermute | solution.py:494
  14.1 7.1 %collective-permute-start.7 = (bf16[160,256]{1,0:T(8,128)(2,1)S(1)}, bf16[160,256]{1,0:T(8,128)(2,1)S(1)}, u32[]{:S(2)}, u32[]{:S(2)}) collective-permute-start(bf16[160,256]{1,0:T(8,128)(2,1)S(1)} %get-tuple-element.82), channel_id=1, source_target_pairs={{2,0},{3,1},{6,4},{7,5},{10,8},{11,9},{14,12},{15,13},{18,16},{19,... | collective-permute-start | bytes 245768 | tf_op jit(solution)/shard_map/ppermute | solution.py:495
  15.5 7.9 %collective-permute-start.8 = (bf16[160,256]{1,0:T(8,128)(2,1)S(1)}, bf16[160,256]{1,0:T(8,128)(2,1)S(1)}, u32[]{:S(2)}, u32[]{:S(2)}) collective-permute-start(bf16[160,256]{1,0:T(8,128)(2,1)S(1)} %get-tuple-element.84), channel_id=1, source_target_pairs={{3,0},{2,1},{7,4},{6,5},{11,8},{10,9},{15,12},{14,13},{19,16},{18,... | collective-permute-start | bytes 245768 | tf_op jit(solution)/shard_map/ppermute | solution.py:494
  16.8 8.9 %collective-permute-start.9 = (bf16[160,256]{1,0:T(8,128)(2,1)S(1)}, bf16[160,256]{1,0:T(8,128)(2,1)S(1)}, u32[]{:S(2)}, u32[]{:S(2)}) collective-permute-start(bf16[160,256]{1,0:T(8,128)(2,1)S(1)} %get-tuple-element.85), channel_id=1, source_target_pairs={{2,0},{3,1},{6,4},{7,5},{10,8},{11,9},{14,12},{15,13},{18,16},{19,... | collective-permute-start | bytes 245768 | tf_op jit(solution)/shard_map/ppermute | solution.py:495
  20.2 5.5 %collective-permute-start.5 = (bf16[176,1536]{1,0:T(8,128)(2,1)S(1)}, bf16[176,1536]{1,0:T(8,128)(2,1)S(1)}, u32[]{:S(2)}, u32[]{:S(2)}) collective-permute-start(bf16[176,1536]{1,0:T(8,128)(2,1)S(1)} %get-tuple-element.77), channel_id=1, source_target_pairs={{0,1},{1,0},{2,3},{3,2},{4,5},{5,4},{6,7},{7,6},{8,9},{9,8},{10,11... | collective-permute-start | bytes 1622024 | tf_op jit(solution)/shard_map/ppermute | solution.py:594

commit v13 on v11

--- a/solution.py
+++ b/solution.py
@@ -18,6 +18,7 @@
 SCALE = DH**-0.5
 LOG2E = math.log2(math.e)
 LN2 = math.log(2.0)
+FAR_COST = 5 * 10**9
 
 NT = (((1,), (1,)), ((), ()))
 NN = (((1,), (0,)), ((), ()))
@@ -79,7 +80,7 @@
 
 def pack_kernel(
     key_in, value_in, query_in, cot_in, gate_in, pos_in, freq_in,
-    key_mine, key_theirs, value_mine, value_theirs, theirs, gate_mine, cos_ref, sin_ref,
+    key_mine, key_theirs, value_mine, value_theirs, theirs, gate_mine, valid, cos_ref, sin_ref,
     key, value, query, gate, pos, freq, sems, *, limit
 ):
     rows, width = key.shape
@@ -120,6 +121,7 @@
         here = slice(i * DH, (i + 1) * DH)
         theirs[:rows, here] = rotate(query[:, here].astype(F32), cosine, sine).astype(BF16)
     loads[5].wait()
+    valid[...] = jnp.where(places < limit, 1.0, 0.0)
     used_gate = jnp.where(places < limit, gate[...], 0.0)
     gate_mine[...] = used_gate
     theirs[rows:, :rows] = split_rows(used_gate, EXTRA)
@@ -147,14 +149,16 @@
 
 
 def local_kernel(
-    key_mine, value_mine, query_in, cot_in, cos_ref, sin_ref, gate_mine, sib,
-    keys, query, cot, gate, raws, grads, tops, sums, crosses, values, *, ratio
+    key_mine, value_mine, value_theirs, query_in, cot_in, cos_ref, sin_ref, gate_mine, sib,
+    send_mine, send_theirs, keys, values, query, cot, gate, raws, tops, sums, crosses, *, ratio
 ):
     rows = key_mine.shape[0]
     half_groups = keys.shape[0]
     wide = ratio * rows
     half = half_groups * ratio * DH
     core = core_of()
+    send_mine[...] = value_mine[...]
+    send_theirs[...] = value_theirs[...]
     spread = chosen((rows, wide), ratio, 1)
     key_sib = sib.at[:rows, 2 * half : 2 * half + half_groups * DH]
     value_sib = sib.at[:rows, 2 * half + half_groups * DH :]
@@ -195,12 +199,18 @@
                     shown = jnp.concatenate([before, shown], axis=0)
                 top = jnp.max(shown, axis=0, keepdims=True)
                 raw = jnp.exp2(shown - top)
-                prob_grad = dot(values[i, :reach, :], cot[i, here, :], NT)
                 raws[i, :reach, here] = raw
-                grads[i, :reach, here] = prob_grad
                 tops[i, :, here] = top
                 sums[i, :, here] = jnp.sum(raw, axis=0, keepdims=True)
-                crosses[i, :, here] = jnp.sum(raw * prob_grad, axis=0, keepdims=True)
+
+    @pl.when(lax.axis_index("ctx") >= 2)
+    def _():
+        for i in range(half_groups):
+            for block in range(2):
+                reach = (block + 1) * rows
+                for here in chunks(block * wide, (block + 1) * wide):
+                    prob_grad = dot(values[i, :reach, :], cot[i, here, :], NT)
+                    crosses[i, :, here] = jnp.sum(raws[i, :reach, here] * prob_grad, axis=0, keepdims=True)
 
 
 def part_of(weights, score_grads, query, cot, out_ref, i, there, lanes):
@@ -262,14 +272,8 @@
     parts, far_values = refs[blocks + 2 : -1], refs[-1]
     rows = packets[0].shape[0]
     half_groups, lanes = query.shape[:2]
-    alone = lax.axis_index("ctx") < 2
-
-    @pl.when(alone)
-    def _():
-        for i in range(half_groups):
-            deltas[i] = crosses[i] * inverses[i]
-
-    @pl.when(jnp.logical_not(alone))
+
+    @pl.when(lax.axis_index("ctx") >= 2)
     def _():
         for i in range(half_groups):
             for j, packet in enumerate(packets):
@@ -290,21 +294,27 @@
 
 
 def near_kernel(
-    raws, grads, factors, deltas, keys, query, cot, far_keys, far_grads, cos_ref, sin_ref,
-    part_mine, query_mine, gate_mine, theirs, weights, score_grads, parts, acc, turned,
+    raws, values, factors, inverses, far_deltas, keys, query, cot, far_keys, far_grads, cos_ref, sin_ref,
+    part_mine, query_mine, gate_mine, theirs, weights, score_grads, parts, acc, turned, deltas,
     *, ratio
 ):
     rows = part_mine.shape[0]
     half_groups = keys.shape[0]
     wide = ratio * rows
     half = half_groups * ratio * DH
+    alone = lax.axis_index("ctx") < 2
     for i in range(half_groups):
         for block in range(2):
             reach = (block + 1) * rows
             for here in chunks(block * wide, (block + 1) * wide):
-                gated = raws[i, :reach, here] * factors[i, :, here]
+                raw = raws[i, :reach, here]
+                prob_grad = dot(values[i, :reach, :], cot[i, here, :], NT)
+                delta = jnp.sum(raw * prob_grad, axis=0, keepdims=True) * inverses[i, :, here]
+                delta = jnp.where(alone, delta, far_deltas[i, :, here])
+                deltas[i, :, here] = delta
+                gated = raw * factors[i, :, here]
                 weights[i, :reach, here] = gated.astype(BF16)
-                score_grads[i, :reach, here] = (gated * (grads[i, :reach, here] - deltas[i, :, here])).astype(BF16)
+                score_grads[i, :reach, here] = (gated * (prob_grad - delta)).astype(BF16)
         for block in range(2):
             there, lanes = slice(block * rows, (block + 1) * rows), slice(block * wide, 2 * wide)
             part_of(weights, score_grads, query, cot, parts.at[block], i, there, lanes)
@@ -368,8 +378,8 @@
 
 
 def finish_kernel(
-    back, query_mine, gate_mine, key_own, value_own, key_other, value_other, pos_ref, cos_ref, sin_ref,
-    query_grad, key_grad, value_grad, gate_grad, *, limit
+    back, query_mine, gate_mine, key_own, value_own, key_other, value_other, valid, cos_ref, sin_ref,
+    query_grad, key_grad, value_grad, gate_grad
 ):
     rows, half = value_own.shape
     wide = query_mine.shape[1]
@@ -393,7 +403,7 @@
         turned = rotate(back[:rows, i * DH : (i + 1) * DH].astype(F32), cosine, sine)
         query_grad[:, side(1 - core, wide, i * DH, DH)] = turned.astype(BF16)
     gate = gate_mine[...] + joined_row(back[rows:, :rows])
-    gate_grad[...] = jnp.where(pos_ref[...] < limit, gate, 0.0)
+    gate_grad[...] = jnp.where(valid[...] > 0.0, gate, 0.0)
 
 
 def per_device(query_rows, key_rows, value_rows, cotangent, router_gate, positions):
@@ -428,10 +438,10 @@
     table = ((rows, DH), F32)
     line = ((1, rows), F32)
     theirs_shape = ((rows + EXTRA, heads_width + group_width), BF16)
-    key_mine, key_theirs, value_mine, value_theirs, theirs, gate_mine, cosine, sine = call(
+    key_mine, key_theirs, value_mine, value_theirs, theirs, gate_mine, valid, cosine, sine = call(
         functools.partial(pack_kernel, limit=limit),
         "pack",
-        [packet, packet, packet, packet, theirs_shape, line, table, table],
+        [packet, packet, packet, packet, theirs_shape, line, line, table, table],
         key_rows[0],
         value_rows[0],
         query_rows[0],
@@ -464,7 +474,6 @@
         return sib, [lax.ppermute(own[s - 1], "ctx", own_pairs[s]) for s in steps]
 
     sib_keys, own_keys = send([key_theirs] * chips, [key_mine] * chips, cross, hop)
-    sib_values, own_values = send([value_theirs] * chips, [value_mine] * chips, cross, hop)
 
     pairs = [[2 * x, 2 * x + 1] for x in range(chips)]
     swap = [pair for a, b in pairs for pair in ((a, b), (b, a))]
@@ -474,21 +483,23 @@
     table = ((half_groups, 2 * rows, 2 * wide), F32)
     kv_table = ((half_groups, 2 * rows, DH), BF16)
     q_table = ((half_groups, 2 * wide, DH), BF16)
-    keys, query, cot, gate_row, raws, grads, tops, sums, crosses = call(
+    send_mine, send_theirs, keys, values, query, cot, gate_row, raws, tops, sums, crosses = call(
         functools.partial(local_kernel, ratio=ratio),
         "local_scores",
-        [kv_table, q_table, q_table, ((1, 2 * wide), F32), table, table, row, row, row],
+        [packet, packet, kv_table, kv_table, q_table, q_table, ((1, 2 * wide), F32), table, row, row, row],
         key_mine,
         value_mine,
+        value_theirs,
         query_rows[0],
         cotangent[0],
         cosine,
         sine,
         gate_mine,
         sib,
-        scratch=[pltpu.VMEM(*kv_table)],
         flops=3 * 10**6,
     )
+
+    sib_values, own_values = send([send_theirs] * chips, [send_mine] * chips, cross, hop)
 
     blocks = 2 * (chips - 1)
     far_rows = ((half_groups, blocks * rows, DH), BF16)
@@ -505,6 +516,7 @@
         sums,
         *sib_keys,
         *own_keys,
+        flops=FAR_COST,
         scratch=[pltpu.VMEM(*far_low)],
     )
     sib_value_got, own_value_got = send(parts[: chips - 1], parts[chips - 1 :], back_cross, back_hop)
@@ -535,8 +547,9 @@
             ((rows + EXTRA, half_width + group_width), BF16),
         ],
         raws,
-        grads,
+        values,
         factors,
+        inverses,
         deltas,
         keys,
         query,
@@ -552,6 +565,7 @@
             pltpu.VMEM((2, rows, group_width), F32),
             pltpu.VMEM((half_groups, DH, 2 * wide), F32),
             pltpu.VMEM((2 * wide, DH), F32),
+            pltpu.VMEM(*row),
         ],
     )
     back = lax.ppermute(theirs, "ctx", swap)
@@ -574,7 +588,7 @@
         flops=5 * 10**9,
     )
     query_grad, key_grad, value_grad, gate_grad = call(
-        functools.partial(finish_kernel, limit=limit),
+        finish_kernel,
         "finish",
         [((rows, heads_width), BF16)] + [((rows, group_width), BF16)] * 2 + [line],
         back,
@@ -584,7 +598,7 @@
         value_own,
         key_other,
         value_other,
-        positions,
+        valid,
         cosine,
         sine,
     )

time: 27.9 us -> 27.6 us (0.989)
  waiting for transfers between devices: 5.29 us -> 4.55 us
  local copies, waits for them, and re-layouts: 0.65 us -> 0.01 us
  starting transfers between devices: 14.2 us -> 14.8 us
  Pallas kernels: 6.62 us -> 7.17 us
    ppermute x4, waiting for transfers between devices: 3.41 us -> 2.33 us  [send(): return (sib, [lax.ppermute(own[s - 1], 'ctx', own_pairs[s]) for s in steps])]
    unnamed x6 -> x4, local copies, waits for them, and re-layouts: 0.65 us -> 0.01 us
    pallas_call x8, Pallas kernels: 6.62 us -> 7.17 us  [call(): pl.pallas_call(kernel, out_shape=[jax.ShapeDtypeStruct(*out) for out in o...]
    ppermute x4, starting transfers between devices: 8.38 us -> 8.91 us  [send(): sib = [lax.ppermute(sib[s - 1], 'ctx', sib_pairs[s]) for s in steps]]
    ppermute x4, waiting for transfers between devices: 1.87 us -> 2.22 us  [send(): sib = [lax.ppermute(sib[s - 1], 'ctx', sib_pairs[s]) for s in steps]]
  transfers between devices with their start and end apart: 10 -> 10, of which waited for: 3 -> 3; matrix products, arithmetic and copies ran while one was open for 0% -> 0% of each run, Pallas kernels for 14% -> 16%
where the time goes in v13:
time: 27.6 us; the launch traced here: 27.3 us
  starting transfers between devices  14.8 us (54%)
  Pallas kernels  7.17 us (26%)
  waiting for transfers between devices  4.55 us (16%)
  between operations  0.82 us (3%)
    ppermute x4, starting transfers between devices, send(): sib = [lax.ppermute(sib[s - 1], 'ctx', sib_pairs[s]) for s in steps]  8.91 us
    pallas_call x8, Pallas kernels, call(): pl.pallas_call(kernel, out_shape=[jax.ShapeDtypeStruct(*out) for out in o...  7.17 us
    ppermute x4, starting transfers between devices, send(): return (sib, [lax.ppermute(own[s - 1], 'ctx', own_pairs[s]) for s in steps])  5.17 us
    ppermute x4, waiting for transfers between devices, send(): return (sib, [lax.ppermute(own[s - 1], 'ctx', own_pairs[s]) for s in steps])  2.33 us
    ppermute x4, waiting for transfers between devices, send(): sib = [lax.ppermute(sib[s - 1], 'ctx', sib_pairs[s]) for s in steps]  2.22 us
  transfers between devices with their start and end apart: 10, of which 3 were waited for; matrix products, arithmetic and copies ran while one was open for 0% of the time, Pallas kernels for 16%

profile of v13, /device:TPU:0, one launch (start us, length us, event | category | flops | bytes accessed | tf_op | source)
XLA Modules:
  0.0 27.3 jit_solution(5403894299890765979)
XLA Ops:
  0.6 0.0 copy-start
  0.6 0.0 copy-start.1
  0.7 1.6 %pack.1 = (bf16[160,256]{1,0:T(8,128)(2,1)S(1)}, bf16[160,256]{1,0:T(8,128)(2,1)S(1)}, bf16[160,256]{1,0:T(8,128)(2,1)S(1)}, bf16[160,256]{1,0:T(8,128)(2,1)S(1)...) custom-call(bf16[160,512]{1,0:T(8,128)(2,1)} %bitcast.12, ...), custom_call_target="tpu_custom_call" | custom-call | flops 5000000000 | bytes 1000 | tf_op jit(solution)/shard_map/pack/pallas_call | solution.py:425
  2.2 0.5 %collective-permute-start = (bf16[176,2560]{1,0:T(8,128)(2,1)S(1)}, bf16[176,2560]{1,0:T(8,128)(2,1)S(1)}, u32[]{:S(2)}, u32[]{:S(2)}) collective-permute-start(bf16[176,2560]{1,0:T(8,128)(2,1)S(1)} %get-tuple-element.54), channel_id=1, source_target_pairs={{0,1},{1,0},{2,3},{3,2},{4,5},{5,4},{6,7},{7,6},{8,9},{9,8},{10,11... | collective-permute-start | bytes 2703368 | tf_op jit(solution)/shard_map/ppermute | solution.py:480
  2.8 4.5 %collective-permute-start.1 = (bf16[160,256]{1,0:T(8,128)(2,1)S(1)}, bf16[160,256]{1,0:T(8,128)(2,1)S(1)}, u32[]{:S(2)}, u32[]{:S(2)}) collective-permute-start(bf16[160,256]{1,0:T(8,128)(2,1)S(1)} %get-tuple-element.62), channel_id=1, source_target_pairs={{0,3},{1,2},{4,7},{5,6},{8,11},{9,10},{12,15},{13,14},{16,19},{17,... | collective-permute-start | bytes 245768 | tf_op jit(solution)/shard_map/ppermute | solution.py:473
  7.3 1.3 %collective-permute-start.2 = (bf16[160,256]{1,0:T(8,128)(2,1)S(1)}, bf16[160,256]{1,0:T(8,128)(2,1)S(1)}, u32[]{:S(2)}, u32[]{:S(2)}) collective-permute-start(bf16[160,256]{1,0:T(8,128)(2,1)S(1)} %get-tuple-element.48.key_mine), channel_id=1, source_target_pairs={{0,2},{1,3},{4,6},{5,7},{8,10},{9,11},{12,14},{13,15},{16,18},{17,... | collective-permute-start | bytes 245768 | tf_op jit(solution)/shard_map/ppermute | solution.py:474
  8.6 0.0 collective-permute-done.sib
  8.6 0.0 copy-done
  8.6 0.0 copy-done.1
  8.6 1.3 %local_scores.1 = (bf16[160,256]{1,0:T(8,128)(2,1)S(1)}, bf16[160,256]{1,0:T(8,128)(2,1)S(1)}, bf16[2,320,128]{2,1,0:T(8,128)(2,1)S(1)}, bf16[2,320,128]{2,1,0:T...) custom-call(bf16[160,256]{1,0:T(8,128)(2,1)S(1)} %get-tuple-element., ...), custom_call_target="tpu_custom_call" | custom-call | flops 3000000 | bytes 1000 | tf_op jit(solution)/shard_map/local_scores/pallas_call | solution.py:425
  9.9 1.8 %collective-permute-start.3 = (bf16[160,256]{1,0:T(8,128)(2,1)S(1)}, bf16[160,256]{1,0:T(8,128)(2,1)S(1)}, u32[]{:S(2)}, u32[]{:S(2)}) collective-permute-start(bf16[160,256]{1,0:T(8,128)(2,1)S(1)} %get-tuple-element.69), channel_id=1, source_target_pairs={{0,3},{1,2},{4,7},{5,6},{8,11},{9,10},{12,15},{13,14},{16,19},{17,... | collective-permute-start | bytes 245768 | tf_op jit(solution)/shard_map/ppermute | solution.py:473
  11.8 1.3 %collective-permute-start.4 = (bf16[160,256]{1,0:T(8,128)(2,1)S(1)}, bf16[160,256]{1,0:T(8,128)(2,1)S(1)}, u32[]{:S(2)}, u32[]{:S(2)}) collective-permute-start(bf16[160,256]{1,0:T(8,128)(2,1)S(1)} %get-tuple-element.70), channel_id=1, source_target_pairs={{0,2},{1,3},{4,6},{5,7},{8,10},{9,11},{12,14},{13,15},{16,18},{17,... | collective-permute-start | bytes 245768 | tf_op jit(solution)/shard_map/ppermute | solution.py:474
  13.1 0.0 collective-permute-done.1.refs_0_
  13.1 0.0 collective-permute-done.2.refs_1_
  13.1 1.3 %collective-permute-start.6 = (bf16[160,256]{1,0:T(8,128)(2,1)S(1)}, bf16[160,256]{1,0:T(8,128)(2,1)S(1)}, u32[]{:S(2)}, u32[]{:S(2)}) collective-permute-start(bf16[160,256]{1,0:T(8,128)(2,1)S(1)} %get-tuple-element.79), channel_id=1, source_target_pairs={{3,0},{2,1},{7,4},{6,5},{11,8},{10,9},{15,12},{14,13},{19,16},{18,... | collective-permute-start | bytes 245768 | tf_op jit(solution)/shard_map/ppermute | solution.py:473
  14.4 1.3 %collective-permute-start.7 = (bf16[160,256]{1,0:T(8,128)(2,1)S(1)}, bf16[160,256]{1,0:T(8,128)(2,1)S(1)}, u32[]{:S(2)}, u32[]{:S(2)}) collective-permute-start(bf16[160,256]{1,0:T(8,128)(2,1)S(1)} %get-tuple-element.80), channel_id=1, source_target_pairs={{2,0},{3,1},{6,4},{7,5},{10,8},{11,9},{14,12},{15,13},{18,16},{19,... | collective-permute-start | bytes 245768 | tf_op jit(solution)/shard_map/ppermute | solution.py:474
  15.7 0.0 collective-permute-done.3.refs_0_
  15.7 0.0 collective-permute-done.4.refs_1_
  15.8 1.3 %collective-permute-start.8 = (bf16[160,256]{1,0:T(8,128)(2,1)S(1)}, bf16[160,256]{1,0:T(8,128)(2,1)S(1)}, u32[]{:S(2)}, u32[]{:S(2)}) collective-permute-start(bf16[160,256]{1,0:T(8,128)(2,1)S(1)} %get-tuple-element.82), channel_id=1, source_target_pairs={{3,0},{2,1},{7,4},{6,5},{11,8},{10,9},{15,12},{14,13},{19,16},{18,... | collective-permute-start | bytes 245768 | tf_op jit(solution)/shard_map/ppermute | solution.py:473
  17.1 1.3 %collective-permute-start.9 = (bf16[160,256]{1,0:T(8,128)(2,1)S(1)}, bf16[160,256]{1,0:T(8,128)(2,1)S(1)}, u32[]{:S(2)}, u32[]{:S(2)}) collective-permute-start(bf16[160,256]{1,0:T(8,128)(2,1)S(1)} %get-tuple-element.83), channel_id=1, source_target_pairs={{2,0},{3,1},{6,4},{7,5},{10,8},{11,9},{14,12},{15,13},{18,16},{19,... | collective-permute-start | bytes 245768 | tf_op jit(solution)/shard_map/ppermute | solution.py:474
  18.4 2.9 %near_grads.1 = (f32[160,512]{1,0:T(8,128)S(1)}, bf16[160,1024]{1,0:T(8,128)(2,1)S(1)}, f32[1,160]{1,0:T(1,128)S(1)}, bf16[176,1536]{1,0:T(8,128)(2,1)S(1)}) custom-call(f32[2,320,1280]{2,1,0:T(8,128)S(1)} %get-tuple-element.55.raws, bf16[2,320,128]{2,1,0:T(8,128)(2,1)S(1)} %get-tuple-element.56.values, f32[2,1,1280]{2,1,0:T(1,128)S(1)} %get-tuple-element.63.factors, ...), custom_call_target="tpu_custom_call" | custom-call | flops 4000000 | bytes 1000 | tf_op jit(solution)/shard_map/near_grads/pallas_call | solution.py:425
  21.3 0.2 collective-permute-start.5
  21.4 0.0 collective-permute-done.6.refs_0_
  21.5 0.1 collective-permute-done.7.refs_1_
  21.5 2.2 %collective-permute-done.8.refs_0_ = bf16[160,256]{1,0:T(8,128)(2,1)S(1)} collective-permute-done((bf16[160,256]{1,0:T(8,128)(2,1)S(1)}, bf16[160,256]{1,0:T(8,128)(2,1)S(1)}, u32[]{:S(2)}, u32[]{:S(2)}) %collective-permute-start.8) | collective-permute-done | bytes 81952 | tf_op jit(solution)/shard_map/ppermute | solution.py:473
  23.7 2.3 %collective-permute-done.9.refs_1_ = bf16[160,256]{1,0:T(8,128)(2,1)S(1)} collective-permute-done((bf16[160,256]{1,0:T(8,128)(2,1)S(1)}, bf16[160,256]{1,0:T(8,128)(2,1)S(1)}, u32[]{:S(2)}, u32[]{:S(2)}) %collective-permute-start.9) | collective-permute-done | bytes 81952 | tf_op jit(solution)/shard_map/ppermute | solution.py:474
  26.0 0.0 collective-permute-done.5.back
  26.1 1.3 %finish.1 = (bf16[160,2048]{1,0:T(8,128)(2,1)}, bf16[160,512]{1,0:T(8,128)(2,1)}, bf16[160,512]{1,0:T(8,128)(2,1)}, f32[1,160]{1,0:T(1,128)}) custom-call(bf16[176,1536]{1,0:T(8,128)(2,1)S(1)} %collective-permute-done.5.back, bf16[160,1024]{1,0:T(8,128)(2,1)S(1)} %get-tuple-element.76.query_mine, f32[1,160]{1,0:T(1,128)S(1)} %get-tuple-element.77.gate_mine, ...), custom_call_target="tpu_custom_call" | custom-call | flops 1000000 | bytes 1000 | tf_op jit(solution)/shard_map/finish/pallas_call | solution.py:425
  (4 shorter events, 0.1 us)
Async XLA Ops:
  0.6 7.9 %copy-start = (bf16[1,160,2048]{2,1,0:T(8,128)(2,1)S(1)}, bf16[1,160,2048]{2,1,0:T(8,128)(2,1)}, u32[]{:S(2)}) copy-start(bf16[1,160,2048]{2,1,0:T(8,128)(2,1)} %param.7) | copy-start | bytes 1966084
  0.6 7.9 %copy-start.1 = (bf16[1,160,2048]{2,1,0:T(8,128)(2,1)S(1)}, bf16[1,160,2048]{2,1,0:T(8,128)(2,1)}, u32[]{:S(2)}) copy-start(bf16[1,160,2048]{2,1,0:T(8,128)(2,1)} %param.10) | copy-start | bytes 1966084
  2.2 6.3 %collective-permute-start = (bf16[176,2560]{1,0:T(8,128)(2,1)S(1)}, bf16[176,2560]{1,0:T(8,128)(2,1)S(1)}, u32[]{:S(2)}, u32[]{:S(2)}) collective-permute-start(bf16[176,2560]{1,0:T(8,128)(2,1)S(1)} %get-tuple-element.54), channel_id=1, source_target_pairs={{0,1},{1,0},{2,3},{3,2},{4,5},{5,4},{6,7},{7,6},{8,9},{9,8},{10,11... | collective-permute-start | bytes 2703368 | tf_op jit(solution)/shard_map/ppermute | solution.py:480
  2.8 10.3 %collective-permute-start.1 = (bf16[160,256]{1,0:T(8,128)(2,1)S(1)}, bf16[160,256]{1,0:T(8,128)(2,1)S(1)}, u32[]{:S(2)}, u32[]{:S(2)}) collective-permute-start(bf16[160,256]{1,0:T(8,128)(2,1)S(1)} %get-tuple-element.62), channel_id=1, source_target_pairs={{0,3},{1,2},{4,7},{5,6},{8,11},{9,10},{12,15},{13,14},{16,19},{17,... | collective-permute-start | bytes 245768 | tf_op jit(solution)/shard_map/ppermute | solution.py:473
  7.3 5.8 %collective-permute-start.2 = (bf16[160,256]{1,0:T(8,128)(2,1)S(1)}, bf16[160,256]{1,0:T(8,128)(2,1)S(1)}, u32[]{:S(2)}, u32[]{:S(2)}) collective-permute-start(bf16[160,256]{1,0:T(8,128)(2,1)S(1)} %get-tuple-element.48.key_mine), channel_id=1, source_target_pairs={{0,2},{1,3},{4,6},{5,7},{8,10},{9,11},{12,14},{13,15},{16,18},{17,... | collective-permute-start | bytes 245768 | tf_op jit(solution)/shard_map/ppermute | solution.py:474
  9.9 5.8 %collective-permute-start.3 = (bf16[160,256]{1,0:T(8,128)(2,1)S(1)}, bf16[160,256]{1,0:T(8,128)(2,1)S(1)}, u32[]{:S(2)}, u32[]{:S(2)}) collective-permute-start(bf16[160,256]{1,0:T(8,128)(2,1)S(1)} %get-tuple-element.69), channel_id=1, source_target_pairs={{0,3},{1,2},{4,7},{5,6},{8,11},{9,10},{12,15},{13,14},{16,19},{17,... | collective-permute-start | bytes 245768 | tf_op jit(solution)/shard_map/ppermute | solution.py:473
  11.8 4.0 %collective-permute-start.4 = (bf16[160,256]{1,0:T(8,128)(2,1)S(1)}, bf16[160,256]{1,0:T(8,128)(2,1)S(1)}, u32[]{:S(2)}, u32[]{:S(2)}) collective-permute-start(bf16[160,256]{1,0:T(8,128)(2,1)S(1)} %get-tuple-element.70), channel_id=1, source_target_pairs={{0,2},{1,3},{4,6},{5,7},{8,10},{9,11},{12,14},{13,15},{16,18},{17,... | collective-permute-start | bytes 245768 | tf_op jit(solution)/shard_map/ppermute | solution.py:474
  13.1 8.3 %collective-permute-start.6 = (bf16[160,256]{1,0:T(8,128)(2,1)S(1)}, bf16[160,256]{1,0:T(8,128)(2,1)S(1)}, u32[]{:S(2)}, u32[]{:S(2)}) collective-permute-start(bf16[160,256]{1,0:T(8,128)(2,1)S(1)} %get-tuple-element.79), channel_id=1, source_target_pairs={{3,0},{2,1},{7,4},{6,5},{11,8},{10,9},{15,12},{14,13},{19,16},{18,... | collective-permute-start | bytes 245768 | tf_op jit(solution)/shard_map/ppermute | solution.py:473
  14.4 7.1 %collective-permute-start.7 = (bf16[160,256]{1,0:T(8,128)(2,1)S(1)}, bf16[160,256]{1,0:T(8,128)(2,1)S(1)}, u32[]{:S(2)}, u32[]{:S(2)}) collective-permute-start(bf16[160,256]{1,0:T(8,128)(2,1)S(1)} %get-tuple-element.80), channel_id=1, source_target_pairs={{2,0},{3,1},{6,4},{7,5},{10,8},{11,9},{14,12},{15,13},{18,16},{19,... | collective-permute-start | bytes 245768 | tf_op jit(solution)/shard_map/ppermute | solution.py:474
  15.8 8.0 %collective-permute-start.8 = (bf16[160,256]{1,0:T(8,128)(2,1)S(1)}, bf16[160,256]{1,0:T(8,128)(2,1)S(1)}, u32[]{:S(2)}, u32[]{:S(2)}) collective-permute-start(bf16[160,256]{1,0:T(8,128)(2,1)S(1)} %get-tuple-element.82), channel_id=1, source_target_pairs={{3,0},{2,1},{7,4},{6,5},{11,8},{10,9},{15,12},{14,13},{19,16},{18,... | collective-permute-start | bytes 245768 | tf_op jit(solution)/shard_map/ppermute | solution.py:473
  17.1 9.0 %collective-permute-start.9 = (bf16[160,256]{1,0:T(8,128)(2,1)S(1)}, bf16[160,256]{1,0:T(8,128)(2,1)S(1)}, u32[]{:S(2)}, u32[]{:S(2)}) collective-permute-start(bf16[160,256]{1,0:T(8,128)(2,1)S(1)} %get-tuple-element.83), channel_id=1, source_target_pairs={{2,0},{3,1},{6,4},{7,5},{10,8},{11,9},{14,12},{15,13},{18,16},{19,... | collective-permute-start | bytes 245768 | tf_op jit(solution)/shard_map/ppermute | solution.py:474
  21.3 4.8 %collective-permute-start.5 = (bf16[176,1536]{1,0:T(8,128)(2,1)S(1)}, bf16[176,1536]{1,0:T(8,128)(2,1)S(1)}, u32[]{:S(2)}, u32[]{:S(2)}) collective-permute-start(bf16[176,1536]{1,0:T(8,128)(2,1)S(1)} %get-tuple-element.75), channel_id=1, source_target_pairs={{0,1},{1,0},{2,3},{3,2},{4,5},{5,4},{6,7},{7,6},{8,9},{9,8},{10,11... | collective-permute-start | bytes 1622024 | tf_op jit(solution)/shard_map/ppermute | solution.py:571

commit v14 on v12

--- a/solution.py
+++ b/solution.py
@@ -314,10 +314,22 @@
                 deltas[i, :, here] = delta
                 score_grad = raw * far_factors[i, :, here] * (prob_grad - delta)
                 score_grads[i, :, here] = score_grad.astype(BF16)
-            for j, out_ref in enumerate(parts):
-                there = slice(j * rows, (j + 1) * rows)
-                part = dot(score_grads[i, there, :], query[i], NN) * LN2
-                out_ref[:, i * DH : (i + 1) * DH] = part.astype(BF16)
+            key_parts(score_grads, query, parts, i, 0)
+
+
+def key_parts(score_grads, query, parts, i, first):
+    rows = parts[0].shape[0]
+    for j, out_ref in enumerate(parts):
+        there = slice((first + j) * rows, (first + j + 1) * rows)
+        part = dot(score_grads[i, there, :], query[i], NN) * LN2
+        out_ref[:, i * DH : (i + 1) * DH] = part.astype(BF16)
+
+
+def far_rest_kernel(query, score_grads, *parts):
+    @pl.when(lax.axis_index("ctx") >= 2)
+    def _():
+        for i in range(query.shape[0]):
+            key_parts(score_grads, query, parts, i, len(parts))
 
 
 def near_kernel(
@@ -384,16 +396,20 @@
         own[:, here] = value
 
 
-def sum_rest_kernel(value_own, part_mine, *refs):
-    got, (own, other) = refs[:-2], refs[-2:]
+def sum_middle_kernel(value_own, *refs):
+    got, other = refs[:-1], refs[-1]
     total = got[0][...].astype(F32)
-    for ref in got[2::2]:
+    for ref in got[1:]:
         total = total + ref[...].astype(F32)
     other[...] = total
+
+
+def sum_rest_kernel(key_other, part_mine, *refs):
+    got, own = refs[:-1], refs[-1]
     for i in range(own.shape[1] // DH):
         here = slice(i * DH, (i + 1) * DH)
         key = part_mine[:, 2 * i * DH : (2 * i + 1) * DH]
-        for ref in got[1::2]:
+        for ref in got:
             key = key + ref[:, here].astype(F32)
         own[:, here] = key
 
@@ -548,7 +564,7 @@
     far_grads, deltas, *parts = call(
         functools.partial(far_values_kernel, blocks=blocks),
         "far_values",
-        [far_low, row] + [packet] * blocks,
+        [far_low, row] + [packet] * (chips - 1),
         query,
         cot,
         far_raws,
@@ -560,7 +576,9 @@
         *own_values,
         scratch=[pltpu.VMEM(*far_rows)],
     )
-    sib_key_got, own_key_got = send(parts[: chips - 1], parts[chips - 1 :], back_cross, back_hop)
+    sib_key_got = [lax.ppermute(parts[s - 1], "ctx", back_cross[s]) for s in steps]
+    parts = call(far_rest_kernel, "far_rest", [packet] * (chips - 1), query, far_grads)
+    own_key_got = [lax.ppermute(parts[s - 1], "ctx", back_hop[s]) for s in steps]
 
     part_mine, query_mine, gate_part, theirs = call(
         functools.partial(near_kernel, ratio=ratio),
@@ -599,17 +617,10 @@
         [total, total],
         part_mine,
         *[part for pair in zip(sib_value_got, own_value_got) for part in pair],
-        flops=5 * 10**9,
-    )
-    key_own, key_other = call(
-        sum_rest_kernel,
-        "sum_rest",
-        [total, total],
-        value_own,
-        part_mine,
-        *[part for pair in zip(sib_key_got, own_key_got) for part in pair],
-        flops=5 * 10**9,
-    )
+        flops=3 * 10**8,
+    )
+    (key_other,) = call(sum_middle_kernel, "sum_middle", [total], value_own, *sib_key_got, flops=5 * 10**9)
+    (key_own,) = call(sum_rest_kernel, "sum_rest", [total], key_other, part_mine, *own_key_got, flops=5 * 10**9)
     query_grad, key_grad, value_grad, gate_grad = call(
         finish_kernel,
         "finish",

time: 27.3 us -> 26.8 us (0.982)
  waiting for transfers between devices: 5.29 us -> 4.83 us
    ppermute x0 -> x2, waiting for transfers between devices: none -> 4 us  [the longest x1 2.25 us: per_device(): lax.ppermute(parts[s - 1], 'ctx', back_hop[s])]
    ppermute x0 -> x2, starting transfers between devices: none -> 2.58 us  [the longest x1 1.29 us: per_device(): lax.ppermute(parts[s - 1], 'ctx', back_cross[s])]
    ppermute x4 -> x3, waiting for transfers between devices: 3.11 us -> 0.82 us  [send(): return (sib, [lax.ppermute(own[s - 1], 'ctx', own_pairs[s]) for s in steps])]
    ppermute x4 -> x3, waiting for transfers between devices: 2.18 us -> 0.01 us  [send(): sib = [lax.ppermute(sib[s - 1], 'ctx', sib_pairs[s]) for s in steps]]
    ppermute x4 -> x3, starting transfers between devices: 8.38 us -> 7.08 us  [send(): sib = [lax.ppermute(sib[s - 1], 'ctx', sib_pairs[s]) for s in steps]]
    ppermute x4 -> x3, starting transfers between devices: 5.17 us -> 3.88 us  [send(): return (sib, [lax.ppermute(own[s - 1], 'ctx', own_pairs[s]) for s in steps])]
    pallas_call x9 -> x11, Pallas kernels: 6.62 us -> 6.63 us  [call(): pl.pallas_call(kernel, out_shape=[jax.ShapeDtypeStruct(*out) for out in o...]
where the time goes in v14:
time: 26.8 us; the launch traced here: 26.5 us
  starting transfers between devices  14.2 us (53%)
  Pallas kernels  6.63 us (25%)
  waiting for transfers between devices  4.83 us (18%)
  between operations  0.83 us (3%)
    ppermute x3, starting transfers between devices, send(): sib = [lax.ppermute(sib[s - 1], 'ctx', sib_pairs[s]) for s in steps]  7.08 us
    pallas_call x11, Pallas kernels, call(): pl.pallas_call(kernel, out_shape=[jax.ShapeDtypeStruct(*out) for out in o...  6.63 us
    ppermute x3, starting transfers between devices, send(): return (sib, [lax.ppermute(own[s - 1], 'ctx', own_pairs[s]) for s in steps])  3.88 us
    ppermute x1, waiting for transfers between devices, per_device(): lax.ppermute(parts[s - 1], 'ctx', back_hop[s])  2.25 us
    ppermute x1, waiting for transfers between devices, per_device(): lax.ppermute(parts[s - 1], 'ctx', back_cross[s])  1.74 us
    ppermute x1, starting transfers between devices, per_device(): lax.ppermute(parts[s - 1], 'ctx', back_cross[s])  1.29 us
    ppermute x1, starting transfers between devices, per_device(): lax.ppermute(parts[s - 1], 'ctx', back_hop[s])  1.29 us
    ppermute x3, waiting for transfers between devices, send(): return (sib, [lax.ppermute(own[s - 1], 'ctx', own_pairs[s]) for s in steps])  0.82 us
  transfers between devices with their start and end apart: 10, of which 3 were waited for; matrix products, arithmetic and copies ran while one was open for 0% of the time, Pallas kernels for 14%

profile of v14, /device:TPU:0, one launch (start us, length us, event | category | flops | bytes accessed | tf_op | source)
XLA Modules:
  0.0 26.5 jit_solution(16539520832507725024)
XLA Ops:
  0.6 0.0 copy-start
  0.6 0.0 copy-start.1
  0.7 1.6 %pack.1 = (bf16[160,256]{1,0:T(8,128)(2,1)S(1)}, bf16[160,256]{1,0:T(8,128)(2,1)S(1)}, bf16[160,256]{1,0:T(8,128)(2,1)S(1)}, bf16[160,256]{1,0:T(8,128)(2,1)S(1)...) custom-call(bf16[160,512]{1,0:T(8,128)(2,1)} %bitcast.12, ...), custom_call_target="tpu_custom_call" | custom-call | flops 5000000000 | bytes 1000 | tf_op jit(solution)/shard_map/pack/pallas_call | solution.py:462
  2.2 0.5 %collective-permute-start = (bf16[176,2560]{1,0:T(8,128)(2,1)S(1)}, bf16[176,2560]{1,0:T(8,128)(2,1)S(1)}, u32[]{:S(2)}, u32[]{:S(2)}) collective-permute-start(bf16[176,2560]{1,0:T(8,128)(2,1)S(1)} %get-tuple-element.51), channel_id=1, source_target_pairs={{0,1},{1,0},{2,3},{3,2},{4,5},{5,4},{6,7},{7,6},{8,9},{9,8},{10,11... | collective-permute-start | bytes 2703368 | tf_op jit(solution)/shard_map/ppermute | solution.py:518
  2.8 4.5 %collective-permute-start.1 = (bf16[160,256]{1,0:T(8,128)(2,1)S(1)}, bf16[160,256]{1,0:T(8,128)(2,1)S(1)}, u32[]{:S(2)}, u32[]{:S(2)}) collective-permute-start(bf16[160,256]{1,0:T(8,128)(2,1)S(1)} %get-tuple-element.59), channel_id=1, source_target_pairs={{0,3},{1,2},{4,7},{5,6},{8,11},{9,10},{12,15},{13,14},{16,19},{17,... | collective-permute-start | bytes 245768 | tf_op jit(solution)/shard_map/ppermute | solution.py:510
  7.3 1.3 %collective-permute-start.2 = (bf16[160,256]{1,0:T(8,128)(2,1)S(1)}, bf16[160,256]{1,0:T(8,128)(2,1)S(1)}, u32[]{:S(2)}, u32[]{:S(2)}) collective-permute-start(bf16[160,256]{1,0:T(8,128)(2,1)S(1)} %get-tuple-element.46.key_mine), channel_id=1, source_target_pairs={{0,2},{1,3},{4,6},{5,7},{8,10},{9,11},{12,14},{13,15},{16,18},{17,... | collective-permute-start | bytes 245768 | tf_op jit(solution)/shard_map/ppermute | solution.py:511
  8.6 1.3 %collective-permute-start.3 = (bf16[160,256]{1,0:T(8,128)(2,1)S(1)}, bf16[160,256]{1,0:T(8,128)(2,1)S(1)}, u32[]{:S(2)}, u32[]{:S(2)}) collective-permute-start(bf16[160,256]{1,0:T(8,128)(2,1)S(1)} %get-tuple-element.69), channel_id=1, source_target_pairs={{0,3},{1,2},{4,7},{5,6},{8,11},{9,10},{12,15},{13,14},{16,19},{17,... | collective-permute-start | bytes 245768 | tf_op jit(solution)/shard_map/ppermute | solution.py:510
  9.9 1.3 %collective-permute-start.4 = (bf16[160,256]{1,0:T(8,128)(2,1)S(1)}, bf16[160,256]{1,0:T(8,128)(2,1)S(1)}, u32[]{:S(2)}, u32[]{:S(2)}) collective-permute-start(bf16[160,256]{1,0:T(8,128)(2,1)S(1)} %get-tuple-element.47.value_mine), channel_id=1, source_target_pairs={{0,2},{1,3},{4,6},{5,7},{8,10},{9,11},{12,14},{13,15},{16,18},{17,... | collective-permute-start | bytes 245768 | tf_op jit(solution)/shard_map/ppermute | solution.py:511
  11.2 0.0 collective-permute-done.sib
  11.2 0.0 copy-done
  11.2 0.0 copy-done.1
  11.2 1.5 %local_scores.1 = (bf16[2,320,128]{2,1,0:T(8,128)(2,1)S(1)}, bf16[2,1280,128]{2,1,0:T(8,128)(2,1)S(1)}, bf16[2,1280,128]{2,1,0:T(8,128)(2,1)S(1)}, f32[1,1280]{1...) custom-call(bf16[160,256]{1,0:T(8,128)(2,1)S(1)} %get-tuple-element., ...), custom_call_target="tpu_custom_call" | custom-call | flops 3000000 | bytes 1000 | tf_op jit(solution)/shard_map/local_scores/pallas_call | solution.py:462
  12.7 0.0 collective-permute-done.1.packet.refs_0_
  12.8 0.0 collective-permute-done.2.refs_1_
  12.8 1.3 %collective-permute-start.6 = (bf16[160,256]{1,0:T(8,128)(2,1)S(1)}, bf16[160,256]{1,0:T(8,128)(2,1)S(1)}, u32[]{:S(2)}, u32[]{:S(2)}) collective-permute-start(bf16[160,256]{1,0:T(8,128)(2,1)S(1)} %get-tuple-element.78), channel_id=1, source_target_pairs={{3,0},{2,1},{7,4},{6,5},{11,8},{10,9},{15,12},{14,13},{19,16},{18,... | collective-permute-start | bytes 245768 | tf_op jit(solution)/shard_map/ppermute | solution.py:510
  14.1 1.3 %collective-permute-start.7 = (bf16[160,256]{1,0:T(8,128)(2,1)S(1)}, bf16[160,256]{1,0:T(8,128)(2,1)S(1)}, u32[]{:S(2)}, u32[]{:S(2)}) collective-permute-start(bf16[160,256]{1,0:T(8,128)(2,1)S(1)} %get-tuple-element.79), channel_id=1, source_target_pairs={{2,0},{3,1},{6,4},{7,5},{10,8},{11,9},{14,12},{15,13},{18,16},{19,... | collective-permute-start | bytes 245768 | tf_op jit(solution)/shard_map/ppermute | solution.py:511
  15.4 0.0 collective-permute-done.3.refs_0_
  15.4 0.0 collective-permute-done.4.refs_1_
  15.5 1.3 %collective-permute-start.8 = (bf16[160,256]{1,0:T(8,128)(2,1)S(1)}, bf16[160,256]{1,0:T(8,128)(2,1)S(1)}, u32[]{:S(2)}, u32[]{:S(2)}) collective-permute-start(bf16[160,256]{1,0:T(8,128)(2,1)S(1)} %get-tuple-element.81), channel_id=1, source_target_pairs={{3,0},{2,1},{7,4},{6,5},{11,8},{10,9},{15,12},{14,13},{19,16},{18,... | collective-permute-start | bytes 245768 | tf_op jit(solution)/shard_map/ppermute | solution.py:579
  16.8 1.3 %collective-permute-start.9 = (bf16[160,256]{1,0:T(8,128)(2,1)S(1)}, bf16[160,256]{1,0:T(8,128)(2,1)S(1)}, u32[]{:S(2)}, u32[]{:S(2)}) collective-permute-start(bf16[160,256]{1,0:T(8,128)(2,1)S(1)} %far_rest.1), channel_id=1, source_target_pairs={{2,0},{3,1},{6,4},{7,5},{10,8},{11,9},{14,12},{15,13},{18,16},{19,... | collective-permute-start | bytes 245768 | tf_op jit(solution)/shard_map/ppermute | solution.py:581
  18.1 2.1 %near_grads.1 = (f32[160,512]{1,0:T(8,128)S(1)}, bf16[160,1024]{1,0:T(8,128)(2,1)S(1)}, f32[1,160]{1,0:T(1,128)S(1)}, bf16[176,1536]{1,0:T(8,128)(2,1)S(1)}) custom-call(f32[2,320,1280]{2,1,0:T(8,128)S(1)} %get-tuple-element.52.raws, f32[2,320,1280]{2,1,0:T(8,128)S(1)} %get-tuple-element.53.grads, f32[2,1,1280]{2,1,0:T(1,128)S(1)} %get-tuple-element.63.factors, ...), custom_call_target="tpu_custom_call" | custom-call | flops 4000000 | bytes 1000 | tf_op jit(solution)/shard_map/near_grads/pallas_call | solution.py:462
  20.2 0.2 collective-permute-start.5
  20.4 0.0 collective-permute-done.6.refs_0_
  20.4 0.8 %collective-permute-done.7.refs_1_ = bf16[160,256]{1,0:T(8,128)(2,1)S(1)} collective-permute-done((bf16[160,256]{1,0:T(8,128)(2,1)S(1)}, bf16[160,256]{1,0:T(8,128)(2,1)S(1)}, u32[]{:S(2)}, u32[]{:S(2)}) %collective-permute-start.7) | collective-permute-done | bytes 81952 | tf_op jit(solution)/shard_map/ppermute | solution.py:511
  21.2 1.7 %collective-permute-done.8.refs_0_ = bf16[160,256]{1,0:T(8,128)(2,1)S(1)} collective-permute-done((bf16[160,256]{1,0:T(8,128)(2,1)S(1)}, bf16[160,256]{1,0:T(8,128)(2,1)S(1)}, u32[]{:S(2)}, u32[]{:S(2)}) %collective-permute-start.8) | collective-permute-done | bytes 81952 | tf_op jit(solution)/shard_map/ppermute | solution.py:579
  23.0 2.3 %collective-permute-done.9.refs_0_ = bf16[160,256]{1,0:T(8,128)(2,1)S(1)} collective-permute-done((bf16[160,256]{1,0:T(8,128)(2,1)S(1)}, bf16[160,256]{1,0:T(8,128)(2,1)S(1)}, u32[]{:S(2)}, u32[]{:S(2)}) %collective-permute-start.9) | collective-permute-done | bytes 81952 | tf_op jit(solution)/shard_map/ppermute | solution.py:581
  25.3 0.0 collective-permute-done.5.back
  25.3 1.3 %finish.1 = (bf16[160,2048]{1,0:T(8,128)(2,1)}, bf16[160,512]{1,0:T(8,128)(2,1)}, bf16[160,512]{1,0:T(8,128)(2,1)}, f32[1,160]{1,0:T(1,128)}) custom-call(bf16[176,1536]{1,0:T(8,128)(2,1)S(1)} %collective-permute-done.5.back, bf16[160,1024]{1,0:T(8,128)(2,1)S(1)} %get-tuple-element.75.query_mine, f32[1,160]{1,0:T(1,128)S(1)} %get-tuple-element.76.gate_mine, ...), custom_call_target="tpu_custom_call" | custom-call | flops 1000000 | bytes 1000 | tf_op jit(solution)/shard_map/finish/pallas_call | solution.py:462
  (7 shorter events, 0.1 us)
Async XLA Ops:
  0.6 10.5 %copy-start = (bf16[1,160,2048]{2,1,0:T(8,128)(2,1)S(1)}, bf16[1,160,2048]{2,1,0:T(8,128)(2,1)}, u32[]{:S(2)}) copy-start(bf16[1,160,2048]{2,1,0:T(8,128)(2,1)} %param.7) | copy-start | bytes 1966084
  0.6 10.5 %copy-start.1 = (bf16[1,160,2048]{2,1,0:T(8,128)(2,1)S(1)}, bf16[1,160,2048]{2,1,0:T(8,128)(2,1)}, u32[]{:S(2)}) copy-start(bf16[1,160,2048]{2,1,0:T(8,128)(2,1)} %param.10) | copy-start | bytes 1966084
  2.2 8.9 %collective-permute-start = (bf16[176,2560]{1,0:T(8,128)(2,1)S(1)}, bf16[176,2560]{1,0:T(8,128)(2,1)S(1)}, u32[]{:S(2)}, u32[]{:S(2)}) collective-permute-start(bf16[176,2560]{1,0:T(8,128)(2,1)S(1)} %get-tuple-element.51), channel_id=1, source_target_pairs={{0,1},{1,0},{2,3},{3,2},{4,5},{5,4},{6,7},{7,6},{8,9},{9,8},{10,11... | collective-permute-start | bytes 2703368 | tf_op jit(solution)/shard_map/ppermute | solution.py:518
  2.8 10.0 %collective-permute-start.1 = (bf16[160,256]{1,0:T(8,128)(2,1)S(1)}, bf16[160,256]{1,0:T(8,128)(2,1)S(1)}, u32[]{:S(2)}, u32[]{:S(2)}) collective-permute-start(bf16[160,256]{1,0:T(8,128)(2,1)S(1)} %get-tuple-element.59), channel_id=1, source_target_pairs={{0,3},{1,2},{4,7},{5,6},{8,11},{9,10},{12,15},{13,14},{16,19},{17,... | collective-permute-start | bytes 245768 | tf_op jit(solution)/shard_map/ppermute | solution.py:510
  7.3 5.5 %collective-permute-start.2 = (bf16[160,256]{1,0:T(8,128)(2,1)S(1)}, bf16[160,256]{1,0:T(8,128)(2,1)S(1)}, u32[]{:S(2)}, u32[]{:S(2)}) collective-permute-start(bf16[160,256]{1,0:T(8,128)(2,1)S(1)} %get-tuple-element.46.key_mine), channel_id=1, source_target_pairs={{0,2},{1,3},{4,6},{5,7},{8,10},{9,11},{12,14},{13,15},{16,18},{17,... | collective-permute-start | bytes 245768 | tf_op jit(solution)/shard_map/ppermute | solution.py:511
  8.6 6.9 %collective-permute-start.3 = (bf16[160,256]{1,0:T(8,128)(2,1)S(1)}, bf16[160,256]{1,0:T(8,128)(2,1)S(1)}, u32[]{:S(2)}, u32[]{:S(2)}) collective-permute-start(bf16[160,256]{1,0:T(8,128)(2,1)S(1)} %get-tuple-element.69), channel_id=1, source_target_pairs={{0,3},{1,2},{4,7},{5,6},{8,11},{9,10},{12,15},{13,14},{16,19},{17,... | collective-permute-start | bytes 245768 | tf_op jit(solution)/shard_map/ppermute | solution.py:510
  9.9 5.6 %collective-permute-start.4 = (bf16[160,256]{1,0:T(8,128)(2,1)S(1)}, bf16[160,256]{1,0:T(8,128)(2,1)S(1)}, u32[]{:S(2)}, u32[]{:S(2)}) collective-permute-start(bf16[160,256]{1,0:T(8,128)(2,1)S(1)} %get-tuple-element.47.value_mine), channel_id=1, source_target_pairs={{0,2},{1,3},{4,6},{5,7},{8,10},{9,11},{12,14},{13,15},{16,18},{17,... | collective-permute-start | bytes 245768 | tf_op jit(solution)/shard_map/ppermute | solution.py:511
  12.8 7.6 %collective-permute-start.6 = (bf16[160,256]{1,0:T(8,128)(2,1)S(1)}, bf16[160,256]{1,0:T(8,128)(2,1)S(1)}, u32[]{:S(2)}, u32[]{:S(2)}) collective-permute-start(bf16[160,256]{1,0:T(8,128)(2,1)S(1)} %get-tuple-element.78), channel_id=1, source_target_pairs={{3,0},{2,1},{7,4},{6,5},{11,8},{10,9},{15,12},{14,13},{19,16},{18,... | collective-permute-start | bytes 245768 | tf_op jit(solution)/shard_map/ppermute | solution.py:510
  14.1 7.1 %collective-permute-start.7 = (bf16[160,256]{1,0:T(8,128)(2,1)S(1)}, bf16[160,256]{1,0:T(8,128)(2,1)S(1)}, u32[]{:S(2)}, u32[]{:S(2)}) collective-permute-start(bf16[160,256]{1,0:T(8,128)(2,1)S(1)} %get-tuple-element.79), channel_id=1, source_target_pairs={{2,0},{3,1},{6,4},{7,5},{10,8},{11,9},{14,12},{15,13},{18,16},{19,... | collective-permute-start | bytes 245768 | tf_op jit(solution)/shard_map/ppermute | solution.py:511
  15.5 7.5 %collective-permute-start.8 = (bf16[160,256]{1,0:T(8,128)(2,1)S(1)}, bf16[160,256]{1,0:T(8,128)(2,1)S(1)}, u32[]{:S(2)}, u32[]{:S(2)}) collective-permute-start(bf16[160,256]{1,0:T(8,128)(2,1)S(1)} %get-tuple-element.81), channel_id=1, source_target_pairs={{3,0},{2,1},{7,4},{6,5},{11,8},{10,9},{15,12},{14,13},{19,16},{18,... | collective-permute-start | bytes 245768 | tf_op jit(solution)/shard_map/ppermute | solution.py:579
  16.8 8.5 %collective-permute-start.9 = (bf16[160,256]{1,0:T(8,128)(2,1)S(1)}, bf16[160,256]{1,0:T(8,128)(2,1)S(1)}, u32[]{:S(2)}, u32[]{:S(2)}) collective-permute-start(bf16[160,256]{1,0:T(8,128)(2,1)S(1)} %far_rest.1), channel_id=1, source_target_pairs={{2,0},{3,1},{6,4},{7,5},{10,8},{11,9},{14,12},{15,13},{18,16},{19,... | collective-permute-start | bytes 245768 | tf_op jit(solution)/shard_map/ppermute | solution.py:581
  20.2 5.1 %collective-permute-start.5 = (bf16[176,1536]{1,0:T(8,128)(2,1)S(1)}, bf16[176,1536]{1,0:T(8,128)(2,1)S(1)}, u32[]{:S(2)}, u32[]{:S(2)}) collective-permute-start(bf16[176,1536]{1,0:T(8,128)(2,1)S(1)} %get-tuple-element.74), channel_id=1, source_target_pairs={{0,1},{1,0},{2,3},{3,2},{4,5},{5,4},{6,7},{7,6},{8,9},{9,8},{10,11... | collective-permute-start | bytes 1622024 | tf_op jit(solution)/shard_map/ppermute | solution.py:612

commit v15 on v14

--- a/solution.py
+++ b/solution.py
@@ -314,7 +314,7 @@
                 deltas[i, :, here] = delta
                 score_grad = raw * far_factors[i, :, here] * (prob_grad - delta)
                 score_grads[i, :, here] = score_grad.astype(BF16)
-            key_parts(score_grads, query, parts, i, 0)
+            key_parts(score_grads, query, parts, i, len(parts))
 
 
 def key_parts(score_grads, query, parts, i, first):
@@ -329,7 +329,7 @@
     @pl.when(lax.axis_index("ctx") >= 2)
     def _():
         for i in range(query.shape[0]):
-            key_parts(score_grads, query, parts, i, len(parts))
+            key_parts(score_grads, query, parts, i, 0)
 
 
 def near_kernel(
@@ -396,15 +396,7 @@
         own[:, here] = value
 
 
-def sum_middle_kernel(value_own, *refs):
-    got, other = refs[:-1], refs[-1]
-    total = got[0][...].astype(F32)
-    for ref in got[1:]:
-        total = total + ref[...].astype(F32)
-    other[...] = total
-
-
-def sum_rest_kernel(key_other, part_mine, *refs):
+def sum_middle_kernel(value_own, part_mine, *refs):
     got, own = refs[:-1], refs[-1]
     for i in range(own.shape[1] // DH):
         here = slice(i * DH, (i + 1) * DH)
@@ -412,6 +404,14 @@
         for ref in got:
             key = key + ref[:, here].astype(F32)
         own[:, here] = key
+
+
+def sum_rest_kernel(key_own, *refs):
+    got, other = refs[:-1], refs[-1]
+    total = got[0][...].astype(F32)
+    for ref in got[1:]:
+        total = total + ref[...].astype(F32)
+    other[...] = total
 
 
 def finish_kernel(
@@ -576,9 +576,9 @@
         *own_values,
         scratch=[pltpu.VMEM(*far_rows)],
     )
+    own_key_got = [lax.ppermute(parts[s - 1], "ctx", back_hop[s]) for s in steps]
+    parts = call(far_rest_kernel, "far_rest", [packet] * (chips - 1), query, far_grads)
     sib_key_got = [lax.ppermute(parts[s - 1], "ctx", back_cross[s]) for s in steps]
-    parts = call(far_rest_kernel, "far_rest", [packet] * (chips - 1), query, far_grads)
-    own_key_got = [lax.ppermute(parts[s - 1], "ctx", back_hop[s]) for s in steps]
 
     part_mine, query_mine, gate_part, theirs = call(
         functools.partial(near_kernel, ratio=ratio),
@@ -619,8 +619,8 @@
         *[part for pair in zip(sib_value_got, own_value_got) for part in pair],
         flops=3 * 10**8,
     )
-    (key_other,) = call(sum_middle_kernel, "sum_middle", [total], value_own, *sib_key_got, flops=5 * 10**9)
-    (key_own,) = call(sum_rest_kernel, "sum_rest", [total], key_other, part_mine, *own_key_got, flops=5 * 10**9)
+    (key_own,) = call(sum_middle_kernel, "sum_middle", [total], value_own, part_mine, *own_key_got, flops=5 * 10**9)
+    (key_other,) = call(sum_rest_kernel, "sum_rest", [total], key_own, *sib_key_got, flops=5 * 10**9)
     query_grad, key_grad, value_grad, gate_grad = call(
         finish_kernel,
         "finish",

time: 26.8 us -> 26.4 us (0.985)
  waiting for transfers between devices: 4.83 us -> 4.43 us
    ppermute x1, waiting for transfers between devices: 1.74 us -> 1.23 us  [per_device(): lax.ppermute(parts[s - 1], 'ctx', back_cross[s])]
  transfers between devices with their start and end apart: 10 -> 10, of which waited for: 3 -> 3; matrix products, arithmetic and copies ran while one was open for 0% -> 0% of each run, Pallas kernels for 14% -> 15%
where the time goes in v15:
time: 26.4 us; the launch traced here: 26.1 us
  starting transfers between devices  14.2 us (54%)
  Pallas kernels  6.63 us (25%)
  waiting for transfers between devices  4.43 us (17%)
  between operations  0.83 us (3%)
    ppermute x3, starting transfers between devices, send(): sib = [lax.ppermute(sib[s - 1], 'ctx', sib_pairs[s]) for s in steps]  7.08 us
    pallas_call x11, Pallas kernels, call(): pl.pallas_call(kernel, out_shape=[jax.ShapeDtypeStruct(*out) for out in o...  6.63 us
    ppermute x3, starting transfers between devices, send(): return (sib, [lax.ppermute(own[s - 1], 'ctx', own_pairs[s]) for s in steps])  3.88 us
    ppermute x1, waiting for transfers between devices, per_device(): lax.ppermute(parts[s - 1], 'ctx', back_hop[s])  2.37 us
    ppermute x1, starting transfers between devices, per_device(): lax.ppermute(parts[s - 1], 'ctx', back_hop[s])  1.29 us
    ppermute x1, starting transfers between devices, per_device(): lax.ppermute(parts[s - 1], 'ctx', back_cross[s])  1.29 us
    ppermute x1, waiting for transfers between devices, per_device(): lax.ppermute(parts[s - 1], 'ctx', back_cross[s])  1.23 us
    ppermute x3, waiting for transfers between devices, send(): return (sib, [lax.ppermute(own[s - 1], 'ctx', own_pairs[s]) for s in steps])  0.82 us
  transfers between devices with their start and end apart: 10, of which 3 were waited for; matrix products, arithmetic and copies ran while one was open for 0% of the time, Pallas kernels for 15%

profile of v15, /device:TPU:0, one launch (start us, length us, event | category | flops | bytes accessed | tf_op | source)
XLA Modules:
  0.0 26.1 jit_solution(8777234941665368886)
XLA Ops:
  0.6 0.0 copy-start
  0.6 0.0 copy-start.1
  0.7 1.6 %pack.1 = (bf16[160,256]{1,0:T(8,128)(2,1)S(1)}, bf16[160,256]{1,0:T(8,128)(2,1)S(1)}, bf16[160,256]{1,0:T(8,128)(2,1)S(1)}, bf16[160,256]{1,0:T(8,128)(2,1)S(1)...) custom-call(bf16[160,512]{1,0:T(8,128)(2,1)} %bitcast.12, ...), custom_call_target="tpu_custom_call" | custom-call | flops 5000000000 | bytes 1000 | tf_op jit(solution)/shard_map/pack/pallas_call | solution.py:462
  2.2 0.5 %collective-permute-start = (bf16[176,2560]{1,0:T(8,128)(2,1)S(1)}, bf16[176,2560]{1,0:T(8,128)(2,1)S(1)}, u32[]{:S(2)}, u32[]{:S(2)}) collective-permute-start(bf16[176,2560]{1,0:T(8,128)(2,1)S(1)} %get-tuple-element.51), channel_id=1, source_target_pairs={{0,1},{1,0},{2,3},{3,2},{4,5},{5,4},{6,7},{7,6},{8,9},{9,8},{10,11... | collective-permute-start | bytes 2703368 | tf_op jit(solution)/shard_map/ppermute | solution.py:518
  2.8 4.5 %collective-permute-start.1 = (bf16[160,256]{1,0:T(8,128)(2,1)S(1)}, bf16[160,256]{1,0:T(8,128)(2,1)S(1)}, u32[]{:S(2)}, u32[]{:S(2)}) collective-permute-start(bf16[160,256]{1,0:T(8,128)(2,1)S(1)} %get-tuple-element.59), channel_id=1, source_target_pairs={{0,3},{1,2},{4,7},{5,6},{8,11},{9,10},{12,15},{13,14},{16,19},{17,... | collective-permute-start | bytes 245768 | tf_op jit(solution)/shard_map/ppermute | solution.py:510
  7.3 1.3 %collective-permute-start.2 = (bf16[160,256]{1,0:T(8,128)(2,1)S(1)}, bf16[160,256]{1,0:T(8,128)(2,1)S(1)}, u32[]{:S(2)}, u32[]{:S(2)}) collective-permute-start(bf16[160,256]{1,0:T(8,128)(2,1)S(1)} %get-tuple-element.46.key_mine), channel_id=1, source_target_pairs={{0,2},{1,3},{4,6},{5,7},{8,10},{9,11},{12,14},{13,15},{16,18},{17,... | collective-permute-start | bytes 245768 | tf_op jit(solution)/shard_map/ppermute | solution.py:511
  8.6 1.3 %collective-permute-start.3 = (bf16[160,256]{1,0:T(8,128)(2,1)S(1)}, bf16[160,256]{1,0:T(8,128)(2,1)S(1)}, u32[]{:S(2)}, u32[]{:S(2)}) collective-permute-start(bf16[160,256]{1,0:T(8,128)(2,1)S(1)} %get-tuple-element.69), channel_id=1, source_target_pairs={{0,3},{1,2},{4,7},{5,6},{8,11},{9,10},{12,15},{13,14},{16,19},{17,... | collective-permute-start | bytes 245768 | tf_op jit(solution)/shard_map/ppermute | solution.py:510
  9.9 1.3 %collective-permute-start.4 = (bf16[160,256]{1,0:T(8,128)(2,1)S(1)}, bf16[160,256]{1,0:T(8,128)(2,1)S(1)}, u32[]{:S(2)}, u32[]{:S(2)}) collective-permute-start(bf16[160,256]{1,0:T(8,128)(2,1)S(1)} %get-tuple-element.47.value_mine), channel_id=1, source_target_pairs={{0,2},{1,3},{4,6},{5,7},{8,10},{9,11},{12,14},{13,15},{16,18},{17,... | collective-permute-start | bytes 245768 | tf_op jit(solution)/shard_map/ppermute | solution.py:511
  11.2 0.0 collective-permute-done.sib
  11.2 0.0 copy-done
  11.2 0.0 copy-done.1
  11.2 1.5 %local_scores.1 = (bf16[2,320,128]{2,1,0:T(8,128)(2,1)S(1)}, bf16[2,1280,128]{2,1,0:T(8,128)(2,1)S(1)}, bf16[2,1280,128]{2,1,0:T(8,128)(2,1)S(1)}, f32[1,1280]{1...) custom-call(bf16[160,256]{1,0:T(8,128)(2,1)S(1)} %get-tuple-element., ...), custom_call_target="tpu_custom_call" | custom-call | flops 3000000 | bytes 1000 | tf_op jit(solution)/shard_map/local_scores/pallas_call | solution.py:462
  12.7 0.0 collective-permute-done.1.packet.refs_0_
  12.8 0.0 collective-permute-done.2.refs_1_
  12.8 1.3 %collective-permute-start.6 = (bf16[160,256]{1,0:T(8,128)(2,1)S(1)}, bf16[160,256]{1,0:T(8,128)(2,1)S(1)}, u32[]{:S(2)}, u32[]{:S(2)}) collective-permute-start(bf16[160,256]{1,0:T(8,128)(2,1)S(1)} %get-tuple-element.78), channel_id=1, source_target_pairs={{3,0},{2,1},{7,4},{6,5},{11,8},{10,9},{15,12},{14,13},{19,16},{18,... | collective-permute-start | bytes 245768 | tf_op jit(solution)/shard_map/ppermute | solution.py:510
  14.1 1.3 %collective-permute-start.7 = (bf16[160,256]{1,0:T(8,128)(2,1)S(1)}, bf16[160,256]{1,0:T(8,128)(2,1)S(1)}, u32[]{:S(2)}, u32[]{:S(2)}) collective-permute-start(bf16[160,256]{1,0:T(8,128)(2,1)S(1)} %get-tuple-element.79), channel_id=1, source_target_pairs={{2,0},{3,1},{6,4},{7,5},{10,8},{11,9},{14,12},{15,13},{18,16},{19,... | collective-permute-start | bytes 245768 | tf_op jit(solution)/shard_map/ppermute | solution.py:511
  15.4 0.0 collective-permute-done.3.refs_0_
  15.4 0.0 collective-permute-done.4.refs_1_
  15.5 1.3 %collective-permute-start.8 = (bf16[160,256]{1,0:T(8,128)(2,1)S(1)}, bf16[160,256]{1,0:T(8,128)(2,1)S(1)}, u32[]{:S(2)}, u32[]{:S(2)}) collective-permute-start(bf16[160,256]{1,0:T(8,128)(2,1)S(1)} %get-tuple-element.81), channel_id=1, source_target_pairs={{2,0},{3,1},{6,4},{7,5},{10,8},{11,9},{14,12},{15,13},{18,16},{19,... | collective-permute-start | bytes 245768 | tf_op jit(solution)/shard_map/ppermute | solution.py:579
  16.8 1.3 %collective-permute-start.9 = (bf16[160,256]{1,0:T(8,128)(2,1)S(1)}, bf16[160,256]{1,0:T(8,128)(2,1)S(1)}, u32[]{:S(2)}, u32[]{:S(2)}) collective-permute-start(bf16[160,256]{1,0:T(8,128)(2,1)S(1)} %far_rest.1), channel_id=1, source_target_pairs={{3,0},{2,1},{7,4},{6,5},{11,8},{10,9},{15,12},{14,13},{19,16},{18,... | collective-permute-start | bytes 245768 | tf_op jit(solution)/shard_map/ppermute | solution.py:581
  18.1 2.1 %near_grads.1 = (f32[160,512]{1,0:T(8,128)S(1)}, bf16[160,1024]{1,0:T(8,128)(2,1)S(1)}, f32[1,160]{1,0:T(1,128)S(1)}, bf16[176,1536]{1,0:T(8,128)(2,1)S(1)}) custom-call(f32[2,320,1280]{2,1,0:T(8,128)S(1)} %get-tuple-element.52.raws, f32[2,320,1280]{2,1,0:T(8,128)S(1)} %get-tuple-element.53.grads, f32[2,1,1280]{2,1,0:T(1,128)S(1)} %get-tuple-element.63.factors, ...), custom_call_target="tpu_custom_call" | custom-call | flops 4000000 | bytes 1000 | tf_op jit(solution)/shard_map/near_grads/pallas_call | solution.py:462
  20.2 0.2 collective-permute-start.5
  20.4 0.0 collective-permute-done.6.refs_0_
  20.4 0.8 %collective-permute-done.7.refs_1_ = bf16[160,256]{1,0:T(8,128)(2,1)S(1)} collective-permute-done((bf16[160,256]{1,0:T(8,128)(2,1)S(1)}, bf16[160,256]{1,0:T(8,128)(2,1)S(1)}, u32[]{:S(2)}, u32[]{:S(2)}) %collective-permute-start.7) | collective-permute-done | bytes 81952 | tf_op jit(solution)/shard_map/ppermute | solution.py:511
  21.2 2.4 %collective-permute-done.8.refs_0_ = bf16[160,256]{1,0:T(8,128)(2,1)S(1)} collective-permute-done((bf16[160,256]{1,0:T(8,128)(2,1)S(1)}, bf16[160,256]{1,0:T(8,128)(2,1)S(1)}, u32[]{:S(2)}, u32[]{:S(2)}) %collective-permute-start.8) | collective-permute-done | bytes 81952 | tf_op jit(solution)/shard_map/ppermute | solution.py:579
  23.6 1.2 %collective-permute-done.9.refs_0_ = bf16[160,256]{1,0:T(8,128)(2,1)S(1)} collective-permute-done((bf16[160,256]{1,0:T(8,128)(2,1)S(1)}, bf16[160,256]{1,0:T(8,128)(2,1)S(1)}, u32[]{:S(2)}, u32[]{:S(2)}) %collective-permute-start.9) | collective-permute-done | bytes 81952 | tf_op jit(solution)/shard_map/ppermute | solution.py:581
  24.9 0.0 collective-permute-done.5.back
  24.9 1.3 %finish.1 = (bf16[160,2048]{1,0:T(8,128)(2,1)}, bf16[160,512]{1,0:T(8,128)(2,1)}, bf16[160,512]{1,0:T(8,128)(2,1)}, f32[1,160]{1,0:T(1,128)}) custom-call(bf16[176,1536]{1,0:T(8,128)(2,1)S(1)} %collective-permute-done.5.back, bf16[160,1024]{1,0:T(8,128)(2,1)S(1)} %get-tuple-element.75.query_mine, f32[1,160]{1,0:T(1,128)S(1)} %get-tuple-element.76.gate_mine, ...), custom_call_target="tpu_custom_call" | custom-call | flops 1000000 | bytes 1000 | tf_op jit(solution)/shard_map/finish/pallas_call | solution.py:462
  (7 shorter events, 0.1 us)
Async XLA Ops:
  0.6 10.5 %copy-start = (bf16[1,160,2048]{2,1,0:T(8,128)(2,1)S(1)}, bf16[1,160,2048]{2,1,0:T(8,128)(2,1)}, u32[]{:S(2)}) copy-start(bf16[1,160,2048]{2,1,0:T(8,128)(2,1)} %param.7) | copy-start | bytes 1966084
  0.6 10.5 %copy-start.1 = (bf16[1,160,2048]{2,1,0:T(8,128)(2,1)S(1)}, bf16[1,160,2048]{2,1,0:T(8,128)(2,1)}, u32[]{:S(2)}) copy-start(bf16[1,160,2048]{2,1,0:T(8,128)(2,1)} %param.10) | copy-start | bytes 1966084
  2.2 8.9 %collective-permute-start = (bf16[176,2560]{1,0:T(8,128)(2,1)S(1)}, bf16[176,2560]{1,0:T(8,128)(2,1)S(1)}, u32[]{:S(2)}, u32[]{:S(2)}) collective-permute-start(bf16[176,2560]{1,0:T(8,128)(2,1)S(1)} %get-tuple-element.51), channel_id=1, source_target_pairs={{0,1},{1,0},{2,3},{3,2},{4,5},{5,4},{6,7},{7,6},{8,9},{9,8},{10,11... | collective-permute-start | bytes 2703368 | tf_op jit(solution)/shard_map/ppermute | solution.py:518
  2.8 10.0 %collective-permute-start.1 = (bf16[160,256]{1,0:T(8,128)(2,1)S(1)}, bf16[160,256]{1,0:T(8,128)(2,1)S(1)}, u32[]{:S(2)}, u32[]{:S(2)}) collective-permute-start(bf16[160,256]{1,0:T(8,128)(2,1)S(1)} %get-tuple-element.59), channel_id=1, source_target_pairs={{0,3},{1,2},{4,7},{5,6},{8,11},{9,10},{12,15},{13,14},{16,19},{17,... | collective-permute-start | bytes 245768 | tf_op jit(solution)/shard_map/ppermute | solution.py:510
  7.3 5.5 %collective-permute-start.2 = (bf16[160,256]{1,0:T(8,128)(2,1)S(1)}, bf16[160,256]{1,0:T(8,128)(2,1)S(1)}, u32[]{:S(2)}, u32[]{:S(2)}) collective-permute-start(bf16[160,256]{1,0:T(8,128)(2,1)S(1)} %get-tuple-element.46.key_mine), channel_id=1, source_target_pairs={{0,2},{1,3},{4,6},{5,7},{8,10},{9,11},{12,14},{13,15},{16,18},{17,... | collective-permute-start | bytes 245768 | tf_op jit(solution)/shard_map/ppermute | solution.py:511
  8.6 6.9 %collective-permute-start.3 = (bf16[160,256]{1,0:T(8,128)(2,1)S(1)}, bf16[160,256]{1,0:T(8,128)(2,1)S(1)}, u32[]{:S(2)}, u32[]{:S(2)}) collective-permute-start(bf16[160,256]{1,0:T(8,128)(2,1)S(1)} %get-tuple-element.69), channel_id=1, source_target_pairs={{0,3},{1,2},{4,7},{5,6},{8,11},{9,10},{12,15},{13,14},{16,19},{17,... | collective-permute-start | bytes 245768 | tf_op jit(solution)/shard_map/ppermute | solution.py:510
  9.9 5.6 %collective-permute-start.4 = (bf16[160,256]{1,0:T(8,128)(2,1)S(1)}, bf16[160,256]{1,0:T(8,128)(2,1)S(1)}, u32[]{:S(2)}, u32[]{:S(2)}) collective-permute-start(bf16[160,256]{1,0:T(8,128)(2,1)S(1)} %get-tuple-element.47.value_mine), channel_id=1, source_target_pairs={{0,2},{1,3},{4,6},{5,7},{8,10},{9,11},{12,14},{13,15},{16,18},{17,... | collective-permute-start | bytes 245768 | tf_op jit(solution)/shard_map/ppermute | solution.py:511
  12.8 7.6 %collective-permute-start.6 = (bf16[160,256]{1,0:T(8,128)(2,1)S(1)}, bf16[160,256]{1,0:T(8,128)(2,1)S(1)}, u32[]{:S(2)}, u32[]{:S(2)}) collective-permute-start(bf16[160,256]{1,0:T(8,128)(2,1)S(1)} %get-tuple-element.78), channel_id=1, source_target_pairs={{3,0},{2,1},{7,4},{6,5},{11,8},{10,9},{15,12},{14,13},{19,16},{18,... | collective-permute-start | bytes 245768 | tf_op jit(solution)/shard_map/ppermute | solution.py:510
  14.1 7.1 %collective-permute-start.7 = (bf16[160,256]{1,0:T(8,128)(2,1)S(1)}, bf16[160,256]{1,0:T(8,128)(2,1)S(1)}, u32[]{:S(2)}, u32[]{:S(2)}) collective-permute-start(bf16[160,256]{1,0:T(8,128)(2,1)S(1)} %get-tuple-element.79), channel_id=1, source_target_pairs={{2,0},{3,1},{6,4},{7,5},{10,8},{11,9},{14,12},{15,13},{18,16},{19,... | collective-permute-start | bytes 245768 | tf_op jit(solution)/shard_map/ppermute | solution.py:511
  15.5 8.1 %collective-permute-start.8 = (bf16[160,256]{1,0:T(8,128)(2,1)S(1)}, bf16[160,256]{1,0:T(8,128)(2,1)S(1)}, u32[]{:S(2)}, u32[]{:S(2)}) collective-permute-start(bf16[160,256]{1,0:T(8,128)(2,1)S(1)} %get-tuple-element.81), channel_id=1, source_target_pairs={{2,0},{3,1},{6,4},{7,5},{10,8},{11,9},{14,12},{15,13},{18,16},{19,... | collective-permute-start | bytes 245768 | tf_op jit(solution)/shard_map/ppermute | solution.py:579
  16.8 8.1 %collective-permute-start.9 = (bf16[160,256]{1,0:T(8,128)(2,1)S(1)}, bf16[160,256]{1,0:T(8,128)(2,1)S(1)}, u32[]{:S(2)}, u32[]{:S(2)}) collective-permute-start(bf16[160,256]{1,0:T(8,128)(2,1)S(1)} %far_rest.1), channel_id=1, source_target_pairs={{3,0},{2,1},{7,4},{6,5},{11,8},{10,9},{15,12},{14,13},{19,16},{18,... | collective-permute-start | bytes 245768 | tf_op jit(solution)/shard_map/ppermute | solution.py:581
  20.2 4.7 %collective-permute-start.5 = (bf16[176,1536]{1,0:T(8,128)(2,1)S(1)}, bf16[176,1536]{1,0:T(8,128)(2,1)S(1)}, u32[]{:S(2)}, u32[]{:S(2)}) collective-permute-start(bf16[176,1536]{1,0:T(8,128)(2,1)S(1)} %get-tuple-element.74), channel_id=1, source_target_pairs={{0,1},{1,0},{2,3},{3,2},{4,5},{5,4},{6,7},{7,6},{8,9},{9,8},{10,11... | collective-permute-start | bytes 1622024 | tf_op jit(solution)/shard_map/ppermute | solution.py:612

commit v16 on v15

--- a/solution.py
+++ b/solution.py
@@ -314,7 +314,7 @@
                 deltas[i, :, here] = delta
                 score_grad = raw * far_factors[i, :, here] * (prob_grad - delta)
                 score_grads[i, :, here] = score_grad.astype(BF16)
-            key_parts(score_grads, query, parts, i, len(parts))
+            key_parts(score_grads, query, parts, i, 0)
 
 
 def key_parts(score_grads, query, parts, i, first):
@@ -329,7 +329,7 @@
     @pl.when(lax.axis_index("ctx") >= 2)
     def _():
         for i in range(query.shape[0]):
-            key_parts(score_grads, query, parts, i, 0)
+            key_parts(score_grads, query, parts, i, len(parts))
 
 
 def near_kernel(
@@ -543,7 +543,7 @@
     far_table = (far_low[0], F32 if chips == 2 else BF16)
     early_table = ((half_groups, rows, 2 * wide), F32)
     early_raws, early_tops, early_sums = call(
-        early_kernel, "early_keys", [early_table, row, row], query, tops, sums, sib_keys[0]
+        early_kernel, "early_keys", [early_table, row, row], query, tops, sums, own_keys[0]
     )
     far_keys, far_raws, factors, far_factors, shrinks, inverses, *parts = call(
         functools.partial(far_keys_kernel, blocks=blocks),
@@ -556,11 +556,11 @@
         early_raws,
         early_tops,
         early_sums,
+        *own_keys,
         *sib_keys,
-        *own_keys,
         scratch=[pltpu.VMEM(*far_low)],
     )
-    sib_value_got, own_value_got = send(parts[: chips - 1], parts[chips - 1 :], back_cross, back_hop)
+    sib_value_got, own_value_got = send(parts[chips - 1 :], parts[: chips - 1], back_cross, back_hop)
     far_grads, deltas, *parts = call(
         functools.partial(far_values_kernel, blocks=blocks),
         "far_values",
@@ -572,8 +572,8 @@
         shrinks,
         inverses,
         crosses,
+        *own_values,
         *sib_values,
-        *own_values,
         scratch=[pltpu.VMEM(*far_rows)],
     )
     own_key_got = [lax.ppermute(parts[s - 1], "ctx", back_hop[s]) for s in steps]

time: 26.4 us -> 26.4 us (level)
    ppermute x3, starting transfers between devices: 7.08 us -> 3.97 us  [send(): sib = [lax.ppermute(sib[s - 1], 'ctx', sib_pairs[s]) for s in steps]]
    ppermute x3, starting transfers between devices: 3.88 us -> 6.99 us  [send(): return (sib, [lax.ppermute(own[s - 1], 'ctx', own_pairs[s]) for s in steps])]
where the time goes in v16:
time: 26.4 us; the launch traced here: 26.1 us
  starting transfers between devices  14.2 us (54%)
  Pallas kernels  6.64 us (25%)
  waiting for transfers between devices  4.37 us (17%)
  between operations  0.83 us (3%)
    ppermute x3, starting transfers between devices, send(): return (sib, [lax.ppermute(own[s - 1], 'ctx', own_pairs[s]) for s in steps])  6.99 us
    pallas_call x11, Pallas kernels, call(): pl.pallas_call(kernel, out_shape=[jax.ShapeDtypeStruct(*out) for out in o...  6.64 us
    ppermute x3, starting transfers between devices, send(): sib = [lax.ppermute(sib[s - 1], 'ctx', sib_pairs[s]) for s in steps]  3.97 us
    ppermute x1, waiting for transfers between devices, per_device(): lax.ppermute(parts[s - 1], 'ctx', back_hop[s])  2.32 us
    ppermute x1, starting transfers between devices, per_device(): lax.ppermute(parts[s - 1], 'ctx', back_cross[s])  1.29 us
    ppermute x1, starting transfers between devices, per_device(): lax.ppermute(parts[s - 1], 'ctx', back_hop[s])  1.29 us
    ppermute x1, waiting for transfers between devices, per_device(): lax.ppermute(parts[s - 1], 'ctx', back_cross[s])  1.23 us
    ppermute x3, waiting for transfers between devices, send(): return (sib, [lax.ppermute(own[s - 1], 'ctx', own_pairs[s]) for s in steps])  0.81 us
  transfers between devices with their start and end apart: 10, of which 3 were waited for; matrix products, arithmetic and copies ran while one was open for 0% of the time, Pallas kernels for 15%

profile of v16, /device:TPU:0, one launch (start us, length us, event | category | flops | bytes accessed | tf_op | source)
XLA Modules:
  0.0 26.1 jit_solution(4019930004587438714)
XLA Ops:
  0.6 0.0 copy-start
  0.6 0.0 copy-start.1
  0.7 1.6 %pack.1 = (bf16[160,256]{1,0:T(8,128)(2,1)S(1)}, bf16[160,256]{1,0:T(8,128)(2,1)S(1)}, bf16[160,256]{1,0:T(8,128)(2,1)S(1)}, bf16[160,256]{1,0:T(8,128)(2,1)S(1)...) custom-call(bf16[160,512]{1,0:T(8,128)(2,1)} %bitcast.12, ...), custom_call_target="tpu_custom_call" | custom-call | flops 5000000000 | bytes 1000 | tf_op jit(solution)/shard_map/pack/pallas_call | solution.py:462
  2.2 0.5 %collective-permute-start = (bf16[176,2560]{1,0:T(8,128)(2,1)S(1)}, bf16[176,2560]{1,0:T(8,128)(2,1)S(1)}, u32[]{:S(2)}, u32[]{:S(2)}) collective-permute-start(bf16[176,2560]{1,0:T(8,128)(2,1)S(1)} %get-tuple-element.51), channel_id=1, source_target_pairs={{0,1},{1,0},{2,3},{3,2},{4,5},{5,4},{6,7},{7,6},{8,9},{9,8},{10,11... | collective-permute-start | bytes 2703368 | tf_op jit(solution)/shard_map/ppermute | solution.py:518
  2.8 4.4 %collective-permute-start.1 = (bf16[160,256]{1,0:T(8,128)(2,1)S(1)}, bf16[160,256]{1,0:T(8,128)(2,1)S(1)}, u32[]{:S(2)}, u32[]{:S(2)}) collective-permute-start(bf16[160,256]{1,0:T(8,128)(2,1)S(1)} %get-tuple-element.46.key_mine), channel_id=1, source_target_pairs={{0,2},{1,3},{4,6},{5,7},{8,10},{9,11},{12,14},{13,15},{16,18},{17,... | collective-permute-start | bytes 245768 | tf_op jit(solution)/shard_map/ppermute | solution.py:511
  7.2 1.4 %collective-permute-start.2 = (bf16[160,256]{1,0:T(8,128)(2,1)S(1)}, bf16[160,256]{1,0:T(8,128)(2,1)S(1)}, u32[]{:S(2)}, u32[]{:S(2)}) collective-permute-start(bf16[160,256]{1,0:T(8,128)(2,1)S(1)} %get-tuple-element.62), channel_id=1, source_target_pairs={{0,3},{1,2},{4,7},{5,6},{8,11},{9,10},{12,15},{13,14},{16,19},{17,... | collective-permute-start | bytes 245768 | tf_op jit(solution)/shard_map/ppermute | solution.py:510
  8.6 1.3 %collective-permute-start.4 = (bf16[160,256]{1,0:T(8,128)(2,1)S(1)}, bf16[160,256]{1,0:T(8,128)(2,1)S(1)}, u32[]{:S(2)}, u32[]{:S(2)}) collective-permute-start(bf16[160,256]{1,0:T(8,128)(2,1)S(1)} %get-tuple-element.69), channel_id=1, source_target_pairs={{0,3},{1,2},{4,7},{5,6},{8,11},{9,10},{12,15},{13,14},{16,19},{17,... | collective-permute-start | bytes 245768 | tf_op jit(solution)/shard_map/ppermute | solution.py:510
  9.9 1.3 %collective-permute-start.3 = (bf16[160,256]{1,0:T(8,128)(2,1)S(1)}, bf16[160,256]{1,0:T(8,128)(2,1)S(1)}, u32[]{:S(2)}, u32[]{:S(2)}) collective-permute-start(bf16[160,256]{1,0:T(8,128)(2,1)S(1)} %get-tuple-element.47.value_mine), channel_id=1, source_target_pairs={{0,2},{1,3},{4,6},{5,7},{8,10},{9,11},{12,14},{13,15},{16,18},{17,... | collective-permute-start | bytes 245768 | tf_op jit(solution)/shard_map/ppermute | solution.py:511
  11.2 0.0 collective-permute-done.sib
  11.2 0.0 copy-done
  11.2 0.0 copy-done.1
  11.2 1.5 %local_scores.1 = (bf16[2,320,128]{2,1,0:T(8,128)(2,1)S(1)}, bf16[2,1280,128]{2,1,0:T(8,128)(2,1)S(1)}, bf16[2,1280,128]{2,1,0:T(8,128)(2,1)S(1)}, f32[1,1280]{1...) custom-call(bf16[160,256]{1,0:T(8,128)(2,1)S(1)} %get-tuple-element., ...), custom_call_target="tpu_custom_call" | custom-call | flops 3000000 | bytes 1000 | tf_op jit(solution)/shard_map/local_scores/pallas_call | solution.py:462
  12.7 0.0 collective-permute-done.1.packet.refs_0_
  12.8 0.0 collective-permute-done.2.refs_1_
  12.8 1.3 %collective-permute-start.6 = (bf16[160,256]{1,0:T(8,128)(2,1)S(1)}, bf16[160,256]{1,0:T(8,128)(2,1)S(1)}, u32[]{:S(2)}, u32[]{:S(2)}) collective-permute-start(bf16[160,256]{1,0:T(8,128)(2,1)S(1)} %get-tuple-element.78), channel_id=1, source_target_pairs={{3,0},{2,1},{7,4},{6,5},{11,8},{10,9},{15,12},{14,13},{19,16},{18,... | collective-permute-start | bytes 245768 | tf_op jit(solution)/shard_map/ppermute | solution.py:510
  14.1 1.3 %collective-permute-start.7 = (bf16[160,256]{1,0:T(8,128)(2,1)S(1)}, bf16[160,256]{1,0:T(8,128)(2,1)S(1)}, u32[]{:S(2)}, u32[]{:S(2)}) collective-permute-start(bf16[160,256]{1,0:T(8,128)(2,1)S(1)} %get-tuple-element.79), channel_id=1, source_target_pairs={{2,0},{3,1},{6,4},{7,5},{10,8},{11,9},{14,12},{15,13},{18,16},{19,... | collective-permute-start | bytes 245768 | tf_op jit(solution)/shard_map/ppermute | solution.py:511
  15.4 0.0 collective-permute-done.4.refs_1_
  15.4 0.0 collective-permute-done.3.refs_0_
  15.5 1.3 %collective-permute-start.8 = (bf16[160,256]{1,0:T(8,128)(2,1)S(1)}, bf16[160,256]{1,0:T(8,128)(2,1)S(1)}, u32[]{:S(2)}, u32[]{:S(2)}) collective-permute-start(bf16[160,256]{1,0:T(8,128)(2,1)S(1)} %get-tuple-element.81), channel_id=1, source_target_pairs={{2,0},{3,1},{6,4},{7,5},{10,8},{11,9},{14,12},{15,13},{18,16},{19,... | collective-permute-start | bytes 245768 | tf_op jit(solution)/shard_map/ppermute | solution.py:579
  16.8 1.3 %collective-permute-start.9 = (bf16[160,256]{1,0:T(8,128)(2,1)S(1)}, bf16[160,256]{1,0:T(8,128)(2,1)S(1)}, u32[]{:S(2)}, u32[]{:S(2)}) collective-permute-start(bf16[160,256]{1,0:T(8,128)(2,1)S(1)} %far_rest.1), channel_id=1, source_target_pairs={{3,0},{2,1},{7,4},{6,5},{11,8},{10,9},{15,12},{14,13},{19,16},{18,... | collective-permute-start | bytes 245768 | tf_op jit(solution)/shard_map/ppermute | solution.py:581
  18.1 2.1 %near_grads.1 = (f32[160,512]{1,0:T(8,128)S(1)}, bf16[160,1024]{1,0:T(8,128)(2,1)S(1)}, f32[1,160]{1,0:T(1,128)S(1)}, bf16[176,1536]{1,0:T(8,128)(2,1)S(1)}) custom-call(f32[2,320,1280]{2,1,0:T(8,128)S(1)} %get-tuple-element.52.raws, f32[2,320,1280]{2,1,0:T(8,128)S(1)} %get-tuple-element.53.grads, f32[2,1,1280]{2,1,0:T(1,128)S(1)} %get-tuple-element.63.factors, ...), custom_call_target="tpu_custom_call" | custom-call | flops 4000000 | bytes 1000 | tf_op jit(solution)/shard_map/near_grads/pallas_call | solution.py:462
  20.2 0.2 collective-permute-start.5
  20.4 0.0 collective-permute-done.6.refs_0_
  20.4 0.8 %collective-permute-done.7.refs_1_ = bf16[160,256]{1,0:T(8,128)(2,1)S(1)} collective-permute-done((bf16[160,256]{1,0:T(8,128)(2,1)S(1)}, bf16[160,256]{1,0:T(8,128)(2,1)S(1)}, u32[]{:S(2)}, u32[]{:S(2)}) %collective-permute-start.7) | collective-permute-done | bytes 81952 | tf_op jit(solution)/shard_map/ppermute | solution.py:511
  21.2 2.3 %collective-permute-done.8.refs_0_ = bf16[160,256]{1,0:T(8,128)(2,1)S(1)} collective-permute-done((bf16[160,256]{1,0:T(8,128)(2,1)S(1)}, bf16[160,256]{1,0:T(8,128)(2,1)S(1)}, u32[]{:S(2)}, u32[]{:S(2)}) %collective-permute-start.8) | collective-permute-done | bytes 81952 | tf_op jit(solution)/shard_map/ppermute | solution.py:579
  23.6 1.2 %collective-permute-done.9.refs_0_ = bf16[160,256]{1,0:T(8,128)(2,1)S(1)} collective-permute-done((bf16[160,256]{1,0:T(8,128)(2,1)S(1)}, bf16[160,256]{1,0:T(8,128)(2,1)S(1)}, u32[]{:S(2)}, u32[]{:S(2)}) %collective-permute-start.9) | collective-permute-done | bytes 81952 | tf_op jit(solution)/shard_map/ppermute | solution.py:581
  24.8 0.0 collective-permute-done.5.back
  24.8 1.3 %finish.1 = (bf16[160,2048]{1,0:T(8,128)(2,1)}, bf16[160,512]{1,0:T(8,128)(2,1)}, bf16[160,512]{1,0:T(8,128)(2,1)}, f32[1,160]{1,0:T(1,128)}) custom-call(bf16[176,1536]{1,0:T(8,128)(2,1)S(1)} %collective-permute-done.5.back, bf16[160,1024]{1,0:T(8,128)(2,1)S(1)} %get-tuple-element.75.query_mine, f32[1,160]{1,0:T(1,128)S(1)} %get-tuple-element.76.gate_mine, ...), custom_call_target="tpu_custom_call" | custom-call | flops 1000000 | bytes 1000 | tf_op jit(solution)/shard_map/finish/pallas_call | solution.py:462
  (7 shorter events, 0.1 us)
Async XLA Ops:
  0.6 10.5 %copy-start = (bf16[1,160,2048]{2,1,0:T(8,128)(2,1)S(1)}, bf16[1,160,2048]{2,1,0:T(8,128)(2,1)}, u32[]{:S(2)}) copy-start(bf16[1,160,2048]{2,1,0:T(8,128)(2,1)} %param.7) | copy-start | bytes 1966084
  0.6 10.5 %copy-start.1 = (bf16[1,160,2048]{2,1,0:T(8,128)(2,1)S(1)}, bf16[1,160,2048]{2,1,0:T(8,128)(2,1)}, u32[]{:S(2)}) copy-start(bf16[1,160,2048]{2,1,0:T(8,128)(2,1)} %param.10) | copy-start | bytes 1966084
  2.2 8.9 %collective-permute-start = (bf16[176,2560]{1,0:T(8,128)(2,1)S(1)}, bf16[176,2560]{1,0:T(8,128)(2,1)S(1)}, u32[]{:S(2)}, u32[]{:S(2)}) collective-permute-start(bf16[176,2560]{1,0:T(8,128)(2,1)S(1)} %get-tuple-element.51), channel_id=1, source_target_pairs={{0,1},{1,0},{2,3},{3,2},{4,5},{5,4},{6,7},{7,6},{8,9},{9,8},{10,11... | collective-permute-start | bytes 2703368 | tf_op jit(solution)/shard_map/ppermute | solution.py:518
  2.8 10.0 %collective-permute-start.1 = (bf16[160,256]{1,0:T(8,128)(2,1)S(1)}, bf16[160,256]{1,0:T(8,128)(2,1)S(1)}, u32[]{:S(2)}, u32[]{:S(2)}) collective-permute-start(bf16[160,256]{1,0:T(8,128)(2,1)S(1)} %get-tuple-element.46.key_mine), channel_id=1, source_target_pairs={{0,2},{1,3},{4,6},{5,7},{8,10},{9,11},{12,14},{13,15},{16,18},{17,... | collective-permute-start | bytes 245768 | tf_op jit(solution)/shard_map/ppermute | solution.py:511
  7.2 5.6 %collective-permute-start.2 = (bf16[160,256]{1,0:T(8,128)(2,1)S(1)}, bf16[160,256]{1,0:T(8,128)(2,1)S(1)}, u32[]{:S(2)}, u32[]{:S(2)}) collective-permute-start(bf16[160,256]{1,0:T(8,128)(2,1)S(1)} %get-tuple-element.62), channel_id=1, source_target_pairs={{0,3},{1,2},{4,7},{5,6},{8,11},{9,10},{12,15},{13,14},{16,19},{17,... | collective-permute-start | bytes 245768 | tf_op jit(solution)/shard_map/ppermute | solution.py:510
  8.6 6.9 %collective-permute-start.4 = (bf16[160,256]{1,0:T(8,128)(2,1)S(1)}, bf16[160,256]{1,0:T(8,128)(2,1)S(1)}, u32[]{:S(2)}, u32[]{:S(2)}) collective-permute-start(bf16[160,256]{1,0:T(8,128)(2,1)S(1)} %get-tuple-element.69), channel_id=1, source_target_pairs={{0,3},{1,2},{4,7},{5,6},{8,11},{9,10},{12,15},{13,14},{16,19},{17,... | collective-permute-start | bytes 245768 | tf_op jit(solution)/shard_map/ppermute | solution.py:510
  9.9 5.6 %collective-permute-start.3 = (bf16[160,256]{1,0:T(8,128)(2,1)S(1)}, bf16[160,256]{1,0:T(8,128)(2,1)S(1)}, u32[]{:S(2)}, u32[]{:S(2)}) collective-permute-start(bf16[160,256]{1,0:T(8,128)(2,1)S(1)} %get-tuple-element.47.value_mine), channel_id=1, source_target_pairs={{0,2},{1,3},{4,6},{5,7},{8,10},{9,11},{12,14},{13,15},{16,18},{17,... | collective-permute-start | bytes 245768 | tf_op jit(solution)/shard_map/ppermute | solution.py:511
  12.8 7.6 %collective-permute-start.6 = (bf16[160,256]{1,0:T(8,128)(2,1)S(1)}, bf16[160,256]{1,0:T(8,128)(2,1)S(1)}, u32[]{:S(2)}, u32[]{:S(2)}) collective-permute-start(bf16[160,256]{1,0:T(8,128)(2,1)S(1)} %get-tuple-element.78), channel_id=1, source_target_pairs={{3,0},{2,1},{7,4},{6,5},{11,8},{10,9},{15,12},{14,13},{19,16},{18,... | collective-permute-start | bytes 245768 | tf_op jit(solution)/shard_map/ppermute | solution.py:510
  14.1 7.1 %collective-permute-start.7 = (bf16[160,256]{1,0:T(8,128)(2,1)S(1)}, bf16[160,256]{1,0:T(8,128)(2,1)S(1)}, u32[]{:S(2)}, u32[]{:S(2)}) collective-permute-start(bf16[160,256]{1,0:T(8,128)(2,1)S(1)} %get-tuple-element.79), channel_id=1, source_target_pairs={{2,0},{3,1},{6,4},{7,5},{10,8},{11,9},{14,12},{15,13},{18,16},{19,... | collective-permute-start | bytes 245768 | tf_op jit(solution)/shard_map/ppermute | solution.py:511
  15.5 8.1 %collective-permute-start.8 = (bf16[160,256]{1,0:T(8,128)(2,1)S(1)}, bf16[160,256]{1,0:T(8,128)(2,1)S(1)}, u32[]{:S(2)}, u32[]{:S(2)}) collective-permute-start(bf16[160,256]{1,0:T(8,128)(2,1)S(1)} %get-tuple-element.81), channel_id=1, source_target_pairs={{2,0},{3,1},{6,4},{7,5},{10,8},{11,9},{14,12},{15,13},{18,16},{19,... | collective-permute-start | bytes 245768 | tf_op jit(solution)/shard_map/ppermute | solution.py:579
  16.8 8.0 %collective-permute-start.9 = (bf16[160,256]{1,0:T(8,128)(2,1)S(1)}, bf16[160,256]{1,0:T(8,128)(2,1)S(1)}, u32[]{:S(2)}, u32[]{:S(2)}) collective-permute-start(bf16[160,256]{1,0:T(8,128)(2,1)S(1)} %far_rest.1), channel_id=1, source_target_pairs={{3,0},{2,1},{7,4},{6,5},{11,8},{10,9},{15,12},{14,13},{19,16},{18,... | collective-permute-start | bytes 245768 | tf_op jit(solution)/shard_map/ppermute | solution.py:581
  20.2 4.6 %collective-permute-start.5 = (bf16[176,1536]{1,0:T(8,128)(2,1)S(1)}, bf16[176,1536]{1,0:T(8,128)(2,1)S(1)}, u32[]{:S(2)}, u32[]{:S(2)}) collective-permute-start(bf16[176,1536]{1,0:T(8,128)(2,1)S(1)} %get-tuple-element.74), channel_id=1, source_target_pairs={{0,1},{1,0},{2,3},{3,2},{4,5},{5,4},{6,7},{7,6},{8,9},{9,8},{10,11... | collective-permute-start | bytes 1622024 | tf_op jit(solution)/shard_map/ppermute | solution.py:612

commit v17 on v16

--- a/solution.py
+++ b/solution.py
@@ -507,8 +507,8 @@
     steps = range(1, chips)
 
     def send(sib, own, sib_pairs, own_pairs):
-        sib = [lax.ppermute(sib[s - 1], "ctx", sib_pairs[s]) for s in steps]
-        return sib, [lax.ppermute(own[s - 1], "ctx", own_pairs[s]) for s in steps]
+        own = [lax.ppermute(own[s - 1], "ctx", own_pairs[s]) for s in steps]
+        return [lax.ppermute(sib[s - 1], "ctx", sib_pairs[s]) for s in steps], own
 
     sib_keys, own_keys = send([key_theirs] * chips, [key_mine] * chips, cross, hop)
     sib_values, own_values = send([value_theirs] * chips, [value_mine] * chips, cross, hop)

time: 26.4 us -> 26.4 us (level)
  no operation moved by 1% of the time
where the time goes in v17:
time: 26.4 us; the launch traced here: 26.1 us
  starting transfers between devices  14.2 us (54%)
  Pallas kernels  6.64 us (25%)
  waiting for transfers between devices  4.37 us (17%)
  between operations  0.83 us (3%)
    ppermute x3, starting transfers between devices, send(): own = [lax.ppermute(own[s - 1], 'ctx', own_pairs[s]) for s in steps]  6.99 us
    pallas_call x11, Pallas kernels, call(): pl.pallas_call(kernel, out_shape=[jax.ShapeDtypeStruct(*out) for out in o...  6.64 us
    ppermute x3, starting transfers between devices, send(): return ([lax.ppermute(sib[s - 1], 'ctx', sib_pairs[s]) for s in steps], own)  3.97 us
    ppermute x1, waiting for transfers between devices, per_device(): lax.ppermute(parts[s - 1], 'ctx', back_hop[s])  2.32 us
    ppermute x1, starting transfers between devices, per_device(): lax.ppermute(parts[s - 1], 'ctx', back_cross[s])  1.29 us
    ppermute x1, starting transfers between devices, per_device(): lax.ppermute(parts[s - 1], 'ctx', back_hop[s])  1.29 us
    ppermute x1, waiting for transfers between devices, per_device(): lax.ppermute(parts[s - 1], 'ctx', back_cross[s])  1.23 us
    ppermute x3, waiting for transfers between devices, send(): own = [lax.ppermute(own[s - 1], 'ctx', own_pairs[s]) for s in steps]  0.81 us
  transfers between devices with their start and end apart: 10, of which 3 were waited for; matrix products, arithmetic and copies ran while one was open for 0% of the time, Pallas kernels for 15%

profile of v17, /device:TPU:0, one launch (start us, length us, event | category | flops | bytes accessed | tf_op | source)
XLA Modules:
  0.0 26.1 jit_solution(4019930004587438714)
XLA Ops:
  0.6 0.0 copy-start
  0.6 0.0 copy-start.1
  0.7 1.6 %pack.1 = (bf16[160,256]{1,0:T(8,128)(2,1)S(1)}, bf16[160,256]{1,0:T(8,128)(2,1)S(1)}, bf16[160,256]{1,0:T(8,128)(2,1)S(1)}, bf16[160,256]{1,0:T(8,128)(2,1)S(1)...) custom-call(bf16[160,512]{1,0:T(8,128)(2,1)} %bitcast.12, ...), custom_call_target="tpu_custom_call" | custom-call | flops 5000000000 | bytes 1000 | tf_op jit(solution)/shard_map/pack/pallas_call | solution.py:462
  2.2 0.5 %collective-permute-start = (bf16[176,2560]{1,0:T(8,128)(2,1)S(1)}, bf16[176,2560]{1,0:T(8,128)(2,1)S(1)}, u32[]{:S(2)}, u32[]{:S(2)}) collective-permute-start(bf16[176,2560]{1,0:T(8,128)(2,1)S(1)} %get-tuple-element.51), channel_id=1, source_target_pairs={{0,1},{1,0},{2,3},{3,2},{4,5},{5,4},{6,7},{7,6},{8,9},{9,8},{10,11... | collective-permute-start | bytes 2703368 | tf_op jit(solution)/shard_map/ppermute | solution.py:518
  2.8 4.4 %collective-permute-start.1 = (bf16[160,256]{1,0:T(8,128)(2,1)S(1)}, bf16[160,256]{1,0:T(8,128)(2,1)S(1)}, u32[]{:S(2)}, u32[]{:S(2)}) collective-permute-start(bf16[160,256]{1,0:T(8,128)(2,1)S(1)} %get-tuple-element.46.key_mine), channel_id=1, source_target_pairs={{0,2},{1,3},{4,6},{5,7},{8,10},{9,11},{12,14},{13,15},{16,18},{17,... | collective-permute-start | bytes 245768 | tf_op jit(solution)/shard_map/ppermute | solution.py:510
  7.2 1.4 %collective-permute-start.2 = (bf16[160,256]{1,0:T(8,128)(2,1)S(1)}, bf16[160,256]{1,0:T(8,128)(2,1)S(1)}, u32[]{:S(2)}, u32[]{:S(2)}) collective-permute-start(bf16[160,256]{1,0:T(8,128)(2,1)S(1)} %get-tuple-element.62), channel_id=1, source_target_pairs={{0,3},{1,2},{4,7},{5,6},{8,11},{9,10},{12,15},{13,14},{16,19},{17,... | collective-permute-start | bytes 245768 | tf_op jit(solution)/shard_map/ppermute | solution.py:511
  8.6 1.3 %collective-permute-start.4 = (bf16[160,256]{1,0:T(8,128)(2,1)S(1)}, bf16[160,256]{1,0:T(8,128)(2,1)S(1)}, u32[]{:S(2)}, u32[]{:S(2)}) collective-permute-start(bf16[160,256]{1,0:T(8,128)(2,1)S(1)} %get-tuple-element.69), channel_id=1, source_target_pairs={{0,3},{1,2},{4,7},{5,6},{8,11},{9,10},{12,15},{13,14},{16,19},{17,... | collective-permute-start | bytes 245768 | tf_op jit(solution)/shard_map/ppermute | solution.py:511
  9.9 1.3 %collective-permute-start.3 = (bf16[160,256]{1,0:T(8,128)(2,1)S(1)}, bf16[160,256]{1,0:T(8,128)(2,1)S(1)}, u32[]{:S(2)}, u32[]{:S(2)}) collective-permute-start(bf16[160,256]{1,0:T(8,128)(2,1)S(1)} %get-tuple-element.47.value_mine), channel_id=1, source_target_pairs={{0,2},{1,3},{4,6},{5,7},{8,10},{9,11},{12,14},{13,15},{16,18},{17,... | collective-permute-start | bytes 245768 | tf_op jit(solution)/shard_map/ppermute | solution.py:510
  11.2 0.0 collective-permute-done.sib
  11.2 0.0 copy-done
  11.2 0.0 copy-done.1
  11.2 1.5 %local_scores.1 = (bf16[2,320,128]{2,1,0:T(8,128)(2,1)S(1)}, bf16[2,1280,128]{2,1,0:T(8,128)(2,1)S(1)}, bf16[2,1280,128]{2,1,0:T(8,128)(2,1)S(1)}, f32[1,1280]{1...) custom-call(bf16[160,256]{1,0:T(8,128)(2,1)S(1)} %get-tuple-element., ...), custom_call_target="tpu_custom_call" | custom-call | flops 3000000 | bytes 1000 | tf_op jit(solution)/shard_map/local_scores/pallas_call | solution.py:462
  12.7 0.0 collective-permute-done.1.packet.refs_0_
  12.8 0.0 collective-permute-done.2.refs_1_
  12.8 1.3 %collective-permute-start.6 = (bf16[160,256]{1,0:T(8,128)(2,1)S(1)}, bf16[160,256]{1,0:T(8,128)(2,1)S(1)}, u32[]{:S(2)}, u32[]{:S(2)}) collective-permute-start(bf16[160,256]{1,0:T(8,128)(2,1)S(1)} %get-tuple-element.78), channel_id=1, source_target_pairs={{3,0},{2,1},{7,4},{6,5},{11,8},{10,9},{15,12},{14,13},{19,16},{18,... | collective-permute-start | bytes 245768 | tf_op jit(solution)/shard_map/ppermute | solution.py:511
  14.1 1.3 %collective-permute-start.7 = (bf16[160,256]{1,0:T(8,128)(2,1)S(1)}, bf16[160,256]{1,0:T(8,128)(2,1)S(1)}, u32[]{:S(2)}, u32[]{:S(2)}) collective-permute-start(bf16[160,256]{1,0:T(8,128)(2,1)S(1)} %get-tuple-element.79), channel_id=1, source_target_pairs={{2,0},{3,1},{6,4},{7,5},{10,8},{11,9},{14,12},{15,13},{18,16},{19,... | collective-permute-start | bytes 245768 | tf_op jit(solution)/shard_map/ppermute | solution.py:510
  15.4 0.0 collective-permute-done.4.refs_1_
  15.4 0.0 collective-permute-done.3.refs_0_
  15.5 1.3 %collective-permute-start.8 = (bf16[160,256]{1,0:T(8,128)(2,1)S(1)}, bf16[160,256]{1,0:T(8,128)(2,1)S(1)}, u32[]{:S(2)}, u32[]{:S(2)}) collective-permute-start(bf16[160,256]{1,0:T(8,128)(2,1)S(1)} %get-tuple-element.81), channel_id=1, source_target_pairs={{2,0},{3,1},{6,4},{7,5},{10,8},{11,9},{14,12},{15,13},{18,16},{19,... | collective-permute-start | bytes 245768 | tf_op jit(solution)/shard_map/ppermute | solution.py:579
  16.8 1.3 %collective-permute-start.9 = (bf16[160,256]{1,0:T(8,128)(2,1)S(1)}, bf16[160,256]{1,0:T(8,128)(2,1)S(1)}, u32[]{:S(2)}, u32[]{:S(2)}) collective-permute-start(bf16[160,256]{1,0:T(8,128)(2,1)S(1)} %far_rest.1), channel_id=1, source_target_pairs={{3,0},{2,1},{7,4},{6,5},{11,8},{10,9},{15,12},{14,13},{19,16},{18,... | collective-permute-start | bytes 245768 | tf_op jit(solution)/shard_map/ppermute | solution.py:581
  18.1 2.1 %near_grads.1 = (f32[160,512]{1,0:T(8,128)S(1)}, bf16[160,1024]{1,0:T(8,128)(2,1)S(1)}, f32[1,160]{1,0:T(1,128)S(1)}, bf16[176,1536]{1,0:T(8,128)(2,1)S(1)}) custom-call(f32[2,320,1280]{2,1,0:T(8,128)S(1)} %get-tuple-element.52.raws, f32[2,320,1280]{2,1,0:T(8,128)S(1)} %get-tuple-element.53.grads, f32[2,1,1280]{2,1,0:T(1,128)S(1)} %get-tuple-element.63.factors, ...), custom_call_target="tpu_custom_call" | custom-call | flops 4000000 | bytes 1000 | tf_op jit(solution)/shard_map/near_grads/pallas_call | solution.py:462
  20.2 0.2 collective-permute-start.5
  20.4 0.0 collective-permute-done.6.refs_0_
  20.4 0.8 %collective-permute-done.7.refs_1_ = bf16[160,256]{1,0:T(8,128)(2,1)S(1)} collective-permute-done((bf16[160,256]{1,0:T(8,128)(2,1)S(1)}, bf16[160,256]{1,0:T(8,128)(2,1)S(1)}, u32[]{:S(2)}, u32[]{:S(2)}) %collective-permute-start.7) | collective-permute-done | bytes 81952 | tf_op jit(solution)/shard_map/ppermute | solution.py:510
  21.2 2.3 %collective-permute-done.8.refs_0_ = bf16[160,256]{1,0:T(8,128)(2,1)S(1)} collective-permute-done((bf16[160,256]{1,0:T(8,128)(2,1)S(1)}, bf16[160,256]{1,0:T(8,128)(2,1)S(1)}, u32[]{:S(2)}, u32[]{:S(2)}) %collective-permute-start.8) | collective-permute-done | bytes 81952 | tf_op jit(solution)/shard_map/ppermute | solution.py:579
  23.6 1.2 %collective-permute-done.9.refs_0_ = bf16[160,256]{1,0:T(8,128)(2,1)S(1)} collective-permute-done((bf16[160,256]{1,0:T(8,128)(2,1)S(1)}, bf16[160,256]{1,0:T(8,128)(2,1)S(1)}, u32[]{:S(2)}, u32[]{:S(2)}) %collective-permute-start.9) | collective-permute-done | bytes 81952 | tf_op jit(solution)/shard_map/ppermute | solution.py:581
  24.8 0.0 collective-permute-done.5.back
  24.8 1.3 %finish.1 = (bf16[160,2048]{1,0:T(8,128)(2,1)}, bf16[160,512]{1,0:T(8,128)(2,1)}, bf16[160,512]{1,0:T(8,128)(2,1)}, f32[1,160]{1,0:T(1,128)}) custom-call(bf16[176,1536]{1,0:T(8,128)(2,1)S(1)} %collective-permute-done.5.back, bf16[160,1024]{1,0:T(8,128)(2,1)S(1)} %get-tuple-element.75.query_mine, f32[1,160]{1,0:T(1,128)S(1)} %get-tuple-element.76.gate_mine, ...), custom_call_target="tpu_custom_call" | custom-call | flops 1000000 | bytes 1000 | tf_op jit(solution)/shard_map/finish/pallas_call | solution.py:462
  (7 shorter events, 0.1 us)
Async XLA Ops:
  0.6 10.5 %copy-start = (bf16[1,160,2048]{2,1,0:T(8,128)(2,1)S(1)}, bf16[1,160,2048]{2,1,0:T(8,128)(2,1)}, u32[]{:S(2)}) copy-start(bf16[1,160,2048]{2,1,0:T(8,128)(2,1)} %param.7) | copy-start | bytes 1966084
  0.6 10.5 %copy-start.1 = (bf16[1,160,2048]{2,1,0:T(8,128)(2,1)S(1)}, bf16[1,160,2048]{2,1,0:T(8,128)(2,1)}, u32[]{:S(2)}) copy-start(bf16[1,160,2048]{2,1,0:T(8,128)(2,1)} %param.10) | copy-start | bytes 1966084
  2.2 8.9 %collective-permute-start = (bf16[176,2560]{1,0:T(8,128)(2,1)S(1)}, bf16[176,2560]{1,0:T(8,128)(2,1)S(1)}, u32[]{:S(2)}, u32[]{:S(2)}) collective-permute-start(bf16[176,2560]{1,0:T(8,128)(2,1)S(1)} %get-tuple-element.51), channel_id=1, source_target_pairs={{0,1},{1,0},{2,3},{3,2},{4,5},{5,4},{6,7},{7,6},{8,9},{9,8},{10,11... | collective-permute-start | bytes 2703368 | tf_op jit(solution)/shard_map/ppermute | solution.py:518
  2.8 10.0 %collective-permute-start.1 = (bf16[160,256]{1,0:T(8,128)(2,1)S(1)}, bf16[160,256]{1,0:T(8,128)(2,1)S(1)}, u32[]{:S(2)}, u32[]{:S(2)}) collective-permute-start(bf16[160,256]{1,0:T(8,128)(2,1)S(1)} %get-tuple-element.46.key_mine), channel_id=1, source_target_pairs={{0,2},{1,3},{4,6},{5,7},{8,10},{9,11},{12,14},{13,15},{16,18},{17,... | collective-permute-start | bytes 245768 | tf_op jit(solution)/shard_map/ppermute | solution.py:510
  7.2 5.6 %collective-permute-start.2 = (bf16[160,256]{1,0:T(8,128)(2,1)S(1)}, bf16[160,256]{1,0:T(8,128)(2,1)S(1)}, u32[]{:S(2)}, u32[]{:S(2)}) collective-permute-start(bf16[160,256]{1,0:T(8,128)(2,1)S(1)} %get-tuple-element.62), channel_id=1, source_target_pairs={{0,3},{1,2},{4,7},{5,6},{8,11},{9,10},{12,15},{13,14},{16,19},{17,... | collective-permute-start | bytes 245768 | tf_op jit(solution)/shard_map/ppermute | solution.py:511
  8.6 6.9 %collective-permute-start.4 = (bf16[160,256]{1,0:T(8,128)(2,1)S(1)}, bf16[160,256]{1,0:T(8,128)(2,1)S(1)}, u32[]{:S(2)}, u32[]{:S(2)}) collective-permute-start(bf16[160,256]{1,0:T(8,128)(2,1)S(1)} %get-tuple-element.69), channel_id=1, source_target_pairs={{0,3},{1,2},{4,7},{5,6},{8,11},{9,10},{12,15},{13,14},{16,19},{17,... | collective-permute-start | bytes 245768 | tf_op jit(solution)/shard_map/ppermute | solution.py:511
  9.9 5.6 %collective-permute-start.3 = (bf16[160,256]{1,0:T(8,128)(2,1)S(1)}, bf16[160,256]{1,0:T(8,128)(2,1)S(1)}, u32[]{:S(2)}, u32[]{:S(2)}) collective-permute-start(bf16[160,256]{1,0:T(8,128)(2,1)S(1)} %get-tuple-element.47.value_mine), channel_id=1, source_target_pairs={{0,2},{1,3},{4,6},{5,7},{8,10},{9,11},{12,14},{13,15},{16,18},{17,... | collective-permute-start | bytes 245768 | tf_op jit(solution)/shard_map/ppermute | solution.py:510
  12.8 7.6 %collective-permute-start.6 = (bf16[160,256]{1,0:T(8,128)(2,1)S(1)}, bf16[160,256]{1,0:T(8,128)(2,1)S(1)}, u32[]{:S(2)}, u32[]{:S(2)}) collective-permute-start(bf16[160,256]{1,0:T(8,128)(2,1)S(1)} %get-tuple-element.78), channel_id=1, source_target_pairs={{3,0},{2,1},{7,4},{6,5},{11,8},{10,9},{15,12},{14,13},{19,16},{18,... | collective-permute-start | bytes 245768 | tf_op jit(solution)/shard_map/ppermute | solution.py:511
  14.1 7.1 %collective-permute-start.7 = (bf16[160,256]{1,0:T(8,128)(2,1)S(1)}, bf16[160,256]{1,0:T(8,128)(2,1)S(1)}, u32[]{:S(2)}, u32[]{:S(2)}) collective-permute-start(bf16[160,256]{1,0:T(8,128)(2,1)S(1)} %get-tuple-element.79), channel_id=1, source_target_pairs={{2,0},{3,1},{6,4},{7,5},{10,8},{11,9},{14,12},{15,13},{18,16},{19,... | collective-permute-start | bytes 245768 | tf_op jit(solution)/shard_map/ppermute | solution.py:510
  15.5 8.1 %collective-permute-start.8 = (bf16[160,256]{1,0:T(8,128)(2,1)S(1)}, bf16[160,256]{1,0:T(8,128)(2,1)S(1)}, u32[]{:S(2)}, u32[]{:S(2)}) collective-permute-start(bf16[160,256]{1,0:T(8,128)(2,1)S(1)} %get-tuple-element.81), channel_id=1, source_target_pairs={{2,0},{3,1},{6,4},{7,5},{10,8},{11,9},{14,12},{15,13},{18,16},{19,... | collective-permute-start | bytes 245768 | tf_op jit(solution)/shard_map/ppermute | solution.py:579
  16.8 8.0 %collective-permute-start.9 = (bf16[160,256]{1,0:T(8,128)(2,1)S(1)}, bf16[160,256]{1,0:T(8,128)(2,1)S(1)}, u32[]{:S(2)}, u32[]{:S(2)}) collective-permute-start(bf16[160,256]{1,0:T(8,128)(2,1)S(1)} %far_rest.1), channel_id=1, source_target_pairs={{3,0},{2,1},{7,4},{6,5},{11,8},{10,9},{15,12},{14,13},{19,16},{18,... | collective-permute-start | bytes 245768 | tf_op jit(solution)/shard_map/ppermute | solution.py:581
  20.2 4.6 %collective-permute-start.5 = (bf16[176,1536]{1,0:T(8,128)(2,1)S(1)}, bf16[176,1536]{1,0:T(8,128)(2,1)S(1)}, u32[]{:S(2)}, u32[]{:S(2)}) collective-permute-start(bf16[176,1536]{1,0:T(8,128)(2,1)S(1)} %get-tuple-element.74), channel_id=1, source_target_pairs={{0,1},{1,0},{2,3},{3,2},{4,5},{5,4},{6,7},{7,6},{8,9},{9,8},{10,11... | collective-permute-start | bytes 1622024 | tf_op jit(solution)/shard_map/ppermute | solution.py:612
